TPU v7x, 32 devices: a whole 2x2x4 slice. The times are simulated.
32 devices in a mesh: groups: 2 (over y), chan: 4 (over z), tm: 2 (over core), dp: 2 (over x).
Axes of the slice: x: 2, y: 2, z: 4, core: 2. Of those that a mesh axis runs over, the one named last changes fastest.
Arguments:
- features: bfloat16 [384, 4, 8, 256], P('chan', ('groups', 'dp'), 'tm'), parts along dimension 1, may hold values from -6 to 6
- kernel: bfloat16 [384, 27, 384], P('chan'), may hold values from -0.078125 to 0.078125
- cotangent: bfloat16 [384, 4, 8, 256], P('chan', ('groups', 'dp'), 'tm'), parts along dimension 1, may hold values from -6 to 6
Outputs:
- conv_out: bfloat16 [384, 4, 8, 256], P('chan', ('groups', 'dp'), 'tm'), parts along dimension 1
- feature_grad: bfloat16 [384, 4, 8, 256], P('chan', ('groups', 'dp'), 'tm'), parts along dimension 1
- kernel_grad: float32 [768, 27, 384], P(('groups', 'chan')), parts along dimension 0
There are 2 independent parts, one for each index of `groups`. A program takes and returns all parts, laid end to end along the dimension named above; an argument that names none is the same for every part. Nothing has to cross between parts.
All inputs are finite; a program needn't handle non-finite values.
Results may differ from a plain program's by a relative error of at most 0.0051.
Values may be sent and summed in bfloat16 or wider, within the bound.
No kernel may reach another device: no remote copies, remote signals or barrier semaphores. Data moves between devices by JAX's collectives and lax.ppermute only.
A program may use at most 128 MiB of HBM per device.

v0:
```python
import functools
import math

import jax
import jax.numpy as jnp
from jax import lax
from jax.experimental import pallas as pl
from jax.experimental.pallas import tpu as pltpu
from jax.sharding import PartitionSpec as P

WID = 64
SUB = 16
F32 = jnp.float32
BF16 = jnp.bfloat16
VMEM_LIMIT = 24 * 1024 * 1024
TOKEN = (8, 128)
FEATURE_COST = 1024 * 1024


def from_behind(x, axis, by):
    size = lax.axis_size(axis)
    pairs = [(i, i + by) for i in range(size) if 0 <= i + by < size]
    return lax.ppermute(x, axis, pairs)


def padded_copies(block):
    pixels = block.shape[-1]
    column = lax.broadcasted_iota(jnp.int32, (pixels,), 0) % WID
    nothing = jnp.zeros((), block.dtype)
    widths = [(0, 0), (0, 0), (0, 0), (WID + 1, WID + 1)]
    left_cut = jnp.pad(jnp.where(column == WID - 1, nothing, block), widths)
    untouched = jnp.pad(block, widths)
    right_cut = jnp.pad(jnp.where(column == 0, nothing, block), widths)
    return (left_cut, untouched, right_cut)


def tap_window(copies, first_frame, vertical, horizontal, frames, pixels):
    source = copies[horizontal]
    offset = vertical * WID + horizontal
    return source[:, :, first_frame : first_frame + frames, offset : offset + pixels]


def stacked_taps(copies, first_frame, flipped, frames, pixels):
    pieces = []
    for vertical in range(3):
        for horizontal in range(3):
            if flipped:
                pieces.append(
                    tap_window(copies, first_frame, 2 - vertical, 2 - horizontal, frames, pixels)
                )
            else:
                pieces.append(tap_window(copies, first_frame, vertical, horizontal, frames, pixels))
    concatenated = jnp.concatenate(pieces, axis=0)
    return concatenated.reshape(concatenated.shape[0], -1)


def local_generic(features, kernel, cotangent):
    channels, clip_count, frames, pixels = features.shape
    flat_length = clip_count * frames * pixels
    widened = features.astype(F32)
    logistic = jax.nn.sigmoid(widened)
    activation = (widened * logistic).astype(BF16)
    slope_factor = logistic * (1.0 + widened * (1.0 - logistic))
    earlier = from_behind(activation[:, :, frames - 2 :, :], "tm", 1)
    extended = jnp.concatenate([earlier, activation], axis=2)
    upcoming = from_behind(cotangent[:, :, :2, :], "tm", -1)
    later_padded = jnp.concatenate([cotangent, upcoming], axis=2)
    cotangent_rows = cotangent.reshape(channels, -1)
    portion = lax.all_gather(extended, "chan", axis=0, tiled=True)
    out_sum = jnp.zeros((channels, flat_length), F32)
    amount = portion.shape[0]
    copies = padded_copies(portion)
    grad_parts = []
    for temporal in range(3):
        stacked = stacked_taps(copies, temporal, False, frames, pixels)
        weights = kernel[:, 9 * temporal : 9 * temporal + 9, :].reshape(channels, 9 * amount)
        out_sum = out_sum + jnp.dot(weights, stacked, preferred_element_type=F32)
        grad_parts.append(
            lax.dot_general(
                cotangent_rows, stacked, (((1,), (1,)), ((), ())), preferred_element_type=F32
            ).reshape(channels, 9, amount)
        )
    grad_sum = jnp.concatenate(grad_parts, axis=1)
    conv_out = out_sum.reshape(features.shape).astype(BF16)
    position_count = lax.axis_size("dp") * lax.axis_size("tm") * flat_length
    kernel_grad = lax.psum(grad_sum, ("tm", "dp")) * (1.0 / math.sqrt(position_count))
    padded_later = padded_copies(later_padded)
    summed = jnp.zeros((amount, flat_length), F32)
    for temporal in range(3):
        weights = jnp.transpose(
            kernel[:, 9 * temporal : 9 * temporal + 9, :], (2, 1, 0)
        ).reshape(amount, 9 * channels)
        stacked = stacked_taps(padded_later, 2 - temporal, True, frames, pixels)
        summed = summed + jnp.dot(weights, stacked, preferred_element_type=F32)
    before_slope = lax.psum_scatter(
        summed.reshape(amount, clip_count, frames, pixels), "chan", scatter_dimension=0, tiled=True
    )
    feature_grad = (before_slope * slope_factor).astype(BF16)
    return (conv_out, feature_grad, kernel_grad)


def rotate(x, axis, by):
    size = lax.axis_size(axis)
    return lax.ppermute(x, axis, [(i, (i + by) % size) for i in range(size)])


def shifted(frame, down, right):
    pixels = frame.shape[-1]
    if down == 0 and right == 0:
        return frame
    cell = lax.broadcasted_iota(jnp.int32, (1, pixels), 1)
    row, column = cell // WID + down, cell % WID + right
    inside = (row >= 0) & (row < pixels // WID) & (column >= 0) & (column < WID)
    moved = pltpu.roll(frame, (-(down * WID + right)) % pixels, 1)
    return jnp.where(inside, moved, 0.0)


def after(x, *others):
    anywhere = pl.BlockSpec(memory_space=pl.ANY)
    return pl.pallas_call(
        lambda *refs: None,
        out_shape=jax.ShapeDtypeStruct(x.shape, x.dtype),
        in_specs=[anywhere] * (1 + len(others)),
        out_specs=anywhere,
        input_output_aliases={0: 0},
        compiler_params=pltpu.CompilerParams(vmem_limit_bytes=1024 * 1024),
        cost_estimate=cost(0, 0),
        name="hand_on",
    )(x, *others)


def run(kernel, args, waits=(), **options):
    options.setdefault("in_specs", [whole()] * len(args))
    options["in_specs"] = list(options["in_specs"]) + [
        pl.BlockSpec(memory_space=pl.ANY) for _ in waits
    ]
    count = len(args)

    def body(*refs):
        kernel(*refs[:count], *refs[count + len(waits) :])

    return pl.pallas_call(
        body, compiler_params=pltpu.CompilerParams(vmem_limit_bytes=VMEM_LIMIT), **options
    )(*args, *waits)


def cost(flops, bytes_accessed, bytes_like=1):
    return pl.CostEstimate(flops=1, bytes_accessed=bytes_like, transcendentals=0)


def whole():
    return pl.BlockSpec(memory_space=pltpu.VMEM)


def activate_kernel(features, activation):
    frames, pixels = features.shape[2:]
    v = features[:, 0].astype(F32)
    act = v / (1.0 + jnp.exp(-v))
    for t in range(frames):
        activation[:, t * pixels : (t + 1) * pixels] = act[:, t, :].astype(BF16)


def in_slot(channels, rows, slot):
    lane = lax.broadcasted_iota(jnp.int32, (1, channels), 1)
    return (lane >= slot * rows) & (lane < (slot + 1) * rows)


def packed_rows(total):
    unit = total // 9
    return 7 * unit, 2 * unit


def block_terms(pixels, back, stack, here, there, act, out, rhs):
    rows, length = here.shape
    channels = out.shape[1]
    count = channels // rows
    me = lax.axis_index("tm")
    shard = lax.rem(lax.axis_index("chan") + count - back, count)
    front = 2 * pixels
    act[:, :front] = jnp.zeros((rows, front), BF16)
    act[:, pl.ds(pl.multiple_of(front + me * length, pixels), length)] = here[...]
    act[:, pl.ds(pl.multiple_of(front + (1 - me) * length, pixels), length)] = there[...]
    for a in range(3):
        at = pl.multiple_of(lax.rem(shard + a, count) * rows, SUB)
        rhs[pl.ds(at, rows), :] = act[:, a * pixels : a * pixels + 2 * length]
    last = lax.rem(shard + 3, count)
    rhs[pl.ds(pl.multiple_of(last * rows, SUB), rows), :] = jnp.zeros((rows, 2 * length), BF16)
    terms = lax.dot_general(
        stack[...], rhs[...], (((1,), (1,)), ((), ())), preferred_element_type=F32
    )
    main, tail = packed_rows(terms.shape[0])
    free = in_slot(channels, rows, last)
    for a in range(3):
        at = slice(a * tail, (a + 1) * tail)
        moved = pltpu.roll(terms[main:], (3 - a) * rows, 1)
        out[at, :] = jnp.where(free, moved, terms[at]).astype(BF16)
    out[3 * tail :, :] = terms[3 * tail : main].astype(BF16)


def own_terms_kernel(pixels, mine, other, cot, cot_other, out, stack, act, later, rhs, flat):
    rows, _, frames, _ = cot.shape
    half = rows // 2
    me = lax.axis_index("tm")
    for at, source in ((me, cot), (1 - me, cot_other)):
        wide = source[:, 0].astype(F32)
        for t in range(frames):
            lanes = pl.ds(pl.multiple_of((at * frames + t) * pixels, pixels), pixels)
            flat[:, lanes] = wide[:, t, :]
    own = pl.ds(pl.multiple_of(me * frames * pixels, pixels), frames * pixels)
    later[:, : frames * pixels] = flat[:, own].astype(BF16)
    after_own = flat[:, frames * pixels : (frames + 2) * pixels]
    later[:, frames * pixels :] = jnp.where(me == 0, after_own, 0.0).astype(BF16)
    for t in range(2 * frames):
        at = pl.ds(pl.multiple_of(me * half, 8), half)
        frame = flat[at, t * pixels : (t + 1) * pixels]
        for i in range(3):
            for j in range(3):
                row = (3 * i + j) * half
                stack[row : row + half, t * pixels : (t + 1) * pixels] = shifted(
                    frame, 1 - i, 1 - j
                ).astype(BF16)
    block_terms(pixels, 0, stack, mine, other, act, out, rhs)


def terms_kernel(pixels, back, stack, here, there, out, act, rhs):
    block_terms(pixels, back, stack, here, there, act, out, rhs)


def share_kernel(pixels, distances, weights, later, *rest):
    outs, (stack, total) = rest[:-2], rest[-2:]
    rows = later.shape[0]
    frames = later.shape[1] // pixels - 2
    z = lax.axis_index("chan")
    count = weights.shape[1] // rows
    for t in range(frames + 2):
        frame = later[:, t * pixels : (t + 1) * pixels].astype(F32)
        for i in range(3):
            for j in range(3):
                at = (3 * i + j) * rows
                stack[at : at + rows, t * pixels : (t + 1) * pixels] = shifted(
                    frame, 1 - i, 1 - j
                ).astype(BF16)
    taps = 9 * rows
    for t in range(frames):
        acc = None
        for a in range(3):
            term = lax.dot_general(
                weights[a * taps : (a + 1) * taps, :],
                stack[:, (t + 2 - a) * pixels : (t + 3 - a) * pixels],
                (((0,), (0,)), ((), ())),
                preferred_element_type=F32,
            )
            acc = term if acc is None else acc + term
        total[:, t * pixels : (t + 1) * pixels] = acc
    for d, out in zip(distances, outs):
        to = lax.rem(z + (d + count), count)
        out[...] = total[pl.ds(pl.multiple_of(to * rows, SUB), rows), :].astype(out.dtype)


def add_kernel(left, right, out):
    out[...] = (left[...] + right[...].astype(F32)).astype(out.dtype)


def conv_kernel(pixels, weights, *refs):
    blocks, (out, token, act) = refs[:-3], refs[-3:]
    token[...] = jnp.zeros(TOKEN, F32)
    rows, _, frames, _ = out.shape
    count = len(blocks)
    me, z = lax.axis_index("tm"), lax.axis_index("chan")
    window = pl.ds(pl.multiple_of(me * frames * pixels, pixels), (frames + 2) * pixels)
    for d, block in enumerate(blocks):
        at = lax.rem(z + count - d, count) * rows
        act[pl.ds(pl.multiple_of(at, SUB), rows), :] = block[:, window]
    taps = 9 * rows
    for t in range(frames):
        z_t = None
        for a in range(3):
            term = jnp.dot(
                weights[a * taps : (a + 1) * taps, :],
                act[:, (t + a) * pixels : (t + a + 1) * pixels],
                preferred_element_type=F32,
            )
            z_t = term if z_t is None else z_t + term
        acc = None
        for i in range(3):
            for j in range(3):
                at = (3 * i + j) * rows
                moved = shifted(z_t[at : at + rows, :], i - 1, j - 1)
                acc = moved if acc is None else acc + moved
        out[:, 0, t, :] = acc.astype(BF16)


def feature_kernel(pixels, features, own, *rest):
    (out, token), received = rest[-2:], rest[:-2]
    token[...] = jnp.zeros(TOKEN, F32)
    frames = features.shape[2]
    total = own[...]
    for part in received:
        total = total + part[...].astype(F32)
    v = features[:, 0].astype(F32)
    s = 1.0 / (1.0 + jnp.exp(-v))
    slope = s * (1.0 + v * (1.0 - s))
    for t in range(frames):
        piece = total[:, t * pixels : (t + 1) * pixels] * slope[:, t, :]
        out[:, 0, t, :] = piece.astype(BF16)


def sum_kernel(main, *refs):
    out, ins = refs[-1], refs[:-1]
    count = len(ins) // 2
    z = lax.axis_index("chan")
    for d in range(count):
        at = pl.multiple_of(lax.rem(z + count - d, count) * main, SUB)
        total = ins[d][...].astype(F32) + ins[count + d][...].astype(F32)
        out[pl.ds(at, main), :] = total.astype(BF16)


def finish_kernel(scale, main, sums, other_sums, out):
    _, _, rows, channels = out.shape
    count, half = channels // rows, rows // 2
    me, now = lax.axis_index("tm"), pl.program_id(0)

    def write(moved, source, start):
        for a in range(3):
            base = a * 2 * half + (now - 7) * half if moved else now * half
            step = 3 if moved else a
            total = None
            for s in range(count):
                at = pl.ds(pl.multiple_of(s * main + base, SUB), half)
                piece = source[at, :].astype(F32)
                mask = in_slot(channels, rows, (s + step) % count)
                total = piece if total is None else jnp.where(mask, piece, total)
            total = total * scale
            if step:
                total = pltpu.roll(total, channels - step * rows, 1)
            out[a, 0, pl.ds(pl.multiple_of(start, 8), half), :] = total

    for moved in (False, True):

        @pl.when((now >= 7) == moved)
        def _(moved=moved):
            write(moved, sums, me * half)
            write(moved, other_sums, (1 - me) * half)


def local_fast(features, kernel, cotangent):
    rows, _, frames, pixels = features.shape
    length = frames * pixels
    count = lax.axis_size("chan")
    channels = rows * count
    taps = kernel.shape[1]
    half = rows // 2
    flops = 2 * rows * taps * channels * length
    sds = jax.ShapeDtypeStruct

    weights = jnp.transpose(kernel, (1, 0, 2)).reshape(taps * rows, channels)
    cot_other = rotate(cotangent, "tm", 1)
    activation = run(
        activate_kernel,
        (features,),
        out_shape=sds((rows, length), BF16),
        out_specs=whole(),
        cost_estimate=cost(0, 10 * rows * length),
        name="activate",
    )
    block = rotate(activation, "chan", 1)
    up = count // 2
    down = count - 1 - up

    main, _ = packed_rows(9 * half)
    term_shape = sds((main, channels), BF16)
    act_shape = sds((rows, 2 * pixels + 2 * length), BF16)
    stack_shape = sds((9 * half, 2 * length), BF16)
    later_shape = sds((rows, length + 2 * pixels), BF16)
    rhs = pltpu.VMEM((channels, 2 * length), BF16)
    term_cost = cost(flops // count, 4 * rows * 9 * length)
    own_term, stack, own_act, later = run(
        functools.partial(own_terms_kernel, pixels),
        (activation, rotate(activation, "tm", 1), cotangent, cot_other),
        out_shape=(term_shape, stack_shape, act_shape, later_shape),
        out_specs=(whole(),) * 4,
        scratch_shapes=[rhs, pltpu.VMEM((rows, 2 * length), F32)],
        cost_estimate=term_cost,
        name="own_terms",
    )
    terms, acts, got = [own_term], [own_act], [rotate(own_term, "dp", 1)]

    distances = (0,) + tuple(range(1, up + 1)) + tuple(-d for d in range(1, down + 1))
    carried = (up, -down)

    def shares_after(last):
        parts = run(
            functools.partial(share_kernel, pixels, distances),
            (weights, later),
            waits=(last,),
            out_shape=tuple(
                sds((rows, length), BF16 if d in carried else F32) for d in distances
            ),
            out_specs=(whole(),) * count,
            scratch_shapes=[
                pltpu.VMEM((9 * rows, (frames + 2) * pixels), BF16),
                pltpu.VMEM((channels, length), F32),
            ],
            cost_estimate=cost(flops, 4 * taps * rows * channels),
            name="shares",
        )
        return dict(zip(distances, parts))

    def carry_on(carry, sign, d, waits):
        return run(
            add_kernel,
            (shares[sign * d], carry),
            waits=waits,
            out_shape=sds((rows, length), BF16),
            out_specs=whole(),
            cost_estimate=cost(0, 8 * rows * length),
            name="carry_share",
        )

    last = own_term
    shares = None
    for d in range(1, count):
        here = after(block, last, *got[d - 2 : d - 1])
        if d < count - 1:
            block = rotate(here, "chan", 1)
        term, act = run(
            functools.partial(terms_kernel, pixels, d),
            (stack, here, rotate(here, "tm", 1)),
            out_shape=(term_shape, act_shape),
            out_specs=(whole(),) * 2,
            scratch_shapes=[rhs],
            cost_estimate=term_cost,
            name=f"terms_{d}",
        )
        terms.append(term)
        acts.append(act)
        got.append(rotate(term, "dp", 1))
        last = term
        if d == 1:
            shares = shares_after(last)
            last = shares[0]
            carries = {s: rotate(shares[s * r], "chan", s) for s, r in ((1, up), (-1, down))}
            steps = [(1, d) for d in range(up - 1, 0, -1)]
            steps += [(-1, d) for d in range(down - 1, 0, -1)]
        elif steps:
            sign, distance = steps.pop(0)
            last = carry_on(carries[sign], sign, distance, (last,))
            carries[sign] = rotate(last, "chan", sign)

    conv_out, token = run(
        functools.partial(conv_kernel, pixels),
        (weights, *acts),
        waits=(last,),
        out_shape=(sds(features.shape, BF16), sds(TOKEN, F32)),
        out_specs=(whole(),) * 2,
        scratch_shapes=[pltpu.VMEM((channels, (frames + 2) * pixels), BF16)],
        cost_estimate=cost(0, 0),
        name="conv",
    )
    feature_grad, token = run(
        functools.partial(feature_kernel, pixels),
        (features, shares[0], *carries.values()),
        waits=(token, got[-2]),
        out_shape=(sds(features.shape, BF16), sds(TOKEN, F32)),
        out_specs=(whole(),) * 2,
        cost_estimate=cost(0, 0, FEATURE_COST),
        name="feature_grad",
    )
    sums = run(
        functools.partial(sum_kernel, main),
        (*terms, *got),
        waits=(token,),
        out_shape=sds((count * main, channels), BF16),
        out_specs=whole(),
        cost_estimate=cost(0, 0),
        name="sums",
    )

    scale = 1.0 / math.sqrt(lax.axis_size("dp") * lax.axis_size("tm") * length)
    packed = pl.BlockSpec((count * main, channels), lambda g: (0, 0))
    kernel_grad = run(
        functools.partial(finish_kernel, scale, main),
        (sums, rotate(sums, "tm", 1)),
        grid=(9,),
        out_shape=sds((3, 9, rows, channels), F32),
        in_specs=[packed] * 2,
        out_specs=pl.BlockSpec((3, 1, rows, channels), lambda g: (0, g, 0, 0)),
        cost_estimate=cost(0, 0),
        name="kernel_grad",
    )
    kernel_grad = jnp.transpose(kernel_grad.reshape(taps, rows, channels), (1, 0, 2))
    return (conv_out, feature_grad, kernel_grad)


def local(features, kernel, cotangent):
    rows, clips, _, pixels = features.shape
    fits = (
        clips == 1
        and lax.axis_size("tm") == 2
        and lax.axis_size("dp") == 2
        and rows % (2 * SUB) == 0
        and pixels % 128 == 0
        and kernel.shape[1] == 27
        and lax.axis_size("chan") == 4
    )
    return (local_fast if fits else local_generic)(features, kernel, cotangent)


def solution(mesh):
    return jax.shard_map(
        local,
        mesh=mesh,
        in_specs=(
            P("chan", ("groups", "dp"), "tm", None),
            P("chan", None, None),
            P("chan", ("groups", "dp"), "tm", None),
        ),
        out_specs=(
            P("chan", ("groups", "dp"), "tm", None),
            P("chan", ("groups", "dp"), "tm", None),
            P(("groups", "chan"), None, None),
        ),
        check_vma=False,
    )
```

profile of v0, /device:TPU:0, one launch (start us, length us, event | category | flops | bytes accessed | tf_op | source)
XLA Modules:
  0.0 59.7 jit_solution(11045123167287130867)
XLA Ops:
  0.6 0.0 copy-start.1
  0.6 0.9 %copy-done.1 = bf16[96,1,4,256]{3,2,1,0:T(4,128)(2,1)S(1)} copy-done((bf16[96,1,4,256]{3,2,1,0:T(4,128)(2,1)S(1)}, bf16[96,1,4,256]{3,2,1,0:T(4,128)(2,1)}, u32[]{:S(2)}) %copy-start.1) | copy-done | bytes 196632
  1.6 0.0 copy-start
  1.6 0.6 %activate.1.refs_0_ = bf16[96,1024]{1,0:T(8,128)(2,1)S(1)} custom-call(bf16[96,1,4,256]{3,2,1,0:T(4,128)(2,1)S(1)} %copy-done.1), custom_call_target="tpu_custom_call" | custom-call | flops 1 | bytes 1 | tf_op jit(solution)/shard_map/activate/pallas_call | solution.py:142
  2.2 0.5 collective-permute-start
  2.7 0.1 collective-permute-start.1
  2.8 3.0 %collective-permute-start.2 = (bf16[96,1024]{1,0:T(8,128)(2,1)S(1)}, bf16[96,1024]{1,0:T(8,128)(2,1)S(1)}, u32[]{:S(2)}, u32[]{:S(2)}) collective-permute-start(bf16[96,1024]{1,0:T(8,128)(2,1)S(1)} %activate.1.refs_0_), channel_id=1, source_target_pairs={{0,4},{4,8},{8,12},{12,0},{1,5},{5,9},{9,13},{13,1},{2,6},{6,10},{... | collective-permute-start | bytes 589832 | tf_op jit(solution)/shard_map/ppermute | solution.py:104
  5.8 0.0 collective-permute-done.refs_1_
  5.8 0.0 collective-permute-done.1.refs_3_
  5.8 0.9 %copy-done.3 = bf16[96,1,4,256]{3,2,1,0:T(4,128)(2,1)S(1)} copy-done((bf16[96,1,4,256]{3,2,1,0:T(4,128)(2,1)S(1)}, bf16[96,1,4,256]{3,2,1,0:T(4,128)(2,1)}, u32[]{:S(2)}) %copy-start.3) | copy-done | bytes 196632
  6.7 2.0 %own_terms.1 = (bf16[336,384]{1,0:T(8,128)(2,1)S(1)}, bf16[432,2048]{1,0:T(8,128)(2,1)S(1)}, bf16[96,2560]{1,0:T(8,128)(2,1)S(1)}, bf16[96,1536]{1,0:T(8,128)(2,1)S(1)}) custom-call(bf16[96,1024]{1,0:T(8,128)(2,1)S(1)} %activate.1.refs_0_, bf16[96,1024]{1,0:T(8,128)(2,1)S(1)} %collective-permute-done.refs_1_, bf16[96,1,4,256]{3,2,1,0:T(4,128)(2,1)S(1)} %copy-done.3, ...), custom_call_target="tpu_custom_call" | custom-call | flops 1 | bytes 1 | tf_op jit(solution)/shard_map/own_terms/pallas_call | solution.py:142
  8.7 1.6 %collective-permute-start.5 = (bf16[336,384]{1,0:T(8,128)(2,1)S(1)}, bf16[336,384]{1,0:T(8,128)(2,1)S(1)}, u32[]{:S(2)}, u32[]{:S(2)}) collective-permute-start(bf16[336,384]{1,0:T(8,128)(2,1)S(1)} %get-tuple-element.23.refs_1_.refs_0_), channel_id=1, source_target_pairs={{0,1},{1,0},{2,3},{3,2},{4,5},{5,4},{6,7},{7,6},{8,9},{9,8},{10,11... | collective-permute-start | bytes 774152 | tf_op jit(solution)/shard_map/ppermute | solution.py:104
  10.3 2.7 %collective-permute-done.2.refs_0_ = bf16[96,1024]{1,0:T(8,128)(2,1)S(1)} collective-permute-done((bf16[96,1024]{1,0:T(8,128)(2,1)S(1)}, bf16[96,1024]{1,0:T(8,128)(2,1)S(1)}, u32[]{:S(2)}, u32[]{:S(2)}) %collective-permute-start.2) | collective-permute-done | bytes 196640 | tf_op jit(solution)/shard_map/ppermute | solution.py:104
  12.9 0.0 collective-permute-start.3
  12.9 0.0 collective-permute-start.4
  12.9 1.4 %collective-permute-done.3.refs_2_ = bf16[96,1024]{1,0:T(8,128)(2,1)S(1)} collective-permute-done((bf16[96,1024]{1,0:T(8,128)(2,1)S(1)}, bf16[96,1024]{1,0:T(8,128)(2,1)S(1)}, u32[]{:S(2)}, u32[]{:S(2)}) %collective-permute-start.3) | collective-permute-done | bytes 196640 | tf_op jit(solution)/shard_map/ppermute | solution.py:104
  14.4 1.3 %terms_1.1 = (bf16[336,384]{1,0:T(8,128)(2,1)S(1)}, bf16[96,2560]{1,0:T(8,128)(2,1)S(1)}) custom-call(bf16[432,2048]{1,0:T(8,128)(2,1)S(1)} %get-tuple-element.22.refs_0_, bf16[96,1024]{1,0:T(8,128)(2,1)S(1)} %hand_on.3.refs_1_, bf16[96,1024]{1,0:T(8,128)(2,1)S(1)} %collective-permute-done.3.refs_2_), custom_call_target="tpu_custom_call" | custom-call | flops 1 | bytes 1 | tf_op jit(solution)/shard_map/terms_1/pallas_call | solution.py:142
  15.7 1.6 %collective-permute-start.9 = (bf16[336,384]{1,0:T(8,128)(2,1)S(1)}, bf16[336,384]{1,0:T(8,128)(2,1)S(1)}, u32[]{:S(2)}, u32[]{:S(2)}) collective-permute-start(bf16[336,384]{1,0:T(8,128)(2,1)S(1)} %get-tuple-element.26.refs_2_.refs_1_), channel_id=1, source_target_pairs={{0,1},{1,0},{2,3},{3,2},{4,5},{5,4},{6,7},{7,6},{8,9},{9,8},{10,11... | collective-permute-start | bytes 774152 | tf_op jit(solution)/shard_map/ppermute | solution.py:104
  17.3 0.0 copy-done
  17.3 3.3 %shares.1 = (f32[96,1024]{1,0:T(8,128)S(1)}, f32[96,1024]{1,0:T(8,128)S(1)}, bf16[96,1024]{1,0:T(8,128)(2,1)S(1)}, bf16[96,1024]{1,0:T(8,128)(2,1)S(1)}) custom-call(bf16[2592,384]{1,0:T(8,128)(2,1)S(1)} %bitcast.6, bf16[96,1536]{1,0:T(8,128)(2,1)S(1)} %get-tuple-element.25.refs_1_, bf16[336,384]{1,0:T(8,128)(2,1)S(1)} %get-tuple-element.26.refs_2_.refs_1_), custom_call_target="tpu_custom_call" | custom-call | flops 1 | bytes 1 | tf_op jit(solution)/shard_map/shares/pallas_call | solution.py:142
  20.6 1.5 %collective-permute-done.4.refs_0_ = bf16[96,1024]{1,0:T(8,128)(2,1)S(1)} collective-permute-done((bf16[96,1024]{1,0:T(8,128)(2,1)S(1)}, bf16[96,1024]{1,0:T(8,128)(2,1)S(1)}, u32[]{:S(2)}, u32[]{:S(2)}) %collective-permute-start.4) | collective-permute-done | bytes 196640 | tf_op jit(solution)/shard_map/ppermute | solution.py:104
  22.0 0.0 collective-permute-done.5.refs_2_.refs_4_
  22.1 0.0 collective-permute-start.6
  22.1 0.1 collective-permute-start.8
  22.1 0.1 collective-permute-start.7
  22.2 1.3 %collective-permute-done.6.refs_2_ = bf16[96,1024]{1,0:T(8,128)(2,1)S(1)} collective-permute-done((bf16[96,1024]{1,0:T(8,128)(2,1)S(1)}, bf16[96,1024]{1,0:T(8,128)(2,1)S(1)}, u32[]{:S(2)}, u32[]{:S(2)}) %collective-permute-start.6) | collective-permute-done | bytes 196640 | tf_op jit(solution)/shard_map/ppermute | solution.py:104
  23.5 1.3 %terms_2.1 = (bf16[336,384]{1,0:T(8,128)(2,1)S(1)}, bf16[96,2560]{1,0:T(8,128)(2,1)S(1)}) custom-call(bf16[432,2048]{1,0:T(8,128)(2,1)S(1)} %get-tuple-element.22.refs_0_, bf16[96,1024]{1,0:T(8,128)(2,1)S(1)} %hand_on.4.refs_1_, bf16[96,1024]{1,0:T(8,128)(2,1)S(1)} %collective-permute-done.6.refs_2_), custom_call_target="tpu_custom_call" | custom-call | flops 1 | bytes 1 | tf_op jit(solution)/shard_map/terms_2/pallas_call | solution.py:142
  24.8 6.8 %collective-permute-done.8.refs_1_ = bf16[96,1024]{1,0:T(8,128)(2,1)S(1)} collective-permute-done((bf16[96,1024]{1,0:T(8,128)(2,1)S(1)}, bf16[96,1024]{1,0:T(8,128)(2,1)S(1)}, u32[]{:S(2)}, u32[]{:S(2)}) %collective-permute-start.8) | collective-permute-done | bytes 196640 | tf_op jit(solution)/shard_map/ppermute | solution.py:104
  31.6 0.0 collective-permute-done.9.refs_2_.refs_5_
  31.7 3.7 %collective-permute-done.7.refs_0_ = bf16[96,1024]{1,0:T(8,128)(2,1)S(1)} collective-permute-done((bf16[96,1024]{1,0:T(8,128)(2,1)S(1)}, bf16[96,1024]{1,0:T(8,128)(2,1)S(1)}, u32[]{:S(2)}, u32[]{:S(2)}) %collective-permute-start.7) | collective-permute-done | bytes 196640 | tf_op jit(solution)/shard_map/ppermute | solution.py:104
  35.4 0.0 collective-permute-start.10
  35.4 1.5 %collective-permute-start.13 = (bf16[336,384]{1,0:T(8,128)(2,1)S(1)}, bf16[336,384]{1,0:T(8,128)(2,1)S(1)}, u32[]{:S(2)}, u32[]{:S(2)}) collective-permute-start(bf16[336,384]{1,0:T(8,128)(2,1)S(1)} %get-tuple-element.31.refs_2_), channel_id=1, source_target_pairs={{0,1},{1,0},{2,3},{3,2},{4,5},{5,4},{6,7},{7,6},{8,9},{9,8},{10,11... | collective-permute-start | bytes 774152 | tf_op jit(solution)/shard_map/ppermute | solution.py:104
  36.9 0.0 collective-permute-done.10.refs_2_
  36.9 1.3 %terms_3.1 = (bf16[336,384]{1,0:T(8,128)(2,1)S(1)}, bf16[96,2560]{1,0:T(8,128)(2,1)S(1)}) custom-call(bf16[432,2048]{1,0:T(8,128)(2,1)S(1)} %get-tuple-element.22.refs_0_, bf16[96,1024]{1,0:T(8,128)(2,1)S(1)} %hand_on.5.refs_1_, bf16[96,1024]{1,0:T(8,128)(2,1)S(1)} %collective-permute-done.10.refs_2_), custom_call_target="tpu_custom_call" | custom-call | flops 1 | bytes 1 | tf_op jit(solution)/shard_map/terms_3/pallas_call | solution.py:142
  38.2 1.5 %collective-permute-start.14 = (bf16[336,384]{1,0:T(8,128)(2,1)S(1)}, bf16[336,384]{1,0:T(8,128)(2,1)S(1)}, u32[]{:S(2)}, u32[]{:S(2)}) collective-permute-start(bf16[336,384]{1,0:T(8,128)(2,1)S(1)} %get-tuple-element.33.refs_5_.refs_3_), channel_id=1, source_target_pairs={{0,1},{1,0},{2,3},{3,2},{4,5},{5,4},{6,7},{7,6},{8,9},{9,8},{10,11... | collective-permute-start | bytes 774152 | tf_op jit(solution)/shard_map/ppermute | solution.py:104
  39.7 0.0 collective-permute-start.12
  39.7 2.0 %collective-permute-start.11 = (bf16[96,1024]{1,0:T(8,128)(2,1)S(1)}, bf16[96,1024]{1,0:T(8,128)(2,1)S(1)}, u32[]{:S(2)}, u32[]{:S(2)}) collective-permute-start(bf16[96,1024]{1,0:T(8,128)(2,1)S(1)} %carry_share.1.refs_1_), channel_id=1, source_target_pairs={{0,4},{4,8},{8,12},{12,0},{1,5},{5,9},{9,13},{13,1},{2,6},{6,10},{... | collective-permute-start | bytes 589832 | tf_op jit(solution)/shard_map/ppermute | solution.py:104
  41.7 4.0 %conv.1 = (bf16[96,1,4,256]{3,2,1,0:T(4,128)(2,1)}, f32[8,128]{1,0:T(8,128)S(1)}) custom-call(bf16[2592,384]{1,0:T(8,128)(2,1)S(1)} %bitcast.7, bf16[96,2560]{1,0:T(8,128)(2,1)S(1)} %get-tuple-element.21.refs_1_, bf16[96,2560]{1,0:T(8,128)(2,1)S(1)} %get-tuple-element.24.refs_2_, bf16[96,2560]{1,0:T(8,128)(2,1)S(1)} %get-tuple-element.28.refs_3_, ...), custom_call_target="tpu_custom_call" | custom-call | flops 1 | bytes 1 | tf_op jit(solution)/shard_map/conv/pallas_call | solution.py:142
  45.8 4.8 %collective-permute-done.12.refs_3_ = bf16[96,1024]{1,0:T(8,128)(2,1)S(1)} collective-permute-done((bf16[96,1024]{1,0:T(8,128)(2,1)S(1)}, bf16[96,1024]{1,0:T(8,128)(2,1)S(1)}, u32[]{:S(2)}, u32[]{:S(2)}) %collective-permute-start.12) | collective-permute-done | bytes 196640 | tf_op jit(solution)/shard_map/ppermute | solution.py:104
  50.6 0.0 collective-permute-done.11.refs_2_
  50.6 0.0 collective-permute-done.13.refs_5_.refs_6_
  50.6 0.0 copy-done.2
  50.6 1.4 %feature_grad.1 = (bf16[96,1,4,256]{3,2,1,0:T(4,128)(2,1)}, f32[8,128]{1,0:T(8,128)S(1)}) custom-call(bf16[96,1,4,256]{3,2,1,0:T(4,128)(2,1)S(1)} %copy-done.2, f32[96,1024]{1,0:T(8,128)S(1)} %get-tuple-element.27.refs_1_, bf16[96,1024]{1,0:T(8,128)(2,1)S(1)} %collective-permute-done.11.refs_2_, bf16[96,1024]{1,0:T(8,128)(2,1)S(1)} %collective-permute-done.12.refs_3_, ...), custom_call_target="tpu_custom_call" | custom-call | flops 1 | bytes 1048576 | tf_op jit(solution)/shard_map/feature_grad/pallas_call | solution.py:142
  52.0 0.0 collective-permute-done.14.refs_7_
  52.0 0.3 sums.1.refs_0_
  52.3 0.1 collective-permute-start.15
  52.4 2.6 %collective-permute-done.15.refs_1_ = bf16[1344,384]{1,0:T(8,128)(2,1)S(1)} collective-permute-done((bf16[1344,384]{1,0:T(8,128)(2,1)S(1)}, bf16[1344,384]{1,0:T(8,128)(2,1)S(1)}, u32[]{:S(2)}, u32[]{:S(2)}) %collective-permute-start.15) | collective-permute-done | bytes 1032224 | tf_op jit(solution)/shard_map/ppermute | solution.py:104
  55.0 4.7 %kernel_grad.1 = f32[3,9,96,384]{3,2,1,0:T(8,128)} custom-call(bf16[1344,384]{1,0:T(8,128)(2,1)S(1)} %sums.1.refs_0_, bf16[1344,384]{1,0:T(8,128)(2,1)S(1)} %collective-permute-done.15.refs_1_), custom_call_target="tpu_custom_call" | custom-call | flops 1 | bytes 1 | tf_op jit(solution)/shard_map/kernel_grad/pallas_call | solution.py:142
  (6 shorter events, 0.0 us)
Async XLA Ops:
  0.6 0.9 %copy-start.1 = (bf16[96,1,4,256]{3,2,1,0:T(4,128)(2,1)S(1)}, bf16[96,1,4,256]{3,2,1,0:T(4,128)(2,1)}, u32[]{:S(2)}) copy-start(bf16[96,1,4,256]{3,2,1,0:T(4,128)(2,1)} %refs_0_.3) | copy-start | bytes 589828
  1.6 15.7 %copy-start = (bf16[96,27,384]{2,0,1:T(8,128)(2,1)S(1)}, bf16[96,27,384]{2,0,1:T(8,128)(2,1)}, u32[]{:S(2)}) copy-start(bf16[96,27,384]{2,0,1:T(8,128)(2,1)} %param.4) | copy-start | bytes 5971972
  2.2 3.6 %collective-permute-start = (bf16[96,1024]{1,0:T(8,128)(2,1)S(1)}, bf16[96,1024]{1,0:T(8,128)(2,1)S(1)}, u32[]{:S(2)}, u32[]{:S(2)}) collective-permute-start(bf16[96,1024]{1,0:T(8,128)(2,1)S(1)} %activate.1.refs_0_), channel_id=1, source_target_pairs={{0,2},{2,0},{1,3},{3,1},{4,6},{6,4},{5,7},{7,5},{8,10},{10,8},{9,1... | collective-permute-start | bytes 589832 | tf_op jit(solution)/shard_map/ppermute | solution.py:104
  2.7 3.1 %collective-permute-start.1 = (bf16[96,1,4,256]{3,2,1,0:T(4,128)(2,1)}, bf16[96,1,4,256]{3,2,1,0:T(4,128)(2,1)S(1)}, u32[]{:S(2)}, u32[]{:S(2)}) collective-permute-start(bf16[96,1,4,256]{3,2,1,0:T(4,128)(2,1)} %refs_2_.1), channel_id=1, source_target_pairs={{0,2},{2,0},{1,3},{3,1},{4,6},{6,4},{5,7},{7,5},{8,10},{10,8},{9,1... | collective-permute-start | bytes 589832 | tf_op jit(solution)/shard_map/ppermute | solution.py:104
  2.8 10.2 %collective-permute-start.2 = (bf16[96,1024]{1,0:T(8,128)(2,1)S(1)}, bf16[96,1024]{1,0:T(8,128)(2,1)S(1)}, u32[]{:S(2)}, u32[]{:S(2)}) collective-permute-start(bf16[96,1024]{1,0:T(8,128)(2,1)S(1)} %activate.1.refs_0_), channel_id=1, source_target_pairs={{0,4},{4,8},{8,12},{12,0},{1,5},{5,9},{9,13},{13,1},{2,6},{6,10},{... | collective-permute-start | bytes 589832 | tf_op jit(solution)/shard_map/ppermute | solution.py:104
  5.8 0.9 %copy-start.3 = (bf16[96,1,4,256]{3,2,1,0:T(4,128)(2,1)S(1)}, bf16[96,1,4,256]{3,2,1,0:T(4,128)(2,1)}, u32[]{:S(2)}) copy-start(bf16[96,1,4,256]{3,2,1,0:T(4,128)(2,1)} %refs_2_.1) | copy-start | bytes 589828
  8.7 13.3 %collective-permute-start.5 = (bf16[336,384]{1,0:T(8,128)(2,1)S(1)}, bf16[336,384]{1,0:T(8,128)(2,1)S(1)}, u32[]{:S(2)}, u32[]{:S(2)}) collective-permute-start(bf16[336,384]{1,0:T(8,128)(2,1)S(1)} %get-tuple-element.23.refs_1_.refs_0_), channel_id=1, source_target_pairs={{0,1},{1,0},{2,3},{3,2},{4,5},{5,4},{6,7},{7,6},{8,9},{9,8},{10,11... | collective-permute-start | bytes 774152 | tf_op jit(solution)/shard_map/ppermute | solution.py:104
  12.9 1.4 %collective-permute-start.3 = (bf16[96,1024]{1,0:T(8,128)(2,1)S(1)}, bf16[96,1024]{1,0:T(8,128)(2,1)S(1)}, u32[]{:S(2)}, u32[]{:S(2)}) collective-permute-start(bf16[96,1024]{1,0:T(8,128)(2,1)S(1)} %hand_on.3.refs_1_), channel_id=1, source_target_pairs={{0,2},{2,0},{1,3},{3,1},{4,6},{6,4},{5,7},{7,5},{8,10},{10,8},{9,1... | collective-permute-start | bytes 589832 | tf_op jit(solution)/shard_map/ppermute | solution.py:104
  12.9 9.1 %collective-permute-start.4 = (bf16[96,1024]{1,0:T(8,128)(2,1)S(1)}, bf16[96,1024]{1,0:T(8,128)(2,1)S(1)}, u32[]{:S(2)}, u32[]{:S(2)}) collective-permute-start(bf16[96,1024]{1,0:T(8,128)(2,1)S(1)} %hand_on.3.refs_1_), channel_id=1, source_target_pairs={{0,4},{4,8},{8,12},{12,0},{1,5},{5,9},{9,13},{13,1},{2,6},{6,10},{... | collective-permute-start | bytes 589832 | tf_op jit(solution)/shard_map/ppermute | solution.py:104
  15.7 15.9 %collective-permute-start.9 = (bf16[336,384]{1,0:T(8,128)(2,1)S(1)}, bf16[336,384]{1,0:T(8,128)(2,1)S(1)}, u32[]{:S(2)}, u32[]{:S(2)}) collective-permute-start(bf16[336,384]{1,0:T(8,128)(2,1)S(1)} %get-tuple-element.26.refs_2_.refs_1_), channel_id=1, source_target_pairs={{0,1},{1,0},{2,3},{3,2},{4,5},{5,4},{6,7},{7,6},{8,9},{9,8},{10,11... | collective-permute-start | bytes 774152 | tf_op jit(solution)/shard_map/ppermute | solution.py:104
  22.1 1.4 %collective-permute-start.6 = (bf16[96,1024]{1,0:T(8,128)(2,1)S(1)}, bf16[96,1024]{1,0:T(8,128)(2,1)S(1)}, u32[]{:S(2)}, u32[]{:S(2)}) collective-permute-start(bf16[96,1024]{1,0:T(8,128)(2,1)S(1)} %hand_on.4.refs_1_), channel_id=1, source_target_pairs={{0,2},{2,0},{1,3},{3,1},{4,6},{6,4},{5,7},{7,5},{8,10},{10,8},{9,1... | collective-permute-start | bytes 589832 | tf_op jit(solution)/shard_map/ppermute | solution.py:104
  22.1 9.5 %collective-permute-start.8 = (bf16[96,1024]{1,0:T(8,128)(2,1)S(1)}, bf16[96,1024]{1,0:T(8,128)(2,1)S(1)}, u32[]{:S(2)}, u32[]{:S(2)}) collective-permute-start(bf16[96,1024]{1,0:T(8,128)(2,1)S(1)} %get-tuple-element.30), channel_id=1, source_target_pairs={{0,4},{4,8},{8,12},{12,0},{1,5},{5,9},{9,13},{13,1},{2,6},{6,10},{... | collective-permute-start | bytes 589832 | tf_op jit(solution)/shard_map/ppermute | solution.py:104
  22.1 13.3 %collective-permute-start.7 = (bf16[96,1024]{1,0:T(8,128)(2,1)S(1)}, bf16[96,1024]{1,0:T(8,128)(2,1)S(1)}, u32[]{:S(2)}, u32[]{:S(2)}) collective-permute-start(bf16[96,1024]{1,0:T(8,128)(2,1)S(1)} %hand_on.4.refs_1_), channel_id=1, source_target_pairs={{0,4},{4,8},{8,12},{12,0},{1,5},{5,9},{9,13},{13,1},{2,6},{6,10},{... | collective-permute-start | bytes 589832 | tf_op jit(solution)/shard_map/ppermute | solution.py:104
  35.4 1.5 %collective-permute-start.10 = (bf16[96,1024]{1,0:T(8,128)(2,1)S(1)}, bf16[96,1024]{1,0:T(8,128)(2,1)S(1)}, u32[]{:S(2)}, u32[]{:S(2)}) collective-permute-start(bf16[96,1024]{1,0:T(8,128)(2,1)S(1)} %hand_on.5.refs_1_), channel_id=1, source_target_pairs={{0,2},{2,0},{1,3},{3,1},{4,6},{6,4},{5,7},{7,5},{8,10},{10,8},{9,1... | collective-permute-start | bytes 589832 | tf_op jit(solution)/shard_map/ppermute | solution.py:104
  35.4 15.2 %collective-permute-start.13 = (bf16[336,384]{1,0:T(8,128)(2,1)S(1)}, bf16[336,384]{1,0:T(8,128)(2,1)S(1)}, u32[]{:S(2)}, u32[]{:S(2)}) collective-permute-start(bf16[336,384]{1,0:T(8,128)(2,1)S(1)} %get-tuple-element.31.refs_2_), channel_id=1, source_target_pairs={{0,1},{1,0},{2,3},{3,2},{4,5},{5,4},{6,7},{7,6},{8,9},{9,8},{10,11... | collective-permute-start | bytes 774152 | tf_op jit(solution)/shard_map/ppermute | solution.py:104
  38.2 13.8 %collective-permute-start.14 = (bf16[336,384]{1,0:T(8,128)(2,1)S(1)}, bf16[336,384]{1,0:T(8,128)(2,1)S(1)}, u32[]{:S(2)}, u32[]{:S(2)}) collective-permute-start(bf16[336,384]{1,0:T(8,128)(2,1)S(1)} %get-tuple-element.33.refs_5_.refs_3_), channel_id=1, source_target_pairs={{0,1},{1,0},{2,3},{3,2},{4,5},{5,4},{6,7},{7,6},{8,9},{9,8},{10,11... | collective-permute-start | bytes 774152 | tf_op jit(solution)/shard_map/ppermute | solution.py:104
  39.7 10.9 %collective-permute-start.12 = (bf16[96,1024]{1,0:T(8,128)(2,1)S(1)}, bf16[96,1024]{1,0:T(8,128)(2,1)S(1)}, u32[]{:S(2)}, u32[]{:S(2)}) collective-permute-start(bf16[96,1024]{1,0:T(8,128)(2,1)S(1)} %get-tuple-element.35), channel_id=1, source_target_pairs={{0,12},{4,0},{8,4},{12,8},{1,13},{5,1},{9,5},{13,9},{2,14},{6,2},{... | collective-permute-start | bytes 589832 | tf_op jit(solution)/shard_map/ppermute | solution.py:104
  39.7 10.9 %collective-permute-start.11 = (bf16[96,1024]{1,0:T(8,128)(2,1)S(1)}, bf16[96,1024]{1,0:T(8,128)(2,1)S(1)}, u32[]{:S(2)}, u32[]{:S(2)}) collective-permute-start(bf16[96,1024]{1,0:T(8,128)(2,1)S(1)} %carry_share.1.refs_1_), channel_id=1, source_target_pairs={{0,4},{4,8},{8,12},{12,0},{1,5},{5,9},{9,13},{13,1},{2,6},{6,10},{... | collective-permute-start | bytes 589832 | tf_op jit(solution)/shard_map/ppermute | solution.py:104
  41.7 8.9 %copy-start.2 = (bf16[96,1,4,256]{3,2,1,0:T(4,128)(2,1)S(1)}, bf16[96,1,4,256]{3,2,1,0:T(4,128)(2,1)}, u32[]{:S(2)}) copy-start(bf16[96,1,4,256]{3,2,1,0:T(4,128)(2,1)} %refs_0_.3) | copy-start | bytes 589828
  52.3 2.7 %collective-permute-start.15 = (bf16[1344,384]{1,0:T(8,128)(2,1)S(1)}, bf16[1344,384]{1,0:T(8,128)(2,1)S(1)}, u32[]{:S(2)}, u32[]{:S(2)}) collective-permute-start(bf16[1344,384]{1,0:T(8,128)(2,1)S(1)} %sums.1.refs_0_), channel_id=1, source_target_pairs={{0,2},{2,0},{1,3},{3,1},{4,6},{6,4},{5,7},{7,5},{8,10},{10,8},{9,1... | collective-permute-start | bytes 3096584 | tf_op jit(solution)/shard_map/ppermute | solution.py:104
where the time goes:
time: 59.8 us; the launch traced here: 59.7 us
  waiting for transfers between devices  24.8 us (41%)
  Pallas kernels  20.3 us (34%)
  starting transfers between devices  11.9 us (20%)
  local copies, waits for them, and re-layouts  1.86 us (3%)
  between operations  0.74 us (1%)
    ppermute x16, waiting for transfers between devices, rotate(): return lax.ppermute(x, axis, [(i, (i + by) % size) for i in range(size)])  24.8 us
    pallas_call x11, Pallas kernels, run(): pl.pallas_call(body, compiler_params=pltpu.CompilerParams(vmem_limit_byte...  20.3 us
    ppermute x16, starting transfers between devices, rotate(): return lax.ppermute(x, axis, [(i, (i + by) % size) for i in range(size)])  11.9 us
    unnamed x8, local copies, waits for them, and re-layouts  1.86 us
  transfers between devices with their start and end apart: 16, of which 8 were waited for; matrix products, arithmetic and copies ran while one was open for 0% of the time, Pallas kernels for 25%

commit v1 on v0

v1 whole, which is shorter than its diff:
```python
import functools
import math

import jax
import jax.numpy as jnp
from jax import lax
from jax.experimental import pallas as pl
from jax.experimental.pallas import tpu as pltpu
from jax.sharding import PartitionSpec as P

WID = 64
SUB = 16
F32 = jnp.float32
BF16 = jnp.bfloat16
VMEM_LIMIT = 24 * 1024 * 1024
TOKEN = (8, 128)
FEATURE_COST = 1024 * 1024


def from_behind(x, axis, by):
    size = lax.axis_size(axis)
    pairs = [(i, i + by) for i in range(size) if 0 <= i + by < size]
    return lax.ppermute(x, axis, pairs)


def padded_copies(block):
    pixels = block.shape[-1]
    column = lax.broadcasted_iota(jnp.int32, (pixels,), 0) % WID
    nothing = jnp.zeros((), block.dtype)
    widths = [(0, 0), (0, 0), (0, 0), (WID + 1, WID + 1)]
    left_cut = jnp.pad(jnp.where(column == WID - 1, nothing, block), widths)
    untouched = jnp.pad(block, widths)
    right_cut = jnp.pad(jnp.where(column == 0, nothing, block), widths)
    return (left_cut, untouched, right_cut)


def tap_window(copies, first_frame, vertical, horizontal, frames, pixels):
    source = copies[horizontal]
    offset = vertical * WID + horizontal
    return source[:, :, first_frame : first_frame + frames, offset : offset + pixels]


def stacked_taps(copies, first_frame, flipped, frames, pixels):
    pieces = []
    for vertical in range(3):
        for horizontal in range(3):
            if flipped:
                pieces.append(
                    tap_window(copies, first_frame, 2 - vertical, 2 - horizontal, frames, pixels)
                )
            else:
                pieces.append(tap_window(copies, first_frame, vertical, horizontal, frames, pixels))
    concatenated = jnp.concatenate(pieces, axis=0)
    return concatenated.reshape(concatenated.shape[0], -1)


def local_generic(features, kernel, cotangent):
    channels, clip_count, frames, pixels = features.shape
    flat_length = clip_count * frames * pixels
    widened = features.astype(F32)
    logistic = jax.nn.sigmoid(widened)
    activation = (widened * logistic).astype(BF16)
    slope_factor = logistic * (1.0 + widened * (1.0 - logistic))
    earlier = from_behind(activation[:, :, frames - 2 :, :], "tm", 1)
    extended = jnp.concatenate([earlier, activation], axis=2)
    upcoming = from_behind(cotangent[:, :, :2, :], "tm", -1)
    later_padded = jnp.concatenate([cotangent, upcoming], axis=2)
    cotangent_rows = cotangent.reshape(channels, -1)
    portion = lax.all_gather(extended, "chan", axis=0, tiled=True)
    out_sum = jnp.zeros((channels, flat_length), F32)
    amount = portion.shape[0]
    copies = padded_copies(portion)
    grad_parts = []
    for temporal in range(3):
        stacked = stacked_taps(copies, temporal, False, frames, pixels)
        weights = kernel[:, 9 * temporal : 9 * temporal + 9, :].reshape(channels, 9 * amount)
        out_sum = out_sum + jnp.dot(weights, stacked, preferred_element_type=F32)
        grad_parts.append(
            lax.dot_general(
                cotangent_rows, stacked, (((1,), (1,)), ((), ())), preferred_element_type=F32
            ).reshape(channels, 9, amount)
        )
    grad_sum = jnp.concatenate(grad_parts, axis=1)
    conv_out = out_sum.reshape(features.shape).astype(BF16)
    position_count = lax.axis_size("dp") * lax.axis_size("tm") * flat_length
    kernel_grad = lax.psum(grad_sum, ("tm", "dp")) * (1.0 / math.sqrt(position_count))
    padded_later = padded_copies(later_padded)
    summed = jnp.zeros((amount, flat_length), F32)
    for temporal in range(3):
        weights = jnp.transpose(
            kernel[:, 9 * temporal : 9 * temporal + 9, :], (2, 1, 0)
        ).reshape(amount, 9 * channels)
        stacked = stacked_taps(padded_later, 2 - temporal, True, frames, pixels)
        summed = summed + jnp.dot(weights, stacked, preferred_element_type=F32)
    before_slope = lax.psum_scatter(
        summed.reshape(amount, clip_count, frames, pixels), "chan", scatter_dimension=0, tiled=True
    )
    feature_grad = (before_slope * slope_factor).astype(BF16)
    return (conv_out, feature_grad, kernel_grad)


def rotate(x, axis, by):
    size = lax.axis_size(axis)
    return lax.ppermute(x, axis, [(i, (i + by) % size) for i in range(size)])


def shifted(frame, down, right):
    pixels = frame.shape[-1]
    if down == 0 and right == 0:
        return frame
    cell = lax.broadcasted_iota(jnp.int32, (1, pixels), 1)
    row, column = cell // WID + down, cell % WID + right
    inside = (row >= 0) & (row < pixels // WID) & (column >= 0) & (column < WID)
    moved = pltpu.roll(frame, (-(down * WID + right)) % pixels, 1)
    return jnp.where(inside, moved, 0.0)


def after(x, *others):
    anywhere = pl.BlockSpec(memory_space=pl.ANY)
    return pl.pallas_call(
        lambda *refs: None,
        out_shape=jax.ShapeDtypeStruct(x.shape, x.dtype),
        in_specs=[anywhere] * (1 + len(others)),
        out_specs=anywhere,
        input_output_aliases={0: 0},
        compiler_params=pltpu.CompilerParams(vmem_limit_bytes=1024 * 1024),
        cost_estimate=cost(),
        name="hand_on",
    )(x, *others)


def run(kernel, args, waits=(), **options):
    options.setdefault("in_specs", [whole()] * len(args))
    options.setdefault("cost_estimate", cost())
    options["in_specs"] = list(options["in_specs"]) + [
        pl.BlockSpec(memory_space=pl.ANY) for _ in waits
    ]
    count = len(args)

    def body(*refs):
        kernel(*refs[:count], *refs[count + len(waits) :])

    return pl.pallas_call(
        body, compiler_params=pltpu.CompilerParams(vmem_limit_bytes=VMEM_LIMIT), **options
    )(*args, *waits)


def cost(bytes_like=1):
    return pl.CostEstimate(flops=1, bytes_accessed=bytes_like, transcendentals=0)


def whole():
    return pl.BlockSpec(memory_space=pltpu.VMEM)


def activate_kernel(features, features_other, full):
    _, _, frames, pixels = features.shape
    me = lax.axis_index("tm")
    for core, source in ((me, features), (1 - me, features_other)):
        v = source[:, 0].astype(F32)
        act = v / (1.0 + jnp.exp(-v))
        for t in range(frames):
            at = pl.multiple_of((core * frames + t) * pixels, pixels)
            full[:, pl.ds(at, pixels)] = act[:, t, :].astype(BF16)


def in_slot(channels, rows, slot):
    lane = lax.broadcasted_iota(jnp.int32, (1, channels), 1)
    return (lane >= slot * rows) & (lane < (slot + 1) * rows)


def packed_rows(total):
    unit = total // 9
    return 7 * unit, 2 * unit


def fill_stack(pixels, flat, stack, which):
    total, lanes = stack.shape
    rows = flat.shape[0]
    unit = rows // 2
    frames = flat.shape[1] // pixels
    stack[:, frames * pixels :] = jnp.zeros((total, lanes - frames * pixels), BF16)
    for half in range(2):

        @pl.when(which == half)
        def _(half=half):
            for t in range(frames):
                at = slice(t * pixels, (t + 1) * pixels)
                for q in range(9):
                    tap, part = divmod(9 * half + q, 2)
                    i, j = divmod(tap, 3)
                    frame = flat[part * unit : (part + 1) * unit, at]
                    stack[q * unit : (q + 1) * unit, at] = shifted(frame, 1 - i, 1 - j).astype(BF16)


def block_terms(pixels, shard, stack, sources, out, rhs):
    channels = out.shape[1]
    rows, lanes = sources[0][1].shape
    count = channels // rows
    for flag, source in sources:

        @pl.when(flag)
        def _(source=source):
            for a in range(3):
                skip = (2 - a) * pixels
                at = pl.ds(pl.multiple_of(lax.rem(shard + a, count) * rows, SUB), rows)
                if skip:
                    rhs[at, :skip] = jnp.zeros((rows, skip), BF16)
                rhs[at, skip:] = source[:, : lanes - skip]

    last = lax.rem(shard + 3, count)
    rhs[pl.ds(pl.multiple_of(last * rows, SUB), rows), :] = jnp.zeros((rows, lanes), BF16)
    terms = lax.dot_general(
        stack[:, :lanes], rhs[...], (((1,), (1,)), ((), ())), preferred_element_type=F32
    )
    main, tail = packed_rows(terms.shape[0])
    free = in_slot(channels, rows, last)
    for a in range(3):
        at = slice(a * tail, (a + 1) * tail)
        moved = pltpu.roll(terms[main:], (3 - a) * rows, 1)
        out[at, :] = jnp.where(free, moved, terms[at]).astype(BF16)
    out[3 * tail :, :] = terms[3 * tail : main].astype(BF16)


def own_terms_kernel(pixels, full, cot, cot_other, out, stack, flat, rhs):
    _, _, frames, _ = cot.shape
    me = lax.axis_index("tm")
    for core, source in ((me, cot), (1 - me, cot_other)):
        wide = source[:, 0].astype(F32)
        for t in range(frames):
            at = pl.multiple_of((core * frames + t) * pixels, pixels)
            flat[:, pl.ds(at, pixels)] = wide[:, t, :]
    fill_stack(pixels, flat, stack, me)
    block_terms(pixels, lax.axis_index("chan"), stack, [(me >= 0, full)], out, rhs)


def arrivals(count, z):
    both = [(hops, below) for hops in range(1, count) for below in (True, False)]
    return [(h, below) for h, below in both if 0 <= (z - h if below else z + h) < count]


def terms_kernel(pixels, count, k, hops, stack, *refs):
    blocks, (out, rhs) = refs[:-2], refs[-2:]
    me, z = lax.axis_index("tm"), lax.axis_index("chan")
    shard = z
    flags = [z < 0] * len(blocks)
    for at_z in range(count):
        hop, below = arrivals(count, at_z)[k]
        shard = jnp.where(z == at_z, at_z - hop if below else at_z + hop, shard)
        n = 2 * hops.index(hop)
        carrier = me == (0 if below else 1)
        flags[n] = flags[n] | ((z == at_z) & carrier)
        flags[n + 1] = flags[n + 1] | ((z == at_z) & jnp.logical_not(carrier))
    block_terms(pixels, shard, stack, list(zip(flags, blocks)), out, rhs)


def write_share(pixels, target, start, weights, mine, other, out):
    half = mine.shape[0]
    rows, length = out.shape
    me = lax.axis_index("tm")
    for shard in range(weights.shape[1] // rows):

        @pl.when(target == shard)
        def _(shard=shard):
            total = None
            for a in range(3):
                lanes = pl.ds(pl.multiple_of(start + (2 - a) * pixels, pixels), length)
                for which, stack in ((me, mine), (1 - me, other)):
                    at = pl.multiple_of((2 * a + which) * half, SUB)
                    term = lax.dot_general(
                        weights[pl.ds(at, half), shard * rows : (shard + 1) * rows],
                        stack[:, lanes],
                        (((0,), (0,)), ((), ())),
                        preferred_element_type=F32,
                    )
                    total = term if total is None else total + term
            out[...] = total


def share_target(hops):
    return lax.axis_index("chan") + jnp.where(lax.axis_index("tm") == 0, hops, -hops)


def far_share_kernel(pixels, hops, weights, mine, flat, out, other):
    fill_stack(pixels, flat, other, 1 - lax.axis_index("tm"))
    write_share(pixels, share_target(hops), 0, weights, mine, other, out)


def share_kernel(pixels, hops, weights, mine, other, out):
    write_share(pixels, share_target(hops), 0, weights, mine, other, out)


def near_share_kernel(pixels, hops, weights, mine, other, out, own):
    write_share(pixels, share_target(hops), 0, weights, mine, other, out)
    start = lax.axis_index("tm") * own.shape[1]
    write_share(pixels, lax.axis_index("chan"), start, weights, mine, other, own)


def message_kernel(count, step, came, share, out):
    me, z = lax.axis_index("tm"), lax.axis_index("chan")
    behind = jnp.where(me == 0, z, count - 1 - z)

    @pl.when(behind <= step - 2)
    def _():
        out[...] = (came[...].astype(F32) + share[...]).astype(BF16)

    @pl.when(behind > step - 2)
    def _():
        out[...] = came[...]


def conv_kernel(pixels, weights, full, *refs):
    blocks, (out, token, act) = refs[:-3], refs[-3:]
    token[...] = jnp.zeros(TOKEN, F32)
    rows, _, frames, _ = out.shape
    count = weights.shape[1] // rows
    length, front = frames * pixels, 2 * pixels
    me, z = lax.axis_index("tm"), lax.axis_index("chan")

    def place(flag, shard, source):
        at = pl.ds(pl.multiple_of(shard * rows, SUB), rows)

        @pl.when(flag & (me == 0))
        def _():
            act[at, :front] = jnp.zeros((rows, front), BF16)
            act[at, front:] = source[:, :length]

        @pl.when(flag & (me == 1))
        def _():
            act[at, :] = source[:, length - front :]

    place(me >= 0, z, full)
    for n in range(count - 1):
        hops = n + 1
        for core, source in ((0, blocks[2 * n]), (1, blocks[2 * n + 1])):
            below = me == core
            place(below & (z - hops >= 0), z - hops, source)
            place(jnp.logical_not(below) & (z + hops < count), z + hops, source)

    taps = 9 * rows
    for t in range(frames):
        z_t = None
        for a in range(3):
            term = jnp.dot(
                weights[a * taps : (a + 1) * taps, :],
                act[:, (t + a) * pixels : (t + a + 1) * pixels],
                preferred_element_type=F32,
            )
            z_t = term if z_t is None else z_t + term
        acc = None
        for i in range(3):
            for j in range(3):
                at = (3 * i + j) * rows
                moved = shifted(z_t[at : at + rows, :], i - 1, j - 1)
                acc = moved if acc is None else acc + moved
        out[:, 0, t, :] = acc.astype(BF16)


def feature_kernel(pixels, features, own, came, came_other, out, token):
    token[...] = jnp.zeros(TOKEN, F32)
    frames = features.shape[2]
    length = frames * pixels
    mine = pl.ds(pl.multiple_of(lax.axis_index("tm") * length, pixels), length)
    total = own[...] + came[:, mine].astype(F32) + came_other[:, mine].astype(F32)
    v = features[:, 0].astype(F32)
    s = 1.0 / (1.0 + jnp.exp(-v))
    slope = s * (1.0 + v * (1.0 - s))
    for t in range(frames):
        piece = total[:, t * pixels : (t + 1) * pixels] * slope[:, t, :]
        out[:, 0, t, :] = piece.astype(BF16)


def shard_at(count, k):
    z = lax.axis_index("chan")
    if k == 0:
        return z
    shard = z
    for at_z in range(count):
        hop, below = arrivals(count, at_z)[k - 1]
        shard = jnp.where(z == at_z, at_z - hop if below else at_z + hop, shard)
    return shard


def sum_kernel(main, *refs):
    out, ins = refs[-1], refs[:-1]
    count = len(ins) // 2
    for k in range(count):
        at = pl.multiple_of(shard_at(count, k) * main, SUB)
        total = ins[k][...].astype(F32) + ins[count + k][...].astype(F32)
        out[pl.ds(at, main), :] = total.astype(BF16)


def finish_kernel(scale, main, count, sums, other_sums, out, laid, sems):
    channels = out.shape[2]
    rows, half = channels // count, out.shape[1] // 2
    unit = rows // 2
    me = lax.axis_index("tm")
    copies = []
    for which, source in ((me, sums), (1 - me, other_sums)):
        start = pl.multiple_of(which * half, 8)
        for a in range(3):
            for q in range(9):
                base = q * unit if q < 7 else a * 2 * unit + (q - 7) * unit
                step = a if q < 7 else 3
                total = None
                for s in range(count):
                    piece = source[s * main + base : s * main + base + unit, :].astype(F32)
                    mask = in_slot(channels, rows, (s + step) % count)
                    total = piece if total is None else jnp.where(mask, piece, total)
                total = total * scale
                if step:
                    total = pltpu.roll(total, channels - step * rows, 1)
                laid[a, pl.ds(start + q * unit, unit), :] = total
            at = pl.ds(start, half)
            copy = pltpu.make_async_copy(laid.at[a, at], out.at[a, at], sems.at[len(copies)])
            copy.start()
            copies.append(copy)
    for copy in copies:
        copy.wait()


def local_fast(features, kernel, cotangent):
    rows, _, frames, pixels = features.shape
    length = frames * pixels
    count = lax.axis_size("chan")
    channels = rows * count
    taps = kernel.shape[1]
    half = 9 * rows // 2
    main, _ = packed_rows(half)
    sds = jax.ShapeDtypeStruct
    chip = sds((rows, 2 * length), BF16)
    term_shape = sds((main, channels), BF16)
    stack_shape = sds((half, 2 * length + 2 * pixels), BF16)
    share_shape = sds((rows, 2 * length), F32)
    rhs = pltpu.VMEM((channels, 2 * length), BF16)

    def hop(x):
        pairs = [(2 * z, 2 * z + 2) for z in range(count - 1)]
        pairs += [(2 * z + 1, 2 * z - 1) for z in range(1, count)]
        return lax.ppermute(x, ("chan", "tm"), pairs)

    weights = jnp.transpose(kernel, (1, 0, 2)).reshape(taps * rows, channels)
    features_other = rotate(features, "tm", 1)
    cot_other = rotate(cotangent, "tm", 1)
    full = run(
        activate_kernel,
        (features, features_other),
        out_shape=chip,
        out_specs=whole(),
        name="activate",
    )
    came = [hop(full)]
    own_term, stack, flat = run(
        functools.partial(own_terms_kernel, pixels),
        (full, cotangent, cot_other),
        out_shape=(term_shape, stack_shape, sds((rows, 2 * length), F32)),
        out_specs=(whole(),) * 3,
        scratch_shapes=[rhs],
        name="own_terms",
    )
    terms, got = [own_term], [rotate(own_term, "dp", 1)]
    share, stack_other = run(
        functools.partial(far_share_kernel, pixels, count - 1),
        (weights, stack, flat),
        waits=(own_term,),
        out_shape=(share_shape, stack_shape),
        out_specs=(whole(),) * 2,
        name="far_share",
    )
    blocks = []
    for step in range(2, count + 1):
        here = after(came[-1], share, *got[step - 3 : step - 2] if step > 2 else ())
        blocks += [here, rotate(here, "tm", 1)]
        message = run(
            functools.partial(message_kernel, count, step),
            (here, share),
            out_shape=chip,
            out_specs=whole(),
            name=f"message_{step}",
        )
        came.append(hop(message))
        hops = sorted({arrivals(count, z)[step - 2][0] for z in range(count)})
        held = [b for h in hops for b in blocks[2 * h - 2 : 2 * h]]
        term = run(
            functools.partial(terms_kernel, pixels, count, step - 2, hops),
            (stack, *held),
            out_shape=term_shape,
            out_specs=whole(),
            scratch_shapes=[rhs],
            name=f"terms_{step - 1}",
        )
        terms.append(term)
        got.append(rotate(term, "dp", 1))
        left = count - step
        if left > 1:
            share = run(
                functools.partial(share_kernel, pixels, left),
                (weights, stack, stack_other),
                waits=(term,),
                out_shape=share_shape,
                out_specs=whole(),
                name=f"share_{left}",
            )
        elif left == 1:
            share, own_share = run(
                functools.partial(near_share_kernel, pixels, left),
                (weights, stack, stack_other),
                waits=(term,),
                out_shape=(share_shape, sds((rows, length), F32)),
                out_specs=(whole(),) * 2,
                name="near_share",
            )

    conv_out, token = run(
        functools.partial(conv_kernel, pixels),
        (weights, full, *blocks),
        waits=(terms[-1],),
        out_shape=(sds(features.shape, BF16), sds(TOKEN, F32)),
        out_specs=(whole(),) * 2,
        scratch_shapes=[pltpu.VMEM((channels, (frames + 2) * pixels), BF16)],
        name="conv",
    )
    sums_of_shares = after(came[-1], token)
    feature_grad, token = run(
        functools.partial(feature_kernel, pixels),
        (features, own_share, sums_of_shares, rotate(sums_of_shares, "tm", 1)),
        waits=(got[-2],),
        out_shape=(sds(features.shape, BF16), sds(TOKEN, F32)),
        out_specs=(whole(),) * 2,
        cost_estimate=cost(FEATURE_COST),
        name="feature_grad",
    )
    sums = run(
        functools.partial(sum_kernel, main),
        (*terms, *got),
        waits=(token,),
        out_shape=sds((count * main, channels), BF16),
        out_specs=whole(),
        name="sums",
    )
    scale = 1.0 / math.sqrt(lax.axis_size("dp") * lax.axis_size("tm") * length)
    grad_shape = (3, 9 * rows, channels)
    kernel_grad = run(
        functools.partial(finish_kernel, scale, main, count),
        (sums, rotate(sums, "tm", 1)),
        out_shape=sds(grad_shape, F32),
        out_specs=pl.BlockSpec(memory_space=pl.ANY),
        scratch_shapes=[pltpu.VMEM(grad_shape, F32), pltpu.SemaphoreType.DMA((6,))],
        name="kernel_grad",
    )
    kernel_grad = jnp.transpose(kernel_grad.reshape(taps, rows, channels), (1, 0, 2))
    return (conv_out, feature_grad, kernel_grad)


def local(features, kernel, cotangent):
    rows, clips, _, pixels = features.shape
    fits = (
        clips == 1
        and lax.axis_size("tm") == 2
        and lax.axis_size("dp") == 2
        and rows % (2 * SUB) == 0
        and pixels % 128 == 0
        and kernel.shape[1] == 27
        and lax.axis_size("chan") == 4
    )
    return (local_fast if fits else local_generic)(features, kernel, cotangent)


def solution(mesh):
    return jax.shard_map(
        local,
        mesh=mesh,
        in_specs=(
            P("chan", ("groups", "dp"), "tm", None),
            P("chan", None, None),
            P("chan", ("groups", "dp"), "tm", None),
        ),
        out_specs=(
            P("chan", ("groups", "dp"), "tm", None),
            P("chan", ("groups", "dp"), "tm", None),
            P(("groups", "chan"), None, None),
        ),
        check_vma=False,
    )
```

time: 59.8 us -> 68.9 us (1.15)
  starting transfers between devices: 11.9 us -> 20.9 us
  waiting for transfers between devices: 24.8 us -> 19.5 us
  Pallas kernels: 20.3 us -> 23.7 us
  local copies, waits for them, and re-layouts: 1.86 us -> 3.41 us
    ppermute x0 -> x4, starting transfers between devices: none -> 15 us  [hop(): return lax.ppermute(x, ('chan', 'tm'), pairs)]
    ppermute x16 -> x11, starting transfers between devices: 11.9 us -> 5.9 us  [rotate(): return lax.ppermute(x, axis, [(i, (i + by) % size) for i in range(size)])]
    ppermute x16 -> x11, waiting for transfers between devices: 24.8 us -> 19.5 us  [rotate(): return lax.ppermute(x, axis, [(i, (i + by) % size) for i in range(size)])]
    pallas_call x11 -> x15, Pallas kernels: 20.3 us -> 23.7 us  [run(): pl.pallas_call(body, compiler_params=pltpu.CompilerParams(vmem_limit_byte...]
    unnamed x8, local copies, waits for them, and re-layouts: 1.86 us -> 3.41 us
  transfers between devices with their start and end apart: 16 -> 15, of which waited for: 8 -> 7; matrix products, arithmetic and copies ran while one was open for 0% -> 0% of each run, Pallas kernels for 25% -> 29%
where the time goes in v1:
time: 68.9 us; the launch traced here: 68.6 us
  Pallas kernels  23.7 us (34%)
  starting transfers between devices  20.9 us (30%)
  waiting for transfers between devices  19.5 us (28%)
  local copies, waits for them, and re-layouts  3.41 us (5%)
  between operations  1.01 us (1%)
    pallas_call x15, Pallas kernels, run(): pl.pallas_call(body, compiler_params=pltpu.CompilerParams(vmem_limit_byte...  23.7 us
    ppermute x11, waiting for transfers between devices, rotate(): return lax.ppermute(x, axis, [(i, (i + by) % size) for i in range(size)])  19.5 us
    ppermute x4, starting transfers between devices, hop(): return lax.ppermute(x, ('chan', 'tm'), pairs)  15 us
    ppermute x11, starting transfers between devices, rotate(): return lax.ppermute(x, axis, [(i, (i + by) % size) for i in range(size)])  5.9 us
    unnamed x8, local copies, waits for them, and re-layouts  3.41 us
  transfers between devices with their start and end apart: 15, of which 7 were waited for; matrix products, arithmetic and copies ran while one was open for 0% of the time, Pallas kernels for 29%

profile of v1, /device:TPU:0, one launch (start us, length us, event | category | flops | bytes accessed | tf_op | source)
XLA Modules:
  0.0 68.6 jit_solution(7046714847255849303)
XLA Ops:
  0.6 0.5 collective-permute-start
  1.1 1.3 %collective-permute-done.refs_1_ = bf16[96,1,4,256]{3,2,1,0:T(4,128)(2,1)S(1)} collective-permute-done((bf16[96,1,4,256]{3,2,1,0:T(4,128)(2,1)}, bf16[96,1,4,256]{3,2,1,0:T(4,128)(2,1)S(1)}, u32[]{:S(2)}, u32[]{:S(2)}) %collective-permute-start) | collective-permute-done | bytes 196640 | tf_op jit(solution)/shard_map/ppermute | solution.py:104
  2.4 0.9 %copy-done.2 = bf16[96,1,4,256]{3,2,1,0:T(4,128)(2,1)S(1)} copy-done((bf16[96,1,4,256]{3,2,1,0:T(4,128)(2,1)S(1)}, bf16[96,1,4,256]{3,2,1,0:T(4,128)(2,1)}, u32[]{:S(2)}) %copy-start.2) | copy-done | bytes 196632
  3.4 1.2 %activate.1.refs_0_.refs_1_ = bf16[96,2048]{1,0:T(8,128)(2,1)S(1)} custom-call(bf16[96,1,4,256]{3,2,1,0:T(4,128)(2,1)S(1)} %copy-done.2, bf16[96,1,4,256]{3,2,1,0:T(4,128)(2,1)S(1)} %collective-permute-done.refs_1_), custom_call_target="tpu_custom_call" | custom-call | flops 1 | bytes 1 | tf_op jit(solution)/shard_map/activate/pallas_call | solution.py:143
  4.6 4.9 %collective-permute-start.1 = (bf16[96,2048]{1,0:T(8,128)(2,1)S(1)}, bf16[96,2048]{1,0:T(8,128)(2,1)S(1)}, u32[]{:S(2)}, u32[]{:S(2)}) collective-permute-start(bf16[96,2048]{1,0:T(8,128)(2,1)S(1)} %activate.1.refs_0_.refs_1_), channel_id=1, source_target_pairs={{0,4},{4,8},{8,12},{6,2},{10,6},{14,10},{1,5},{5,9},{9,13},{7,3},{... | collective-permute-start | bytes 1179656 | tf_op jit(solution)/shard_map/ppermute | solution.py:440
  9.5 0.1 collective-permute-start.2
  9.5 1.6 %collective-permute-done.2.refs_2_ = bf16[96,1,4,256]{3,2,1,0:T(4,128)(2,1)S(1)} collective-permute-done((bf16[96,1,4,256]{3,2,1,0:T(4,128)(2,1)}, bf16[96,1,4,256]{3,2,1,0:T(4,128)(2,1)S(1)}, u32[]{:S(2)}, u32[]{:S(2)}) %collective-permute-start.2) | collective-permute-done | bytes 196640 | tf_op jit(solution)/shard_map/ppermute | solution.py:104
  11.2 0.9 %copy-done.3 = bf16[96,1,4,256]{3,2,1,0:T(4,128)(2,1)S(1)} copy-done((bf16[96,1,4,256]{3,2,1,0:T(4,128)(2,1)S(1)}, bf16[96,1,4,256]{3,2,1,0:T(4,128)(2,1)}, u32[]{:S(2)}) %copy-start.3) | copy-done | bytes 196632
  12.1 2.1 %own_terms.1 = (bf16[336,384]{1,0:T(8,128)(2,1)S(1)}, bf16[432,2560]{1,0:T(8,128)(2,1)S(1)}, f32[96,2048]{1,0:T(8,128)S(1)}) custom-call(bf16[96,2048]{1,0:T(8,128)(2,1)S(1)} %activate.1.refs_0_.refs_1_, bf16[96,1,4,256]{3,2,1,0:T(4,128)(2,1)S(1)} %copy-done.3, bf16[96,1,4,256]{3,2,1,0:T(4,128)(2,1)S(1)} %collective-permute-done.2.refs_2_), custom_call_target="tpu_custom_call" | custom-call | flops 1 | bytes 1 | tf_op jit(solution)/shard_map/own_terms/pallas_call | solution.py:143
  14.2 0.0 copy-start
  14.2 1.5 %copy-done = bf16[96,27,384]{2,0,1:T(8,128)(2,1)S(1)} copy-done((bf16[96,27,384]{2,0,1:T(8,128)(2,1)S(1)}, bf16[96,27,384]{2,0,1:T(8,128)(2,1)}, u32[]{:S(2)}) %copy-start) | copy-done | bytes 1990680
  15.8 2.5 %far_share.1 = (f32[96,2048]{1,0:T(8,128)S(1)}, bf16[432,2560]{1,0:T(8,128)(2,1)S(1)}) custom-call(bf16[2592,384]{1,0:T(8,128)(2,1)S(1)} %bitcast.6, bf16[432,2560]{1,0:T(8,128)(2,1)S(1)} %get-tuple-element.14.refs_1_.refs_0_, f32[96,2048]{1,0:T(8,128)S(1)} %get-tuple-element.15.refs_2_, bf16[336,384]{1,0:T(8,128)(2,1)S(1)} %get-tuple-element.16.refs_3_.refs_0_), custom_call_target="tpu_custom_call" | custom-call | flops 1 | bytes 1 | tf_op jit(solution)/shard_map/far_share/pallas_call | solution.py:143
  18.3 0.0 collective-permute-done.1.refs_0_
  18.3 0.0 copy-start.1
  18.3 0.1 collective-permute-start.3
  18.4 0.1 message_2.1
  18.5 1.7 %collective-permute-start.4 = (bf16[96,2048]{1,0:T(8,128)(2,1)S(1)}, bf16[96,2048]{1,0:T(8,128)(2,1)S(1)}, u32[]{:S(2)}, u32[]{:S(2)}) collective-permute-start(bf16[96,2048]{1,0:T(8,128)(2,1)S(1)} %message_2.1), channel_id=1, source_target_pairs={{0,4},{4,8},{8,12},{6,2},{10,6},{14,10},{1,5},{5,9},{9,13},{7,3},{... | collective-permute-start | bytes 1179656 | tf_op jit(solution)/shard_map/ppermute | solution.py:440
  20.2 1.6 %collective-permute-start.5 = (bf16[336,384]{1,0:T(8,128)(2,1)S(1)}, bf16[336,384]{1,0:T(8,128)(2,1)S(1)}, u32[]{:S(2)}, u32[]{:S(2)}) collective-permute-start(bf16[336,384]{1,0:T(8,128)(2,1)S(1)} %get-tuple-element.16.refs_3_.refs_0_), channel_id=1, source_target_pairs={{0,1},{1,0},{2,3},{3,2},{4,5},{5,4},{6,7},{7,6},{8,9},{9,8},{10,11... | collective-permute-start | bytes 774152 | tf_op jit(solution)/shard_map/ppermute | solution.py:104
  21.8 0.0 collective-permute-done.3.refs_2_.refs_3_
  21.8 1.3 %terms_1.1.refs_3_.refs_1_ = bf16[336,384]{1,0:T(8,128)(2,1)S(1)} custom-call(bf16[432,2560]{1,0:T(8,128)(2,1)S(1)} %get-tuple-element.14.refs_1_.refs_0_, bf16[96,2048]{1,0:T(8,128)(2,1)S(1)} %hand_on.4.refs_0_.refs_1_.refs_2_, bf16[96,2048]{1,0:T(8,128)(2,1)S(1)} %collective-permute-done.3.refs_2_.refs_3_), custom_call_target="tpu_custom_call" | custom-call | flops 1 | bytes 1 | tf_op jit(solution)/shard_map/terms_1/pallas_call | solution.py:143
  23.1 2.2 %share_2.1.refs_1_ = f32[96,2048]{1,0:T(8,128)S(1)} custom-call(bf16[2592,384]{1,0:T(8,128)(2,1)S(1)} %bitcast.7, bf16[432,2560]{1,0:T(8,128)(2,1)S(1)} %get-tuple-element.14.refs_1_.refs_0_, bf16[432,2560]{1,0:T(8,128)(2,1)S(1)} %get-tuple-element.18.refs_2_, bf16[336,384]{1,0:T(8,128)(2,1)S(1)} %terms_1.1.refs_3_.refs_1_), custom_call_target="tpu_custom_call" | custom-call | flops 1 | bytes 1 | tf_op jit(solution)/shard_map/share_2/pallas_call | solution.py:143
  25.3 3.1 %collective-permute-done.5.refs_2_.refs_4_ = bf16[336,384]{1,0:T(8,128)(2,1)S(1)} collective-permute-done((bf16[336,384]{1,0:T(8,128)(2,1)S(1)}, bf16[336,384]{1,0:T(8,128)(2,1)S(1)}, u32[]{:S(2)}, u32[]{:S(2)}) %collective-permute-start.5) | collective-permute-done | bytes 258080 | tf_op jit(solution)/shard_map/ppermute | solution.py:104
  28.4 0.0 collective-permute-done.4.refs_0_
  28.4 0.0 collective-permute-start.6
  28.4 0.1 message_3.1
  28.5 4.3 %collective-permute-start.7 = (bf16[96,2048]{1,0:T(8,128)(2,1)S(1)}, bf16[96,2048]{1,0:T(8,128)(2,1)S(1)}, u32[]{:S(2)}, u32[]{:S(2)}) collective-permute-start(bf16[96,2048]{1,0:T(8,128)(2,1)S(1)} %message_3.1), channel_id=1, source_target_pairs={{0,4},{4,8},{8,12},{6,2},{10,6},{14,10},{1,5},{5,9},{9,13},{7,3},{... | collective-permute-start | bytes 1179656 | tf_op jit(solution)/shard_map/ppermute | solution.py:440
  32.8 1.6 %collective-permute-start.8 = (bf16[336,384]{1,0:T(8,128)(2,1)S(1)}, bf16[336,384]{1,0:T(8,128)(2,1)S(1)}, u32[]{:S(2)}, u32[]{:S(2)}) collective-permute-start(bf16[336,384]{1,0:T(8,128)(2,1)S(1)} %terms_1.1.refs_3_.refs_1_), channel_id=1, source_target_pairs={{0,1},{1,0},{2,3},{3,2},{4,5},{5,4},{6,7},{7,6},{8,9},{9,8},{10,11... | collective-permute-start | bytes 774152 | tf_op jit(solution)/shard_map/ppermute | solution.py:104
  34.4 0.0 collective-permute-done.6.refs_4_.refs_2_.refs_5_
  34.4 1.3 %terms_2.1.refs_3_.refs_2_ = bf16[336,384]{1,0:T(8,128)(2,1)S(1)} custom-call(bf16[432,2560]{1,0:T(8,128)(2,1)S(1)} %get-tuple-element.14.refs_1_.refs_0_, bf16[96,2048]{1,0:T(8,128)(2,1)S(1)} %hand_on.4.refs_0_.refs_1_.refs_2_, bf16[96,2048]{1,0:T(8,128)(2,1)S(1)} %collective-permute-done.3.refs_2_.refs_3_, ...), custom_call_target="tpu_custom_call" | custom-call | flops 1 | bytes 1 | tf_op jit(solution)/shard_map/terms_2/pallas_call | solution.py:143
  35.7 3.3 %near_share.1 = (f32[96,2048]{1,0:T(8,128)S(1)}, f32[96,1024]{1,0:T(8,128)S(1)}) custom-call(bf16[2592,384]{1,0:T(8,128)(2,1)S(1)} %bitcast.8, bf16[432,2560]{1,0:T(8,128)(2,1)S(1)} %get-tuple-element.14.refs_1_.refs_0_, bf16[432,2560]{1,0:T(8,128)(2,1)S(1)} %get-tuple-element.18.refs_2_, bf16[336,384]{1,0:T(8,128)(2,1)S(1)} %terms_2.1.refs_3_.refs_2_), custom_call_target="tpu_custom_call" | custom-call | flops 1 | bytes 1 | tf_op jit(solution)/shard_map/near_share/pallas_call | solution.py:143
  39.0 0.2 collective-permute-done.8.refs_2_.refs_5_
  39.2 0.0 collective-permute-done.7.refs_0_
  39.2 0.0 collective-permute-start.9
  39.2 0.1 message_4.1
  39.3 4.2 %collective-permute-start.10 = (bf16[96,2048]{1,0:T(8,128)(2,1)S(1)}, bf16[96,2048]{1,0:T(8,128)(2,1)S(1)}, u32[]{:S(2)}, u32[]{:S(2)}) collective-permute-start(bf16[96,2048]{1,0:T(8,128)(2,1)S(1)} %message_4.1), channel_id=1, source_target_pairs={{0,4},{4,8},{8,12},{6,2},{10,6},{14,10},{1,5},{5,9},{9,13},{7,3},{... | collective-permute-start | bytes 1179656 | tf_op jit(solution)/shard_map/ppermute | solution.py:440
  43.5 1.4 %terms_3.1.refs_8_.refs_3_ = bf16[336,384]{1,0:T(8,128)(2,1)S(1)} custom-call(bf16[432,2560]{1,0:T(8,128)(2,1)S(1)} %get-tuple-element.14.refs_1_.refs_0_, bf16[96,2048]{1,0:T(8,128)(2,1)S(1)} %hand_on.5.refs_0_.refs_3_.refs_1_.refs_4_, bf16[96,2048]{1,0:T(8,128)(2,1)S(1)} %collective-permute-done.6.refs_4_.refs_2_.refs_5_, ...), custom_call_target="tpu_custom_call" | custom-call | flops 1 | bytes 1 | tf_op jit(solution)/shard_map/terms_3/pallas_call | solution.py:143
  44.9 4.2 %conv.1 = (bf16[96,1,4,256]{3,2,1,0:T(4,128)(2,1)}, f32[8,128]{1,0:T(8,128)S(1)}) custom-call(bf16[2592,384]{1,0:T(8,128)(2,1)S(1)} %bitcast.9, bf16[96,2048]{1,0:T(8,128)(2,1)S(1)} %activate.1.refs_0_.refs_1_, bf16[96,2048]{1,0:T(8,128)(2,1)S(1)} %hand_on.4.refs_0_.refs_1_.refs_2_, bf16[96,2048]{1,0:T(8,128)(2,1)S(1)} %collective-permute-done.3.refs_2_.refs_3_, ...), custom_call_target="tpu_custom_call" | custom-call | flops 1 | bytes 1 | tf_op jit(solution)/shard_map/conv/pallas_call | solution.py:143
  49.1 0.0 collective-permute-done.10.refs_0_
  49.1 1.5 %collective-permute-start.12 = (bf16[336,384]{1,0:T(8,128)(2,1)S(1)}, bf16[336,384]{1,0:T(8,128)(2,1)S(1)}, u32[]{:S(2)}, u32[]{:S(2)}) collective-permute-start(bf16[336,384]{1,0:T(8,128)(2,1)S(1)} %terms_2.1.refs_3_.refs_2_), channel_id=1, source_target_pairs={{0,1},{1,0},{2,3},{3,2},{4,5},{5,4},{6,7},{7,6},{8,9},{9,8},{10,11... | collective-permute-start | bytes 774152 | tf_op jit(solution)/shard_map/ppermute | solution.py:104
  50.6 0.5 collective-permute-start.13
  51.2 7.0 %collective-permute-done.12.refs_4_.refs_6_ = bf16[336,384]{1,0:T(8,128)(2,1)S(1)} collective-permute-done((bf16[336,384]{1,0:T(8,128)(2,1)S(1)}, bf16[336,384]{1,0:T(8,128)(2,1)S(1)}, u32[]{:S(2)}, u32[]{:S(2)}) %collective-permute-start.12) | collective-permute-done | bytes 258080 | tf_op jit(solution)/shard_map/ppermute | solution.py:104
  58.1 0.0 collective-permute-done.11.refs_3_
  58.1 1.4 %feature_grad.1 = (bf16[96,1,4,256]{3,2,1,0:T(4,128)(2,1)}, f32[8,128]{1,0:T(8,128)S(1)}) custom-call(bf16[96,1,4,256]{3,2,1,0:T(4,128)(2,1)S(1)} %copy-done.2, f32[96,1024]{1,0:T(8,128)S(1)} %get-tuple-element.21.refs_1_, bf16[96,2048]{1,0:T(8,128)(2,1)S(1)} %hand_on.7.refs_2_, bf16[96,2048]{1,0:T(8,128)(2,1)S(1)} %collective-permute-done.11.refs_3_, ...), custom_call_target="tpu_custom_call" | custom-call | flops 1 | bytes 1048576 | tf_op jit(solution)/shard_map/feature_grad/pallas_call | solution.py:143
  59.6 3.7 %collective-permute-done.13.refs_7_ = bf16[336,384]{1,0:T(8,128)(2,1)S(1)} collective-permute-done((bf16[336,384]{1,0:T(8,128)(2,1)S(1)}, bf16[336,384]{1,0:T(8,128)(2,1)S(1)}, u32[]{:S(2)}, u32[]{:S(2)}) %collective-permute-start.13) | collective-permute-done | bytes 258080 | tf_op jit(solution)/shard_map/ppermute | solution.py:104
  63.3 0.3 sums.1.refs_0_
  63.5 0.1 collective-permute-start.14
  63.6 2.6 %collective-permute-done.14.refs_1_ = bf16[1344,384]{1,0:T(8,128)(2,1)S(1)} collective-permute-done((bf16[1344,384]{1,0:T(8,128)(2,1)S(1)}, bf16[1344,384]{1,0:T(8,128)(2,1)S(1)}, u32[]{:S(2)}, u32[]{:S(2)}) %collective-permute-start.14) | collective-permute-done | bytes 1032224 | tf_op jit(solution)/shard_map/ppermute | solution.py:104
  66.2 2.2 %kernel_grad.1 = f32[3,864,384]{2,1,0:T(8,128)} custom-call(bf16[1344,384]{1,0:T(8,128)(2,1)S(1)} %sums.1.refs_0_, bf16[1344,384]{1,0:T(8,128)(2,1)S(1)} %collective-permute-done.14.refs_1_), custom_call_target="tpu_custom_call" | custom-call | flops 1 | bytes 1 | tf_op jit(solution)/shard_map/kernel_grad/pallas_call | solution.py:143
  (9 shorter events, 0.0 us)
Async XLA Ops:
  0.6 1.8 %collective-permute-start = (bf16[96,1,4,256]{3,2,1,0:T(4,128)(2,1)}, bf16[96,1,4,256]{3,2,1,0:T(4,128)(2,1)S(1)}, u32[]{:S(2)}, u32[]{:S(2)}) collective-permute-start(bf16[96,1,4,256]{3,2,1,0:T(4,128)(2,1)} %refs_0_.3), channel_id=1, source_target_pairs={{0,2},{2,0},{1,3},{3,1},{4,6},{6,4},{5,7},{7,5},{8,10},{10,8},{9,1... | collective-permute-start | bytes 589832 | tf_op jit(solution)/shard_map/ppermute | solution.py:104
  2.4 0.9 %copy-start.2 = (bf16[96,1,4,256]{3,2,1,0:T(4,128)(2,1)S(1)}, bf16[96,1,4,256]{3,2,1,0:T(4,128)(2,1)}, u32[]{:S(2)}) copy-start(bf16[96,1,4,256]{3,2,1,0:T(4,128)(2,1)} %refs_0_.3) | copy-start | bytes 589828
  4.6 13.7 %collective-permute-start.1 = (bf16[96,2048]{1,0:T(8,128)(2,1)S(1)}, bf16[96,2048]{1,0:T(8,128)(2,1)S(1)}, u32[]{:S(2)}, u32[]{:S(2)}) collective-permute-start(bf16[96,2048]{1,0:T(8,128)(2,1)S(1)} %activate.1.refs_0_.refs_1_), channel_id=1, source_target_pairs={{0,4},{4,8},{8,12},{6,2},{10,6},{14,10},{1,5},{5,9},{9,13},{7,3},{... | collective-permute-start | bytes 1179656 | tf_op jit(solution)/shard_map/ppermute | solution.py:440
  9.5 1.7 %collective-permute-start.2 = (bf16[96,1,4,256]{3,2,1,0:T(4,128)(2,1)}, bf16[96,1,4,256]{3,2,1,0:T(4,128)(2,1)S(1)}, u32[]{:S(2)}, u32[]{:S(2)}) collective-permute-start(bf16[96,1,4,256]{3,2,1,0:T(4,128)(2,1)} %refs_1_.1), channel_id=1, source_target_pairs={{0,2},{2,0},{1,3},{3,1},{4,6},{6,4},{5,7},{7,5},{8,10},{10,8},{9,1... | collective-permute-start | bytes 589832 | tf_op jit(solution)/shard_map/ppermute | solution.py:104
  11.2 0.9 %copy-start.3 = (bf16[96,1,4,256]{3,2,1,0:T(4,128)(2,1)S(1)}, bf16[96,1,4,256]{3,2,1,0:T(4,128)(2,1)}, u32[]{:S(2)}) copy-start(bf16[96,1,4,256]{3,2,1,0:T(4,128)(2,1)} %refs_1_.1) | copy-start | bytes 589828
  14.2 1.6 %copy-start = (bf16[96,27,384]{2,0,1:T(8,128)(2,1)S(1)}, bf16[96,27,384]{2,0,1:T(8,128)(2,1)}, u32[]{:S(2)}) copy-start(bf16[96,27,384]{2,0,1:T(8,128)(2,1)} %param.4) | copy-start | bytes 5971972
  18.3 4.8 %copy-start.1 = (bf16[96,27,384]{2,0,1:T(8,128)(2,1)S(1)}, bf16[96,27,384]{2,0,1:T(8,128)(2,1)}, u32[]{:S(2)}) copy-start(bf16[96,27,384]{2,0,1:T(8,128)(2,1)} %param.4) | copy-start | bytes 5971972
  18.3 3.4 %collective-permute-start.3 = (bf16[96,2048]{1,0:T(8,128)(2,1)S(1)}, bf16[96,2048]{1,0:T(8,128)(2,1)S(1)}, u32[]{:S(2)}, u32[]{:S(2)}) collective-permute-start(bf16[96,2048]{1,0:T(8,128)(2,1)S(1)} %hand_on.4.refs_0_.refs_1_.refs_2_), channel_id=1, source_target_pairs={{0,2},{2,0},{1,3},{3,1},{4,6},{6,4},{5,7},{7,5},{8,10},{10,8},{9,1... | collective-permute-start | bytes 1179656 | tf_op jit(solution)/shard_map/ppermute | solution.py:104
  18.5 9.9 %collective-permute-start.4 = (bf16[96,2048]{1,0:T(8,128)(2,1)S(1)}, bf16[96,2048]{1,0:T(8,128)(2,1)S(1)}, u32[]{:S(2)}, u32[]{:S(2)}) collective-permute-start(bf16[96,2048]{1,0:T(8,128)(2,1)S(1)} %message_2.1), channel_id=1, source_target_pairs={{0,4},{4,8},{8,12},{6,2},{10,6},{14,10},{1,5},{5,9},{9,13},{7,3},{... | collective-permute-start | bytes 1179656 | tf_op jit(solution)/shard_map/ppermute | solution.py:440
  20.2 8.2 %collective-permute-start.5 = (bf16[336,384]{1,0:T(8,128)(2,1)S(1)}, bf16[336,384]{1,0:T(8,128)(2,1)S(1)}, u32[]{:S(2)}, u32[]{:S(2)}) collective-permute-start(bf16[336,384]{1,0:T(8,128)(2,1)S(1)} %get-tuple-element.16.refs_3_.refs_0_), channel_id=1, source_target_pairs={{0,1},{1,0},{2,3},{3,2},{4,5},{5,4},{6,7},{7,6},{8,9},{9,8},{10,11... | collective-permute-start | bytes 774152 | tf_op jit(solution)/shard_map/ppermute | solution.py:104
  28.4 6.0 %collective-permute-start.6 = (bf16[96,2048]{1,0:T(8,128)(2,1)S(1)}, bf16[96,2048]{1,0:T(8,128)(2,1)S(1)}, u32[]{:S(2)}, u32[]{:S(2)}) collective-permute-start(bf16[96,2048]{1,0:T(8,128)(2,1)S(1)} %hand_on.5.refs_0_.refs_3_.refs_1_.refs_4_), channel_id=1, source_target_pairs={{0,2},{2,0},{1,3},{3,1},{4,6},{6,4},{5,7},{7,5},{8,10},{10,8},{9,1... | collective-permute-start | bytes 1179656 | tf_op jit(solution)/shard_map/ppermute | solution.py:104
  28.5 10.7 %collective-permute-start.7 = (bf16[96,2048]{1,0:T(8,128)(2,1)S(1)}, bf16[96,2048]{1,0:T(8,128)(2,1)S(1)}, u32[]{:S(2)}, u32[]{:S(2)}) collective-permute-start(bf16[96,2048]{1,0:T(8,128)(2,1)S(1)} %message_3.1), channel_id=1, source_target_pairs={{0,4},{4,8},{8,12},{6,2},{10,6},{14,10},{1,5},{5,9},{9,13},{7,3},{... | collective-permute-start | bytes 1179656 | tf_op jit(solution)/shard_map/ppermute | solution.py:440
  32.8 6.4 %collective-permute-start.8 = (bf16[336,384]{1,0:T(8,128)(2,1)S(1)}, bf16[336,384]{1,0:T(8,128)(2,1)S(1)}, u32[]{:S(2)}, u32[]{:S(2)}) collective-permute-start(bf16[336,384]{1,0:T(8,128)(2,1)S(1)} %terms_1.1.refs_3_.refs_1_), channel_id=1, source_target_pairs={{0,1},{1,0},{2,3},{3,2},{4,5},{5,4},{6,7},{7,6},{8,9},{9,8},{10,11... | collective-permute-start | bytes 774152 | tf_op jit(solution)/shard_map/ppermute | solution.py:104
  39.2 4.3 %collective-permute-start.9 = (bf16[96,2048]{1,0:T(8,128)(2,1)S(1)}, bf16[96,2048]{1,0:T(8,128)(2,1)S(1)}, u32[]{:S(2)}, u32[]{:S(2)}) collective-permute-start(bf16[96,2048]{1,0:T(8,128)(2,1)S(1)} %hand_on.6.refs_3_.refs_6_.refs_0_), channel_id=1, source_target_pairs={{0,2},{2,0},{1,3},{3,1},{4,6},{6,4},{5,7},{7,5},{8,10},{10,8},{9,1... | collective-permute-start | bytes 1179656 | tf_op jit(solution)/shard_map/ppermute | solution.py:104
  39.3 9.8 %collective-permute-start.10 = (bf16[96,2048]{1,0:T(8,128)(2,1)S(1)}, bf16[96,2048]{1,0:T(8,128)(2,1)S(1)}, u32[]{:S(2)}, u32[]{:S(2)}) collective-permute-start(bf16[96,2048]{1,0:T(8,128)(2,1)S(1)} %message_4.1), channel_id=1, source_target_pairs={{0,4},{4,8},{8,12},{6,2},{10,6},{14,10},{1,5},{5,9},{9,13},{7,3},{... | collective-permute-start | bytes 1179656 | tf_op jit(solution)/shard_map/ppermute | solution.py:440
  49.1 9.0 %collective-permute-start.11 = (bf16[96,2048]{1,0:T(8,128)(2,1)S(1)}, bf16[96,2048]{1,0:T(8,128)(2,1)S(1)}, u32[]{:S(2)}, u32[]{:S(2)}) collective-permute-start(bf16[96,2048]{1,0:T(8,128)(2,1)S(1)} %hand_on.7.refs_2_), channel_id=1, source_target_pairs={{0,2},{2,0},{1,3},{3,1},{4,6},{6,4},{5,7},{7,5},{8,10},{10,8},{9,1... | collective-permute-start | bytes 1179656 | tf_op jit(solution)/shard_map/ppermute | solution.py:104
  49.1 9.0 %collective-permute-start.12 = (bf16[336,384]{1,0:T(8,128)(2,1)S(1)}, bf16[336,384]{1,0:T(8,128)(2,1)S(1)}, u32[]{:S(2)}, u32[]{:S(2)}) collective-permute-start(bf16[336,384]{1,0:T(8,128)(2,1)S(1)} %terms_2.1.refs_3_.refs_2_), channel_id=1, source_target_pairs={{0,1},{1,0},{2,3},{3,2},{4,5},{5,4},{6,7},{7,6},{8,9},{9,8},{10,11... | collective-permute-start | bytes 774152 | tf_op jit(solution)/shard_map/ppermute | solution.py:104
  50.6 12.7 %collective-permute-start.13 = (bf16[336,384]{1,0:T(8,128)(2,1)S(1)}, bf16[336,384]{1,0:T(8,128)(2,1)S(1)}, u32[]{:S(2)}, u32[]{:S(2)}) collective-permute-start(bf16[336,384]{1,0:T(8,128)(2,1)S(1)} %terms_3.1.refs_8_.refs_3_), channel_id=1, source_target_pairs={{0,1},{1,0},{2,3},{3,2},{4,5},{5,4},{6,7},{7,6},{8,9},{9,8},{10,11... | collective-permute-start | bytes 774152 | tf_op jit(solution)/shard_map/ppermute | solution.py:104
  63.5 2.7 %collective-permute-start.14 = (bf16[1344,384]{1,0:T(8,128)(2,1)S(1)}, bf16[1344,384]{1,0:T(8,128)(2,1)S(1)}, u32[]{:S(2)}, u32[]{:S(2)}) collective-permute-start(bf16[1344,384]{1,0:T(8,128)(2,1)S(1)} %sums.1.refs_0_), channel_id=1, source_target_pairs={{0,2},{2,0},{1,3},{3,1},{4,6},{6,4},{5,7},{7,5},{8,10},{10,8},{9,1... | collective-permute-start | bytes 3096584 | tf_op jit(solution)/shard_map/ppermute | solution.py:104

commit v2 on v1

--- a/solution.py
+++ b/solution.py
@@ -153,15 +153,17 @@
     return pl.BlockSpec(memory_space=pltpu.VMEM)
 
 
-def activate_kernel(features, features_other, full):
-    _, _, frames, pixels = features.shape
-    me = lax.axis_index("tm")
-    for core, source in ((me, features), (1 - me, features_other)):
-        v = source[:, 0].astype(F32)
-        act = v / (1.0 + jnp.exp(-v))
-        for t in range(frames):
-            at = pl.multiple_of((core * frames + t) * pixels, pixels)
-            full[:, pl.ds(at, pixels)] = act[:, t, :].astype(BF16)
+def activate_kernel(features, activation):
+    frames, pixels = features.shape[2:]
+    v = features[:, 0].astype(F32)
+    act = v / (1.0 + jnp.exp(-v))
+    for t in range(frames):
+        activation[:, t * pixels : (t + 1) * pixels] = act[:, t, :].astype(BF16)
+
+
+def shard_at(count, k):
+    z = lax.axis_index("chan")
+    return (z, lax.rem(z + 2, count), z + 1 - 2 * lax.rem(z, 2), count - 1 - z)[k]
 
 
 def in_slot(channels, rows, slot):
@@ -175,11 +177,9 @@
 
 
 def fill_stack(pixels, flat, stack, which):
-    total, lanes = stack.shape
     rows = flat.shape[0]
     unit = rows // 2
     frames = flat.shape[1] // pixels
-    stack[:, frames * pixels :] = jnp.zeros((total, lanes - frames * pixels), BF16)
     for half in range(2):
 
         @pl.when(which == half)
@@ -193,25 +193,27 @@
                     stack[q * unit : (q + 1) * unit, at] = shifted(frame, 1 - i, 1 - j).astype(BF16)
 
 
-def block_terms(pixels, shard, stack, sources, out, rhs):
+def block_terms(pixels, k, stack, here, there, out, rhs):
     channels = out.shape[1]
-    rows, lanes = sources[0][1].shape
-    count = channels // rows
-    for flag, source in sources:
-
-        @pl.when(flag)
-        def _(source=source):
+    rows, length = here.shape
+    lanes, count = 2 * length, channels // rows
+    shard = shard_at(count, k)
+    for core in range(2):
+
+        @pl.when(lax.axis_index("tm") == core)
+        def _(first=(here, there)[core], second=(there, here)[core]):
             for a in range(3):
                 skip = (2 - a) * pixels
                 at = pl.ds(pl.multiple_of(lax.rem(shard + a, count) * rows, SUB), rows)
                 if skip:
                     rhs[at, :skip] = jnp.zeros((rows, skip), BF16)
-                rhs[at, skip:] = source[:, : lanes - skip]
+                rhs[at, skip : skip + length] = first[...]
+                rhs[at, skip + length :] = second[:, : length - skip]
 
     last = lax.rem(shard + 3, count)
     rhs[pl.ds(pl.multiple_of(last * rows, SUB), rows), :] = jnp.zeros((rows, lanes), BF16)
     terms = lax.dot_general(
-        stack[:, :lanes], rhs[...], (((1,), (1,)), ((), ())), preferred_element_type=F32
+        stack[...], rhs[...], (((1,), (1,)), ((), ())), preferred_element_type=F32
     )
     main, tail = packed_rows(terms.shape[0])
     free = in_slot(channels, rows, last)
@@ -222,120 +224,77 @@
     out[3 * tail :, :] = terms[3 * tail : main].astype(BF16)
 
 
-def own_terms_kernel(pixels, full, cot, cot_other, out, stack, flat, rhs):
+def own_terms_kernel(pixels, mine, other, cot, cot_other, out, stack, later, rhs, flat):
     _, _, frames, _ = cot.shape
+    length = frames * pixels
     me = lax.axis_index("tm")
     for core, source in ((me, cot), (1 - me, cot_other)):
         wide = source[:, 0].astype(F32)
         for t in range(frames):
             at = pl.multiple_of((core * frames + t) * pixels, pixels)
             flat[:, pl.ds(at, pixels)] = wide[:, t, :]
+    own = pl.ds(pl.multiple_of(me * length, pixels), length)
+    later[:, :length] = flat[:, own].astype(BF16)
+    after_own = flat[:, length : length + 2 * pixels]
+    later[:, length:] = jnp.where(me == 0, after_own, 0.0).astype(BF16)
     fill_stack(pixels, flat, stack, me)
-    block_terms(pixels, lax.axis_index("chan"), stack, [(me >= 0, full)], out, rhs)
-
-
-def arrivals(count, z):
-    both = [(hops, below) for hops in range(1, count) for below in (True, False)]
-    return [(h, below) for h, below in both if 0 <= (z - h if below else z + h) < count]
-
-
-def terms_kernel(pixels, count, k, hops, stack, *refs):
-    blocks, (out, rhs) = refs[:-2], refs[-2:]
-    me, z = lax.axis_index("tm"), lax.axis_index("chan")
-    shard = z
-    flags = [z < 0] * len(blocks)
-    for at_z in range(count):
-        hop, below = arrivals(count, at_z)[k]
-        shard = jnp.where(z == at_z, at_z - hop if below else at_z + hop, shard)
-        n = 2 * hops.index(hop)
-        carrier = me == (0 if below else 1)
-        flags[n] = flags[n] | ((z == at_z) & carrier)
-        flags[n + 1] = flags[n + 1] | ((z == at_z) & jnp.logical_not(carrier))
-    block_terms(pixels, shard, stack, list(zip(flags, blocks)), out, rhs)
-
-
-def write_share(pixels, target, start, weights, mine, other, out):
-    half = mine.shape[0]
-    rows, length = out.shape
-    me = lax.axis_index("tm")
-    for shard in range(weights.shape[1] // rows):
-
-        @pl.when(target == shard)
-        def _(shard=shard):
-            total = None
-            for a in range(3):
-                lanes = pl.ds(pl.multiple_of(start + (2 - a) * pixels, pixels), length)
-                for which, stack in ((me, mine), (1 - me, other)):
-                    at = pl.multiple_of((2 * a + which) * half, SUB)
-                    term = lax.dot_general(
-                        weights[pl.ds(at, half), shard * rows : (shard + 1) * rows],
-                        stack[:, lanes],
-                        (((0,), (0,)), ((), ())),
-                        preferred_element_type=F32,
-                    )
-                    total = term if total is None else total + term
-            out[...] = total
-
-
-def share_target(hops):
-    return lax.axis_index("chan") + jnp.where(lax.axis_index("tm") == 0, hops, -hops)
-
-
-def far_share_kernel(pixels, hops, weights, mine, flat, out, other):
-    fill_stack(pixels, flat, other, 1 - lax.axis_index("tm"))
-    write_share(pixels, share_target(hops), 0, weights, mine, other, out)
-
-
-def share_kernel(pixels, hops, weights, mine, other, out):
-    write_share(pixels, share_target(hops), 0, weights, mine, other, out)
-
-
-def near_share_kernel(pixels, hops, weights, mine, other, out, own):
-    write_share(pixels, share_target(hops), 0, weights, mine, other, out)
-    start = lax.axis_index("tm") * own.shape[1]
-    write_share(pixels, lax.axis_index("chan"), start, weights, mine, other, own)
-
-
-def message_kernel(count, step, came, share, out):
-    me, z = lax.axis_index("tm"), lax.axis_index("chan")
-    behind = jnp.where(me == 0, z, count - 1 - z)
-
-    @pl.when(behind <= step - 2)
-    def _():
-        out[...] = (came[...].astype(F32) + share[...]).astype(BF16)
-
-    @pl.when(behind > step - 2)
-    def _():
-        out[...] = came[...]
-
-
-def conv_kernel(pixels, weights, full, *refs):
+    block_terms(pixels, 0, stack, mine, other, out, rhs)
+
+
+def terms_kernel(pixels, k, stack, here, there, out, rhs):
+    block_terms(pixels, k, stack, here, there, out, rhs)
+
+
+def share_kernel(pixels, weights, later, own, kept, sent, stack, total):
+    rows = later.shape[0]
+    length = own.shape[1]
+    frames = length // pixels
+    count = weights.shape[1] // rows
+    for t in range(frames + 2):
+        at = slice(t * pixels, (t + 1) * pixels)
+        frame = later[:, at].astype(F32)
+        for i in range(3):
+            for j in range(3):
+                row = (3 * i + j) * rows
+                stack[row : row + rows, at] = shifted(frame, 1 - i, 1 - j).astype(BF16)
+    taps = 9 * rows
+    acc = None
+    for a in range(3):
+        term = lax.dot_general(
+            weights[a * taps : (a + 1) * taps, :],
+            stack[:, (2 - a) * pixels : (2 - a) * pixels + length],
+            (((0,), (0,)), ((), ())),
+            preferred_element_type=F32,
+        )
+        acc = term if acc is None else acc + term
+    total[...] = acc
+
+    def part(k):
+        return total[pl.ds(pl.multiple_of(shard_at(count, k) * rows, SUB), rows), :]
+
+    own[...] = part(0)
+    kept[...] = part(1)
+    sent[0] = part(2).astype(BF16)
+    sent[1] = part(3).astype(BF16)
+
+
+def add_kernel(kept, came, out):
+    out[...] = (kept[...] + came[1].astype(F32)).astype(out.dtype)
+
+
+def conv_kernel(pixels, weights, *refs):
     blocks, (out, token, act) = refs[:-3], refs[-3:]
     token[...] = jnp.zeros(TOKEN, F32)
     rows, _, frames, _ = out.shape
     count = weights.shape[1] // rows
     length, front = frames * pixels, 2 * pixels
-    me, z = lax.axis_index("tm"), lax.axis_index("chan")
-
-    def place(flag, shard, source):
-        at = pl.ds(pl.multiple_of(shard * rows, SUB), rows)
-
-        @pl.when(flag & (me == 0))
-        def _():
-            act[at, :front] = jnp.zeros((rows, front), BF16)
-            act[at, front:] = source[:, :length]
-
-        @pl.when(flag & (me == 1))
-        def _():
-            act[at, :] = source[:, length - front :]
-
-    place(me >= 0, z, full)
-    for n in range(count - 1):
-        hops = n + 1
-        for core, source in ((0, blocks[2 * n]), (1, blocks[2 * n + 1])):
-            below = me == core
-            place(below & (z - hops >= 0), z - hops, source)
-            place(jnp.logical_not(below) & (z + hops < count), z + hops, source)
+    me = lax.axis_index("tm")
+    for k in range(count):
+        here, there = blocks[2 * k], blocks[2 * k + 1]
+        at = pl.ds(pl.multiple_of(shard_at(count, k) * rows, SUB), rows)
+        earlier = there[:, length - front :]
+        act[at, :front] = jnp.where(me == 0, jnp.zeros_like(earlier), earlier)
+        act[at, front:] = here[...]
 
     taps = 9 * rows
     for t in range(frames):
@@ -356,29 +315,16 @@
         out[:, 0, t, :] = acc.astype(BF16)
 
 
-def feature_kernel(pixels, features, own, came, came_other, out, token):
+def feature_kernel(pixels, features, own, first, second, out, token):
     token[...] = jnp.zeros(TOKEN, F32)
     frames = features.shape[2]
-    length = frames * pixels
-    mine = pl.ds(pl.multiple_of(lax.axis_index("tm") * length, pixels), length)
-    total = own[...] + came[:, mine].astype(F32) + came_other[:, mine].astype(F32)
+    total = own[...] + first[0].astype(F32) + second[...].astype(F32)
     v = features[:, 0].astype(F32)
     s = 1.0 / (1.0 + jnp.exp(-v))
     slope = s * (1.0 + v * (1.0 - s))
     for t in range(frames):
         piece = total[:, t * pixels : (t + 1) * pixels] * slope[:, t, :]
         out[:, 0, t, :] = piece.astype(BF16)
-
-
-def shard_at(count, k):
-    z = lax.axis_index("chan")
-    if k == 0:
-        return z
-    shard = z
-    for at_z in range(count):
-        hop, below = arrivals(count, at_z)[k - 1]
-        shard = jnp.where(z == at_z, at_z - hop if below else at_z + hop, shard)
-    return shard
 
 
 def sum_kernel(main, *refs):
@@ -428,103 +374,97 @@
     half = 9 * rows // 2
     main, _ = packed_rows(half)
     sds = jax.ShapeDtypeStruct
-    chip = sds((rows, 2 * length), BF16)
+    block_shape = sds((rows, length), BF16)
     term_shape = sds((main, channels), BF16)
-    stack_shape = sds((half, 2 * length + 2 * pixels), BF16)
-    share_shape = sds((rows, 2 * length), F32)
+    stack_shape = sds((half, 2 * length), BF16)
     rhs = pltpu.VMEM((channels, 2 * length), BF16)
 
-    def hop(x):
-        pairs = [(2 * z, 2 * z + 2) for z in range(count - 1)]
-        pairs += [(2 * z + 1, 2 * z - 1) for z in range(1, count)]
-        return lax.ppermute(x, ("chan", "tm"), pairs)
+    def swap(x, far):
+        return lax.ppermute(x, "chan", [(z, z ^ far) for z in range(count)])
 
     weights = jnp.transpose(kernel, (1, 0, 2)).reshape(taps * rows, channels)
-    features_other = rotate(features, "tm", 1)
     cot_other = rotate(cotangent, "tm", 1)
-    full = run(
+    activation = run(
         activate_kernel,
-        (features, features_other),
-        out_shape=chip,
+        (features,),
+        out_shape=block_shape,
         out_specs=whole(),
         name="activate",
     )
-    came = [hop(full)]
-    own_term, stack, flat = run(
+    other = rotate(activation, "tm", 1)
+    far, near = swap(activation, 2), swap(activation, 1)
+    own_term, stack, later = run(
         functools.partial(own_terms_kernel, pixels),
-        (full, cotangent, cot_other),
-        out_shape=(term_shape, stack_shape, sds((rows, 2 * length), F32)),
+        (activation, other, cotangent, cot_other),
+        out_shape=(term_shape, stack_shape, sds((rows, length + 2 * pixels), BF16)),
         out_specs=(whole(),) * 3,
-        scratch_shapes=[rhs],
+        scratch_shapes=[rhs, pltpu.VMEM((rows, 2 * length), F32)],
         name="own_terms",
     )
     terms, got = [own_term], [rotate(own_term, "dp", 1)]
-    share, stack_other = run(
-        functools.partial(far_share_kernel, pixels, count - 1),
-        (weights, stack, flat),
+    own_share, kept, sent = run(
+        functools.partial(share_kernel, pixels),
+        (weights, later),
         waits=(own_term,),
-        out_shape=(share_shape, stack_shape),
-        out_specs=(whole(),) * 2,
-        name="far_share",
-    )
-    blocks = []
-    for step in range(2, count + 1):
-        here = after(came[-1], share, *got[step - 3 : step - 2] if step > 2 else ())
-        blocks += [here, rotate(here, "tm", 1)]
-        message = run(
-            functools.partial(message_kernel, count, step),
-            (here, share),
-            out_shape=chip,
-            out_specs=whole(),
-            name=f"message_{step}",
-        )
-        came.append(hop(message))
-        hops = sorted({arrivals(count, z)[step - 2][0] for z in range(count)})
-        held = [b for h in hops for b in blocks[2 * h - 2 : 2 * h]]
+        out_shape=(
+            sds((rows, length), F32),
+            sds((rows, length), F32),
+            sds((2, rows, length), BF16),
+        ),
+        out_specs=(whole(),) * 3,
+        scratch_shapes=[
+            pltpu.VMEM((9 * rows, (frames + 2) * pixels), BF16),
+            pltpu.VMEM((channels, length), F32),
+        ],
+        name="shares",
+    )
+    first_share = swap(sent, 1)
+    blocks = [activation, other]
+
+    def terms_of(k, here, waits=()):
+        blocks.extend((here, rotate(here, "tm", 1)))
         term = run(
-            functools.partial(terms_kernel, pixels, count, step - 2, hops),
-            (stack, *held),
+            functools.partial(terms_kernel, pixels, k),
+            (stack, *blocks[-2:]),
+            waits=waits,
             out_shape=term_shape,
             out_specs=whole(),
             scratch_shapes=[rhs],
-            name=f"terms_{step - 1}",
+            name=f"terms_{k}",
         )
         terms.append(term)
         got.append(rotate(term, "dp", 1))
-        left = count - step
-        if left > 1:
-            share = run(
-                functools.partial(share_kernel, pixels, left),
-                (weights, stack, stack_other),
-                waits=(term,),
-                out_shape=share_shape,
-                out_specs=whole(),
-                name=f"share_{left}",
-            )
-        elif left == 1:
-            share, own_share = run(
-                functools.partial(near_share_kernel, pixels, left),
-                (weights, stack, stack_other),
-                waits=(term,),
-                out_shape=(share_shape, sds((rows, length), F32)),
-                out_specs=(whole(),) * 2,
-                name="near_share",
-            )
+        return term
+
+    far = after(far, own_share, near)
+    near = after(near, far)
+    last = swap(far, 1)
+    term = terms_of(1, far, (got[0],))
+    term = terms_of(2, near, (term,))
+    carry = run(
+        add_kernel,
+        (kept, first_share),
+        waits=(term,),
+        out_shape=block_shape,
+        out_specs=whole(),
+        name="carry_share",
+    )
+    second_share = swap(carry, 2)
+    term = terms_of(3, after(last, carry, got[1]))
 
     conv_out, token = run(
         functools.partial(conv_kernel, pixels),
-        (weights, full, *blocks),
-        waits=(terms[-1],),
+        (weights, *blocks),
+        waits=(term,),
         out_shape=(sds(features.shape, BF16), sds(TOKEN, F32)),
         out_specs=(whole(),) * 2,
         scratch_shapes=[pltpu.VMEM((channels, (frames + 2) * pixels), BF16)],
         name="conv",
     )
-    sums_of_shares = after(came[-1], token)
     feature_grad, token = run(
         functools.partial(feature_kernel, pixels),
-        (features, own_share, sums_of_shares, rotate(sums_of_shares, "tm", 1)),
-        waits=(got[-2],),
+        (features, own_share, first_share, second_share),
+        waits=(token, got[2]),
         out_shape=(sds(features.shape, BF16), sds(TOKEN, F32)),
         out_specs=(whole(),) * 2,
         cost_estimate=cost(FEATURE_COST),

time: 68.9 us -> 56.4 us (0.82)
  starting transfers between devices: 20.9 us -> 14.6 us
  Pallas kernels: 23.7 us -> 17.9 us
    ppermute x11 -> x10, waiting for transfers between devices: 19.5 us -> 4.63 us  [rotate(): return lax.ppermute(x, axis, [(i, (i + by) % size) for i in range(size)])]
    ppermute x4 -> x5, waiting for transfers between devices: 0.01 us -> 14.8 us  [swap(): return lax.ppermute(x, 'chan', [(z, z ^ far) for z in range(count)])]
    ppermute x4 -> x5, starting transfers between devices: 15 us -> 7.85 us  [swap(): return lax.ppermute(x, 'chan', [(z, z ^ far) for z in range(count)])]
    pallas_call x15 -> x11, Pallas kernels: 23.7 us -> 17.9 us  [run(): pl.pallas_call(body, compiler_params=pltpu.CompilerParams(vmem_limit_byte...]
    ppermute x11 -> x10, starting transfers between devices: 5.9 us -> 6.73 us  [rotate(): return lax.ppermute(x, axis, [(i, (i + by) % size) for i in range(size)])]
    unnamed x8 -> x10, local copies, waits for them, and re-layouts: 3.41 us -> 3.41 us
  transfers between devices with their start and end apart: 15 -> 15, of which waited for: 7 -> 7; matrix products, arithmetic and copies ran while one was open for 0% -> 0% of each run, Pallas kernels for 29% -> 26%
where the time goes in v2:
time: 56.4 us; the launch traced here: 56.2 us
  waiting for transfers between devices  19.4 us (34%)
  Pallas kernels  17.9 us (32%)
  starting transfers between devices  14.6 us (26%)
  local copies, waits for them, and re-layouts  3.41 us (6%)
  between operations  0.91 us (2%)
    pallas_call x11, Pallas kernels, run(): pl.pallas_call(body, compiler_params=pltpu.CompilerParams(vmem_limit_byte...  17.9 us
    ppermute x5, waiting for transfers between devices, swap(): return lax.ppermute(x, 'chan', [(z, z ^ far) for z in range(count)])  14.8 us
    ppermute x5, starting transfers between devices, swap(): return lax.ppermute(x, 'chan', [(z, z ^ far) for z in range(count)])  7.85 us
    ppermute x10, starting transfers between devices, rotate(): return lax.ppermute(x, axis, [(i, (i + by) % size) for i in range(size)])  6.73 us
    ppermute x10, waiting for transfers between devices, rotate(): return lax.ppermute(x, axis, [(i, (i + by) % size) for i in range(size)])  4.63 us
    unnamed x10, local copies, waits for them, and re-layouts  3.41 us
  transfers between devices with their start and end apart: 15, of which 7 were waited for; matrix products, arithmetic and copies ran while one was open for 0% of the time, Pallas kernels for 26%

profile of v2, /device:TPU:0, one launch (start us, length us, event | category | flops | bytes accessed | tf_op | source)
XLA Modules:
  0.0 56.2 jit_solution(14808723304546840252)
XLA Ops:
  0.6 0.0 copy-start.2
  0.6 0.9 %copy-done.2 = bf16[96,1,4,256]{3,2,1,0:T(4,128)(2,1)S(1)} copy-done((bf16[96,1,4,256]{3,2,1,0:T(4,128)(2,1)S(1)}, bf16[96,1,4,256]{3,2,1,0:T(4,128)(2,1)}, u32[]{:S(2)}) %copy-start.2) | copy-done | bytes 196632
  1.6 0.6 %activate.1.refs_0_.refs_1_ = bf16[96,1024]{1,0:T(8,128)(2,1)S(1)} custom-call(bf16[96,1,4,256]{3,2,1,0:T(4,128)(2,1)S(1)} %copy-done.2), custom_call_target="tpu_custom_call" | custom-call | flops 1 | bytes 1 | tf_op jit(solution)/shard_map/activate/pallas_call | solution.py:143
  2.2 0.5 collective-permute-start
  2.7 0.1 collective-permute-start.2
  2.8 3.0 %collective-permute-start.3 = (bf16[96,1024]{1,0:T(8,128)(2,1)S(1)}, bf16[96,1024]{1,0:T(8,128)(2,1)S(1)}, u32[]{:S(2)}, u32[]{:S(2)}) collective-permute-start(bf16[96,1024]{1,0:T(8,128)(2,1)S(1)} %activate.1.refs_0_.refs_1_), channel_id=1, source_target_pairs={{0,4},{4,0},{8,12},{12,8},{1,5},{5,1},{9,13},{13,9},{2,6},{6,2},{1... | collective-permute-start | bytes 589832 | tf_op jit(solution)/shard_map/ppermute | solution.py:383
  5.8 2.6 %collective-permute-start.1 = (bf16[96,1024]{1,0:T(8,128)(2,1)S(1)}, bf16[96,1024]{1,0:T(8,128)(2,1)S(1)}, u32[]{:S(2)}, u32[]{:S(2)}) collective-permute-start(bf16[96,1024]{1,0:T(8,128)(2,1)S(1)} %activate.1.refs_0_.refs_1_), channel_id=1, source_target_pairs={{0,8},{4,12},{8,0},{12,4},{1,9},{5,13},{9,1},{13,5},{2,10},{6,14},... | collective-permute-start | bytes 589832 | tf_op jit(solution)/shard_map/ppermute | solution.py:383
  8.4 0.0 collective-permute-done.refs_1_.refs_2_
  8.4 0.0 collective-permute-done.2.refs_3_
  8.4 0.0 copy-start.4
  8.4 0.9 %copy-done.4 = bf16[96,1,4,256]{3,2,1,0:T(4,128)(2,1)S(1)} copy-done((bf16[96,1,4,256]{3,2,1,0:T(4,128)(2,1)S(1)}, bf16[96,1,4,256]{3,2,1,0:T(4,128)(2,1)}, u32[]{:S(2)}) %copy-start.4) | copy-done | bytes 196632
  9.3 2.2 %own_terms.1 = (bf16[336,384]{1,0:T(8,128)(2,1)S(1)}, bf16[432,2048]{1,0:T(8,128)(2,1)S(1)}, bf16[96,1536]{1,0:T(8,128)(2,1)S(1)}) custom-call(bf16[96,1024]{1,0:T(8,128)(2,1)S(1)} %activate.1.refs_0_.refs_1_, bf16[96,1024]{1,0:T(8,128)(2,1)S(1)} %collective-permute-done.refs_1_.refs_2_, bf16[96,1,4,256]{3,2,1,0:T(4,128)(2,1)S(1)} %copy-done.4, ...), custom_call_target="tpu_custom_call" | custom-call | flops 1 | bytes 1 | tf_op jit(solution)/shard_map/own_terms/pallas_call | solution.py:143
  11.5 1.6 %collective-permute-start.8 = (bf16[336,384]{1,0:T(8,128)(2,1)S(1)}, bf16[336,384]{1,0:T(8,128)(2,1)S(1)}, u32[]{:S(2)}, u32[]{:S(2)}) collective-permute-start(bf16[336,384]{1,0:T(8,128)(2,1)S(1)} %get-tuple-element.14.refs_2_.refs_0_), channel_id=1, source_target_pairs={{0,1},{1,0},{2,3},{3,2},{4,5},{5,4},{6,7},{7,6},{8,9},{9,8},{10,11... | collective-permute-start | bytes 774152 | tf_op jit(solution)/shard_map/ppermute | solution.py:104
  13.0 1.6 %copy-done = bf16[96,27,384]{2,0,1:T(8,128)(2,1)S(1)} copy-done((bf16[96,27,384]{2,0,1:T(8,128)(2,1)S(1)}, bf16[96,27,384]{2,0,1:T(8,128)(2,1)}, u32[]{:S(2)}) %copy-start) | copy-done | bytes 1990680
  14.6 3.0 %shares.1 = (f32[96,1024]{1,0:T(8,128)S(1)}, f32[96,1024]{1,0:T(8,128)S(1)}, bf16[2,96,1024]{2,1,0:T(8,128)(2,1)S(1)}) custom-call(bf16[2592,384]{1,0:T(8,128)(2,1)S(1)} %bitcast.6, bf16[96,1536]{1,0:T(8,128)(2,1)S(1)} %get-tuple-element.13.refs_1_, bf16[336,384]{1,0:T(8,128)(2,1)S(1)} %get-tuple-element.14.refs_2_.refs_0_), custom_call_target="tpu_custom_call" | custom-call | flops 1 | bytes 1 | tf_op jit(solution)/shard_map/shares/pallas_call | solution.py:143
  17.5 0.0 collective-permute-done.3.refs_2_.refs_0_
  17.6 0.0 collective-permute-done.1.refs_0_
  17.6 0.1 collective-permute-start.4
  17.6 0.5 collective-permute-start.7
  18.2 0.9 %collective-permute-done.4.refs_2_.refs_4_ = bf16[96,1024]{1,0:T(8,128)(2,1)S(1)} collective-permute-done((bf16[96,1024]{1,0:T(8,128)(2,1)S(1)}, bf16[96,1024]{1,0:T(8,128)(2,1)S(1)}, u32[]{:S(2)}, u32[]{:S(2)}) %collective-permute-start.4) | collective-permute-done | bytes 196640 | tf_op jit(solution)/shard_map/ppermute | solution.py:104
  19.1 0.1 collective-permute-done.8.refs_3_.refs_4_
  19.2 1.3 %terms_1.1.refs_3_.refs_1_ = bf16[336,384]{1,0:T(8,128)(2,1)S(1)} custom-call(bf16[432,2048]{1,0:T(8,128)(2,1)S(1)} %get-tuple-element.18.refs_0_, bf16[96,1024]{1,0:T(8,128)(2,1)S(1)} %hand_on.3.refs_1_.refs_3_, bf16[96,1024]{1,0:T(8,128)(2,1)S(1)} %collective-permute-done.4.refs_2_.refs_4_, bf16[336,384]{1,0:T(8,128)(2,1)S(1)} %collective-permute-done.8.refs_3_.refs_4_), custom_call_target="tpu_custom_call" | custom-call | flops 1 | bytes 1 | tf_op jit(solution)/shard_map/terms_1/pallas_call | solution.py:143
  20.5 1.6 %collective-permute-start.9 = (bf16[336,384]{1,0:T(8,128)(2,1)S(1)}, bf16[336,384]{1,0:T(8,128)(2,1)S(1)}, u32[]{:S(2)}, u32[]{:S(2)}) collective-permute-start(bf16[336,384]{1,0:T(8,128)(2,1)S(1)} %terms_1.1.refs_3_.refs_1_), channel_id=1, source_target_pairs={{0,1},{1,0},{2,3},{3,2},{4,5},{5,4},{6,7},{7,6},{8,9},{9,8},{10,11... | collective-permute-start | bytes 774152 | tf_op jit(solution)/shard_map/ppermute | solution.py:104
  22.1 0.0 collective-permute-start.5
  22.1 0.5 collective-permute-start.6
  22.5 1.0 %collective-permute-done.5.refs_2_.refs_6_ = bf16[96,1024]{1,0:T(8,128)(2,1)S(1)} collective-permute-done((bf16[96,1024]{1,0:T(8,128)(2,1)S(1)}, bf16[96,1024]{1,0:T(8,128)(2,1)S(1)}, u32[]{:S(2)}, u32[]{:S(2)}) %collective-permute-start.5) | collective-permute-done | bytes 196640 | tf_op jit(solution)/shard_map/ppermute | solution.py:104
  23.5 1.3 %terms_2.1.refs_2_ = bf16[336,384]{1,0:T(8,128)(2,1)S(1)} custom-call(bf16[432,2048]{1,0:T(8,128)(2,1)S(1)} %get-tuple-element.18.refs_0_, bf16[96,1024]{1,0:T(8,128)(2,1)S(1)} %hand_on.4.refs_1_.refs_5_, bf16[96,1024]{1,0:T(8,128)(2,1)S(1)} %collective-permute-done.5.refs_2_.refs_6_, bf16[336,384]{1,0:T(8,128)(2,1)S(1)} %terms_1.1.refs_3_.refs_1_), custom_call_target="tpu_custom_call" | custom-call | flops 1 | bytes 1 | tf_op jit(solution)/shard_map/terms_2/pallas_call | solution.py:143
  24.8 4.8 %collective-permute-done.7.refs_1_.refs_2_ = bf16[2,96,1024]{2,1,0:T(8,128)(2,1)S(1)} collective-permute-done((bf16[2,96,1024]{2,1,0:T(8,128)(2,1)S(1)}, bf16[2,96,1024]{2,1,0:T(8,128)(2,1)S(1)}, u32[]{:S(2)}, u32[]{:S(2)}) %collective-permute-start.7) | collective-permute-done | bytes 393248 | tf_op jit(solution)/shard_map/ppermute | solution.py:383
  29.7 3.7 %collective-permute-done.6.refs_0_ = bf16[96,1024]{1,0:T(8,128)(2,1)S(1)} collective-permute-done((bf16[96,1024]{1,0:T(8,128)(2,1)S(1)}, bf16[96,1024]{1,0:T(8,128)(2,1)S(1)}, u32[]{:S(2)}, u32[]{:S(2)}) %collective-permute-start.6) | collective-permute-done | bytes 196640 | tf_op jit(solution)/shard_map/ppermute | solution.py:383
  33.4 0.0 collective-permute-done.9.refs_2_.refs_5_
  33.4 0.0 collective-permute-start.10
  33.4 1.4 %collective-permute-start.12 = (bf16[336,384]{1,0:T(8,128)(2,1)S(1)}, bf16[336,384]{1,0:T(8,128)(2,1)S(1)}, u32[]{:S(2)}, u32[]{:S(2)}) collective-permute-start(bf16[336,384]{1,0:T(8,128)(2,1)S(1)} %terms_2.1.refs_2_), channel_id=1, source_target_pairs={{0,1},{1,0},{2,3},{3,2},{4,5},{5,4},{6,7},{7,6},{8,9},{9,8},{10,11... | collective-permute-start | bytes 774152 | tf_op jit(solution)/shard_map/ppermute | solution.py:104
  34.8 0.0 collective-permute-done.10.refs_2_.refs_8_
  34.8 1.5 %terms_3.1.refs_9_.refs_3_ = bf16[336,384]{1,0:T(8,128)(2,1)S(1)} custom-call(bf16[432,2048]{1,0:T(8,128)(2,1)S(1)} %get-tuple-element.18.refs_0_, bf16[96,1024]{1,0:T(8,128)(2,1)S(1)} %hand_on.5.refs_1_.refs_7_, bf16[96,1024]{1,0:T(8,128)(2,1)S(1)} %collective-permute-done.10.refs_2_.refs_8_), custom_call_target="tpu_custom_call" | custom-call | flops 1 | bytes 1 | tf_op jit(solution)/shard_map/terms_3/pallas_call | solution.py:143
  36.4 0.0 copy-start.3
  36.4 1.4 %collective-permute-start.13 = (bf16[336,384]{1,0:T(8,128)(2,1)S(1)}, bf16[336,384]{1,0:T(8,128)(2,1)S(1)}, u32[]{:S(2)}, u32[]{:S(2)}) collective-permute-start(bf16[336,384]{1,0:T(8,128)(2,1)S(1)} %terms_3.1.refs_9_.refs_3_), channel_id=1, source_target_pairs={{0,1},{1,0},{2,3},{3,2},{4,5},{5,4},{6,7},{7,6},{8,9},{9,8},{10,11... | collective-permute-start | bytes 774152 | tf_op jit(solution)/shard_map/ppermute | solution.py:104
  37.8 1.3 %collective-permute-start.11 = (bf16[96,1024]{1,0:T(8,128)(2,1)S(1)}, bf16[96,1024]{1,0:T(8,128)(2,1)S(1)}, u32[]{:S(2)}, u32[]{:S(2)}) collective-permute-start(bf16[96,1024]{1,0:T(8,128)(2,1)S(1)} %carry_share.1.refs_1_), channel_id=1, source_target_pairs={{0,8},{4,12},{8,0},{12,4},{1,9},{5,13},{9,1},{13,5},{2,10},{6,14},... | collective-permute-start | bytes 589832 | tf_op jit(solution)/shard_map/ppermute | solution.py:383
  39.1 0.0 copy-done.1
  39.1 4.1 %conv.1 = (bf16[96,1,4,256]{3,2,1,0:T(4,128)(2,1)}, f32[8,128]{1,0:T(8,128)S(1)}) custom-call(bf16[2592,384]{1,0:T(8,128)(2,1)S(1)} %bitcast.7, bf16[96,1024]{1,0:T(8,128)(2,1)S(1)} %activate.1.refs_0_.refs_1_, bf16[96,1024]{1,0:T(8,128)(2,1)S(1)} %collective-permute-done.refs_1_.refs_2_, bf16[96,1024]{1,0:T(8,128)(2,1)S(1)} %hand_on.3.refs_1_.refs_3_, ...), custom_call_target="tpu_custom_call" | custom-call | flops 1 | bytes 1 | tf_op jit(solution)/shard_map/conv/pallas_call | solution.py:143
  43.2 0.0 collective-permute-done.12.refs_5_.refs_6_
  43.2 6.2 %collective-permute-done.11.refs_3_ = bf16[96,1024]{1,0:T(8,128)(2,1)S(1)} collective-permute-done((bf16[96,1024]{1,0:T(8,128)(2,1)S(1)}, bf16[96,1024]{1,0:T(8,128)(2,1)S(1)}, u32[]{:S(2)}, u32[]{:S(2)}) %collective-permute-start.11) | collective-permute-done | bytes 196640 | tf_op jit(solution)/shard_map/ppermute | solution.py:383
  49.5 0.0 copy-done.3
  49.5 1.4 %feature_grad.1 = (bf16[96,1,4,256]{3,2,1,0:T(4,128)(2,1)}, f32[8,128]{1,0:T(8,128)S(1)}) custom-call(bf16[96,1,4,256]{3,2,1,0:T(4,128)(2,1)S(1)} %copy-done.3, f32[96,1024]{1,0:T(8,128)S(1)} %get-tuple-element.15.refs_1_, bf16[2,96,1024]{2,1,0:T(8,128)(2,1)S(1)} %collective-permute-done.7.refs_1_.refs_2_, ...), custom_call_target="tpu_custom_call" | custom-call | flops 1 | bytes 1048576 | tf_op jit(solution)/shard_map/feature_grad/pallas_call | solution.py:143
  50.9 0.0 collective-permute-done.13.refs_7_
  50.9 0.3 sums.1.refs_0_
  51.2 0.1 collective-permute-start.14
  51.2 2.6 %collective-permute-done.14.refs_1_ = bf16[1344,384]{1,0:T(8,128)(2,1)S(1)} collective-permute-done((bf16[1344,384]{1,0:T(8,128)(2,1)S(1)}, bf16[1344,384]{1,0:T(8,128)(2,1)S(1)}, u32[]{:S(2)}, u32[]{:S(2)}) %collective-permute-start.14) | collective-permute-done | bytes 1032224 | tf_op jit(solution)/shard_map/ppermute | solution.py:104
  53.9 2.2 %kernel_grad.1 = f32[3,864,384]{2,1,0:T(8,128)} custom-call(bf16[1344,384]{1,0:T(8,128)(2,1)S(1)} %sums.1.refs_0_, bf16[1344,384]{1,0:T(8,128)(2,1)S(1)} %collective-permute-done.14.refs_1_), custom_call_target="tpu_custom_call" | custom-call | flops 1 | bytes 1 | tf_op jit(solution)/shard_map/kernel_grad/pallas_call | solution.py:143
  (6 shorter events, 0.0 us)
Async XLA Ops:
  0.6 0.9 %copy-start.2 = (bf16[96,1,4,256]{3,2,1,0:T(4,128)(2,1)S(1)}, bf16[96,1,4,256]{3,2,1,0:T(4,128)(2,1)}, u32[]{:S(2)}) copy-start(bf16[96,1,4,256]{3,2,1,0:T(4,128)(2,1)} %refs_0_.3) | copy-start | bytes 589828
  2.2 6.2 %collective-permute-start = (bf16[96,1024]{1,0:T(8,128)(2,1)S(1)}, bf16[96,1024]{1,0:T(8,128)(2,1)S(1)}, u32[]{:S(2)}, u32[]{:S(2)}) collective-permute-start(bf16[96,1024]{1,0:T(8,128)(2,1)S(1)} %activate.1.refs_0_.refs_1_), channel_id=1, source_target_pairs={{0,2},{2,0},{1,3},{3,1},{4,6},{6,4},{5,7},{7,5},{8,10},{10,8},{9,1... | collective-permute-start | bytes 589832 | tf_op jit(solution)/shard_map/ppermute | solution.py:104
  2.7 5.7 %collective-permute-start.2 = (bf16[96,1,4,256]{3,2,1,0:T(4,128)(2,1)}, bf16[96,1,4,256]{3,2,1,0:T(4,128)(2,1)S(1)}, u32[]{:S(2)}, u32[]{:S(2)}) collective-permute-start(bf16[96,1,4,256]{3,2,1,0:T(4,128)(2,1)} %refs_2_.1), channel_id=1, source_target_pairs={{0,2},{2,0},{1,3},{3,1},{4,6},{6,4},{5,7},{7,5},{8,10},{10,8},{9,1... | collective-permute-start | bytes 589832 | tf_op jit(solution)/shard_map/ppermute | solution.py:104
  2.8 14.8 %collective-permute-start.3 = (bf16[96,1024]{1,0:T(8,128)(2,1)S(1)}, bf16[96,1024]{1,0:T(8,128)(2,1)S(1)}, u32[]{:S(2)}, u32[]{:S(2)}) collective-permute-start(bf16[96,1024]{1,0:T(8,128)(2,1)S(1)} %activate.1.refs_0_.refs_1_), channel_id=1, source_target_pairs={{0,4},{4,0},{8,12},{12,8},{1,5},{5,1},{9,13},{13,9},{2,6},{6,2},{1... | collective-permute-start | bytes 589832 | tf_op jit(solution)/shard_map/ppermute | solution.py:383
  5.8 11.8 %collective-permute-start.1 = (bf16[96,1024]{1,0:T(8,128)(2,1)S(1)}, bf16[96,1024]{1,0:T(8,128)(2,1)S(1)}, u32[]{:S(2)}, u32[]{:S(2)}) collective-permute-start(bf16[96,1024]{1,0:T(8,128)(2,1)S(1)} %activate.1.refs_0_.refs_1_), channel_id=1, source_target_pairs={{0,8},{4,12},{8,0},{12,4},{1,9},{5,13},{9,1},{13,5},{2,10},{6,14},... | collective-permute-start | bytes 589832 | tf_op jit(solution)/shard_map/ppermute | solution.py:383
  8.4 0.9 %copy-start.4 = (bf16[96,1,4,256]{3,2,1,0:T(4,128)(2,1)S(1)}, bf16[96,1,4,256]{3,2,1,0:T(4,128)(2,1)}, u32[]{:S(2)}) copy-start(bf16[96,1,4,256]{3,2,1,0:T(4,128)(2,1)} %refs_2_.1) | copy-start | bytes 589828
  11.5 7.7 %collective-permute-start.8 = (bf16[336,384]{1,0:T(8,128)(2,1)S(1)}, bf16[336,384]{1,0:T(8,128)(2,1)S(1)}, u32[]{:S(2)}, u32[]{:S(2)}) collective-permute-start(bf16[336,384]{1,0:T(8,128)(2,1)S(1)} %get-tuple-element.14.refs_2_.refs_0_), channel_id=1, source_target_pairs={{0,1},{1,0},{2,3},{3,2},{4,5},{5,4},{6,7},{7,6},{8,9},{9,8},{10,11... | collective-permute-start | bytes 774152 | tf_op jit(solution)/shard_map/ppermute | solution.py:104
  13.0 1.6 %copy-start = (bf16[96,27,384]{2,0,1:T(8,128)(2,1)S(1)}, bf16[96,27,384]{2,0,1:T(8,128)(2,1)}, u32[]{:S(2)}) copy-start(bf16[96,27,384]{2,0,1:T(8,128)(2,1)} %param.4) | copy-start | bytes 5971972
  17.6 1.5 %collective-permute-start.4 = (bf16[96,1024]{1,0:T(8,128)(2,1)S(1)}, bf16[96,1024]{1,0:T(8,128)(2,1)S(1)}, u32[]{:S(2)}, u32[]{:S(2)}) collective-permute-start(bf16[96,1024]{1,0:T(8,128)(2,1)S(1)} %hand_on.3.refs_1_.refs_3_), channel_id=1, source_target_pairs={{0,2},{2,0},{1,3},{3,1},{4,6},{6,4},{5,7},{7,5},{8,10},{10,8},{9,1... | collective-permute-start | bytes 589832 | tf_op jit(solution)/shard_map/ppermute | solution.py:104
  17.6 12.0 %collective-permute-start.7 = (bf16[2,96,1024]{2,1,0:T(8,128)(2,1)S(1)}, bf16[2,96,1024]{2,1,0:T(8,128)(2,1)S(1)}, u32[]{:S(2)}, u32[]{:S(2)}) collective-permute-start(bf16[2,96,1024]{2,1,0:T(8,128)(2,1)S(1)} %get-tuple-element.17), channel_id=1, source_target_pairs={{0,4},{4,0},{8,12},{12,8},{1,5},{5,1},{9,13},{13,9},{2,6},{6,2},{1... | collective-permute-start | bytes 1179656 | tf_op jit(solution)/shard_map/ppermute | solution.py:383
  20.5 12.9 %collective-permute-start.9 = (bf16[336,384]{1,0:T(8,128)(2,1)S(1)}, bf16[336,384]{1,0:T(8,128)(2,1)S(1)}, u32[]{:S(2)}, u32[]{:S(2)}) collective-permute-start(bf16[336,384]{1,0:T(8,128)(2,1)S(1)} %terms_1.1.refs_3_.refs_1_), channel_id=1, source_target_pairs={{0,1},{1,0},{2,3},{3,2},{4,5},{5,4},{6,7},{7,6},{8,9},{9,8},{10,11... | collective-permute-start | bytes 774152 | tf_op jit(solution)/shard_map/ppermute | solution.py:104
  22.1 1.4 %collective-permute-start.5 = (bf16[96,1024]{1,0:T(8,128)(2,1)S(1)}, bf16[96,1024]{1,0:T(8,128)(2,1)S(1)}, u32[]{:S(2)}, u32[]{:S(2)}) collective-permute-start(bf16[96,1024]{1,0:T(8,128)(2,1)S(1)} %hand_on.4.refs_1_.refs_5_), channel_id=1, source_target_pairs={{0,2},{2,0},{1,3},{3,1},{4,6},{6,4},{5,7},{7,5},{8,10},{10,8},{9,1... | collective-permute-start | bytes 589832 | tf_op jit(solution)/shard_map/ppermute | solution.py:104
  22.1 11.3 %collective-permute-start.6 = (bf16[96,1024]{1,0:T(8,128)(2,1)S(1)}, bf16[96,1024]{1,0:T(8,128)(2,1)S(1)}, u32[]{:S(2)}, u32[]{:S(2)}) collective-permute-start(bf16[96,1024]{1,0:T(8,128)(2,1)S(1)} %hand_on.3.refs_1_.refs_3_), channel_id=1, source_target_pairs={{0,4},{4,0},{8,12},{12,8},{1,5},{5,1},{9,13},{13,9},{2,6},{6,2},{1... | collective-permute-start | bytes 589832 | tf_op jit(solution)/shard_map/ppermute | solution.py:383
  29.6 9.5 %copy-start.1 = (bf16[96,27,384]{2,0,1:T(8,128)(2,1)S(1)}, bf16[96,27,384]{2,0,1:T(8,128)(2,1)}, u32[]{:S(2)}) copy-start(bf16[96,27,384]{2,0,1:T(8,128)(2,1)} %param.4) | copy-start | bytes 5971972
  33.4 1.4 %collective-permute-start.10 = (bf16[96,1024]{1,0:T(8,128)(2,1)S(1)}, bf16[96,1024]{1,0:T(8,128)(2,1)S(1)}, u32[]{:S(2)}, u32[]{:S(2)}) collective-permute-start(bf16[96,1024]{1,0:T(8,128)(2,1)S(1)} %hand_on.5.refs_1_.refs_7_), channel_id=1, source_target_pairs={{0,2},{2,0},{1,3},{3,1},{4,6},{6,4},{5,7},{7,5},{8,10},{10,8},{9,1... | collective-permute-start | bytes 589832 | tf_op jit(solution)/shard_map/ppermute | solution.py:104
  33.4 9.8 %collective-permute-start.12 = (bf16[336,384]{1,0:T(8,128)(2,1)S(1)}, bf16[336,384]{1,0:T(8,128)(2,1)S(1)}, u32[]{:S(2)}, u32[]{:S(2)}) collective-permute-start(bf16[336,384]{1,0:T(8,128)(2,1)S(1)} %terms_2.1.refs_2_), channel_id=1, source_target_pairs={{0,1},{1,0},{2,3},{3,2},{4,5},{5,4},{6,7},{7,6},{8,9},{9,8},{10,11... | collective-permute-start | bytes 774152 | tf_op jit(solution)/shard_map/ppermute | solution.py:104
  36.4 13.1 %copy-start.3 = (bf16[96,1,4,256]{3,2,1,0:T(4,128)(2,1)S(1)}, bf16[96,1,4,256]{3,2,1,0:T(4,128)(2,1)}, u32[]{:S(2)}) copy-start(bf16[96,1,4,256]{3,2,1,0:T(4,128)(2,1)} %refs_0_.3) | copy-start | bytes 589828
  36.4 14.5 %collective-permute-start.13 = (bf16[336,384]{1,0:T(8,128)(2,1)S(1)}, bf16[336,384]{1,0:T(8,128)(2,1)S(1)}, u32[]{:S(2)}, u32[]{:S(2)}) collective-permute-start(bf16[336,384]{1,0:T(8,128)(2,1)S(1)} %terms_3.1.refs_9_.refs_3_), channel_id=1, source_target_pairs={{0,1},{1,0},{2,3},{3,2},{4,5},{5,4},{6,7},{7,6},{8,9},{9,8},{10,11... | collective-permute-start | bytes 774152 | tf_op jit(solution)/shard_map/ppermute | solution.py:104
  37.8 11.7 %collective-permute-start.11 = (bf16[96,1024]{1,0:T(8,128)(2,1)S(1)}, bf16[96,1024]{1,0:T(8,128)(2,1)S(1)}, u32[]{:S(2)}, u32[]{:S(2)}) collective-permute-start(bf16[96,1024]{1,0:T(8,128)(2,1)S(1)} %carry_share.1.refs_1_), channel_id=1, source_target_pairs={{0,8},{4,12},{8,0},{12,4},{1,9},{5,13},{9,1},{13,5},{2,10},{6,14},... | collective-permute-start | bytes 589832 | tf_op jit(solution)/shard_map/ppermute | solution.py:383
  51.2 2.7 %collective-permute-start.14 = (bf16[1344,384]{1,0:T(8,128)(2,1)S(1)}, bf16[1344,384]{1,0:T(8,128)(2,1)S(1)}, u32[]{:S(2)}, u32[]{:S(2)}) collective-permute-start(bf16[1344,384]{1,0:T(8,128)(2,1)S(1)} %sums.1.refs_0_), channel_id=1, source_target_pairs={{0,2},{2,0},{1,3},{3,1},{4,6},{6,4},{5,7},{7,5},{8,10},{10,8},{9,1... | collective-permute-start | bytes 3096584 | tf_op jit(solution)/shard_map/ppermute | solution.py:104

commit v3 on v2

--- a/solution.py
+++ b/solution.py
@@ -14,7 +14,7 @@
 BF16 = jnp.bfloat16
 VMEM_LIMIT = 24 * 1024 * 1024
 TOKEN = (8, 128)
-FEATURE_COST = 1024 * 1024
+FEATURE_COST = 3 * 10**9
 
 
 def from_behind(x, axis, by):
@@ -145,8 +145,8 @@
     )(*args, *waits)
 
 
-def cost(bytes_like=1):
-    return pl.CostEstimate(flops=1, bytes_accessed=bytes_like, transcendentals=0)
+def cost(flops=1):
+    return pl.CostEstimate(flops=flops, bytes_accessed=1, transcendentals=0)
 
 
 def whole():
@@ -224,44 +224,52 @@
     out[3 * tail :, :] = terms[3 * tail : main].astype(BF16)
 
 
-def own_terms_kernel(pixels, mine, other, cot, cot_other, out, stack, later, rhs, flat):
-    _, _, frames, _ = cot.shape
-    length = frames * pixels
+def own_terms_kernel(pixels, mine, other, flat, out, stack, rhs):
+    fill_stack(pixels, flat, stack, lax.axis_index("tm"))
+    block_terms(pixels, 0, stack, mine, other, out, rhs)
+
+
+def terms_kernel(pixels, k, stack, here, there, out, rhs):
+    block_terms(pixels, k, stack, here, there, out, rhs)
+
+
+def share_kernel(pixels, weights, cot, cot_other, own, kept, sent, flat, held, mine, stack, total, sems):
+    loads = [
+        pltpu.make_async_copy(source, target, sems.at[n])
+        for n, (source, target) in enumerate(((cot, mine), (weights, held)))
+    ]
+    for load in loads:
+        load.start()
+    rows, length = own.shape
+    frames = length // pixels
+    count = held.shape[1] // rows
     me = lax.axis_index("tm")
-    for core, source in ((me, cot), (1 - me, cot_other)):
+
+    def flatten(core, source):
         wide = source[:, 0].astype(F32)
         for t in range(frames):
             at = pl.multiple_of((core * frames + t) * pixels, pixels)
             flat[:, pl.ds(at, pixels)] = wide[:, t, :]
-    own = pl.ds(pl.multiple_of(me * length, pixels), length)
-    later[:, :length] = flat[:, own].astype(BF16)
-    after_own = flat[:, length : length + 2 * pixels]
-    later[:, length:] = jnp.where(me == 0, after_own, 0.0).astype(BF16)
-    fill_stack(pixels, flat, stack, me)
-    block_terms(pixels, 0, stack, mine, other, out, rhs)
-
-
-def terms_kernel(pixels, k, stack, here, there, out, rhs):
-    block_terms(pixels, k, stack, here, there, out, rhs)
-
-
-def share_kernel(pixels, weights, later, own, kept, sent, stack, total):
-    rows = later.shape[0]
-    length = own.shape[1]
-    frames = length // pixels
-    count = weights.shape[1] // rows
+
+    flatten(1 - me, cot_other)
+    loads[0].wait()
+    flatten(me, mine)
     for t in range(frames + 2):
         at = slice(t * pixels, (t + 1) * pixels)
-        frame = later[:, at].astype(F32)
+        if t < frames:
+            frame = flat[:, pl.ds(pl.multiple_of((me * frames + t) * pixels, pixels), pixels)]
+        else:
+            frame = jnp.where(me == 0, flat[:, at], 0.0)
         for i in range(3):
             for j in range(3):
                 row = (3 * i + j) * rows
                 stack[row : row + rows, at] = shifted(frame, 1 - i, 1 - j).astype(BF16)
+    loads[1].wait()
     taps = 9 * rows
     acc = None
     for a in range(3):
         term = lax.dot_general(
-            weights[a * taps : (a + 1) * taps, :],
+            held[a * taps : (a + 1) * taps, :],
             stack[:, (2 - a) * pixels : (2 - a) * pixels + length],
             (((0,), (0,)), ((), ())),
             preferred_element_type=F32,
@@ -331,27 +339,31 @@
     out, ins = refs[-1], refs[:-1]
     count = len(ins) // 2
     for k in range(count):
-        at = pl.multiple_of(shard_at(count, k) * main, SUB)
         total = ins[k][...].astype(F32) + ins[count + k][...].astype(F32)
-        out[pl.ds(at, main), :] = total.astype(BF16)
-
-
-def finish_kernel(scale, main, count, sums, other_sums, out, laid, sems):
+        out[k * main : (k + 1) * main, :] = total.astype(BF16)
+
+
+def finish_kernel(scale, main, early, other_early, late, other_late, out, laid, sems):
     channels = out.shape[2]
+    first = early.shape[0] // main
+    count = first + late.shape[0] // main
     rows, half = channels // count, out.shape[1] // 2
     unit = rows // 2
     me = lax.axis_index("tm")
+    shards = [shard_at(count, k) for k in range(count)]
     copies = []
-    for which, source in ((me, sums), (1 - me, other_sums)):
+    for which, one, two in ((me, early, late), (1 - me, other_early, other_late)):
         start = pl.multiple_of(which * half, 8)
         for a in range(3):
             for q in range(9):
                 base = q * unit if q < 7 else a * 2 * unit + (q - 7) * unit
                 step = a if q < 7 else 3
                 total = None
-                for s in range(count):
-                    piece = source[s * main + base : s * main + base + unit, :].astype(F32)
-                    mask = in_slot(channels, rows, (s + step) % count)
+                for k, shard in enumerate(shards):
+                    source, place = (one, k) if k < first else (two, k - first)
+                    at = place * main + base
+                    piece = source[at : at + unit, :].astype(F32)
+                    mask = in_slot(channels, rows, lax.rem(shard + step, count))
                     total = piece if total is None else jnp.where(mask, piece, total)
                 total = total * scale
                 if step:
@@ -363,6 +375,10 @@
             copies.append(copy)
     for copy in copies:
         copy.wait()
+
+
+def in_place(x):
+    return pltpu.with_memory_space_constraint(x, pltpu.HBM)
 
 
 def local_fast(features, kernel, cotangent):
@@ -393,32 +409,37 @@
     )
     other = rotate(activation, "tm", 1)
     far, near = swap(activation, 2), swap(activation, 1)
-    own_term, stack, later = run(
-        functools.partial(own_terms_kernel, pixels),
-        (activation, other, cotangent, cot_other),
-        out_shape=(term_shape, stack_shape, sds((rows, length + 2 * pixels), BF16)),
-        out_specs=(whole(),) * 3,
-        scratch_shapes=[rhs, pltpu.VMEM((rows, 2 * length), F32)],
-        name="own_terms",
-    )
-    terms, got = [own_term], [rotate(own_term, "dp", 1)]
-    own_share, kept, sent = run(
+    own_share, kept, sent, flat = run(
         functools.partial(share_kernel, pixels),
-        (weights, later),
-        waits=(own_term,),
+        (in_place(weights), in_place(cotangent), cot_other),
+        in_specs=[pl.BlockSpec(memory_space=pltpu.HBM)] * 2 + [whole()],
         out_shape=(
             sds((rows, length), F32),
             sds((rows, length), F32),
             sds((2, rows, length), BF16),
+            sds((rows, 2 * length), F32),
         ),
-        out_specs=(whole(),) * 3,
+        out_specs=(whole(),) * 4,
         scratch_shapes=[
+            pltpu.VMEM((taps * rows, channels), BF16),
+            pltpu.VMEM(cotangent.shape, BF16),
             pltpu.VMEM((9 * rows, (frames + 2) * pixels), BF16),
             pltpu.VMEM((channels, length), F32),
+            pltpu.SemaphoreType.DMA((2,)),
         ],
         name="shares",
     )
     first_share = swap(sent, 1)
+    own_term, stack = run(
+        functools.partial(own_terms_kernel, pixels),
+        (activation, other, flat),
+        out_shape=(term_shape, stack_shape),
+        out_specs=(whole(),) * 2,
+        scratch_shapes=[rhs],
+        name="own_terms",
+    )
+    terms, got = [own_term], [rotate(own_term, "dp", 1)]
+
     blocks = [activation, other]
 
     def terms_of(k, here, waits=()):
@@ -436,11 +457,10 @@
         got.append(rotate(term, "dp", 1))
         return term
 
-    far = after(far, own_share, near)
+    far = after(far, own_term, near)
     near = after(near, far)
     last = swap(far, 1)
     term = terms_of(1, far, (got[0],))
-    term = terms_of(2, near, (term,))
     carry = run(
         add_kernel,
         (kept, first_share),
@@ -450,39 +470,44 @@
         name="carry_share",
     )
     second_share = swap(carry, 2)
-    term = terms_of(3, after(last, carry, got[1]))
+    term = terms_of(2, near, (carry,))
+    term = terms_of(3, after(last, term, got[1]))
+
+    def sums(first, stop, waits=()):
+        return run(
+            functools.partial(sum_kernel, main),
+            (*terms[first:stop], *got[first:stop]),
+            waits=waits,
+            out_shape=sds(((stop - first) * main, channels), BF16),
+            out_specs=whole(),
+            name=f"sums_{first}",
+        )
 
     conv_out, token = run(
         functools.partial(conv_kernel, pixels),
         (weights, *blocks),
-        waits=(term,),
+        waits=(term, got[2]),
         out_shape=(sds(features.shape, BF16), sds(TOKEN, F32)),
         out_specs=(whole(),) * 2,
         scratch_shapes=[pltpu.VMEM((channels, (frames + 2) * pixels), BF16)],
         name="conv",
     )
+    early = sums(0, 2)
     feature_grad, token = run(
         functools.partial(feature_kernel, pixels),
         (features, own_share, first_share, second_share),
-        waits=(token, got[2]),
+        waits=(token, early),
         out_shape=(sds(features.shape, BF16), sds(TOKEN, F32)),
         out_specs=(whole(),) * 2,
         cost_estimate=cost(FEATURE_COST),
         name="feature_grad",
     )
-    sums = run(
-        functools.partial(sum_kernel, main),
-        (*terms, *got),
-        waits=(token,),
-        out_shape=sds((count * main, channels), BF16),
-        out_specs=whole(),
-        name="sums",
-    )
+    late = sums(2, count, (token,))
     scale = 1.0 / math.sqrt(lax.axis_size("dp") * lax.axis_size("tm") * length)
     grad_shape = (3, 9 * rows, channels)
     kernel_grad = run(
-        functools.partial(finish_kernel, scale, main, count),
-        (sums, rotate(sums, "tm", 1)),
+        functools.partial(finish_kernel, scale, main),
+        (early, rotate(early, "tm", 1), late, rotate(late, "tm", 1)),
         out_shape=sds(grad_shape, F32),
         out_specs=pl.BlockSpec(memory_space=pl.ANY),
         scratch_shapes=[pltpu.VMEM(grad_shape, F32), pltpu.SemaphoreType.DMA((6,))],

time: 56.4 us -> 51.8 us (0.918)
  waiting for transfers between devices: 19.4 us -> 15.5 us
  local copies, waits for them, and re-layouts: 3.41 us -> 0.94 us
  Pallas kernels: 17.9 us -> 19.2 us
    ppermute x5, waiting for transfers between devices: 14.8 us -> 8.97 us  [swap(): return lax.ppermute(x, 'chan', [(z, z ^ far) for z in range(count)])]
    unnamed x10 -> x6, local copies, waits for them, and re-layouts: 3.41 us -> 0.94 us
    ppermute x10 -> x11, waiting for transfers between devices: 4.63 us -> 6.55 us  [rotate(): return lax.ppermute(x, axis, [(i, (i + by) % size) for i in range(size)])]
    pallas_call x11 -> x12, Pallas kernels: 17.9 us -> 19.2 us  [run(): pl.pallas_call(body, compiler_params=pltpu.CompilerParams(vmem_limit_byte...]
    ppermute x10 -> x11, starting transfers between devices: 6.73 us -> 7.24 us  [rotate(): return lax.ppermute(x, axis, [(i, (i + by) % size) for i in range(size)])]
  transfers between devices with their start and end apart: 15 -> 16, of which waited for: 7 -> 8; matrix products, arithmetic and copies ran while one was open for 0% -> 0% of each run, Pallas kernels for 26% -> 33%
where the time goes in v3:
time: 51.8 us; the launch traced here: 51.6 us
  Pallas kernels  19.2 us (37%)
  waiting for transfers between devices  15.5 us (30%)
  starting transfers between devices  15.1 us (29%)
  local copies, waits for them, and re-layouts  0.94 us (2%)
  between operations  0.89 us (2%)
    pallas_call x12, Pallas kernels, run(): pl.pallas_call(body, compiler_params=pltpu.CompilerParams(vmem_limit_byte...  19.2 us
    ppermute x5, waiting for transfers between devices, swap(): return lax.ppermute(x, 'chan', [(z, z ^ far) for z in range(count)])  8.97 us
    ppermute x5, starting transfers between devices, swap(): return lax.ppermute(x, 'chan', [(z, z ^ far) for z in range(count)])  7.87 us
    ppermute x11, starting transfers between devices, rotate(): return lax.ppermute(x, axis, [(i, (i + by) % size) for i in range(size)])  7.24 us
    ppermute x11, waiting for transfers between devices, rotate(): return lax.ppermute(x, axis, [(i, (i + by) % size) for i in range(size)])  6.55 us
  transfers between devices with their start and end apart: 16, of which 8 were waited for; matrix products, arithmetic and copies ran while one was open for 0% of the time, Pallas kernels for 33%

profile of v3, /device:TPU:0, one launch (start us, length us, event | category | flops | bytes accessed | tf_op | source)
XLA Modules:
  0.0 51.6 jit_solution(3293582355686623182)
XLA Ops:
  0.6 0.5 %collective-permute-start.2 = (bf16[96,1,4,256]{3,2,1,0:T(4,128)(2,1)}, bf16[96,1,4,256]{3,2,1,0:T(4,128)(2,1)S(1)}, u32[]{:S(2)}, u32[]{:S(2)}) collective-permute-start(bf16[96,1,4,256]{3,2,1,0:T(4,128)(2,1)} %refs_1_.1), channel_id=1, source_target_pairs={{0,2},{2,0},{1,3},{3,1},{4,6},{6,4},{5,7},{7,5},{8,10},{10,8},{9,1... | collective-permute-start | bytes 589832 | tf_op jit(solution)/shard_map/ppermute | solution.py:104
  1.1 0.0 copy-start.1
  1.1 0.9 %copy-done.1 = bf16[96,1,4,256]{3,2,1,0:T(4,128)(2,1)S(1)} copy-done((bf16[96,1,4,256]{3,2,1,0:T(4,128)(2,1)S(1)}, bf16[96,1,4,256]{3,2,1,0:T(4,128)(2,1)}, u32[]{:S(2)}) %copy-start.1) | copy-done | bytes 196632
  2.1 0.6 %activate.1.refs_0_.refs_1_ = bf16[96,1024]{1,0:T(8,128)(2,1)S(1)} custom-call(bf16[96,1,4,256]{3,2,1,0:T(4,128)(2,1)S(1)} %copy-done.1), custom_call_target="tpu_custom_call" | custom-call | flops 1 | bytes 1 | tf_op jit(solution)/shard_map/activate/pallas_call | solution.py:143
  2.7 0.1 collective-permute-start
  2.8 3.0 %collective-permute-start.3 = (bf16[96,1024]{1,0:T(8,128)(2,1)S(1)}, bf16[96,1024]{1,0:T(8,128)(2,1)S(1)}, u32[]{:S(2)}, u32[]{:S(2)}) collective-permute-start(bf16[96,1024]{1,0:T(8,128)(2,1)S(1)} %activate.1.refs_0_.refs_1_), channel_id=1, source_target_pairs={{0,4},{4,0},{8,12},{12,8},{1,5},{5,1},{9,13},{13,9},{2,6},{6,2},{1... | collective-permute-start | bytes 589832 | tf_op jit(solution)/shard_map/ppermute | solution.py:399
  5.8 2.6 %collective-permute-start.1 = (bf16[96,1024]{1,0:T(8,128)(2,1)S(1)}, bf16[96,1024]{1,0:T(8,128)(2,1)S(1)}, u32[]{:S(2)}, u32[]{:S(2)}) collective-permute-start(bf16[96,1024]{1,0:T(8,128)(2,1)S(1)} %activate.1.refs_0_.refs_1_), channel_id=1, source_target_pairs={{0,8},{4,12},{8,0},{12,4},{1,9},{5,13},{9,1},{13,5},{2,10},{6,14},... | collective-permute-start | bytes 589832 | tf_op jit(solution)/shard_map/ppermute | solution.py:399
  8.4 0.0 collective-permute-done.2.refs_2_
  8.4 4.5 %shares.1 = (f32[96,1024]{1,0:T(8,128)S(1)}, f32[96,1024]{1,0:T(8,128)S(1)}, bf16[2,96,1024]{2,1,0:T(8,128)(2,1)S(1)}, f32[96,2048]{1,0:T(8,128)S(1)}) custom-call(bf16[2592,384]{1,0:T(8,128)(2,1)} %bitcast.6, bf16[96,1,4,256]{3,2,1,0:T(4,128)(2,1)} %refs_1_.1, bf16[96,1,4,256]{3,2,1,0:T(4,128)(2,1)S(1)} %collective-permute-done.2.refs_2_), custom_call_target="tpu_custom_call" | custom-call | flops 1 | bytes 1 | tf_op jit(solution)/shard_map/shares/pallas_call | solution.py:143
  12.9 0.0 collective-permute-done.refs_1_.refs_2_
  12.9 1.8 %own_terms.1 = (bf16[336,384]{1,0:T(8,128)(2,1)S(1)}, bf16[432,2048]{1,0:T(8,128)(2,1)S(1)}) custom-call(bf16[96,1024]{1,0:T(8,128)(2,1)S(1)} %activate.1.refs_0_.refs_1_, bf16[96,1024]{1,0:T(8,128)(2,1)S(1)} %collective-permute-done.refs_1_.refs_2_, f32[96,2048]{1,0:T(8,128)S(1)} %get-tuple-element.13.refs_2_), custom_call_target="tpu_custom_call" | custom-call | flops 1 | bytes 1 | tf_op jit(solution)/shard_map/own_terms/pallas_call | solution.py:143
  14.7 1.6 %collective-permute-start.8 = (bf16[336,384]{1,0:T(8,128)(2,1)S(1)}, bf16[336,384]{1,0:T(8,128)(2,1)S(1)}, u32[]{:S(2)}, u32[]{:S(2)}) collective-permute-start(bf16[336,384]{1,0:T(8,128)(2,1)S(1)} %get-tuple-element.14.refs_1_.refs_0_), channel_id=1, source_target_pairs={{0,1},{1,0},{2,3},{3,2},{4,5},{5,4},{6,7},{7,6},{8,9},{9,8},{10,11... | collective-permute-start | bytes 774152 | tf_op jit(solution)/shard_map/ppermute | solution.py:104
  16.3 0.0 collective-permute-done.3.refs_2_.refs_0_
  16.3 1.3 %collective-permute-done.1.refs_0_ = bf16[96,1024]{1,0:T(8,128)(2,1)S(1)} collective-permute-done((bf16[96,1024]{1,0:T(8,128)(2,1)S(1)}, bf16[96,1024]{1,0:T(8,128)(2,1)S(1)}, u32[]{:S(2)}, u32[]{:S(2)}) %collective-permute-start.1) | collective-permute-done | bytes 196640 | tf_op jit(solution)/shard_map/ppermute | solution.py:399
  17.6 0.0 collective-permute-start.4
  17.6 0.4 collective-permute-start.7
  18.0 1.0 %collective-permute-done.4.refs_2_.refs_4_ = bf16[96,1024]{1,0:T(8,128)(2,1)S(1)} collective-permute-done((bf16[96,1024]{1,0:T(8,128)(2,1)S(1)}, bf16[96,1024]{1,0:T(8,128)(2,1)S(1)}, u32[]{:S(2)}, u32[]{:S(2)}) %collective-permute-start.4) | collective-permute-done | bytes 196640 | tf_op jit(solution)/shard_map/ppermute | solution.py:104
  19.0 3.4 %collective-permute-done.8.refs_3_.refs_2_ = bf16[336,384]{1,0:T(8,128)(2,1)S(1)} collective-permute-done((bf16[336,384]{1,0:T(8,128)(2,1)S(1)}, bf16[336,384]{1,0:T(8,128)(2,1)S(1)}, u32[]{:S(2)}, u32[]{:S(2)}) %collective-permute-start.8) | collective-permute-done | bytes 258080 | tf_op jit(solution)/shard_map/ppermute | solution.py:104
  22.4 1.3 %terms_1.1.refs_2_.refs_1_ = bf16[336,384]{1,0:T(8,128)(2,1)S(1)} custom-call(bf16[432,2048]{1,0:T(8,128)(2,1)S(1)} %get-tuple-element.15.refs_0_, bf16[96,1024]{1,0:T(8,128)(2,1)S(1)} %hand_on.3.refs_1_.refs_3_, bf16[96,1024]{1,0:T(8,128)(2,1)S(1)} %collective-permute-done.4.refs_2_.refs_4_, bf16[336,384]{1,0:T(8,128)(2,1)S(1)} %collective-permute-done.8.refs_3_.refs_2_), custom_call_target="tpu_custom_call" | custom-call | flops 1 | bytes 1 | tf_op jit(solution)/shard_map/terms_1/pallas_call | solution.py:143
  23.8 1.6 %collective-permute-start.9 = (bf16[336,384]{1,0:T(8,128)(2,1)S(1)}, bf16[336,384]{1,0:T(8,128)(2,1)S(1)}, u32[]{:S(2)}, u32[]{:S(2)}) collective-permute-start(bf16[336,384]{1,0:T(8,128)(2,1)S(1)} %terms_1.1.refs_2_.refs_1_), channel_id=1, source_target_pairs={{0,1},{1,0},{2,3},{3,2},{4,5},{5,4},{6,7},{7,6},{8,9},{9,8},{10,11... | collective-permute-start | bytes 774152 | tf_op jit(solution)/shard_map/ppermute | solution.py:104
  25.3 0.0 collective-permute-start.5
  25.3 0.4 collective-permute-start.6
  25.8 3.7 %collective-permute-done.7.refs_1_.refs_2_ = bf16[2,96,1024]{2,1,0:T(8,128)(2,1)S(1)} collective-permute-done((bf16[2,96,1024]{2,1,0:T(8,128)(2,1)S(1)}, bf16[2,96,1024]{2,1,0:T(8,128)(2,1)S(1)}, u32[]{:S(2)}, u32[]{:S(2)}) %collective-permute-start.7) | collective-permute-done | bytes 393248 | tf_op jit(solution)/shard_map/ppermute | solution.py:399
  29.6 0.0 collective-permute-done.5.refs_2_.refs_6_
  29.6 1.3 %terms_2.1.refs_1_.refs_0_ = bf16[336,384]{1,0:T(8,128)(2,1)S(1)} custom-call(bf16[432,2048]{1,0:T(8,128)(2,1)S(1)} %get-tuple-element.15.refs_0_, bf16[96,1024]{1,0:T(8,128)(2,1)S(1)} %hand_on.4.refs_1_.refs_5_, bf16[96,1024]{1,0:T(8,128)(2,1)S(1)} %collective-permute-done.5.refs_2_.refs_6_, bf16[96,1024]{1,0:T(8,128)(2,1)S(1)} %carry_share.1.refs_3_), custom_call_target="tpu_custom_call" | custom-call | flops 1 | bytes 1 | tf_op jit(solution)/shard_map/terms_2/pallas_call | solution.py:143
  30.9 1.6 %collective-permute-start.11 = (bf16[336,384]{1,0:T(8,128)(2,1)S(1)}, bf16[336,384]{1,0:T(8,128)(2,1)S(1)}, u32[]{:S(2)}, u32[]{:S(2)}) collective-permute-start(bf16[336,384]{1,0:T(8,128)(2,1)S(1)} %terms_2.1.refs_1_.refs_0_), channel_id=1, source_target_pairs={{0,1},{1,0},{2,3},{3,2},{4,5},{5,4},{6,7},{7,6},{8,9},{9,8},{10,11... | collective-permute-start | bytes 774152 | tf_op jit(solution)/shard_map/ppermute | solution.py:104
  32.5 0.9 %collective-permute-done.6.refs_0_ = bf16[96,1024]{1,0:T(8,128)(2,1)S(1)} collective-permute-done((bf16[96,1024]{1,0:T(8,128)(2,1)S(1)}, bf16[96,1024]{1,0:T(8,128)(2,1)S(1)}, u32[]{:S(2)}, u32[]{:S(2)}) %collective-permute-start.6) | collective-permute-done | bytes 196640 | tf_op jit(solution)/shard_map/ppermute | solution.py:399
  33.3 0.0 collective-permute-done.9.refs_2_.refs_3_
  33.3 0.0 collective-permute-start.10
  33.4 1.4 %collective-permute-start.12 = (bf16[96,1024]{1,0:T(8,128)(2,1)S(1)}, bf16[96,1024]{1,0:T(8,128)(2,1)S(1)}, u32[]{:S(2)}, u32[]{:S(2)}) collective-permute-start(bf16[96,1024]{1,0:T(8,128)(2,1)S(1)} %carry_share.1.refs_3_), channel_id=1, source_target_pairs={{0,8},{4,12},{8,0},{12,4},{1,9},{5,13},{9,1},{13,5},{2,10},{6,14},... | collective-permute-start | bytes 589832 | tf_op jit(solution)/shard_map/ppermute | solution.py:399
  34.7 0.1 sums_0.1.refs_5_.refs_0_
  34.8 0.2 collective-permute-start.13
  35.1 0.0 collective-permute-done.10.refs_2_.refs_8_
  35.1 1.5 %terms_3.1.refs_9_.refs_1_ = bf16[336,384]{1,0:T(8,128)(2,1)S(1)} custom-call(bf16[432,2048]{1,0:T(8,128)(2,1)S(1)} %get-tuple-element.15.refs_0_, bf16[96,1024]{1,0:T(8,128)(2,1)S(1)} %hand_on.5.refs_1_.refs_7_, bf16[96,1024]{1,0:T(8,128)(2,1)S(1)} %collective-permute-done.10.refs_2_.refs_8_), custom_call_target="tpu_custom_call" | custom-call | flops 1 | bytes 1 | tf_op jit(solution)/shard_map/terms_3/pallas_call | solution.py:143
  36.6 0.0 copy-start.2
  36.6 1.6 %collective-permute-start.14 = (bf16[336,384]{1,0:T(8,128)(2,1)S(1)}, bf16[336,384]{1,0:T(8,128)(2,1)S(1)}, u32[]{:S(2)}, u32[]{:S(2)}) collective-permute-start(bf16[336,384]{1,0:T(8,128)(2,1)S(1)} %terms_3.1.refs_9_.refs_1_), channel_id=1, source_target_pairs={{0,1},{1,0},{2,3},{3,2},{4,5},{5,4},{6,7},{7,6},{8,9},{9,8},{10,11... | collective-permute-start | bytes 774152 | tf_op jit(solution)/shard_map/ppermute | solution.py:104
  38.2 0.3 collective-permute-done.11.refs_10_.refs_2_
  38.5 0.0 copy-done
  38.5 4.1 %conv.1 = (bf16[96,1,4,256]{3,2,1,0:T(4,128)(2,1)}, f32[8,128]{1,0:T(8,128)S(1)}) custom-call(bf16[2592,384]{1,0:T(8,128)(2,1)S(1)} %bitcast.7, bf16[96,1024]{1,0:T(8,128)(2,1)S(1)} %activate.1.refs_0_.refs_1_, bf16[96,1024]{1,0:T(8,128)(2,1)S(1)} %collective-permute-done.refs_1_.refs_2_, bf16[96,1024]{1,0:T(8,128)(2,1)S(1)} %hand_on.3.refs_1_.refs_3_, ...), custom_call_target="tpu_custom_call" | custom-call | flops 1 | bytes 1 | tf_op jit(solution)/shard_map/conv/pallas_call | solution.py:143
  42.5 3.1 %collective-permute-done.12.refs_3_ = bf16[96,1024]{1,0:T(8,128)(2,1)S(1)} collective-permute-done((bf16[96,1024]{1,0:T(8,128)(2,1)S(1)}, bf16[96,1024]{1,0:T(8,128)(2,1)S(1)}, u32[]{:S(2)}, u32[]{:S(2)}) %collective-permute-start.12) | collective-permute-done | bytes 196640 | tf_op jit(solution)/shard_map/ppermute | solution.py:399
  45.7 0.0 copy-done.2
  45.7 1.4 %feature_grad.1 = (bf16[96,1,4,256]{3,2,1,0:T(4,128)(2,1)}, f32[8,128]{1,0:T(8,128)S(1)}) custom-call(bf16[96,1,4,256]{3,2,1,0:T(4,128)(2,1)S(1)} %copy-done.2, f32[96,1024]{1,0:T(8,128)S(1)} %get-tuple-element.19.refs_1_, bf16[2,96,1024]{2,1,0:T(8,128)(2,1)S(1)} %collective-permute-done.7.refs_1_.refs_2_, ...), custom_call_target="tpu_custom_call" | custom-call | flops 3000000000 | bytes 1 | tf_op jit(solution)/shard_map/feature_grad/pallas_call | solution.py:143
  47.1 0.0 collective-permute-done.14.refs_3_
  47.1 0.1 sums_2.1.refs_2_
  47.2 0.1 collective-permute-start.15
  47.3 0.0 collective-permute-done.13.refs_1_
  47.3 1.8 %collective-permute-done.15.refs_3_ = bf16[672,384]{1,0:T(8,128)(2,1)S(1)} collective-permute-done((bf16[672,384]{1,0:T(8,128)(2,1)S(1)}, bf16[672,384]{1,0:T(8,128)(2,1)S(1)}, u32[]{:S(2)}, u32[]{:S(2)}) %collective-permute-start.15) | collective-permute-done | bytes 516128 | tf_op jit(solution)/shard_map/ppermute | solution.py:104
  49.2 2.3 %kernel_grad.1 = f32[3,864,384]{2,1,0:T(8,128)} custom-call(bf16[672,384]{1,0:T(8,128)(2,1)S(1)} %sums_0.1.refs_5_.refs_0_, bf16[672,384]{1,0:T(8,128)(2,1)S(1)} %collective-permute-done.13.refs_1_, bf16[672,384]{1,0:T(8,128)(2,1)S(1)} %sums_2.1.refs_2_, bf16[672,384]{1,0:T(8,128)(2,1)S(1)} %collective-permute-done.15.refs_3_), custom_call_target="tpu_custom_call" | custom-call | flops 1 | bytes 1 | tf_op jit(solution)/shard_map/kernel_grad/pallas_call | solution.py:143
  (5 shorter events, 0.1 us)
Async XLA Ops:
  0.6 7.8 %collective-permute-start.2 = (bf16[96,1,4,256]{3,2,1,0:T(4,128)(2,1)}, bf16[96,1,4,256]{3,2,1,0:T(4,128)(2,1)S(1)}, u32[]{:S(2)}, u32[]{:S(2)}) collective-permute-start(bf16[96,1,4,256]{3,2,1,0:T(4,128)(2,1)} %refs_1_.1), channel_id=1, source_target_pairs={{0,2},{2,0},{1,3},{3,1},{4,6},{6,4},{5,7},{7,5},{8,10},{10,8},{9,1... | collective-permute-start | bytes 589832 | tf_op jit(solution)/shard_map/ppermute | solution.py:104
  1.1 0.9 %copy-start.1 = (bf16[96,1,4,256]{3,2,1,0:T(4,128)(2,1)S(1)}, bf16[96,1,4,256]{3,2,1,0:T(4,128)(2,1)}, u32[]{:S(2)}) copy-start(bf16[96,1,4,256]{3,2,1,0:T(4,128)(2,1)} %refs_0_.3) | copy-start | bytes 589828
  2.7 10.2 %collective-permute-start = (bf16[96,1024]{1,0:T(8,128)(2,1)S(1)}, bf16[96,1024]{1,0:T(8,128)(2,1)S(1)}, u32[]{:S(2)}, u32[]{:S(2)}) collective-permute-start(bf16[96,1024]{1,0:T(8,128)(2,1)S(1)} %activate.1.refs_0_.refs_1_), channel_id=1, source_target_pairs={{0,2},{2,0},{1,3},{3,1},{4,6},{6,4},{5,7},{7,5},{8,10},{10,8},{9,1... | collective-permute-start | bytes 589832 | tf_op jit(solution)/shard_map/ppermute | solution.py:104
  2.8 13.5 %collective-permute-start.3 = (bf16[96,1024]{1,0:T(8,128)(2,1)S(1)}, bf16[96,1024]{1,0:T(8,128)(2,1)S(1)}, u32[]{:S(2)}, u32[]{:S(2)}) collective-permute-start(bf16[96,1024]{1,0:T(8,128)(2,1)S(1)} %activate.1.refs_0_.refs_1_), channel_id=1, source_target_pairs={{0,4},{4,0},{8,12},{12,8},{1,5},{5,1},{9,13},{13,9},{2,6},{6,2},{1... | collective-permute-start | bytes 589832 | tf_op jit(solution)/shard_map/ppermute | solution.py:399
  5.8 11.8 %collective-permute-start.1 = (bf16[96,1024]{1,0:T(8,128)(2,1)S(1)}, bf16[96,1024]{1,0:T(8,128)(2,1)S(1)}, u32[]{:S(2)}, u32[]{:S(2)}) collective-permute-start(bf16[96,1024]{1,0:T(8,128)(2,1)S(1)} %activate.1.refs_0_.refs_1_), channel_id=1, source_target_pairs={{0,8},{4,12},{8,0},{12,4},{1,9},{5,13},{9,1},{13,5},{2,10},{6,14},... | collective-permute-start | bytes 589832 | tf_op jit(solution)/shard_map/ppermute | solution.py:399
  14.7 7.7 %collective-permute-start.8 = (bf16[336,384]{1,0:T(8,128)(2,1)S(1)}, bf16[336,384]{1,0:T(8,128)(2,1)S(1)}, u32[]{:S(2)}, u32[]{:S(2)}) collective-permute-start(bf16[336,384]{1,0:T(8,128)(2,1)S(1)} %get-tuple-element.14.refs_1_.refs_0_), channel_id=1, source_target_pairs={{0,1},{1,0},{2,3},{3,2},{4,5},{5,4},{6,7},{7,6},{8,9},{9,8},{10,11... | collective-permute-start | bytes 774152 | tf_op jit(solution)/shard_map/ppermute | solution.py:104
  17.6 1.4 %collective-permute-start.4 = (bf16[96,1024]{1,0:T(8,128)(2,1)S(1)}, bf16[96,1024]{1,0:T(8,128)(2,1)S(1)}, u32[]{:S(2)}, u32[]{:S(2)}) collective-permute-start(bf16[96,1024]{1,0:T(8,128)(2,1)S(1)} %hand_on.3.refs_1_.refs_3_), channel_id=1, source_target_pairs={{0,2},{2,0},{1,3},{3,1},{4,6},{6,4},{5,7},{7,5},{8,10},{10,8},{9,1... | collective-permute-start | bytes 589832 | tf_op jit(solution)/shard_map/ppermute | solution.py:104
  17.6 11.9 %collective-permute-start.7 = (bf16[2,96,1024]{2,1,0:T(8,128)(2,1)S(1)}, bf16[2,96,1024]{2,1,0:T(8,128)(2,1)S(1)}, u32[]{:S(2)}, u32[]{:S(2)}) collective-permute-start(bf16[2,96,1024]{2,1,0:T(8,128)(2,1)S(1)} %get-tuple-element.17), channel_id=1, source_target_pairs={{0,4},{4,0},{8,12},{12,8},{1,5},{5,1},{9,13},{13,9},{2,6},{6,2},{1... | collective-permute-start | bytes 1179656 | tf_op jit(solution)/shard_map/ppermute | solution.py:399
  23.8 9.6 %collective-permute-start.9 = (bf16[336,384]{1,0:T(8,128)(2,1)S(1)}, bf16[336,384]{1,0:T(8,128)(2,1)S(1)}, u32[]{:S(2)}, u32[]{:S(2)}) collective-permute-start(bf16[336,384]{1,0:T(8,128)(2,1)S(1)} %terms_1.1.refs_2_.refs_1_), channel_id=1, source_target_pairs={{0,1},{1,0},{2,3},{3,2},{4,5},{5,4},{6,7},{7,6},{8,9},{9,8},{10,11... | collective-permute-start | bytes 774152 | tf_op jit(solution)/shard_map/ppermute | solution.py:104
  25.3 4.2 %collective-permute-start.5 = (bf16[96,1024]{1,0:T(8,128)(2,1)S(1)}, bf16[96,1024]{1,0:T(8,128)(2,1)S(1)}, u32[]{:S(2)}, u32[]{:S(2)}) collective-permute-start(bf16[96,1024]{1,0:T(8,128)(2,1)S(1)} %hand_on.4.refs_1_.refs_5_), channel_id=1, source_target_pairs={{0,2},{2,0},{1,3},{3,1},{4,6},{6,4},{5,7},{7,5},{8,10},{10,8},{9,1... | collective-permute-start | bytes 589832 | tf_op jit(solution)/shard_map/ppermute | solution.py:104
  25.3 8.0 %collective-permute-start.6 = (bf16[96,1024]{1,0:T(8,128)(2,1)S(1)}, bf16[96,1024]{1,0:T(8,128)(2,1)S(1)}, u32[]{:S(2)}, u32[]{:S(2)}) collective-permute-start(bf16[96,1024]{1,0:T(8,128)(2,1)S(1)} %hand_on.3.refs_1_.refs_3_), channel_id=1, source_target_pairs={{0,4},{4,0},{8,12},{12,8},{1,5},{5,1},{9,13},{13,9},{2,6},{6,2},{1... | collective-permute-start | bytes 589832 | tf_op jit(solution)/shard_map/ppermute | solution.py:399
  30.9 7.5 %collective-permute-start.11 = (bf16[336,384]{1,0:T(8,128)(2,1)S(1)}, bf16[336,384]{1,0:T(8,128)(2,1)S(1)}, u32[]{:S(2)}, u32[]{:S(2)}) collective-permute-start(bf16[336,384]{1,0:T(8,128)(2,1)S(1)} %terms_2.1.refs_1_.refs_0_), channel_id=1, source_target_pairs={{0,1},{1,0},{2,3},{3,2},{4,5},{5,4},{6,7},{7,6},{8,9},{9,8},{10,11... | collective-permute-start | bytes 774152 | tf_op jit(solution)/shard_map/ppermute | solution.py:104
  33.3 5.1 %copy-start = (bf16[96,27,384]{2,0,1:T(8,128)(2,1)S(1)}, bf16[96,27,384]{2,0,1:T(8,128)(2,1)}, u32[]{:S(2)}) copy-start(bf16[96,27,384]{2,0,1:T(8,128)(2,1)} %param.4) | copy-start | bytes 5971972
  33.3 1.7 %collective-permute-start.10 = (bf16[96,1024]{1,0:T(8,128)(2,1)S(1)}, bf16[96,1024]{1,0:T(8,128)(2,1)S(1)}, u32[]{:S(2)}, u32[]{:S(2)}) collective-permute-start(bf16[96,1024]{1,0:T(8,128)(2,1)S(1)} %hand_on.5.refs_1_.refs_7_), channel_id=1, source_target_pairs={{0,2},{2,0},{1,3},{3,1},{4,6},{6,4},{5,7},{7,5},{8,10},{10,8},{9,1... | collective-permute-start | bytes 589832 | tf_op jit(solution)/shard_map/ppermute | solution.py:104
  33.4 12.3 %collective-permute-start.12 = (bf16[96,1024]{1,0:T(8,128)(2,1)S(1)}, bf16[96,1024]{1,0:T(8,128)(2,1)S(1)}, u32[]{:S(2)}, u32[]{:S(2)}) collective-permute-start(bf16[96,1024]{1,0:T(8,128)(2,1)S(1)} %carry_share.1.refs_3_), channel_id=1, source_target_pairs={{0,8},{4,12},{8,0},{12,4},{1,9},{5,13},{9,1},{13,5},{2,10},{6,14},... | collective-permute-start | bytes 589832 | tf_op jit(solution)/shard_map/ppermute | solution.py:399
  34.8 12.5 %collective-permute-start.13 = (bf16[672,384]{1,0:T(8,128)(2,1)S(1)}, bf16[672,384]{1,0:T(8,128)(2,1)S(1)}, u32[]{:S(2)}, u32[]{:S(2)}) collective-permute-start(bf16[672,384]{1,0:T(8,128)(2,1)S(1)} %sums_0.1.refs_5_.refs_0_), channel_id=1, source_target_pairs={{0,2},{2,0},{1,3},{3,1},{4,6},{6,4},{5,7},{7,5},{8,10},{10,8},{9,1... | collective-permute-start | bytes 1548296 | tf_op jit(solution)/shard_map/ppermute | solution.py:104
  36.6 9.1 %copy-start.2 = (bf16[96,1,4,256]{3,2,1,0:T(4,128)(2,1)S(1)}, bf16[96,1,4,256]{3,2,1,0:T(4,128)(2,1)}, u32[]{:S(2)}) copy-start(bf16[96,1,4,256]{3,2,1,0:T(4,128)(2,1)} %refs_0_.3) | copy-start | bytes 589828
  36.6 10.5 %collective-permute-start.14 = (bf16[336,384]{1,0:T(8,128)(2,1)S(1)}, bf16[336,384]{1,0:T(8,128)(2,1)S(1)}, u32[]{:S(2)}, u32[]{:S(2)}) collective-permute-start(bf16[336,384]{1,0:T(8,128)(2,1)S(1)} %terms_3.1.refs_9_.refs_1_), channel_id=1, source_target_pairs={{0,1},{1,0},{2,3},{3,2},{4,5},{5,4},{6,7},{7,6},{8,9},{9,8},{10,11... | collective-permute-start | bytes 774152 | tf_op jit(solution)/shard_map/ppermute | solution.py:104
  47.2 2.0 %collective-permute-start.15 = (bf16[672,384]{1,0:T(8,128)(2,1)S(1)}, bf16[672,384]{1,0:T(8,128)(2,1)S(1)}, u32[]{:S(2)}, u32[]{:S(2)}) collective-permute-start(bf16[672,384]{1,0:T(8,128)(2,1)S(1)} %sums_2.1.refs_2_), channel_id=1, source_target_pairs={{0,2},{2,0},{1,3},{3,1},{4,6},{6,4},{5,7},{7,5},{8,10},{10,8},{9,1... | collective-permute-start | bytes 1548296 | tf_op jit(solution)/shard_map/ppermute | solution.py:104

commit v4 on v3

--- a/solution.py
+++ b/solution.py
@@ -153,17 +153,34 @@
     return pl.BlockSpec(memory_space=pltpu.VMEM)
 
 
-def activate_kernel(features, activation):
-    frames, pixels = features.shape[2:]
-    v = features[:, 0].astype(F32)
+def activate_kernel(features, cotangent, activation, flat, feat, cot, sems):
+    loads = [
+        pltpu.make_async_copy(source, target, sems.at[n])
+        for n, (source, target) in enumerate(((features, feat), (cotangent, cot)))
+    ]
+    for load in loads:
+        load.start()
+    frames, pixels = feat.shape[2:]
+    loads[0].wait()
+    v = feat[:, 0].astype(F32)
     act = v / (1.0 + jnp.exp(-v))
     for t in range(frames):
         activation[:, t * pixels : (t + 1) * pixels] = act[:, t, :].astype(BF16)
+    loads[1].wait()
+    flatten(pixels, cot, flat, 0)
+
+
+def flatten(pixels, source, flat, first):
+    wide = source[:, 0].astype(F32)
+    for t in range(wide.shape[1]):
+        at = (first + t) * pixels
+        at = at if isinstance(at, int) else pl.multiple_of(at, pixels)
+        flat[:, pl.ds(at, pixels)] = wide[:, t, :]
 
 
 def shard_at(count, k):
     z = lax.axis_index("chan")
-    return (z, lax.rem(z + 2, count), z + 1 - 2 * lax.rem(z, 2), count - 1 - z)[k]
+    return (z, z + 1 - 2 * lax.rem(z, 2), lax.rem(z + 2, count), count - 1 - z)[k]
 
 
 def in_slot(channels, rows, slot):
@@ -224,36 +241,29 @@
     out[3 * tail :, :] = terms[3 * tail : main].astype(BF16)
 
 
-def own_terms_kernel(pixels, mine, other, flat, out, stack, rhs):
-    fill_stack(pixels, flat, stack, lax.axis_index("tm"))
+def own_terms_kernel(
+    pixels, mine, other, flat_own, cot_other, weights, out, stack, flat, held, rhs, sems
+):
+    load = pltpu.make_async_copy(weights, held, sems.at[0])
+    load.start()
+    length = flat_own.shape[1]
+    me = lax.axis_index("tm")
+    flat[:, pl.ds(pl.multiple_of(me * length, pixels), length)] = flat_own[...]
+    flatten(pixels, cot_other, flat, (1 - me) * (length // pixels))
+    fill_stack(pixels, flat, stack, me)
     block_terms(pixels, 0, stack, mine, other, out, rhs)
+    load.wait()
 
 
 def terms_kernel(pixels, k, stack, here, there, out, rhs):
     block_terms(pixels, k, stack, here, there, out, rhs)
 
 
-def share_kernel(pixels, weights, cot, cot_other, own, kept, sent, flat, held, mine, stack, total, sems):
-    loads = [
-        pltpu.make_async_copy(source, target, sems.at[n])
-        for n, (source, target) in enumerate(((cot, mine), (weights, held)))
-    ]
-    for load in loads:
-        load.start()
+def share_kernel(pixels, weights, flat, own, kept, sent, stack, total):
     rows, length = own.shape
     frames = length // pixels
-    count = held.shape[1] // rows
+    count = weights.shape[1] // rows
     me = lax.axis_index("tm")
-
-    def flatten(core, source):
-        wide = source[:, 0].astype(F32)
-        for t in range(frames):
-            at = pl.multiple_of((core * frames + t) * pixels, pixels)
-            flat[:, pl.ds(at, pixels)] = wide[:, t, :]
-
-    flatten(1 - me, cot_other)
-    loads[0].wait()
-    flatten(me, mine)
     for t in range(frames + 2):
         at = slice(t * pixels, (t + 1) * pixels)
         if t < frames:
@@ -264,12 +274,11 @@
             for j in range(3):
                 row = (3 * i + j) * rows
                 stack[row : row + rows, at] = shifted(frame, 1 - i, 1 - j).astype(BF16)
-    loads[1].wait()
     taps = 9 * rows
     acc = None
     for a in range(3):
         term = lax.dot_general(
-            held[a * taps : (a + 1) * taps, :],
+            weights[a * taps : (a + 1) * taps, :],
             stack[:, (2 - a) * pixels : (2 - a) * pixels + length],
             (((0,), (0,)), ((), ())),
             preferred_element_type=F32,
@@ -281,8 +290,8 @@
         return total[pl.ds(pl.multiple_of(shard_at(count, k) * rows, SUB), rows), :]
 
     own[...] = part(0)
-    kept[...] = part(1)
-    sent[0] = part(2).astype(BF16)
+    kept[...] = part(2)
+    sent[0] = part(1).astype(BF16)
     sent[1] = part(3).astype(BF16)
 
 
@@ -343,36 +352,34 @@
         out[k * main : (k + 1) * main, :] = total.astype(BF16)
 
 
-def finish_kernel(scale, main, early, other_early, late, other_late, out, laid, sems):
+def finish_kernel(scale, main, whose, early, late, *refs):
+    out, laid, sems = refs[-3:]
     channels = out.shape[2]
     first = early.shape[0] // main
     count = first + late.shape[0] // main
     rows, half = channels // count, out.shape[1] // 2
     unit = rows // 2
-    me = lax.axis_index("tm")
+    which = lax.rem(lax.axis_index("tm") + whose, 2)
+    at = pl.ds(pl.multiple_of(which * half, 8), half)
     shards = [shard_at(count, k) for k in range(count)]
     copies = []
-    for which, one, two in ((me, early, late), (1 - me, other_early, other_late)):
-        start = pl.multiple_of(which * half, 8)
-        for a in range(3):
-            for q in range(9):
-                base = q * unit if q < 7 else a * 2 * unit + (q - 7) * unit
-                step = a if q < 7 else 3
-                total = None
-                for k, shard in enumerate(shards):
-                    source, place = (one, k) if k < first else (two, k - first)
-                    at = place * main + base
-                    piece = source[at : at + unit, :].astype(F32)
-                    mask = in_slot(channels, rows, lax.rem(shard + step, count))
-                    total = piece if total is None else jnp.where(mask, piece, total)
-                total = total * scale
-                if step:
-                    total = pltpu.roll(total, channels - step * rows, 1)
-                laid[a, pl.ds(start + q * unit, unit), :] = total
-            at = pl.ds(start, half)
-            copy = pltpu.make_async_copy(laid.at[a, at], out.at[a, at], sems.at[len(copies)])
-            copy.start()
-            copies.append(copy)
+    for a in range(3):
+        for q in range(9):
+            base = q * unit if q < 7 else a * 2 * unit + (q - 7) * unit
+            step = a if q < 7 else 3
+            total = None
+            for k, shard in enumerate(shards):
+                source, place = (early, k) if k < first else (late, k - first)
+                piece = source[place * main + base : place * main + base + unit, :].astype(F32)
+                mask = in_slot(channels, rows, lax.rem(shard + step, count))
+                total = piece if total is None else jnp.where(mask, piece, total)
+            total = total * scale
+            if step:
+                total = pltpu.roll(total, channels - step * rows, 1)
+            laid[a, q * unit : (q + 1) * unit, :] = total
+        copy = pltpu.make_async_copy(laid.at[a], out.at[a, at], sems.at[a])
+        copy.start()
+        copies.append(copy)
     for copy in copies:
         copy.wait()
 
@@ -399,47 +406,38 @@
         return lax.ppermute(x, "chan", [(z, z ^ far) for z in range(count)])
 
     weights = jnp.transpose(kernel, (1, 0, 2)).reshape(taps * rows, channels)
+    hbm = pl.BlockSpec(memory_space=pltpu.HBM)
     cot_other = rotate(cotangent, "tm", 1)
-    activation = run(
+    activation, flat_own = run(
         activate_kernel,
-        (features,),
-        out_shape=block_shape,
-        out_specs=whole(),
+        (in_place(features), in_place(cotangent)),
+        in_specs=[hbm] * 2,
+        out_shape=(block_shape, sds((rows, length), F32)),
+        out_specs=(whole(),) * 2,
+        scratch_shapes=[
+            pltpu.VMEM(features.shape, BF16),
+            pltpu.VMEM(features.shape, BF16),
+            pltpu.SemaphoreType.DMA((2,)),
+        ],
         name="activate",
     )
     other = rotate(activation, "tm", 1)
-    far, near = swap(activation, 2), swap(activation, 1)
-    own_share, kept, sent, flat = run(
-        functools.partial(share_kernel, pixels),
-        (in_place(weights), in_place(cotangent), cot_other),
-        in_specs=[pl.BlockSpec(memory_space=pltpu.HBM)] * 2 + [whole()],
+    near, far = swap(activation, 1), swap(activation, 2)
+    own_term, stack, flat, weights = run(
+        functools.partial(own_terms_kernel, pixels),
+        (activation, other, flat_own, cot_other, in_place(weights)),
+        in_specs=[whole()] * 4 + [hbm],
         out_shape=(
-            sds((rows, length), F32),
-            sds((rows, length), F32),
-            sds((2, rows, length), BF16),
+            term_shape,
+            stack_shape,
             sds((rows, 2 * length), F32),
+            sds(weights.shape, BF16),
         ),
         out_specs=(whole(),) * 4,
-        scratch_shapes=[
-            pltpu.VMEM((taps * rows, channels), BF16),
-            pltpu.VMEM(cotangent.shape, BF16),
-            pltpu.VMEM((9 * rows, (frames + 2) * pixels), BF16),
-            pltpu.VMEM((channels, length), F32),
-            pltpu.SemaphoreType.DMA((2,)),
-        ],
-        name="shares",
-    )
-    first_share = swap(sent, 1)
-    own_term, stack = run(
-        functools.partial(own_terms_kernel, pixels),
-        (activation, other, flat),
-        out_shape=(term_shape, stack_shape),
-        out_specs=(whole(),) * 2,
-        scratch_shapes=[rhs],
+        scratch_shapes=[rhs, pltpu.SemaphoreType.DMA((1,))],
         name="own_terms",
     )
     terms, got = [own_term], [rotate(own_term, "dp", 1)]
-
     blocks = [activation, other]
 
     def terms_of(k, here, waits=()):
@@ -457,10 +455,28 @@
         got.append(rotate(term, "dp", 1))
         return term
 
-    far = after(far, own_term, near)
-    near = after(near, far)
+    near = after(near, own_term)
+    own_share, kept, sent = run(
+        functools.partial(share_kernel, pixels),
+        (weights, flat),
+        waits=(near,),
+        out_shape=(
+            sds((rows, length), F32),
+            sds((rows, length), F32),
+            sds((2, rows, length), BF16),
+        ),
+        out_specs=(whole(),) * 3,
+        scratch_shapes=[
+            pltpu.VMEM((9 * rows, (frames + 2) * pixels), BF16),
+            pltpu.VMEM((channels, length), F32),
+        ],
+        name="shares",
+    )
+    first_share = swap(sent, 1)
+    term = terms_of(1, near, (own_share, got[0]))
+    far = after(far, term)
     last = swap(far, 1)
-    term = terms_of(1, far, (got[0],))
+    term = terms_of(2, far)
     carry = run(
         add_kernel,
         (kept, first_share),
@@ -470,8 +486,7 @@
         name="carry_share",
     )
     second_share = swap(carry, 2)
-    term = terms_of(2, near, (carry,))
-    term = terms_of(3, after(last, term, got[1]))
+    term = terms_of(3, after(last, carry, got[1]))
 
     def sums(first, stop, waits=()):
         return run(
@@ -504,15 +519,22 @@
     )
     late = sums(2, count, (token,))
     scale = 1.0 / math.sqrt(lax.axis_size("dp") * lax.axis_size("tm") * length)
-    grad_shape = (3, 9 * rows, channels)
-    kernel_grad = run(
-        functools.partial(finish_kernel, scale, main),
-        (early, rotate(early, "tm", 1), late, rotate(late, "tm", 1)),
-        out_shape=sds(grad_shape, F32),
-        out_specs=pl.BlockSpec(memory_space=pl.ANY),
-        scratch_shapes=[pltpu.VMEM(grad_shape, F32), pltpu.SemaphoreType.DMA((6,))],
-        name="kernel_grad",
-    )
+
+    def finish(whose, sums, base=()):
+        anywhere = pl.BlockSpec(memory_space=pl.ANY)
+        return run(
+            functools.partial(finish_kernel, scale, main, whose),
+            (*sums, *base),
+            in_specs=[whole()] * 2 + [anywhere] * len(base),
+            out_shape=sds((3, 9 * rows, channels), F32),
+            out_specs=anywhere,
+            input_output_aliases={2: 0} if base else {},
+            scratch_shapes=[pltpu.VMEM((3, half, channels), F32), pltpu.SemaphoreType.DMA((3,))],
+            name=f"kernel_grad_{whose}",
+        )
+
+    kernel_grad = finish(0, (early, late))
+    kernel_grad = finish(1, (rotate(early, "tm", 1), rotate(late, "tm", 1)), (kernel_grad,))
     kernel_grad = jnp.transpose(kernel_grad.reshape(taps, rows, channels), (1, 0, 2))
     return (conv_out, feature_grad, kernel_grad)
 

time: 51.8 us -> 53.1 us (1.025)
  starting transfers between devices: 15.1 us -> 16.1 us
  local copies, waits for them, and re-layouts: 0.94 us -> 0.01 us
  Pallas kernels: 19.2 us -> 19.9 us
  waiting for transfers between devices: 15.5 us -> 16.1 us
    ppermute x5, waiting for transfers between devices: 8.97 us -> 14.7 us  [swap(): return lax.ppermute(x, 'chan', [(z, z ^ far) for z in range(count)])]
    ppermute x11, waiting for transfers between devices: 6.55 us -> 1.42 us  [rotate(): return lax.ppermute(x, axis, [(i, (i + by) % size) for i in range(size)])]
    unnamed x6 -> x2, local copies, waits for them, and re-layouts: 0.94 us -> 0.01 us
    ppermute x5, starting transfers between devices: 7.87 us -> 8.66 us  [swap(): return lax.ppermute(x, 'chan', [(z, z ^ far) for z in range(count)])]
    pallas_call x12 -> x13, Pallas kernels: 19.2 us -> 19.9 us  [run(): pl.pallas_call(body, compiler_params=pltpu.CompilerParams(vmem_limit_byte...]
  transfers between devices with their start and end apart: 16 -> 16, of which waited for: 8 -> 8; matrix products, arithmetic and copies ran while one was open for 0% -> 0% of each run, Pallas kernels for 33% -> 34%
where the time goes in v4:
time: 53.1 us; the launch traced here: 52.9 us
  Pallas kernels  19.9 us (37%)
  starting transfers between devices  16.1 us (30%)
  waiting for transfers between devices  16.1 us (30%)
  between operations  0.89 us (2%)
    pallas_call x13, Pallas kernels, run(): pl.pallas_call(body, compiler_params=pltpu.CompilerParams(vmem_limit_byte...  19.9 us
    ppermute x5, waiting for transfers between devices, swap(): return lax.ppermute(x, 'chan', [(z, z ^ far) for z in range(count)])  14.7 us
    ppermute x5, starting transfers between devices, swap(): return lax.ppermute(x, 'chan', [(z, z ^ far) for z in range(count)])  8.66 us
    ppermute x11, starting transfers between devices, rotate(): return lax.ppermute(x, axis, [(i, (i + by) % size) for i in range(size)])  7.41 us
    ppermute x11, waiting for transfers between devices, rotate(): return lax.ppermute(x, axis, [(i, (i + by) % size) for i in range(size)])  1.42 us
  transfers between devices with their start and end apart: 16, of which 8 were waited for; matrix products, arithmetic and copies ran while one was open for 0% of the time, Pallas kernels for 34%

profile of v4, /device:TPU:0, one launch (start us, length us, event | category | flops | bytes accessed | tf_op | source)
XLA Modules:
  0.0 52.9 jit_solution(12181554689971240685)
XLA Ops:
  0.6 0.5 collective-permute-start.1
  1.1 1.7 %activate.1 = (bf16[96,1024]{1,0:T(8,128)(2,1)S(1)}, f32[96,1024]{1,0:T(8,128)S(1)}) custom-call(bf16[96,1,4,256]{3,2,1,0:T(4,128)(2,1)} %refs_0_.3, bf16[96,1,4,256]{3,2,1,0:T(4,128)(2,1)} %refs_1_.1), custom_call_target="tpu_custom_call" | custom-call | flops 1 | bytes 1 | tf_op jit(solution)/shard_map/activate/pallas_call | solution.py:143
  2.8 0.1 collective-permute-start
  3.0 3.0 %collective-permute-start.2 = (bf16[96,1024]{1,0:T(8,128)(2,1)S(1)}, bf16[96,1024]{1,0:T(8,128)(2,1)S(1)}, u32[]{:S(2)}, u32[]{:S(2)}) collective-permute-start(bf16[96,1024]{1,0:T(8,128)(2,1)S(1)} %get-tuple-element.16.refs_0_.refs_1_), channel_id=1, source_target_pairs={{0,4},{4,0},{8,12},{12,8},{1,5},{5,1},{9,13},{13,9},{2,6},{6,2},{1... | collective-permute-start | bytes 589832 | tf_op jit(solution)/shard_map/ppermute | solution.py:406
  6.0 0.0 collective-permute-done.1.refs_3_
  6.0 0.0 collective-permute-done.refs_1_.refs_2_
  6.0 2.0 %own_terms.1 = (bf16[336,384]{1,0:T(8,128)(2,1)S(1)}, bf16[432,2048]{1,0:T(8,128)(2,1)S(1)}, f32[96,2048]{1,0:T(8,128)S(1)}, bf16[2592,384]{1,0:T(8,128)(2,1)S(1)}) custom-call(bf16[96,1024]{1,0:T(8,128)(2,1)S(1)} %get-tuple-element.16.refs_0_.refs_1_, bf16[96,1024]{1,0:T(8,128)(2,1)S(1)} %collective-permute-done.refs_1_.refs_2_, ...), custom_call_target="tpu_custom_call" | custom-call | flops 1 | bytes 1 | tf_op jit(solution)/shard_map/own_terms/pallas_call | solution.py:143
  8.0 1.6 %collective-permute-start.5 = (bf16[336,384]{1,0:T(8,128)(2,1)S(1)}, bf16[336,384]{1,0:T(8,128)(2,1)S(1)}, u32[]{:S(2)}, u32[]{:S(2)}) collective-permute-start(bf16[336,384]{1,0:T(8,128)(2,1)S(1)} %get-tuple-element.19.refs_1_.refs_0_), channel_id=1, source_target_pairs={{0,1},{1,0},{2,3},{3,2},{4,5},{5,4},{6,7},{7,6},{8,9},{9,8},{10,11... | collective-permute-start | bytes 774152 | tf_op jit(solution)/shard_map/ppermute | solution.py:104
  9.5 1.6 %collective-permute-done.2.refs_0_ = bf16[96,1024]{1,0:T(8,128)(2,1)S(1)} collective-permute-done((bf16[96,1024]{1,0:T(8,128)(2,1)S(1)}, bf16[96,1024]{1,0:T(8,128)(2,1)S(1)}, u32[]{:S(2)}, u32[]{:S(2)}) %collective-permute-start.2) | collective-permute-done | bytes 196640 | tf_op jit(solution)/shard_map/ppermute | solution.py:406
  11.1 0.0 collective-permute-start.3
  11.1 2.8 %collective-permute-start.4 = (bf16[96,1024]{1,0:T(8,128)(2,1)S(1)}, bf16[96,1024]{1,0:T(8,128)(2,1)S(1)}, u32[]{:S(2)}, u32[]{:S(2)}) collective-permute-start(bf16[96,1024]{1,0:T(8,128)(2,1)S(1)} %get-tuple-element.16.refs_0_.refs_1_), channel_id=1, source_target_pairs={{0,8},{4,12},{8,0},{12,4},{1,9},{5,13},{9,1},{13,5},{2,10},{6,14},... | collective-permute-start | bytes 589832 | tf_op jit(solution)/shard_map/ppermute | solution.py:406
  13.9 3.0 %shares.1 = (f32[96,1024]{1,0:T(8,128)S(1)}, f32[96,1024]{1,0:T(8,128)S(1)}, bf16[2,96,1024]{2,1,0:T(8,128)(2,1)S(1)}) custom-call(bf16[2592,384]{1,0:T(8,128)(2,1)S(1)} %get-tuple-element.18.refs_0_, f32[96,2048]{1,0:T(8,128)S(1)} %get-tuple-element.21.refs_1_, bf16[96,1024]{1,0:T(8,128)(2,1)S(1)} %hand_on.3.refs_2_.refs_1_.refs_3_), custom_call_target="tpu_custom_call" | custom-call | flops 1 | bytes 1 | tf_op jit(solution)/shard_map/shares/pallas_call | solution.py:143
  16.8 1.6 %collective-permute-start.8 = (bf16[2,96,1024]{2,1,0:T(8,128)(2,1)S(1)}, bf16[2,96,1024]{2,1,0:T(8,128)(2,1)S(1)}, u32[]{:S(2)}, u32[]{:S(2)}) collective-permute-start(bf16[2,96,1024]{2,1,0:T(8,128)(2,1)S(1)} %get-tuple-element.24), channel_id=1, source_target_pairs={{0,4},{4,0},{8,12},{12,8},{1,5},{5,1},{9,13},{13,9},{2,6},{6,2},{1... | collective-permute-start | bytes 1179656 | tf_op jit(solution)/shard_map/ppermute | solution.py:406
  18.5 0.0 collective-permute-done.3.refs_2_.refs_4_
  18.5 0.0 collective-permute-done.5.refs_4_.refs_2_
  18.5 1.3 %terms_1.1.refs_1_ = bf16[336,384]{1,0:T(8,128)(2,1)S(1)} custom-call(bf16[432,2048]{1,0:T(8,128)(2,1)S(1)} %get-tuple-element.20.refs_0_, bf16[96,1024]{1,0:T(8,128)(2,1)S(1)} %hand_on.3.refs_2_.refs_1_.refs_3_, bf16[96,1024]{1,0:T(8,128)(2,1)S(1)} %collective-permute-done.3.refs_2_.refs_4_, f32[96,1024]{1,0:T(8,128)S(1)} %get-tuple-element.22.refs_3_.refs_1_, ...), custom_call_target="tpu_custom_call" | custom-call | flops 1 | bytes 1 | tf_op jit(solution)/shard_map/terms_1/pallas_call | solution.py:143
  19.8 1.6 %collective-permute-start.9 = (bf16[336,384]{1,0:T(8,128)(2,1)S(1)}, bf16[336,384]{1,0:T(8,128)(2,1)S(1)}, u32[]{:S(2)}, u32[]{:S(2)}) collective-permute-start(bf16[336,384]{1,0:T(8,128)(2,1)S(1)} %terms_1.1.refs_1_), channel_id=1, source_target_pairs={{0,1},{1,0},{2,3},{3,2},{4,5},{5,4},{6,7},{7,6},{8,9},{9,8},{10,11... | collective-permute-start | bytes 774152 | tf_op jit(solution)/shard_map/ppermute | solution.py:104
  21.4 2.4 %collective-permute-done.4.refs_0_ = bf16[96,1024]{1,0:T(8,128)(2,1)S(1)} collective-permute-done((bf16[96,1024]{1,0:T(8,128)(2,1)S(1)}, bf16[96,1024]{1,0:T(8,128)(2,1)S(1)}, u32[]{:S(2)}, u32[]{:S(2)}) %collective-permute-start.4) | collective-permute-done | bytes 196640 | tf_op jit(solution)/shard_map/ppermute | solution.py:406
  23.8 0.0 collective-permute-start.6
  23.8 0.7 %collective-permute-start.7 = (bf16[96,1024]{1,0:T(8,128)(2,1)S(1)}, bf16[96,1024]{1,0:T(8,128)(2,1)S(1)}, u32[]{:S(2)}, u32[]{:S(2)}) collective-permute-start(bf16[96,1024]{1,0:T(8,128)(2,1)S(1)} %hand_on.4.refs_1_.refs_5_), channel_id=1, source_target_pairs={{0,4},{4,0},{8,12},{12,8},{1,5},{5,1},{9,13},{13,9},{2,6},{6,2},{1... | collective-permute-start | bytes 589832 | tf_op jit(solution)/shard_map/ppermute | solution.py:406
  24.5 0.7 %collective-permute-done.6.refs_2_.refs_6_ = bf16[96,1024]{1,0:T(8,128)(2,1)S(1)} collective-permute-done((bf16[96,1024]{1,0:T(8,128)(2,1)S(1)}, bf16[96,1024]{1,0:T(8,128)(2,1)S(1)}, u32[]{:S(2)}, u32[]{:S(2)}) %collective-permute-start.6) | collective-permute-done | bytes 196640 | tf_op jit(solution)/shard_map/ppermute | solution.py:104
  25.2 1.3 %terms_2.1.refs_2_.refs_0_ = bf16[336,384]{1,0:T(8,128)(2,1)S(1)} custom-call(bf16[432,2048]{1,0:T(8,128)(2,1)S(1)} %get-tuple-element.20.refs_0_, bf16[96,1024]{1,0:T(8,128)(2,1)S(1)} %hand_on.4.refs_1_.refs_5_, bf16[96,1024]{1,0:T(8,128)(2,1)S(1)} %collective-permute-done.6.refs_2_.refs_6_), custom_call_target="tpu_custom_call" | custom-call | flops 1 | bytes 1 | tf_op jit(solution)/shard_map/terms_2/pallas_call | solution.py:143
  26.6 1.6 %collective-permute-start.11 = (bf16[336,384]{1,0:T(8,128)(2,1)S(1)}, bf16[336,384]{1,0:T(8,128)(2,1)S(1)}, u32[]{:S(2)}, u32[]{:S(2)}) collective-permute-start(bf16[336,384]{1,0:T(8,128)(2,1)S(1)} %terms_2.1.refs_2_.refs_0_), channel_id=1, source_target_pairs={{0,1},{1,0},{2,3},{3,2},{4,5},{5,4},{6,7},{7,6},{8,9},{9,8},{10,11... | collective-permute-start | bytes 774152 | tf_op jit(solution)/shard_map/ppermute | solution.py:104
  28.2 3.6 %collective-permute-done.8.refs_1_.refs_2_ = bf16[2,96,1024]{2,1,0:T(8,128)(2,1)S(1)} collective-permute-done((bf16[2,96,1024]{2,1,0:T(8,128)(2,1)S(1)}, bf16[2,96,1024]{2,1,0:T(8,128)(2,1)S(1)}, u32[]{:S(2)}, u32[]{:S(2)}) %collective-permute-start.8) | collective-permute-done | bytes 393248 | tf_op jit(solution)/shard_map/ppermute | solution.py:406
  31.9 3.6 %collective-permute-done.7.refs_0_ = bf16[96,1024]{1,0:T(8,128)(2,1)S(1)} collective-permute-done((bf16[96,1024]{1,0:T(8,128)(2,1)S(1)}, bf16[96,1024]{1,0:T(8,128)(2,1)S(1)}, u32[]{:S(2)}, u32[]{:S(2)}) %collective-permute-start.7) | collective-permute-done | bytes 196640 | tf_op jit(solution)/shard_map/ppermute | solution.py:406
  35.4 0.0 collective-permute-done.9.refs_2_.refs_3_
  35.4 0.0 collective-permute-start.10
  35.4 0.5 collective-permute-start.12
  35.9 0.1 sums_0.1.refs_5_.refs_0_
  36.1 0.3 collective-permute-start.13
  36.4 0.5 collective-permute-done.10.refs_2_.refs_8_
  36.9 1.5 %terms_3.1.refs_9_.refs_1_ = bf16[336,384]{1,0:T(8,128)(2,1)S(1)} custom-call(bf16[432,2048]{1,0:T(8,128)(2,1)S(1)} %get-tuple-element.20.refs_0_, bf16[96,1024]{1,0:T(8,128)(2,1)S(1)} %hand_on.5.refs_1_.refs_7_, bf16[96,1024]{1,0:T(8,128)(2,1)S(1)} %collective-permute-done.10.refs_2_.refs_8_), custom_call_target="tpu_custom_call" | custom-call | flops 1 | bytes 1 | tf_op jit(solution)/shard_map/terms_3/pallas_call | solution.py:143
  38.4 0.0 copy-start
  38.4 1.6 %collective-permute-start.14 = (bf16[336,384]{1,0:T(8,128)(2,1)S(1)}, bf16[336,384]{1,0:T(8,128)(2,1)S(1)}, u32[]{:S(2)}, u32[]{:S(2)}) collective-permute-start(bf16[336,384]{1,0:T(8,128)(2,1)S(1)} %terms_3.1.refs_9_.refs_1_), channel_id=1, source_target_pairs={{0,1},{1,0},{2,3},{3,2},{4,5},{5,4},{6,7},{7,6},{8,9},{9,8},{10,11... | collective-permute-start | bytes 774152 | tf_op jit(solution)/shard_map/ppermute | solution.py:104
  40.0 0.0 collective-permute-done.11.refs_10_.refs_2_
  40.0 4.1 %conv.1 = (bf16[96,1,4,256]{3,2,1,0:T(4,128)(2,1)}, f32[8,128]{1,0:T(8,128)S(1)}) custom-call(bf16[2592,384]{1,0:T(8,128)(2,1)S(1)} %get-tuple-element.18.refs_0_, bf16[96,1024]{1,0:T(8,128)(2,1)S(1)} %get-tuple-element.16.refs_0_.refs_1_, bf16[96,1024]{1,0:T(8,128)(2,1)S(1)} %collective-permute-done.refs_1_.refs_2_, ...), custom_call_target="tpu_custom_call" | custom-call | flops 1 | bytes 1 | tf_op jit(solution)/shard_map/conv/pallas_call | solution.py:143
  44.1 3.5 %collective-permute-done.12.refs_3_ = bf16[96,1024]{1,0:T(8,128)(2,1)S(1)} collective-permute-done((bf16[96,1024]{1,0:T(8,128)(2,1)S(1)}, bf16[96,1024]{1,0:T(8,128)(2,1)S(1)}, u32[]{:S(2)}, u32[]{:S(2)}) %collective-permute-start.12) | collective-permute-done | bytes 196640 | tf_op jit(solution)/shard_map/ppermute | solution.py:406
  47.6 0.0 copy-done
  47.6 1.4 %feature_grad.1 = (bf16[96,1,4,256]{3,2,1,0:T(4,128)(2,1)}, f32[8,128]{1,0:T(8,128)S(1)}) custom-call(bf16[96,1,4,256]{3,2,1,0:T(4,128)(2,1)S(1)} %copy-done, f32[96,1024]{1,0:T(8,128)S(1)} %get-tuple-element.22.refs_3_.refs_1_, bf16[2,96,1024]{2,1,0:T(8,128)(2,1)S(1)} %collective-permute-done.8.refs_1_.refs_2_, ...), custom_call_target="tpu_custom_call" | custom-call | flops 3000000000 | bytes 1 | tf_op jit(solution)/shard_map/feature_grad/pallas_call | solution.py:143
  49.1 0.0 collective-permute-done.14.refs_3_
  49.1 0.1 sums_2.1.refs_1_
  49.2 0.1 collective-permute-start.15
  49.3 1.6 %kernel_grad_0.1.refs_2_ = f32[3,864,384]{2,1,0:T(8,128)} custom-call(bf16[672,384]{1,0:T(8,128)(2,1)S(1)} %sums_0.1.refs_5_.refs_0_, bf16[672,384]{1,0:T(8,128)(2,1)S(1)} %sums_2.1.refs_1_), custom_call_target="tpu_custom_call" | custom-call | flops 1 | bytes 1 | tf_op jit(solution)/shard_map/kernel_grad_0/pallas_call | solution.py:143
  50.9 0.0 collective-permute-done.13.refs_0_
  51.0 0.2 collective-permute-done.15.refs_1_
  51.2 1.6 %kernel_grad_1.1 = f32[3,864,384]{2,1,0:T(8,128)} custom-call(bf16[672,384]{1,0:T(8,128)(2,1)S(1)} %collective-permute-done.13.refs_0_, bf16[672,384]{1,0:T(8,128)(2,1)S(1)} %collective-permute-done.15.refs_1_, f32[3,864,384]{2,1,0:T(8,128)} %kernel_grad_0.1.refs_2_), custom_call_target="tpu_custom_call", output_to_operand_aliasing={{}: (2, {})} | custom-call | flops 1 | bytes 1 | tf_op jit(solution)/shard_map/kernel_grad_1/pallas_call | solution.py:143
  (4 shorter events, 0.0 us)
Async XLA Ops:
  0.6 5.4 %collective-permute-start.1 = (bf16[96,1,4,256]{3,2,1,0:T(4,128)(2,1)}, bf16[96,1,4,256]{3,2,1,0:T(4,128)(2,1)S(1)}, u32[]{:S(2)}, u32[]{:S(2)}) collective-permute-start(bf16[96,1,4,256]{3,2,1,0:T(4,128)(2,1)} %refs_1_.1), channel_id=1, source_target_pairs={{0,2},{2,0},{1,3},{3,1},{4,6},{6,4},{5,7},{7,5},{8,10},{10,8},{9,1... | collective-permute-start | bytes 589832 | tf_op jit(solution)/shard_map/ppermute | solution.py:104
  2.8 3.2 %collective-permute-start = (bf16[96,1024]{1,0:T(8,128)(2,1)S(1)}, bf16[96,1024]{1,0:T(8,128)(2,1)S(1)}, u32[]{:S(2)}, u32[]{:S(2)}) collective-permute-start(bf16[96,1024]{1,0:T(8,128)(2,1)S(1)} %get-tuple-element.16.refs_0_.refs_1_), channel_id=1, source_target_pairs={{0,2},{2,0},{1,3},{3,1},{4,6},{6,4},{5,7},{7,5},{8,10},{10,8},{9,1... | collective-permute-start | bytes 589832 | tf_op jit(solution)/shard_map/ppermute | solution.py:104
  3.0 8.2 %collective-permute-start.2 = (bf16[96,1024]{1,0:T(8,128)(2,1)S(1)}, bf16[96,1024]{1,0:T(8,128)(2,1)S(1)}, u32[]{:S(2)}, u32[]{:S(2)}) collective-permute-start(bf16[96,1024]{1,0:T(8,128)(2,1)S(1)} %get-tuple-element.16.refs_0_.refs_1_), channel_id=1, source_target_pairs={{0,4},{4,0},{8,12},{12,8},{1,5},{5,1},{9,13},{13,9},{2,6},{6,2},{1... | collective-permute-start | bytes 589832 | tf_op jit(solution)/shard_map/ppermute | solution.py:406
  8.0 10.5 %collective-permute-start.5 = (bf16[336,384]{1,0:T(8,128)(2,1)S(1)}, bf16[336,384]{1,0:T(8,128)(2,1)S(1)}, u32[]{:S(2)}, u32[]{:S(2)}) collective-permute-start(bf16[336,384]{1,0:T(8,128)(2,1)S(1)} %get-tuple-element.19.refs_1_.refs_0_), channel_id=1, source_target_pairs={{0,1},{1,0},{2,3},{3,2},{4,5},{5,4},{6,7},{7,6},{8,9},{9,8},{10,11... | collective-permute-start | bytes 774152 | tf_op jit(solution)/shard_map/ppermute | solution.py:104
  11.1 7.4 %collective-permute-start.3 = (bf16[96,1024]{1,0:T(8,128)(2,1)S(1)}, bf16[96,1024]{1,0:T(8,128)(2,1)S(1)}, u32[]{:S(2)}, u32[]{:S(2)}) collective-permute-start(bf16[96,1024]{1,0:T(8,128)(2,1)S(1)} %hand_on.3.refs_2_.refs_1_.refs_3_), channel_id=1, source_target_pairs={{0,2},{2,0},{1,3},{3,1},{4,6},{6,4},{5,7},{7,5},{8,10},{10,8},{9,1... | collective-permute-start | bytes 589832 | tf_op jit(solution)/shard_map/ppermute | solution.py:104
  11.1 12.6 %collective-permute-start.4 = (bf16[96,1024]{1,0:T(8,128)(2,1)S(1)}, bf16[96,1024]{1,0:T(8,128)(2,1)S(1)}, u32[]{:S(2)}, u32[]{:S(2)}) collective-permute-start(bf16[96,1024]{1,0:T(8,128)(2,1)S(1)} %get-tuple-element.16.refs_0_.refs_1_), channel_id=1, source_target_pairs={{0,8},{4,12},{8,0},{12,4},{1,9},{5,13},{9,1},{13,5},{2,10},{6,14},... | collective-permute-start | bytes 589832 | tf_op jit(solution)/shard_map/ppermute | solution.py:406
  16.8 15.0 %collective-permute-start.8 = (bf16[2,96,1024]{2,1,0:T(8,128)(2,1)S(1)}, bf16[2,96,1024]{2,1,0:T(8,128)(2,1)S(1)}, u32[]{:S(2)}, u32[]{:S(2)}) collective-permute-start(bf16[2,96,1024]{2,1,0:T(8,128)(2,1)S(1)} %get-tuple-element.24), channel_id=1, source_target_pairs={{0,4},{4,0},{8,12},{12,8},{1,5},{5,1},{9,13},{13,9},{2,6},{6,2},{1... | collective-permute-start | bytes 1179656 | tf_op jit(solution)/shard_map/ppermute | solution.py:406
  19.8 15.6 %collective-permute-start.9 = (bf16[336,384]{1,0:T(8,128)(2,1)S(1)}, bf16[336,384]{1,0:T(8,128)(2,1)S(1)}, u32[]{:S(2)}, u32[]{:S(2)}) collective-permute-start(bf16[336,384]{1,0:T(8,128)(2,1)S(1)} %terms_1.1.refs_1_), channel_id=1, source_target_pairs={{0,1},{1,0},{2,3},{3,2},{4,5},{5,4},{6,7},{7,6},{8,9},{9,8},{10,11... | collective-permute-start | bytes 774152 | tf_op jit(solution)/shard_map/ppermute | solution.py:104
  23.8 1.4 %collective-permute-start.6 = (bf16[96,1024]{1,0:T(8,128)(2,1)S(1)}, bf16[96,1024]{1,0:T(8,128)(2,1)S(1)}, u32[]{:S(2)}, u32[]{:S(2)}) collective-permute-start(bf16[96,1024]{1,0:T(8,128)(2,1)S(1)} %hand_on.4.refs_1_.refs_5_), channel_id=1, source_target_pairs={{0,2},{2,0},{1,3},{3,1},{4,6},{6,4},{5,7},{7,5},{8,10},{10,8},{9,1... | collective-permute-start | bytes 589832 | tf_op jit(solution)/shard_map/ppermute | solution.py:104
  23.8 11.6 %collective-permute-start.7 = (bf16[96,1024]{1,0:T(8,128)(2,1)S(1)}, bf16[96,1024]{1,0:T(8,128)(2,1)S(1)}, u32[]{:S(2)}, u32[]{:S(2)}) collective-permute-start(bf16[96,1024]{1,0:T(8,128)(2,1)S(1)} %hand_on.4.refs_1_.refs_5_), channel_id=1, source_target_pairs={{0,4},{4,0},{8,12},{12,8},{1,5},{5,1},{9,13},{13,9},{2,6},{6,2},{1... | collective-permute-start | bytes 589832 | tf_op jit(solution)/shard_map/ppermute | solution.py:406
  26.6 13.5 %collective-permute-start.11 = (bf16[336,384]{1,0:T(8,128)(2,1)S(1)}, bf16[336,384]{1,0:T(8,128)(2,1)S(1)}, u32[]{:S(2)}, u32[]{:S(2)}) collective-permute-start(bf16[336,384]{1,0:T(8,128)(2,1)S(1)} %terms_2.1.refs_2_.refs_0_), channel_id=1, source_target_pairs={{0,1},{1,0},{2,3},{3,2},{4,5},{5,4},{6,7},{7,6},{8,9},{9,8},{10,11... | collective-permute-start | bytes 774152 | tf_op jit(solution)/shard_map/ppermute | solution.py:104
  35.4 1.4 %collective-permute-start.10 = (bf16[96,1024]{1,0:T(8,128)(2,1)S(1)}, bf16[96,1024]{1,0:T(8,128)(2,1)S(1)}, u32[]{:S(2)}, u32[]{:S(2)}) collective-permute-start(bf16[96,1024]{1,0:T(8,128)(2,1)S(1)} %hand_on.5.refs_1_.refs_7_), channel_id=1, source_target_pairs={{0,2},{2,0},{1,3},{3,1},{4,6},{6,4},{5,7},{7,5},{8,10},{10,8},{9,1... | collective-permute-start | bytes 589832 | tf_op jit(solution)/shard_map/ppermute | solution.py:104
  35.4 12.2 %collective-permute-start.12 = (bf16[96,1024]{1,0:T(8,128)(2,1)S(1)}, bf16[96,1024]{1,0:T(8,128)(2,1)S(1)}, u32[]{:S(2)}, u32[]{:S(2)}) collective-permute-start(bf16[96,1024]{1,0:T(8,128)(2,1)S(1)} %carry_share.1.refs_1_), channel_id=1, source_target_pairs={{0,8},{4,12},{8,0},{12,4},{1,9},{5,13},{9,1},{13,5},{2,10},{6,14},... | collective-permute-start | bytes 589832 | tf_op jit(solution)/shard_map/ppermute | solution.py:406
  36.1 14.9 %collective-permute-start.13 = (bf16[672,384]{1,0:T(8,128)(2,1)S(1)}, bf16[672,384]{1,0:T(8,128)(2,1)S(1)}, u32[]{:S(2)}, u32[]{:S(2)}) collective-permute-start(bf16[672,384]{1,0:T(8,128)(2,1)S(1)} %sums_0.1.refs_5_.refs_0_), channel_id=1, source_target_pairs={{0,2},{2,0},{1,3},{3,1},{4,6},{6,4},{5,7},{7,5},{8,10},{10,8},{9,1... | collective-permute-start | bytes 1548296 | tf_op jit(solution)/shard_map/ppermute | solution.py:104
  38.4 9.2 %copy-start = (bf16[96,1,4,256]{3,2,1,0:T(4,128)(2,1)S(1)}, bf16[96,1,4,256]{3,2,1,0:T(4,128)(2,1)}, u32[]{:S(2)}) copy-start(bf16[96,1,4,256]{3,2,1,0:T(4,128)(2,1)} %refs_0_.3) | copy-start | bytes 589828
  38.4 10.7 %collective-permute-start.14 = (bf16[336,384]{1,0:T(8,128)(2,1)S(1)}, bf16[336,384]{1,0:T(8,128)(2,1)S(1)}, u32[]{:S(2)}, u32[]{:S(2)}) collective-permute-start(bf16[336,384]{1,0:T(8,128)(2,1)S(1)} %terms_3.1.refs_9_.refs_1_), channel_id=1, source_target_pairs={{0,1},{1,0},{2,3},{3,2},{4,5},{5,4},{6,7},{7,6},{8,9},{9,8},{10,11... | collective-permute-start | bytes 774152 | tf_op jit(solution)/shard_map/ppermute | solution.py:104
  49.2 2.0 %collective-permute-start.15 = (bf16[672,384]{1,0:T(8,128)(2,1)S(1)}, bf16[672,384]{1,0:T(8,128)(2,1)S(1)}, u32[]{:S(2)}, u32[]{:S(2)}) collective-permute-start(bf16[672,384]{1,0:T(8,128)(2,1)S(1)} %sums_2.1.refs_1_), channel_id=1, source_target_pairs={{0,2},{2,0},{1,3},{3,1},{4,6},{6,4},{5,7},{7,5},{8,10},{10,8},{9,1... | collective-permute-start | bytes 1548296 | tf_op jit(solution)/shard_map/ppermute | solution.py:104

commit v5 on v4

--- a/solution.py
+++ b/solution.py
@@ -15,6 +15,7 @@
 VMEM_LIMIT = 24 * 1024 * 1024
 TOKEN = (8, 128)
 FEATURE_COST = 3 * 10**9
+FAR_COST = 2 * 10**9
 
 
 def from_behind(x, axis, by):
@@ -115,7 +116,7 @@
     return jnp.where(inside, moved, 0.0)
 
 
-def after(x, *others):
+def after(x, *others, flops=1):
     anywhere = pl.BlockSpec(memory_space=pl.ANY)
     return pl.pallas_call(
         lambda *refs: None,
@@ -124,7 +125,7 @@
         out_specs=anywhere,
         input_output_aliases={0: 0},
         compiler_params=pltpu.CompilerParams(vmem_limit_bytes=1024 * 1024),
-        cost_estimate=cost(),
+        cost_estimate=cost(flops),
         name="hand_on",
     )(x, *others)
 
@@ -473,10 +474,10 @@
         name="shares",
     )
     first_share = swap(sent, 1)
-    term = terms_of(1, near, (own_share, got[0]))
-    far = after(far, term)
+    far = after(far, own_share, flops=FAR_COST)
     last = swap(far, 1)
-    term = terms_of(2, far)
+    term = terms_of(1, near, (far, got[0]))
+    term = terms_of(2, far, (term,))
     carry = run(
         add_kernel,
         (kept, first_share),

time: 53.1 us -> 51.9 us (0.977)
  waiting for transfers between devices: 16.1 us -> 15.4 us
  starting transfers between devices: 16.1 us -> 15.5 us
    ppermute x11, waiting for transfers between devices: 1.42 us -> 0.21 us  [rotate(): return lax.ppermute(x, axis, [(i, (i + by) % size) for i in range(size)])]
    ppermute x11, starting transfers between devices: 7.41 us -> 6.51 us  [rotate(): return lax.ppermute(x, axis, [(i, (i + by) % size) for i in range(size)])]
    ppermute x5, waiting for transfers between devices: 14.7 us -> 15.2 us  [swap(): return lax.ppermute(x, 'chan', [(z, z ^ far) for z in range(count)])]
  transfers between devices with their start and end apart: 16 -> 16, of which waited for: 8 -> 5; matrix products, arithmetic and copies ran while one was open for 0% -> 0% of each run, Pallas kernels for 34% -> 35%
where the time goes in v5:
time: 51.9 us; the launch traced here: 51.8 us
  Pallas kernels  19.9 us (38%)
  starting transfers between devices  15.5 us (30%)
  waiting for transfers between devices  15.4 us (30%)
  between operations  0.93 us (2%)
    pallas_call x13, Pallas kernels, run(): pl.pallas_call(body, compiler_params=pltpu.CompilerParams(vmem_limit_byte...  19.9 us
    ppermute x5, waiting for transfers between devices, swap(): return lax.ppermute(x, 'chan', [(z, z ^ far) for z in range(count)])  15.2 us
    ppermute x5, starting transfers between devices, swap(): return lax.ppermute(x, 'chan', [(z, z ^ far) for z in range(count)])  8.97 us
    ppermute x11, starting transfers between devices, rotate(): return lax.ppermute(x, axis, [(i, (i + by) % size) for i in range(size)])  6.51 us
  transfers between devices with their start and end apart: 16, of which 5 were waited for; matrix products, arithmetic and copies ran while one was open for 0% of the time, Pallas kernels for 35%

profile of v5, /device:TPU:0, one launch (start us, length us, event | category | flops | bytes accessed | tf_op | source)
XLA Modules:
  0.0 51.8 jit_solution(9587974703439368329)
XLA Ops:
  0.6 0.5 %collective-permute-start.1 = (bf16[96,1,4,256]{3,2,1,0:T(4,128)(2,1)}, bf16[96,1,4,256]{3,2,1,0:T(4,128)(2,1)S(1)}, u32[]{:S(2)}, u32[]{:S(2)}) collective-permute-start(bf16[96,1,4,256]{3,2,1,0:T(4,128)(2,1)} %refs_1_.1), channel_id=1, source_target_pairs={{0,2},{2,0},{1,3},{3,1},{4,6},{6,4},{5,7},{7,5},{8,10},{10,8},{9,1... | collective-permute-start | bytes 589832 | tf_op jit(solution)/shard_map/ppermute | solution.py:105
  1.1 1.7 %activate.1 = (bf16[96,1024]{1,0:T(8,128)(2,1)S(1)}, f32[96,1024]{1,0:T(8,128)S(1)}) custom-call(bf16[96,1,4,256]{3,2,1,0:T(4,128)(2,1)} %refs_0_.3, bf16[96,1,4,256]{3,2,1,0:T(4,128)(2,1)} %refs_1_.1), custom_call_target="tpu_custom_call" | custom-call | flops 1 | bytes 1 | tf_op jit(solution)/shard_map/activate/pallas_call | solution.py:144
  2.8 0.1 collective-permute-start
  3.0 3.0 %collective-permute-start.2 = (bf16[96,1024]{1,0:T(8,128)(2,1)S(1)}, bf16[96,1024]{1,0:T(8,128)(2,1)S(1)}, u32[]{:S(2)}, u32[]{:S(2)}) collective-permute-start(bf16[96,1024]{1,0:T(8,128)(2,1)S(1)} %get-tuple-element.16.refs_0_.refs_1_), channel_id=1, source_target_pairs={{0,4},{4,0},{8,12},{12,8},{1,5},{5,1},{9,13},{13,9},{2,6},{6,2},{1... | collective-permute-start | bytes 589832 | tf_op jit(solution)/shard_map/ppermute | solution.py:407
  6.0 2.6 %collective-permute-start.4 = (bf16[96,1024]{1,0:T(8,128)(2,1)S(1)}, bf16[96,1024]{1,0:T(8,128)(2,1)S(1)}, u32[]{:S(2)}, u32[]{:S(2)}) collective-permute-start(bf16[96,1024]{1,0:T(8,128)(2,1)S(1)} %get-tuple-element.16.refs_0_.refs_1_), channel_id=1, source_target_pairs={{0,8},{4,12},{8,0},{12,4},{1,9},{5,13},{9,1},{13,5},{2,10},{6,14},... | collective-permute-start | bytes 589832 | tf_op jit(solution)/shard_map/ppermute | solution.py:407
  8.6 0.0 collective-permute-done.1.refs_3_
  8.6 0.0 collective-permute-done.refs_1_.refs_2_
  8.6 2.0 %own_terms.1 = (bf16[336,384]{1,0:T(8,128)(2,1)S(1)}, bf16[432,2048]{1,0:T(8,128)(2,1)S(1)}, f32[96,2048]{1,0:T(8,128)S(1)}, bf16[2592,384]{1,0:T(8,128)(2,1)S(1)}) custom-call(bf16[96,1024]{1,0:T(8,128)(2,1)S(1)} %get-tuple-element.16.refs_0_.refs_1_, bf16[96,1024]{1,0:T(8,128)(2,1)S(1)} %collective-permute-done.refs_1_.refs_2_, ...), custom_call_target="tpu_custom_call" | custom-call | flops 1 | bytes 1 | tf_op jit(solution)/shard_map/own_terms/pallas_call | solution.py:144
  10.6 1.6 %collective-permute-start.8 = (bf16[336,384]{1,0:T(8,128)(2,1)S(1)}, bf16[336,384]{1,0:T(8,128)(2,1)S(1)}, u32[]{:S(2)}, u32[]{:S(2)}) collective-permute-start(bf16[336,384]{1,0:T(8,128)(2,1)S(1)} %get-tuple-element.19.refs_1_.refs_0_), channel_id=1, source_target_pairs={{0,1},{1,0},{2,3},{3,2},{4,5},{5,4},{6,7},{7,6},{8,9},{9,8},{10,11... | collective-permute-start | bytes 774152 | tf_op jit(solution)/shard_map/ppermute | solution.py:105
  12.1 3.1 %collective-permute-done.2.refs_0_ = bf16[96,1024]{1,0:T(8,128)(2,1)S(1)} collective-permute-done((bf16[96,1024]{1,0:T(8,128)(2,1)S(1)}, bf16[96,1024]{1,0:T(8,128)(2,1)S(1)}, u32[]{:S(2)}, u32[]{:S(2)}) %collective-permute-start.2) | collective-permute-done | bytes 196640 | tf_op jit(solution)/shard_map/ppermute | solution.py:407
  15.2 0.0 collective-permute-start.3
  15.2 3.0 %shares.1 = (f32[96,1024]{1,0:T(8,128)S(1)}, f32[96,1024]{1,0:T(8,128)S(1)}, bf16[2,96,1024]{2,1,0:T(8,128)(2,1)S(1)}) custom-call(bf16[2592,384]{1,0:T(8,128)(2,1)S(1)} %get-tuple-element.18.refs_0_, f32[96,2048]{1,0:T(8,128)S(1)} %get-tuple-element.20.refs_1_, bf16[96,1024]{1,0:T(8,128)(2,1)S(1)} %hand_on.3.refs_2_.refs_1_.refs_3_), custom_call_target="tpu_custom_call" | custom-call | flops 1 | bytes 1 | tf_op jit(solution)/shard_map/shares/pallas_call | solution.py:144
  18.2 0.1 collective-permute-start.7
  18.3 0.0 collective-permute-done.4.refs_0_
  18.3 0.0 collective-permute-done.3.refs_2_.refs_4_
  18.3 0.0 collective-permute-done.8.refs_4_.refs_2_
  18.3 1.4 %terms_1.1.refs_3_.refs_1_ = bf16[336,384]{1,0:T(8,128)(2,1)S(1)} custom-call(bf16[432,2048]{1,0:T(8,128)(2,1)S(1)} %get-tuple-element.24.refs_0_, bf16[96,1024]{1,0:T(8,128)(2,1)S(1)} %hand_on.3.refs_2_.refs_1_.refs_3_, bf16[96,1024]{1,0:T(8,128)(2,1)S(1)} %collective-permute-done.3.refs_2_.refs_4_, bf16[96,1024]{1,0:T(8,128)(2,1)S(1)} %hand_on.4.refs_3_.refs_1_.refs_5_, ...), custom_call_target="tpu_custom_call" | custom-call | flops 1 | bytes 1 | tf_op jit(solution)/shard_map/terms_1/pallas_call | solution.py:144
  19.7 1.7 %collective-permute-start.9 = (bf16[336,384]{1,0:T(8,128)(2,1)S(1)}, bf16[336,384]{1,0:T(8,128)(2,1)S(1)}, u32[]{:S(2)}, u32[]{:S(2)}) collective-permute-start(bf16[336,384]{1,0:T(8,128)(2,1)S(1)} %terms_1.1.refs_3_.refs_1_), channel_id=1, source_target_pairs={{0,1},{1,0},{2,3},{3,2},{4,5},{5,4},{6,7},{7,6},{8,9},{9,8},{10,11... | collective-permute-start | bytes 774152 | tf_op jit(solution)/shard_map/ppermute | solution.py:105
  21.4 0.2 collective-permute-start.5
  21.6 1.8 %collective-permute-start.6 = (bf16[96,1024]{1,0:T(8,128)(2,1)S(1)}, bf16[96,1024]{1,0:T(8,128)(2,1)S(1)}, u32[]{:S(2)}, u32[]{:S(2)}) collective-permute-start(bf16[96,1024]{1,0:T(8,128)(2,1)S(1)} %hand_on.4.refs_3_.refs_1_.refs_5_), channel_id=1, source_target_pairs={{0,4},{4,0},{8,12},{12,8},{1,5},{5,1},{9,13},{13,9},{2,6},{6,2},{1... | collective-permute-start | bytes 589832 | tf_op jit(solution)/shard_map/ppermute | solution.py:407
  23.4 0.0 collective-permute-done.5.refs_2_.refs_6_
  23.4 1.3 %terms_2.1.refs_2_.refs_0_ = bf16[336,384]{1,0:T(8,128)(2,1)S(1)} custom-call(bf16[432,2048]{1,0:T(8,128)(2,1)S(1)} %get-tuple-element.24.refs_0_, bf16[96,1024]{1,0:T(8,128)(2,1)S(1)} %hand_on.4.refs_3_.refs_1_.refs_5_, bf16[96,1024]{1,0:T(8,128)(2,1)S(1)} %collective-permute-done.5.refs_2_.refs_6_, bf16[336,384]{1,0:T(8,128)(2,1)S(1)} %terms_1.1.refs_3_.refs_1_), custom_call_target="tpu_custom_call" | custom-call | flops 1 | bytes 1 | tf_op jit(solution)/shard_map/terms_2/pallas_call | solution.py:144
  24.7 0.4 collective-permute-start.11
  25.2 5.0 %collective-permute-done.7.refs_1_.refs_2_ = bf16[2,96,1024]{2,1,0:T(8,128)(2,1)S(1)} collective-permute-done((bf16[2,96,1024]{2,1,0:T(8,128)(2,1)S(1)}, bf16[2,96,1024]{2,1,0:T(8,128)(2,1)S(1)}, u32[]{:S(2)}, u32[]{:S(2)}) %collective-permute-start.7) | collective-permute-done | bytes 393248 | tf_op jit(solution)/shard_map/ppermute | solution.py:407
  30.2 3.8 %collective-permute-done.6.refs_0_ = bf16[96,1024]{1,0:T(8,128)(2,1)S(1)} collective-permute-done((bf16[96,1024]{1,0:T(8,128)(2,1)S(1)}, bf16[96,1024]{1,0:T(8,128)(2,1)S(1)}, u32[]{:S(2)}, u32[]{:S(2)}) %collective-permute-start.6) | collective-permute-done | bytes 196640 | tf_op jit(solution)/shard_map/ppermute | solution.py:407
  34.0 0.0 collective-permute-done.9.refs_2_.refs_3_
  34.0 0.0 collective-permute-start.10
  34.0 1.5 %collective-permute-start.12 = (bf16[96,1024]{1,0:T(8,128)(2,1)S(1)}, bf16[96,1024]{1,0:T(8,128)(2,1)S(1)}, u32[]{:S(2)}, u32[]{:S(2)}) collective-permute-start(bf16[96,1024]{1,0:T(8,128)(2,1)S(1)} %carry_share.1.refs_1_), channel_id=1, source_target_pairs={{0,8},{4,12},{8,0},{12,4},{1,9},{5,13},{9,1},{13,5},{2,10},{6,14},... | collective-permute-start | bytes 589832 | tf_op jit(solution)/shard_map/ppermute | solution.py:407
  35.5 0.1 sums_0.1.refs_5_.refs_0_
  35.7 0.2 collective-permute-start.13
  35.9 0.0 collective-permute-done.10.refs_2_.refs_8_
  35.9 1.5 %terms_3.1.refs_9_.refs_1_ = bf16[336,384]{1,0:T(8,128)(2,1)S(1)} custom-call(bf16[432,2048]{1,0:T(8,128)(2,1)S(1)} %get-tuple-element.24.refs_0_, bf16[96,1024]{1,0:T(8,128)(2,1)S(1)} %hand_on.5.refs_1_.refs_7_, bf16[96,1024]{1,0:T(8,128)(2,1)S(1)} %collective-permute-done.10.refs_2_.refs_8_), custom_call_target="tpu_custom_call" | custom-call | flops 1 | bytes 1 | tf_op jit(solution)/shard_map/terms_3/pallas_call | solution.py:144
  37.4 0.0 copy-start
  37.4 1.6 %collective-permute-start.14 = (bf16[336,384]{1,0:T(8,128)(2,1)S(1)}, bf16[336,384]{1,0:T(8,128)(2,1)S(1)}, u32[]{:S(2)}, u32[]{:S(2)}) collective-permute-start(bf16[336,384]{1,0:T(8,128)(2,1)S(1)} %terms_3.1.refs_9_.refs_1_), channel_id=1, source_target_pairs={{0,1},{1,0},{2,3},{3,2},{4,5},{5,4},{6,7},{7,6},{8,9},{9,8},{10,11... | collective-permute-start | bytes 774152 | tf_op jit(solution)/shard_map/ppermute | solution.py:105
  39.0 0.0 collective-permute-done.11.refs_10_.refs_2_
  39.0 4.1 %conv.1 = (bf16[96,1,4,256]{3,2,1,0:T(4,128)(2,1)}, f32[8,128]{1,0:T(8,128)S(1)}) custom-call(bf16[2592,384]{1,0:T(8,128)(2,1)S(1)} %get-tuple-element.18.refs_0_, bf16[96,1024]{1,0:T(8,128)(2,1)S(1)} %get-tuple-element.16.refs_0_.refs_1_, bf16[96,1024]{1,0:T(8,128)(2,1)S(1)} %collective-permute-done.refs_1_.refs_2_, ...), custom_call_target="tpu_custom_call" | custom-call | flops 1 | bytes 1 | tf_op jit(solution)/shard_map/conv/pallas_call | solution.py:144
  43.1 3.3 %collective-permute-done.12.refs_3_ = bf16[96,1024]{1,0:T(8,128)(2,1)S(1)} collective-permute-done((bf16[96,1024]{1,0:T(8,128)(2,1)S(1)}, bf16[96,1024]{1,0:T(8,128)(2,1)S(1)}, u32[]{:S(2)}, u32[]{:S(2)}) %collective-permute-start.12) | collective-permute-done | bytes 196640 | tf_op jit(solution)/shard_map/ppermute | solution.py:407
  46.4 0.0 copy-done
  46.4 1.4 %feature_grad.1 = (bf16[96,1,4,256]{3,2,1,0:T(4,128)(2,1)}, f32[8,128]{1,0:T(8,128)S(1)}) custom-call(bf16[96,1,4,256]{3,2,1,0:T(4,128)(2,1)S(1)} %copy-done, f32[96,1024]{1,0:T(8,128)S(1)} %get-tuple-element.21.refs_1_, bf16[2,96,1024]{2,1,0:T(8,128)(2,1)S(1)} %collective-permute-done.7.refs_1_.refs_2_, ...), custom_call_target="tpu_custom_call" | custom-call | flops 3000000000 | bytes 1 | tf_op jit(solution)/shard_map/feature_grad/pallas_call | solution.py:144
  47.9 0.0 collective-permute-done.14.refs_3_
  47.9 0.1 sums_2.1.refs_1_
  48.0 0.1 collective-permute-start.15
  48.1 1.6 %kernel_grad_0.1.refs_2_ = f32[3,864,384]{2,1,0:T(8,128)} custom-call(bf16[672,384]{1,0:T(8,128)(2,1)S(1)} %sums_0.1.refs_5_.refs_0_, bf16[672,384]{1,0:T(8,128)(2,1)S(1)} %sums_2.1.refs_1_), custom_call_target="tpu_custom_call" | custom-call | flops 1 | bytes 1 | tf_op jit(solution)/shard_map/kernel_grad_0/pallas_call | solution.py:144
  49.8 0.0 collective-permute-done.13.refs_0_
  49.8 0.2 collective-permute-done.15.refs_1_
  50.0 1.6 %kernel_grad_1.1 = f32[3,864,384]{2,1,0:T(8,128)} custom-call(bf16[672,384]{1,0:T(8,128)(2,1)S(1)} %collective-permute-done.13.refs_0_, bf16[672,384]{1,0:T(8,128)(2,1)S(1)} %collective-permute-done.15.refs_1_, f32[3,864,384]{2,1,0:T(8,128)} %kernel_grad_0.1.refs_2_), custom_call_target="tpu_custom_call", output_to_operand_aliasing={{}: (2, {})} | custom-call | flops 1 | bytes 1 | tf_op jit(solution)/shard_map/kernel_grad_1/pallas_call | solution.py:144
  (4 shorter events, 0.1 us)
Async XLA Ops:
  0.6 7.9 %collective-permute-start.1 = (bf16[96,1,4,256]{3,2,1,0:T(4,128)(2,1)}, bf16[96,1,4,256]{3,2,1,0:T(4,128)(2,1)S(1)}, u32[]{:S(2)}, u32[]{:S(2)}) collective-permute-start(bf16[96,1,4,256]{3,2,1,0:T(4,128)(2,1)} %refs_1_.1), channel_id=1, source_target_pairs={{0,2},{2,0},{1,3},{3,1},{4,6},{6,4},{5,7},{7,5},{8,10},{10,8},{9,1... | collective-permute-start | bytes 589832 | tf_op jit(solution)/shard_map/ppermute | solution.py:105
  2.8 5.7 %collective-permute-start = (bf16[96,1024]{1,0:T(8,128)(2,1)S(1)}, bf16[96,1024]{1,0:T(8,128)(2,1)S(1)}, u32[]{:S(2)}, u32[]{:S(2)}) collective-permute-start(bf16[96,1024]{1,0:T(8,128)(2,1)S(1)} %get-tuple-element.16.refs_0_.refs_1_), channel_id=1, source_target_pairs={{0,2},{2,0},{1,3},{3,1},{4,6},{6,4},{5,7},{7,5},{8,10},{10,8},{9,1... | collective-permute-start | bytes 589832 | tf_op jit(solution)/shard_map/ppermute | solution.py:105
  3.0 12.3 %collective-permute-start.2 = (bf16[96,1024]{1,0:T(8,128)(2,1)S(1)}, bf16[96,1024]{1,0:T(8,128)(2,1)S(1)}, u32[]{:S(2)}, u32[]{:S(2)}) collective-permute-start(bf16[96,1024]{1,0:T(8,128)(2,1)S(1)} %get-tuple-element.16.refs_0_.refs_1_), channel_id=1, source_target_pairs={{0,4},{4,0},{8,12},{12,8},{1,5},{5,1},{9,13},{13,9},{2,6},{6,2},{1... | collective-permute-start | bytes 589832 | tf_op jit(solution)/shard_map/ppermute | solution.py:407
  6.0 12.3 %collective-permute-start.4 = (bf16[96,1024]{1,0:T(8,128)(2,1)S(1)}, bf16[96,1024]{1,0:T(8,128)(2,1)S(1)}, u32[]{:S(2)}, u32[]{:S(2)}) collective-permute-start(bf16[96,1024]{1,0:T(8,128)(2,1)S(1)} %get-tuple-element.16.refs_0_.refs_1_), channel_id=1, source_target_pairs={{0,8},{4,12},{8,0},{12,4},{1,9},{5,13},{9,1},{13,5},{2,10},{6,14},... | collective-permute-start | bytes 589832 | tf_op jit(solution)/shard_map/ppermute | solution.py:407
  10.6 7.7 %collective-permute-start.8 = (bf16[336,384]{1,0:T(8,128)(2,1)S(1)}, bf16[336,384]{1,0:T(8,128)(2,1)S(1)}, u32[]{:S(2)}, u32[]{:S(2)}) collective-permute-start(bf16[336,384]{1,0:T(8,128)(2,1)S(1)} %get-tuple-element.19.refs_1_.refs_0_), channel_id=1, source_target_pairs={{0,1},{1,0},{2,3},{3,2},{4,5},{5,4},{6,7},{7,6},{8,9},{9,8},{10,11... | collective-permute-start | bytes 774152 | tf_op jit(solution)/shard_map/ppermute | solution.py:105
  15.2 3.1 %collective-permute-start.3 = (bf16[96,1024]{1,0:T(8,128)(2,1)S(1)}, bf16[96,1024]{1,0:T(8,128)(2,1)S(1)}, u32[]{:S(2)}, u32[]{:S(2)}) collective-permute-start(bf16[96,1024]{1,0:T(8,128)(2,1)S(1)} %hand_on.3.refs_2_.refs_1_.refs_3_), channel_id=1, source_target_pairs={{0,2},{2,0},{1,3},{3,1},{4,6},{6,4},{5,7},{7,5},{8,10},{10,8},{9,1... | collective-permute-start | bytes 589832 | tf_op jit(solution)/shard_map/ppermute | solution.py:105
  18.2 12.0 %collective-permute-start.7 = (bf16[2,96,1024]{2,1,0:T(8,128)(2,1)S(1)}, bf16[2,96,1024]{2,1,0:T(8,128)(2,1)S(1)}, u32[]{:S(2)}, u32[]{:S(2)}) collective-permute-start(bf16[2,96,1024]{2,1,0:T(8,128)(2,1)S(1)} %get-tuple-element.23), channel_id=1, source_target_pairs={{0,4},{4,0},{8,12},{12,8},{1,5},{5,1},{9,13},{13,9},{2,6},{6,2},{1... | collective-permute-start | bytes 1179656 | tf_op jit(solution)/shard_map/ppermute | solution.py:407
  19.7 14.3 %collective-permute-start.9 = (bf16[336,384]{1,0:T(8,128)(2,1)S(1)}, bf16[336,384]{1,0:T(8,128)(2,1)S(1)}, u32[]{:S(2)}, u32[]{:S(2)}) collective-permute-start(bf16[336,384]{1,0:T(8,128)(2,1)S(1)} %terms_1.1.refs_3_.refs_1_), channel_id=1, source_target_pairs={{0,1},{1,0},{2,3},{3,2},{4,5},{5,4},{6,7},{7,6},{8,9},{9,8},{10,11... | collective-permute-start | bytes 774152 | tf_op jit(solution)/shard_map/ppermute | solution.py:105
  21.4 2.0 %collective-permute-start.5 = (bf16[96,1024]{1,0:T(8,128)(2,1)S(1)}, bf16[96,1024]{1,0:T(8,128)(2,1)S(1)}, u32[]{:S(2)}, u32[]{:S(2)}) collective-permute-start(bf16[96,1024]{1,0:T(8,128)(2,1)S(1)} %hand_on.4.refs_3_.refs_1_.refs_5_), channel_id=1, source_target_pairs={{0,2},{2,0},{1,3},{3,1},{4,6},{6,4},{5,7},{7,5},{8,10},{10,8},{9,1... | collective-permute-start | bytes 589832 | tf_op jit(solution)/shard_map/ppermute | solution.py:105
  21.6 12.4 %collective-permute-start.6 = (bf16[96,1024]{1,0:T(8,128)(2,1)S(1)}, bf16[96,1024]{1,0:T(8,128)(2,1)S(1)}, u32[]{:S(2)}, u32[]{:S(2)}) collective-permute-start(bf16[96,1024]{1,0:T(8,128)(2,1)S(1)} %hand_on.4.refs_3_.refs_1_.refs_5_), channel_id=1, source_target_pairs={{0,4},{4,0},{8,12},{12,8},{1,5},{5,1},{9,13},{13,9},{2,6},{6,2},{1... | collective-permute-start | bytes 589832 | tf_op jit(solution)/shard_map/ppermute | solution.py:407
  24.7 14.3 %collective-permute-start.11 = (bf16[336,384]{1,0:T(8,128)(2,1)S(1)}, bf16[336,384]{1,0:T(8,128)(2,1)S(1)}, u32[]{:S(2)}, u32[]{:S(2)}) collective-permute-start(bf16[336,384]{1,0:T(8,128)(2,1)S(1)} %terms_2.1.refs_2_.refs_0_), channel_id=1, source_target_pairs={{0,1},{1,0},{2,3},{3,2},{4,5},{5,4},{6,7},{7,6},{8,9},{9,8},{10,11... | collective-permute-start | bytes 774152 | tf_op jit(solution)/shard_map/ppermute | solution.py:105
  34.0 1.9 %collective-permute-start.10 = (bf16[96,1024]{1,0:T(8,128)(2,1)S(1)}, bf16[96,1024]{1,0:T(8,128)(2,1)S(1)}, u32[]{:S(2)}, u32[]{:S(2)}) collective-permute-start(bf16[96,1024]{1,0:T(8,128)(2,1)S(1)} %hand_on.5.refs_1_.refs_7_), channel_id=1, source_target_pairs={{0,2},{2,0},{1,3},{3,1},{4,6},{6,4},{5,7},{7,5},{8,10},{10,8},{9,1... | collective-permute-start | bytes 589832 | tf_op jit(solution)/shard_map/ppermute | solution.py:105
  34.0 12.4 %collective-permute-start.12 = (bf16[96,1024]{1,0:T(8,128)(2,1)S(1)}, bf16[96,1024]{1,0:T(8,128)(2,1)S(1)}, u32[]{:S(2)}, u32[]{:S(2)}) collective-permute-start(bf16[96,1024]{1,0:T(8,128)(2,1)S(1)} %carry_share.1.refs_1_), channel_id=1, source_target_pairs={{0,8},{4,12},{8,0},{12,4},{1,9},{5,13},{9,1},{13,5},{2,10},{6,14},... | collective-permute-start | bytes 589832 | tf_op jit(solution)/shard_map/ppermute | solution.py:407
  35.7 14.1 %collective-permute-start.13 = (bf16[672,384]{1,0:T(8,128)(2,1)S(1)}, bf16[672,384]{1,0:T(8,128)(2,1)S(1)}, u32[]{:S(2)}, u32[]{:S(2)}) collective-permute-start(bf16[672,384]{1,0:T(8,128)(2,1)S(1)} %sums_0.1.refs_5_.refs_0_), channel_id=1, source_target_pairs={{0,2},{2,0},{1,3},{3,1},{4,6},{6,4},{5,7},{7,5},{8,10},{10,8},{9,1... | collective-permute-start | bytes 1548296 | tf_op jit(solution)/shard_map/ppermute | solution.py:105
  37.4 9.0 %copy-start = (bf16[96,1,4,256]{3,2,1,0:T(4,128)(2,1)S(1)}, bf16[96,1,4,256]{3,2,1,0:T(4,128)(2,1)}, u32[]{:S(2)}) copy-start(bf16[96,1,4,256]{3,2,1,0:T(4,128)(2,1)} %refs_0_.3) | copy-start | bytes 589828
  37.4 10.4 %collective-permute-start.14 = (bf16[336,384]{1,0:T(8,128)(2,1)S(1)}, bf16[336,384]{1,0:T(8,128)(2,1)S(1)}, u32[]{:S(2)}, u32[]{:S(2)}) collective-permute-start(bf16[336,384]{1,0:T(8,128)(2,1)S(1)} %terms_3.1.refs_9_.refs_1_), channel_id=1, source_target_pairs={{0,1},{1,0},{2,3},{3,2},{4,5},{5,4},{6,7},{7,6},{8,9},{9,8},{10,11... | collective-permute-start | bytes 774152 | tf_op jit(solution)/shard_map/ppermute | solution.py:105
  48.0 2.0 %collective-permute-start.15 = (bf16[672,384]{1,0:T(8,128)(2,1)S(1)}, bf16[672,384]{1,0:T(8,128)(2,1)S(1)}, u32[]{:S(2)}, u32[]{:S(2)}) collective-permute-start(bf16[672,384]{1,0:T(8,128)(2,1)S(1)} %sums_2.1.refs_1_), channel_id=1, source_target_pairs={{0,2},{2,0},{1,3},{3,1},{4,6},{6,4},{5,7},{7,5},{8,10},{10,8},{9,1... | collective-permute-start | bytes 1548296 | tf_op jit(solution)/shard_map/ppermute | solution.py:105

commit v6 on v5

--- a/solution.py
+++ b/solution.py
@@ -15,7 +15,8 @@
 VMEM_LIMIT = 24 * 1024 * 1024
 TOKEN = (8, 128)
 FEATURE_COST = 3 * 10**9
-FAR_COST = 2 * 10**9
+FAR_COST = 3 * 10**8
+NEAR_COST = 10**9
 
 
 def from_behind(x, axis, by):
@@ -296,6 +297,19 @@
     sent[1] = part(3).astype(BF16)
 
 
+def split_kernel(block, out, first, second):
+    out[...] = block[...]
+    middle = block.shape[1] // 2
+    first[...] = block[:, :middle]
+    second[...] = block[:, middle:]
+
+
+def join_kernel(first, second, out):
+    middle = out.shape[1] // 2
+    out[:, :middle] = first[...]
+    out[:, middle:] = second[...]
+
+
 def add_kernel(kept, came, out):
     out[...] = (kept[...] + came[1].astype(F32)).astype(out.dtype)
 
@@ -441,8 +455,8 @@
     terms, got = [own_term], [rotate(own_term, "dp", 1)]
     blocks = [activation, other]
 
-    def terms_of(k, here, waits=()):
-        blocks.extend((here, rotate(here, "tm", 1)))
+    def terms_of(k, here, there, waits=()):
+        blocks.extend((here, there))
         term = run(
             functools.partial(terms_kernel, pixels, k),
             (stack, *blocks[-2:]),
@@ -456,11 +470,10 @@
         got.append(rotate(term, "dp", 1))
         return term
 
-    near = after(near, own_term)
     own_share, kept, sent = run(
         functools.partial(share_kernel, pixels),
         (weights, flat),
-        waits=(near,),
+        waits=(own_term,),
         out_shape=(
             sds((rows, length), F32),
             sds((rows, length), F32),
@@ -474,10 +487,11 @@
         name="shares",
     )
     first_share = swap(sent, 1)
+    near = after(near, own_share, flops=NEAR_COST)
     far = after(far, own_share, flops=FAR_COST)
     last = swap(far, 1)
-    term = terms_of(1, near, (far, got[0]))
-    term = terms_of(2, far, (term,))
+    term = terms_of(1, near, rotate(near, "tm", 1), (own_share, far, got[0]))
+    term = terms_of(2, far, rotate(far, "tm", 1), (term,))
     carry = run(
         add_kernel,
         (kept, first_share),
@@ -487,7 +501,22 @@
         name="carry_share",
     )
     second_share = swap(carry, 2)
-    term = terms_of(3, after(last, carry, got[1]))
+    last, *parts = run(
+        split_kernel,
+        (last,),
+        waits=(carry, got[1]),
+        out_shape=(block_shape,) + (sds((rows, length // 2), BF16),) * 2,
+        out_specs=(whole(),) * 3,
+        name="split",
+    )
+    last_other = run(
+        join_kernel,
+        [rotate(part, "tm", 1) for part in parts],
+        out_shape=block_shape,
+        out_specs=whole(),
+        name="join",
+    )
+    term = terms_of(3, last, last_other)
 
     def sums(first, stop, waits=()):
         return run(
@@ -508,7 +537,7 @@
         scratch_shapes=[pltpu.VMEM((channels, (frames + 2) * pixels), BF16)],
         name="conv",
     )
-    early = sums(0, 2)
+    early = sums(0, 2, (term,))
     feature_grad, token = run(
         functools.partial(feature_kernel, pixels),
         (features, own_share, first_share, second_share),

time: 51.9 us -> 47.5 us (0.915)
  starting transfers between devices: 15.5 us -> 13 us
  waiting for transfers between devices: 15.4 us -> 13.5 us
    ppermute x5, waiting for transfers between devices: 15.2 us -> 9.16 us  [swap(): return lax.ppermute(x, 'chan', [(z, z ^ far) for z in range(count)])]
    ppermute x11 -> x12, waiting for transfers between devices: 0.21 us -> 4.36 us  [rotate(): return lax.ppermute(x, axis, [(i, (i + by) % size) for i in range(size)])]
    ppermute x5, starting transfers between devices: 8.97 us -> 7.3 us  [swap(): return lax.ppermute(x, 'chan', [(z, z ^ far) for z in range(count)])]
    ppermute x11 -> x12, starting transfers between devices: 6.51 us -> 5.7 us  [rotate(): return lax.ppermute(x, axis, [(i, (i + by) % size) for i in range(size)])]
    pallas_call x13 -> x15, Pallas kernels: 19.9 us -> 19.9 us  [run(): pl.pallas_call(body, compiler_params=pltpu.CompilerParams(vmem_limit_byte...]
  transfers between devices with their start and end apart: 16 -> 17, of which waited for: 5 -> 8; matrix products, arithmetic and copies ran while one was open for 0% -> 0% of each run, Pallas kernels for 35% -> 39%
where the time goes in v6:
time: 47.5 us; the launch traced here: 47.4 us
  Pallas kernels  19.9 us (42%)
  waiting for transfers between devices  13.5 us (28%)
  starting transfers between devices  13 us (27%)
  between operations  0.91 us (2%)
    pallas_call x15, Pallas kernels, run(): pl.pallas_call(body, compiler_params=pltpu.CompilerParams(vmem_limit_byte...  19.9 us
    ppermute x5, waiting for transfers between devices, swap(): return lax.ppermute(x, 'chan', [(z, z ^ far) for z in range(count)])  9.16 us
    ppermute x5, starting transfers between devices, swap(): return lax.ppermute(x, 'chan', [(z, z ^ far) for z in range(count)])  7.3 us
    ppermute x12, starting transfers between devices, rotate(): return lax.ppermute(x, axis, [(i, (i + by) % size) for i in range(size)])  5.7 us
    ppermute x12, waiting for transfers between devices, rotate(): return lax.ppermute(x, axis, [(i, (i + by) % size) for i in range(size)])  4.36 us
  transfers between devices with their start and end apart: 17, of which 8 were waited for; matrix products, arithmetic and copies ran while one was open for 0% of the time, Pallas kernels for 39%

profile of v6, /device:TPU:0, one launch (start us, length us, event | category | flops | bytes accessed | tf_op | source)
XLA Modules:
  0.0 47.4 jit_solution(3939230445166486712)
XLA Ops:
  0.6 0.5 %collective-permute-start.1 = (bf16[96,1,4,256]{3,2,1,0:T(4,128)(2,1)}, bf16[96,1,4,256]{3,2,1,0:T(4,128)(2,1)S(1)}, u32[]{:S(2)}, u32[]{:S(2)}) collective-permute-start(bf16[96,1,4,256]{3,2,1,0:T(4,128)(2,1)} %refs_1_.1), channel_id=1, source_target_pairs={{0,2},{2,0},{1,3},{3,1},{4,6},{6,4},{5,7},{7,5},{8,10},{10,8},{9,1... | collective-permute-start | bytes 589832 | tf_op jit(solution)/shard_map/ppermute | solution.py:106
  1.1 1.7 %activate.1 = (bf16[96,1024]{1,0:T(8,128)(2,1)S(1)}, f32[96,1024]{1,0:T(8,128)S(1)}) custom-call(bf16[96,1,4,256]{3,2,1,0:T(4,128)(2,1)} %refs_0_.3, bf16[96,1,4,256]{3,2,1,0:T(4,128)(2,1)} %refs_1_.1), custom_call_target="tpu_custom_call" | custom-call | flops 1 | bytes 1 | tf_op jit(solution)/shard_map/activate/pallas_call | solution.py:145
  2.8 0.1 collective-permute-start
  3.0 3.0 %collective-permute-start.2 = (bf16[96,1024]{1,0:T(8,128)(2,1)S(1)}, bf16[96,1024]{1,0:T(8,128)(2,1)S(1)}, u32[]{:S(2)}, u32[]{:S(2)}) collective-permute-start(bf16[96,1024]{1,0:T(8,128)(2,1)S(1)} %get-tuple-element.19.refs_0_.refs_1_), channel_id=1, source_target_pairs={{0,4},{4,0},{8,12},{12,8},{1,5},{5,1},{9,13},{13,9},{2,6},{6,2},{1... | collective-permute-start | bytes 589832 | tf_op jit(solution)/shard_map/ppermute | solution.py:421
  6.0 2.6 %collective-permute-start.4 = (bf16[96,1024]{1,0:T(8,128)(2,1)S(1)}, bf16[96,1024]{1,0:T(8,128)(2,1)S(1)}, u32[]{:S(2)}, u32[]{:S(2)}) collective-permute-start(bf16[96,1024]{1,0:T(8,128)(2,1)S(1)} %get-tuple-element.19.refs_0_.refs_1_), channel_id=1, source_target_pairs={{0,8},{4,12},{8,0},{12,4},{1,9},{5,13},{9,1},{13,5},{2,10},{6,14},... | collective-permute-start | bytes 589832 | tf_op jit(solution)/shard_map/ppermute | solution.py:421
  8.6 0.0 collective-permute-done.1.refs_3_
  8.6 0.0 collective-permute-done.refs_1_.refs_2_
  8.6 2.0 %own_terms.1 = (bf16[336,384]{1,0:T(8,128)(2,1)S(1)}, bf16[432,2048]{1,0:T(8,128)(2,1)S(1)}, f32[96,2048]{1,0:T(8,128)S(1)}, bf16[2592,384]{1,0:T(8,128)(2,1)S(1)}) custom-call(bf16[96,1024]{1,0:T(8,128)(2,1)S(1)} %get-tuple-element.19.refs_0_.refs_1_, bf16[96,1024]{1,0:T(8,128)(2,1)S(1)} %collective-permute-done.refs_1_.refs_2_, ...), custom_call_target="tpu_custom_call" | custom-call | flops 1 | bytes 1 | tf_op jit(solution)/shard_map/own_terms/pallas_call | solution.py:145
  10.6 1.6 %collective-permute-start.8 = (bf16[336,384]{1,0:T(8,128)(2,1)S(1)}, bf16[336,384]{1,0:T(8,128)(2,1)S(1)}, u32[]{:S(2)}, u32[]{:S(2)}) collective-permute-start(bf16[336,384]{1,0:T(8,128)(2,1)S(1)} %get-tuple-element.23.refs_2_.refs_0_), channel_id=1, source_target_pairs={{0,1},{1,0},{2,3},{3,2},{4,5},{5,4},{6,7},{7,6},{8,9},{9,8},{10,11... | collective-permute-start | bytes 774152 | tf_op jit(solution)/shard_map/ppermute | solution.py:106
  12.1 3.0 %shares.1 = (f32[96,1024]{1,0:T(8,128)S(1)}, f32[96,1024]{1,0:T(8,128)S(1)}, bf16[2,96,1024]{2,1,0:T(8,128)(2,1)S(1)}) custom-call(bf16[2592,384]{1,0:T(8,128)(2,1)S(1)} %get-tuple-element.21.refs_0_, f32[96,2048]{1,0:T(8,128)S(1)} %get-tuple-element.22.refs_1_, bf16[336,384]{1,0:T(8,128)(2,1)S(1)} %get-tuple-element.23.refs_2_.refs_0_), custom_call_target="tpu_custom_call" | custom-call | flops 1 | bytes 1 | tf_op jit(solution)/shard_map/shares/pallas_call | solution.py:145
  15.1 0.5 %collective-permute-start.7 = (bf16[2,96,1024]{2,1,0:T(8,128)(2,1)S(1)}, bf16[2,96,1024]{2,1,0:T(8,128)(2,1)S(1)}, u32[]{:S(2)}, u32[]{:S(2)}) collective-permute-start(bf16[2,96,1024]{2,1,0:T(8,128)(2,1)S(1)} %get-tuple-element.26), channel_id=1, source_target_pairs={{0,4},{4,0},{8,12},{12,8},{1,5},{5,1},{9,13},{13,9},{2,6},{6,2},{1... | collective-permute-start | bytes 1179656 | tf_op jit(solution)/shard_map/ppermute | solution.py:421
  15.6 0.0 collective-permute-done.2.refs_0_
  15.6 0.0 collective-permute-start.3
  15.6 1.5 %collective-permute-done.4.refs_0_ = bf16[96,1024]{1,0:T(8,128)(2,1)S(1)} collective-permute-done((bf16[96,1024]{1,0:T(8,128)(2,1)S(1)}, bf16[96,1024]{1,0:T(8,128)(2,1)S(1)}, u32[]{:S(2)}, u32[]{:S(2)}) %collective-permute-start.4) | collective-permute-done | bytes 196640 | tf_op jit(solution)/shard_map/ppermute | solution.py:421
  17.2 0.0 collective-permute-start.5
  17.2 0.0 collective-permute-done.3.refs_2_.refs_4_
  17.2 1.1 %collective-permute-done.8.refs_5_.refs_2_ = bf16[336,384]{1,0:T(8,128)(2,1)S(1)} collective-permute-done((bf16[336,384]{1,0:T(8,128)(2,1)S(1)}, bf16[336,384]{1,0:T(8,128)(2,1)S(1)}, u32[]{:S(2)}, u32[]{:S(2)}) %collective-permute-start.8) | collective-permute-done | bytes 258080 | tf_op jit(solution)/shard_map/ppermute | solution.py:106
  18.3 1.3 %terms_1.1.refs_3_.refs_1_ = bf16[336,384]{1,0:T(8,128)(2,1)S(1)} custom-call(bf16[432,2048]{1,0:T(8,128)(2,1)S(1)} %get-tuple-element.27.refs_0_, bf16[96,1024]{1,0:T(8,128)(2,1)S(1)} %hand_on.2.refs_1_.refs_3_, bf16[96,1024]{1,0:T(8,128)(2,1)S(1)} %collective-permute-done.3.refs_2_.refs_4_, f32[96,1024]{1,0:T(8,128)S(1)} %get-tuple-element.24.refs_1_.refs_3_, ...), custom_call_target="tpu_custom_call" | custom-call | flops 1 | bytes 1 | tf_op jit(solution)/shard_map/terms_1/pallas_call | solution.py:145
  19.6 1.6 %collective-permute-start.9 = (bf16[336,384]{1,0:T(8,128)(2,1)S(1)}, bf16[336,384]{1,0:T(8,128)(2,1)S(1)}, u32[]{:S(2)}, u32[]{:S(2)}) collective-permute-start(bf16[336,384]{1,0:T(8,128)(2,1)S(1)} %terms_1.1.refs_3_.refs_1_), channel_id=1, source_target_pairs={{0,1},{1,0},{2,3},{3,2},{4,5},{5,4},{6,7},{7,6},{8,9},{9,8},{10,11... | collective-permute-start | bytes 774152 | tf_op jit(solution)/shard_map/ppermute | solution.py:106
  21.2 0.8 %collective-permute-start.6 = (bf16[96,1024]{1,0:T(8,128)(2,1)S(1)}, bf16[96,1024]{1,0:T(8,128)(2,1)S(1)}, u32[]{:S(2)}, u32[]{:S(2)}) collective-permute-start(bf16[96,1024]{1,0:T(8,128)(2,1)S(1)} %hand_on.3.refs_4_.refs_1_.refs_5_), channel_id=1, source_target_pairs={{0,4},{4,0},{8,12},{12,8},{1,5},{5,1},{9,13},{13,9},{2,6},{6,2},{1... | collective-permute-start | bytes 589832 | tf_op jit(solution)/shard_map/ppermute | solution.py:421
  21.9 0.0 collective-permute-done.5.refs_2_.refs_6_
  21.9 1.3 %terms_2.1.refs_2_.refs_0_ = bf16[336,384]{1,0:T(8,128)(2,1)S(1)} custom-call(bf16[432,2048]{1,0:T(8,128)(2,1)S(1)} %get-tuple-element.27.refs_0_, bf16[96,1024]{1,0:T(8,128)(2,1)S(1)} %hand_on.3.refs_4_.refs_1_.refs_5_, bf16[96,1024]{1,0:T(8,128)(2,1)S(1)} %collective-permute-done.5.refs_2_.refs_6_, bf16[336,384]{1,0:T(8,128)(2,1)S(1)} %terms_1.1.refs_3_.refs_1_), custom_call_target="tpu_custom_call" | custom-call | flops 1 | bytes 1 | tf_op jit(solution)/shard_map/terms_2/pallas_call | solution.py:145
  23.3 0.5 %collective-permute-start.12 = (bf16[336,384]{1,0:T(8,128)(2,1)S(1)}, bf16[336,384]{1,0:T(8,128)(2,1)S(1)}, u32[]{:S(2)}, u32[]{:S(2)}) collective-permute-start(bf16[336,384]{1,0:T(8,128)(2,1)S(1)} %terms_2.1.refs_2_.refs_0_), channel_id=1, source_target_pairs={{0,1},{1,0},{2,3},{3,2},{4,5},{5,4},{6,7},{7,6},{8,9},{9,8},{10,11... | collective-permute-start | bytes 774152 | tf_op jit(solution)/shard_map/ppermute | solution.py:106
  23.8 3.4 %collective-permute-done.7.refs_1_.refs_2_ = bf16[2,96,1024]{2,1,0:T(8,128)(2,1)S(1)} collective-permute-done((bf16[2,96,1024]{2,1,0:T(8,128)(2,1)S(1)}, bf16[2,96,1024]{2,1,0:T(8,128)(2,1)S(1)}, u32[]{:S(2)}, u32[]{:S(2)}) %collective-permute-start.7) | collective-permute-done | bytes 393248 | tf_op jit(solution)/shard_map/ppermute | solution.py:421
  27.3 0.4 collective-permute-start.13
  27.7 4.2 %collective-permute-done.6.refs_0_ = bf16[96,1024]{1,0:T(8,128)(2,1)S(1)} collective-permute-done((bf16[96,1024]{1,0:T(8,128)(2,1)S(1)}, bf16[96,1024]{1,0:T(8,128)(2,1)S(1)}, u32[]{:S(2)}, u32[]{:S(2)}) %collective-permute-start.6) | collective-permute-done | bytes 196640 | tf_op jit(solution)/shard_map/ppermute | solution.py:421
  31.8 0.0 collective-permute-done.9.refs_2_.refs_3_
  31.9 0.1 collective-permute-start.10
  31.9 0.5 %collective-permute-start.11 = (bf16[96,512]{1,0:T(8,128)(2,1)S(1)}, bf16[96,512]{1,0:T(8,128)(2,1)S(1)}, u32[]{:S(2)}, u32[]{:S(2)}) collective-permute-start(bf16[96,512]{1,0:T(8,128)(2,1)S(1)} %get-tuple-element.30), channel_id=1, source_target_pairs={{0,2},{2,0},{1,3},{3,1},{4,6},{6,4},{5,7},{7,5},{8,10},{10,8},{9,1... | collective-permute-start | bytes 294920 | tf_op jit(solution)/shard_map/ppermute | solution.py:106
  32.4 0.8 %collective-permute-done.10.refs_0_ = bf16[96,512]{1,0:T(8,128)(2,1)S(1)} collective-permute-done((bf16[96,512]{1,0:T(8,128)(2,1)S(1)}, bf16[96,512]{1,0:T(8,128)(2,1)S(1)}, u32[]{:S(2)}, u32[]{:S(2)}) %collective-permute-start.10) | collective-permute-done | bytes 98336 | tf_op jit(solution)/shard_map/ppermute | solution.py:106
  33.2 0.2 collective-permute-done.11.refs_1_
  33.4 1.5 %terms_3.1.refs_9_.refs_4_.refs_1_ = bf16[336,384]{1,0:T(8,128)(2,1)S(1)} custom-call(bf16[432,2048]{1,0:T(8,128)(2,1)S(1)} %get-tuple-element.27.refs_0_, bf16[96,1024]{1,0:T(8,128)(2,1)S(1)} %get-tuple-element.28.refs_1_.refs_7_, bf16[96,1024]{1,0:T(8,128)(2,1)S(1)} %join.1.refs_2_.refs_8_), custom_call_target="tpu_custom_call" | custom-call | flops 1 | bytes 1 | tf_op jit(solution)/shard_map/terms_3/pallas_call | solution.py:145
  34.9 0.7 %collective-permute-start.15 = (bf16[336,384]{1,0:T(8,128)(2,1)S(1)}, bf16[336,384]{1,0:T(8,128)(2,1)S(1)}, u32[]{:S(2)}, u32[]{:S(2)}) collective-permute-start(bf16[336,384]{1,0:T(8,128)(2,1)S(1)} %terms_3.1.refs_9_.refs_4_.refs_1_), channel_id=1, source_target_pairs={{0,1},{1,0},{2,3},{3,2},{4,5},{5,4},{6,7},{7,6},{8,9},{9,8},{10,11... | collective-permute-start | bytes 774152 | tf_op jit(solution)/shard_map/ppermute | solution.py:106
  35.6 0.1 sums_0.1.refs_5_.refs_0_
  35.8 0.0 copy-start
  35.8 0.1 collective-permute-start.14
  35.9 0.0 collective-permute-done.12.refs_10_.refs_2_
  35.9 4.1 %conv.1 = (bf16[96,1,4,256]{3,2,1,0:T(4,128)(2,1)}, f32[8,128]{1,0:T(8,128)S(1)}) custom-call(bf16[2592,384]{1,0:T(8,128)(2,1)S(1)} %get-tuple-element.21.refs_0_, bf16[96,1024]{1,0:T(8,128)(2,1)S(1)} %get-tuple-element.19.refs_0_.refs_1_, bf16[96,1024]{1,0:T(8,128)(2,1)S(1)} %collective-permute-done.refs_1_.refs_2_, ...), custom_call_target="tpu_custom_call" | custom-call | flops 1 | bytes 1 | tf_op jit(solution)/shard_map/conv/pallas_call | solution.py:145
  40.0 0.0 collective-permute-done.13.refs_3_
  40.0 0.0 copy-done
  40.0 1.4 %feature_grad.1 = (bf16[96,1,4,256]{3,2,1,0:T(4,128)(2,1)}, f32[8,128]{1,0:T(8,128)S(1)}) custom-call(bf16[96,1,4,256]{3,2,1,0:T(4,128)(2,1)S(1)} %copy-done, f32[96,1024]{1,0:T(8,128)S(1)} %get-tuple-element.24.refs_1_.refs_3_, bf16[2,96,1024]{2,1,0:T(8,128)(2,1)S(1)} %collective-permute-done.7.refs_1_.refs_2_, ...), custom_call_target="tpu_custom_call" | custom-call | flops 3000000000 | bytes 1 | tf_op jit(solution)/shard_map/feature_grad/pallas_call | solution.py:145
  41.4 2.1 %collective-permute-done.15.refs_3_ = bf16[336,384]{1,0:T(8,128)(2,1)S(1)} collective-permute-done((bf16[336,384]{1,0:T(8,128)(2,1)S(1)}, bf16[336,384]{1,0:T(8,128)(2,1)S(1)}, u32[]{:S(2)}, u32[]{:S(2)}) %collective-permute-start.15) | collective-permute-done | bytes 258080 | tf_op jit(solution)/shard_map/ppermute | solution.py:106
  43.5 0.1 sums_2.1.refs_1_
  43.6 0.1 collective-permute-start.16
  43.7 1.6 %kernel_grad_0.1.refs_2_ = f32[3,864,384]{2,1,0:T(8,128)} custom-call(bf16[672,384]{1,0:T(8,128)(2,1)S(1)} %sums_0.1.refs_5_.refs_0_, bf16[672,384]{1,0:T(8,128)(2,1)S(1)} %sums_2.1.refs_1_), custom_call_target="tpu_custom_call" | custom-call | flops 1 | bytes 1 | tf_op jit(solution)/shard_map/kernel_grad_0/pallas_call | solution.py:145
  45.3 0.0 collective-permute-done.14.refs_0_
  45.3 0.2 collective-permute-done.16.refs_1_
  45.6 1.6 %kernel_grad_1.1 = f32[3,864,384]{2,1,0:T(8,128)} custom-call(bf16[672,384]{1,0:T(8,128)(2,1)S(1)} %collective-permute-done.14.refs_0_, bf16[672,384]{1,0:T(8,128)(2,1)S(1)} %collective-permute-done.16.refs_1_, f32[3,864,384]{2,1,0:T(8,128)} %kernel_grad_0.1.refs_2_), custom_call_target="tpu_custom_call", output_to_operand_aliasing={{}: (2, {})} | custom-call | flops 1 | bytes 1 | tf_op jit(solution)/shard_map/kernel_grad_1/pallas_call | solution.py:145
  (5 shorter events, 0.1 us)
Async XLA Ops:
  0.6 7.9 %collective-permute-start.1 = (bf16[96,1,4,256]{3,2,1,0:T(4,128)(2,1)}, bf16[96,1,4,256]{3,2,1,0:T(4,128)(2,1)S(1)}, u32[]{:S(2)}, u32[]{:S(2)}) collective-permute-start(bf16[96,1,4,256]{3,2,1,0:T(4,128)(2,1)} %refs_1_.1), channel_id=1, source_target_pairs={{0,2},{2,0},{1,3},{3,1},{4,6},{6,4},{5,7},{7,5},{8,10},{10,8},{9,1... | collective-permute-start | bytes 589832 | tf_op jit(solution)/shard_map/ppermute | solution.py:106
  2.8 5.7 %collective-permute-start = (bf16[96,1024]{1,0:T(8,128)(2,1)S(1)}, bf16[96,1024]{1,0:T(8,128)(2,1)S(1)}, u32[]{:S(2)}, u32[]{:S(2)}) collective-permute-start(bf16[96,1024]{1,0:T(8,128)(2,1)S(1)} %get-tuple-element.19.refs_0_.refs_1_), channel_id=1, source_target_pairs={{0,2},{2,0},{1,3},{3,1},{4,6},{6,4},{5,7},{7,5},{8,10},{10,8},{9,1... | collective-permute-start | bytes 589832 | tf_op jit(solution)/shard_map/ppermute | solution.py:106
  3.0 12.7 %collective-permute-start.2 = (bf16[96,1024]{1,0:T(8,128)(2,1)S(1)}, bf16[96,1024]{1,0:T(8,128)(2,1)S(1)}, u32[]{:S(2)}, u32[]{:S(2)}) collective-permute-start(bf16[96,1024]{1,0:T(8,128)(2,1)S(1)} %get-tuple-element.19.refs_0_.refs_1_), channel_id=1, source_target_pairs={{0,4},{4,0},{8,12},{12,8},{1,5},{5,1},{9,13},{13,9},{2,6},{6,2},{1... | collective-permute-start | bytes 589832 | tf_op jit(solution)/shard_map/ppermute | solution.py:421
  6.0 11.2 %collective-permute-start.4 = (bf16[96,1024]{1,0:T(8,128)(2,1)S(1)}, bf16[96,1024]{1,0:T(8,128)(2,1)S(1)}, u32[]{:S(2)}, u32[]{:S(2)}) collective-permute-start(bf16[96,1024]{1,0:T(8,128)(2,1)S(1)} %get-tuple-element.19.refs_0_.refs_1_), channel_id=1, source_target_pairs={{0,8},{4,12},{8,0},{12,4},{1,9},{5,13},{9,1},{13,5},{2,10},{6,14},... | collective-permute-start | bytes 589832 | tf_op jit(solution)/shard_map/ppermute | solution.py:421
  10.6 7.7 %collective-permute-start.8 = (bf16[336,384]{1,0:T(8,128)(2,1)S(1)}, bf16[336,384]{1,0:T(8,128)(2,1)S(1)}, u32[]{:S(2)}, u32[]{:S(2)}) collective-permute-start(bf16[336,384]{1,0:T(8,128)(2,1)S(1)} %get-tuple-element.23.refs_2_.refs_0_), channel_id=1, source_target_pairs={{0,1},{1,0},{2,3},{3,2},{4,5},{5,4},{6,7},{7,6},{8,9},{9,8},{10,11... | collective-permute-start | bytes 774152 | tf_op jit(solution)/shard_map/ppermute | solution.py:106
  15.1 12.1 %collective-permute-start.7 = (bf16[2,96,1024]{2,1,0:T(8,128)(2,1)S(1)}, bf16[2,96,1024]{2,1,0:T(8,128)(2,1)S(1)}, u32[]{:S(2)}, u32[]{:S(2)}) collective-permute-start(bf16[2,96,1024]{2,1,0:T(8,128)(2,1)S(1)} %get-tuple-element.26), channel_id=1, source_target_pairs={{0,4},{4,0},{8,12},{12,8},{1,5},{5,1},{9,13},{13,9},{2,6},{6,2},{1... | collective-permute-start | bytes 1179656 | tf_op jit(solution)/shard_map/ppermute | solution.py:421
  15.6 1.6 %collective-permute-start.3 = (bf16[96,1024]{1,0:T(8,128)(2,1)S(1)}, bf16[96,1024]{1,0:T(8,128)(2,1)S(1)}, u32[]{:S(2)}, u32[]{:S(2)}) collective-permute-start(bf16[96,1024]{1,0:T(8,128)(2,1)S(1)} %hand_on.2.refs_1_.refs_3_), channel_id=1, source_target_pairs={{0,2},{2,0},{1,3},{3,1},{4,6},{6,4},{5,7},{7,5},{8,10},{10,8},{9,1... | collective-permute-start | bytes 589832 | tf_op jit(solution)/shard_map/ppermute | solution.py:106
  17.2 4.8 %collective-permute-start.5 = (bf16[96,1024]{1,0:T(8,128)(2,1)S(1)}, bf16[96,1024]{1,0:T(8,128)(2,1)S(1)}, u32[]{:S(2)}, u32[]{:S(2)}) collective-permute-start(bf16[96,1024]{1,0:T(8,128)(2,1)S(1)} %hand_on.3.refs_4_.refs_1_.refs_5_), channel_id=1, source_target_pairs={{0,2},{2,0},{1,3},{3,1},{4,6},{6,4},{5,7},{7,5},{8,10},{10,8},{9,1... | collective-permute-start | bytes 589832 | tf_op jit(solution)/shard_map/ppermute | solution.py:106
  19.6 12.2 %collective-permute-start.9 = (bf16[336,384]{1,0:T(8,128)(2,1)S(1)}, bf16[336,384]{1,0:T(8,128)(2,1)S(1)}, u32[]{:S(2)}, u32[]{:S(2)}) collective-permute-start(bf16[336,384]{1,0:T(8,128)(2,1)S(1)} %terms_1.1.refs_3_.refs_1_), channel_id=1, source_target_pairs={{0,1},{1,0},{2,3},{3,2},{4,5},{5,4},{6,7},{7,6},{8,9},{9,8},{10,11... | collective-permute-start | bytes 774152 | tf_op jit(solution)/shard_map/ppermute | solution.py:106
  21.2 10.7 %collective-permute-start.6 = (bf16[96,1024]{1,0:T(8,128)(2,1)S(1)}, bf16[96,1024]{1,0:T(8,128)(2,1)S(1)}, u32[]{:S(2)}, u32[]{:S(2)}) collective-permute-start(bf16[96,1024]{1,0:T(8,128)(2,1)S(1)} %hand_on.3.refs_4_.refs_1_.refs_5_), channel_id=1, source_target_pairs={{0,4},{4,0},{8,12},{12,8},{1,5},{5,1},{9,13},{13,9},{2,6},{6,2},{1... | collective-permute-start | bytes 589832 | tf_op jit(solution)/shard_map/ppermute | solution.py:421
  23.3 12.6 %collective-permute-start.12 = (bf16[336,384]{1,0:T(8,128)(2,1)S(1)}, bf16[336,384]{1,0:T(8,128)(2,1)S(1)}, u32[]{:S(2)}, u32[]{:S(2)}) collective-permute-start(bf16[336,384]{1,0:T(8,128)(2,1)S(1)} %terms_2.1.refs_2_.refs_0_), channel_id=1, source_target_pairs={{0,1},{1,0},{2,3},{3,2},{4,5},{5,4},{6,7},{7,6},{8,9},{9,8},{10,11... | collective-permute-start | bytes 774152 | tf_op jit(solution)/shard_map/ppermute | solution.py:106
  27.3 12.7 %collective-permute-start.13 = (bf16[96,1024]{1,0:T(8,128)(2,1)S(1)}, bf16[96,1024]{1,0:T(8,128)(2,1)S(1)}, u32[]{:S(2)}, u32[]{:S(2)}) collective-permute-start(bf16[96,1024]{1,0:T(8,128)(2,1)S(1)} %carry_share.1.refs_1_), channel_id=1, source_target_pairs={{0,8},{4,12},{8,0},{12,4},{1,9},{5,13},{9,1},{13,5},{2,10},{6,14},... | collective-permute-start | bytes 589832 | tf_op jit(solution)/shard_map/ppermute | solution.py:421
  31.9 1.4 %collective-permute-start.10 = (bf16[96,512]{1,0:T(8,128)(2,1)S(1)}, bf16[96,512]{1,0:T(8,128)(2,1)S(1)}, u32[]{:S(2)}, u32[]{:S(2)}) collective-permute-start(bf16[96,512]{1,0:T(8,128)(2,1)S(1)} %get-tuple-element.29), channel_id=1, source_target_pairs={{0,2},{2,0},{1,3},{3,1},{4,6},{6,4},{5,7},{7,5},{8,10},{10,8},{9,1... | collective-permute-start | bytes 294920 | tf_op jit(solution)/shard_map/ppermute | solution.py:106
  31.9 1.4 %collective-permute-start.11 = (bf16[96,512]{1,0:T(8,128)(2,1)S(1)}, bf16[96,512]{1,0:T(8,128)(2,1)S(1)}, u32[]{:S(2)}, u32[]{:S(2)}) collective-permute-start(bf16[96,512]{1,0:T(8,128)(2,1)S(1)} %get-tuple-element.30), channel_id=1, source_target_pairs={{0,2},{2,0},{1,3},{3,1},{4,6},{6,4},{5,7},{7,5},{8,10},{10,8},{9,1... | collective-permute-start | bytes 294920 | tf_op jit(solution)/shard_map/ppermute | solution.py:106
  34.9 8.5 %collective-permute-start.15 = (bf16[336,384]{1,0:T(8,128)(2,1)S(1)}, bf16[336,384]{1,0:T(8,128)(2,1)S(1)}, u32[]{:S(2)}, u32[]{:S(2)}) collective-permute-start(bf16[336,384]{1,0:T(8,128)(2,1)S(1)} %terms_3.1.refs_9_.refs_4_.refs_1_), channel_id=1, source_target_pairs={{0,1},{1,0},{2,3},{3,2},{4,5},{5,4},{6,7},{7,6},{8,9},{9,8},{10,11... | collective-permute-start | bytes 774152 | tf_op jit(solution)/shard_map/ppermute | solution.py:106
  35.8 4.2 %copy-start = (bf16[96,1,4,256]{3,2,1,0:T(4,128)(2,1)S(1)}, bf16[96,1,4,256]{3,2,1,0:T(4,128)(2,1)}, u32[]{:S(2)}) copy-start(bf16[96,1,4,256]{3,2,1,0:T(4,128)(2,1)} %refs_0_.3) | copy-start | bytes 589828
  35.8 9.5 %collective-permute-start.14 = (bf16[672,384]{1,0:T(8,128)(2,1)S(1)}, bf16[672,384]{1,0:T(8,128)(2,1)S(1)}, u32[]{:S(2)}, u32[]{:S(2)}) collective-permute-start(bf16[672,384]{1,0:T(8,128)(2,1)S(1)} %sums_0.1.refs_5_.refs_0_), channel_id=1, source_target_pairs={{0,2},{2,0},{1,3},{3,1},{4,6},{6,4},{5,7},{7,5},{8,10},{10,8},{9,1... | collective-permute-start | bytes 1548296 | tf_op jit(solution)/shard_map/ppermute | solution.py:106
  43.6 2.0 %collective-permute-start.16 = (bf16[672,384]{1,0:T(8,128)(2,1)S(1)}, bf16[672,384]{1,0:T(8,128)(2,1)S(1)}, u32[]{:S(2)}, u32[]{:S(2)}) collective-permute-start(bf16[672,384]{1,0:T(8,128)(2,1)S(1)} %sums_2.1.refs_1_), channel_id=1, source_target_pairs={{0,2},{2,0},{1,3},{3,1},{4,6},{6,4},{5,7},{7,5},{8,10},{10,8},{9,1... | collective-permute-start | bytes 1548296 | tf_op jit(solution)/shard_map/ppermute | solution.py:106

commit v7 on v6

--- a/solution.py
+++ b/solution.py
@@ -15,8 +15,8 @@
 VMEM_LIMIT = 24 * 1024 * 1024
 TOKEN = (8, 128)
 FEATURE_COST = 3 * 10**9
-FAR_COST = 3 * 10**8
-NEAR_COST = 10**9
+FAR_COST = 6 * 10**8
+NEAR_COST = 3 * 10**9
 
 
 def from_behind(x, axis, by):
@@ -156,19 +156,25 @@
 
 
 def activate_kernel(features, cotangent, activation, flat, feat, cot, sems):
-    loads = [
-        pltpu.make_async_copy(source, target, sems.at[n])
-        for n, (source, target) in enumerate(((features, feat), (cotangent, cot)))
-    ]
+    parts = sems.shape[1]
+    rows, _, frames, pixels = feat.shape
+    size = rows // parts
+    loads = []
+    for n, (source, target) in enumerate(((features, feat), (cotangent, cot))):
+        for part in range(parts):
+            at = pl.ds(part * size, size)
+            loads.append(pltpu.make_async_copy(source.at[at], target.at[at], sems.at[n, part]))
     for load in loads:
         load.start()
-    frames, pixels = feat.shape[2:]
-    loads[0].wait()
-    v = feat[:, 0].astype(F32)
-    act = v / (1.0 + jnp.exp(-v))
-    for t in range(frames):
-        activation[:, t * pixels : (t + 1) * pixels] = act[:, t, :].astype(BF16)
-    loads[1].wait()
+    for part in range(parts):
+        loads[part].wait()
+        at = slice(part * size, (part + 1) * size)
+        v = feat[at, 0].astype(F32)
+        act = v / (1.0 + jnp.exp(-v))
+        for t in range(frames):
+            activation[at, t * pixels : (t + 1) * pixels] = act[:, t, :].astype(BF16)
+    for load in loads[parts:]:
+        load.wait()
     flatten(pixels, cot, flat, 0)
 
 
@@ -195,21 +201,16 @@
     return 7 * unit, 2 * unit
 
 
-def fill_stack(pixels, flat, stack, which):
-    rows = flat.shape[0]
-    unit = rows // 2
-    frames = flat.shape[1] // pixels
-    for half in range(2):
-
-        @pl.when(which == half)
-        def _(half=half):
-            for t in range(frames):
-                at = slice(t * pixels, (t + 1) * pixels)
-                for q in range(9):
-                    tap, part = divmod(9 * half + q, 2)
-                    i, j = divmod(tap, 3)
-                    frame = flat[part * unit : (part + 1) * unit, at]
-                    stack[q * unit : (q + 1) * unit, at] = shifted(frame, 1 - i, 1 - j).astype(BF16)
+def fill_stack(pixels, flat, stack, half, first, frames):
+    unit = flat.shape[0] // 2
+    for t in range(frames):
+        at = slice(t * pixels, (t + 1) * pixels)
+        source = slice((first + t) * pixels, (first + t + 1) * pixels)
+        for q in range(9):
+            tap, part = divmod(9 * half + q, 2)
+            i, j = divmod(tap, 3)
+            frame = flat[part * unit : (part + 1) * unit, source]
+            stack[q * unit : (q + 1) * unit, at] = shifted(frame, 1 - i, 1 - j).astype(BF16)
 
 
 def block_terms(pixels, k, stack, here, there, out, rhs):
@@ -252,7 +253,12 @@
     me = lax.axis_index("tm")
     flat[:, pl.ds(pl.multiple_of(me * length, pixels), length)] = flat_own[...]
     flatten(pixels, cot_other, flat, (1 - me) * (length // pixels))
-    fill_stack(pixels, flat, stack, me)
+    for core in range(2):
+
+        @pl.when(me == core)
+        def _(core=core):
+            fill_stack(pixels, flat, stack, core, 0, flat.shape[1] // pixels)
+
     block_terms(pixels, 0, stack, mine, other, out, rhs)
     load.wait()
 
@@ -261,31 +267,36 @@
     block_terms(pixels, k, stack, here, there, out, rhs)
 
 
-def share_kernel(pixels, weights, flat, own, kept, sent, stack, total):
+def share_kernel(pixels, weights, flat, mine, own, kept, sent, window, other, total):
     rows, length = own.shape
-    frames = length // pixels
+    frames, half = length // pixels, mine.shape[0]
     count = weights.shape[1] // rows
     me = lax.axis_index("tm")
-    for t in range(frames + 2):
-        at = slice(t * pixels, (t + 1) * pixels)
-        if t < frames:
-            frame = flat[:, pl.ds(pl.multiple_of((me * frames + t) * pixels, pixels), pixels)]
-        else:
-            frame = jnp.where(me == 0, flat[:, at], 0.0)
-        for i in range(3):
-            for j in range(3):
-                row = (3 * i + j) * rows
-                stack[row : row + rows, at] = shifted(frame, 1 - i, 1 - j).astype(BF16)
-    taps = 9 * rows
+    front = 2 * pixels
+    for core in range(2):
+
+        @pl.when(me == core)
+        def _(core=core):
+            first = core * length
+            held = min(length + front, mine.shape[1] - first)
+            window[:, :held] = mine[:, first : first + held]
+            if held < length + front:
+                window[:, held:] = jnp.zeros((half, length + front - held), BF16)
+                other[:, held:] = jnp.zeros((half, length + front - held), BF16)
+            fill_stack(pixels, flat, other, 1 - core, core * frames, held // pixels)
+
     acc = None
     for a in range(3):
-        term = lax.dot_general(
-            weights[a * taps : (a + 1) * taps, :],
-            stack[:, (2 - a) * pixels : (2 - a) * pixels + length],
-            (((0,), (0,)), ((), ())),
-            preferred_element_type=F32,
-        )
-        acc = term if acc is None else acc + term
+        lanes = slice((2 - a) * pixels, (2 - a) * pixels + length)
+        for which, stack in ((me, window), (1 - me, other)):
+            at = pl.multiple_of((2 * a + which) * half, SUB)
+            term = lax.dot_general(
+                weights[pl.ds(at, half), :],
+                stack[:, lanes],
+                (((0,), (0,)), ((), ())),
+                preferred_element_type=F32,
+            )
+            acc = term if acc is None else acc + term
     total[...] = acc
 
     def part(k):
@@ -432,7 +443,7 @@
         scratch_shapes=[
             pltpu.VMEM(features.shape, BF16),
             pltpu.VMEM(features.shape, BF16),
-            pltpu.SemaphoreType.DMA((2,)),
+            pltpu.SemaphoreType.DMA((2, 3)),
         ],
         name="activate",
     )
@@ -472,7 +483,7 @@
 
     own_share, kept, sent = run(
         functools.partial(share_kernel, pixels),
-        (weights, flat),
+        (weights, flat, stack),
         waits=(own_term,),
         out_shape=(
             sds((rows, length), F32),
@@ -481,7 +492,8 @@
         ),
         out_specs=(whole(),) * 3,
         scratch_shapes=[
-            pltpu.VMEM((9 * rows, (frames + 2) * pixels), BF16),
+            pltpu.VMEM((half, (frames + 2) * pixels), BF16),
+            pltpu.VMEM((half, (frames + 2) * pixels), BF16),
             pltpu.VMEM((channels, length), F32),
         ],
         name="shares",
@@ -504,7 +516,7 @@
     last, *parts = run(
         split_kernel,
         (last,),
-        waits=(carry, got[1]),
+        waits=(carry,),
         out_shape=(block_shape,) + (sds((rows, length // 2), BF16),) * 2,
         out_specs=(whole(),) * 3,
         name="split",
@@ -516,7 +528,7 @@
         out_specs=whole(),
         name="join",
     )
-    term = terms_of(3, last, last_other)
+    term = terms_of(3, last, last_other, (got[1],))
 
     def sums(first, stop, waits=()):
         return run(

time: 47.5 us -> 47.6 us (level)
  waiting for transfers between devices: 13.5 us -> 12.6 us
  starting transfers between devices: 13 us -> 13.8 us
    ppermute x12, waiting for transfers between devices: 4.36 us -> 3.32 us  [rotate(): return lax.ppermute(x, axis, [(i, (i + by) % size) for i in range(size)])]
    ppermute x5, starting transfers between devices: 7.3 us -> 8 us  [swap(): return lax.ppermute(x, 'chan', [(z, z ^ far) for z in range(count)])]
  transfers between devices with their start and end apart: 17 -> 17, of which waited for: 8 -> 7; matrix products, arithmetic and copies ran while one was open for 0% -> 0% of each run, Pallas kernels for 39% -> 39%
where the time goes in v7:
time: 47.6 us; the launch traced here: 47.5 us
  Pallas kernels  20.1 us (42%)
  starting transfers between devices  13.8 us (29%)
  waiting for transfers between devices  12.6 us (26%)
  between operations  0.92 us (2%)
    pallas_call x15, Pallas kernels, run(): pl.pallas_call(body, compiler_params=pltpu.CompilerParams(vmem_limit_byte...  20.1 us
    ppermute x5, waiting for transfers between devices, swap(): return lax.ppermute(x, 'chan', [(z, z ^ far) for z in range(count)])  9.31 us
    ppermute x5, starting transfers between devices, swap(): return lax.ppermute(x, 'chan', [(z, z ^ far) for z in range(count)])  8 us
    ppermute x12, starting transfers between devices, rotate(): return lax.ppermute(x, axis, [(i, (i + by) % size) for i in range(size)])  5.77 us
    ppermute x12, waiting for transfers between devices, rotate(): return lax.ppermute(x, axis, [(i, (i + by) % size) for i in range(size)])  3.32 us
  transfers between devices with their start and end apart: 17, of which 7 were waited for; matrix products, arithmetic and copies ran while one was open for 0% of the time, Pallas kernels for 39%

profile of v7, /device:TPU:0, one launch (start us, length us, event | category | flops | bytes accessed | tf_op | source)
XLA Modules:
  0.0 47.5 jit_solution(1327334223903310115)
XLA Ops:
  0.6 0.5 %collective-permute-start.1 = (bf16[96,1,4,256]{3,2,1,0:T(4,128)(2,1)}, bf16[96,1,4,256]{3,2,1,0:T(4,128)(2,1)S(1)}, u32[]{:S(2)}, u32[]{:S(2)}) collective-permute-start(bf16[96,1,4,256]{3,2,1,0:T(4,128)(2,1)} %refs_1_.1), channel_id=1, source_target_pairs={{0,2},{2,0},{1,3},{3,1},{4,6},{6,4},{5,7},{7,5},{8,10},{10,8},{9,1... | collective-permute-start | bytes 589832 | tf_op jit(solution)/shard_map/ppermute | solution.py:106
  1.1 1.6 %activate.1 = (bf16[96,1024]{1,0:T(8,128)(2,1)S(1)}, f32[96,1024]{1,0:T(8,128)S(1)}) custom-call(bf16[96,1,4,256]{3,2,1,0:T(4,128)(2,1)} %refs_0_.3, bf16[96,1,4,256]{3,2,1,0:T(4,128)(2,1)} %refs_1_.1), custom_call_target="tpu_custom_call" | custom-call | flops 1 | bytes 1 | tf_op jit(solution)/shard_map/activate/pallas_call | solution.py:145
  2.8 0.1 collective-permute-start
  2.9 3.0 %collective-permute-start.2 = (bf16[96,1024]{1,0:T(8,128)(2,1)S(1)}, bf16[96,1024]{1,0:T(8,128)(2,1)S(1)}, u32[]{:S(2)}, u32[]{:S(2)}) collective-permute-start(bf16[96,1024]{1,0:T(8,128)(2,1)S(1)} %get-tuple-element.19.refs_0_.refs_1_), channel_id=1, source_target_pairs={{0,4},{4,0},{8,12},{12,8},{1,5},{5,1},{9,13},{13,9},{2,6},{6,2},{1... | collective-permute-start | bytes 589832 | tf_op jit(solution)/shard_map/ppermute | solution.py:432
  5.9 2.6 %collective-permute-start.4 = (bf16[96,1024]{1,0:T(8,128)(2,1)S(1)}, bf16[96,1024]{1,0:T(8,128)(2,1)S(1)}, u32[]{:S(2)}, u32[]{:S(2)}) collective-permute-start(bf16[96,1024]{1,0:T(8,128)(2,1)S(1)} %get-tuple-element.19.refs_0_.refs_1_), channel_id=1, source_target_pairs={{0,8},{4,12},{8,0},{12,4},{1,9},{5,13},{9,1},{13,5},{2,10},{6,14},... | collective-permute-start | bytes 589832 | tf_op jit(solution)/shard_map/ppermute | solution.py:432
  8.5 0.0 collective-permute-done.1.refs_3_
  8.5 0.0 collective-permute-done.refs_1_.refs_2_
  8.5 2.0 %own_terms.1 = (bf16[336,384]{1,0:T(8,128)(2,1)S(1)}, bf16[432,2048]{1,0:T(8,128)(2,1)S(1)}, f32[96,2048]{1,0:T(8,128)S(1)}, bf16[2592,384]{1,0:T(8,128)(2,1)S(1)}) custom-call(bf16[96,1024]{1,0:T(8,128)(2,1)S(1)} %get-tuple-element.19.refs_0_.refs_1_, bf16[96,1024]{1,0:T(8,128)(2,1)S(1)} %collective-permute-done.refs_1_.refs_2_, ...), custom_call_target="tpu_custom_call" | custom-call | flops 1 | bytes 1 | tf_op jit(solution)/shard_map/own_terms/pallas_call | solution.py:145
  10.5 1.6 %collective-permute-start.8 = (bf16[336,384]{1,0:T(8,128)(2,1)S(1)}, bf16[336,384]{1,0:T(8,128)(2,1)S(1)}, u32[]{:S(2)}, u32[]{:S(2)}) collective-permute-start(bf16[336,384]{1,0:T(8,128)(2,1)S(1)} %get-tuple-element.24.refs_3_.refs_0_), channel_id=1, source_target_pairs={{0,1},{1,0},{2,3},{3,2},{4,5},{5,4},{6,7},{7,6},{8,9},{9,8},{10,11... | collective-permute-start | bytes 774152 | tf_op jit(solution)/shard_map/ppermute | solution.py:106
  12.1 3.2 %shares.1 = (f32[96,1024]{1,0:T(8,128)S(1)}, f32[96,1024]{1,0:T(8,128)S(1)}, bf16[2,96,1024]{2,1,0:T(8,128)(2,1)S(1)}) custom-call(bf16[2592,384]{1,0:T(8,128)(2,1)S(1)} %get-tuple-element.21.refs_0_, f32[96,2048]{1,0:T(8,128)S(1)} %get-tuple-element.22.refs_1_, bf16[432,2048]{1,0:T(8,128)(2,1)S(1)} %get-tuple-element.23.refs_2_.refs_0_, ...), custom_call_target="tpu_custom_call" | custom-call | flops 1 | bytes 1 | tf_op jit(solution)/shard_map/shares/pallas_call | solution.py:145
  15.3 0.5 %collective-permute-start.7 = (bf16[2,96,1024]{2,1,0:T(8,128)(2,1)S(1)}, bf16[2,96,1024]{2,1,0:T(8,128)(2,1)S(1)}, u32[]{:S(2)}, u32[]{:S(2)}) collective-permute-start(bf16[2,96,1024]{2,1,0:T(8,128)(2,1)S(1)} %get-tuple-element.27), channel_id=1, source_target_pairs={{0,4},{4,0},{8,12},{12,8},{1,5},{5,1},{9,13},{13,9},{2,6},{6,2},{1... | collective-permute-start | bytes 1179656 | tf_op jit(solution)/shard_map/ppermute | solution.py:432
  15.8 0.0 collective-permute-done.2.refs_0_
  15.8 0.0 collective-permute-start.3
  15.8 1.4 %collective-permute-done.4.refs_0_ = bf16[96,1024]{1,0:T(8,128)(2,1)S(1)} collective-permute-done((bf16[96,1024]{1,0:T(8,128)(2,1)S(1)}, bf16[96,1024]{1,0:T(8,128)(2,1)S(1)}, u32[]{:S(2)}, u32[]{:S(2)}) %collective-permute-start.4) | collective-permute-done | bytes 196640 | tf_op jit(solution)/shard_map/ppermute | solution.py:432
  17.2 0.0 collective-permute-start.5
  17.2 1.5 %collective-permute-start.6 = (bf16[96,1024]{1,0:T(8,128)(2,1)S(1)}, bf16[96,1024]{1,0:T(8,128)(2,1)S(1)}, u32[]{:S(2)}, u32[]{:S(2)}) collective-permute-start(bf16[96,1024]{1,0:T(8,128)(2,1)S(1)} %hand_on.3.refs_4_.refs_1_.refs_5_), channel_id=1, source_target_pairs={{0,4},{4,0},{8,12},{12,8},{1,5},{5,1},{9,13},{13,9},{2,6},{6,2},{1... | collective-permute-start | bytes 589832 | tf_op jit(solution)/shard_map/ppermute | solution.py:432
  18.7 0.0 collective-permute-done.3.refs_2_.refs_4_
  18.7 0.0 collective-permute-done.8.refs_5_.refs_2_
  18.7 1.3 %terms_1.1.refs_3_.refs_1_ = bf16[336,384]{1,0:T(8,128)(2,1)S(1)} custom-call(bf16[432,2048]{1,0:T(8,128)(2,1)S(1)} %get-tuple-element.23.refs_2_.refs_0_, bf16[96,1024]{1,0:T(8,128)(2,1)S(1)} %hand_on.2.refs_1_.refs_3_, bf16[96,1024]{1,0:T(8,128)(2,1)S(1)} %collective-permute-done.3.refs_2_.refs_4_, f32[96,1024]{1,0:T(8,128)S(1)} %get-tuple-element.25.refs_1_.refs_3_, ...), custom_call_target="tpu_custom_call" | custom-call | flops 1 | bytes 1 | tf_op jit(solution)/shard_map/terms_1/pallas_call | solution.py:145
  20.1 1.8 %collective-permute-start.11 = (bf16[336,384]{1,0:T(8,128)(2,1)S(1)}, bf16[336,384]{1,0:T(8,128)(2,1)S(1)}, u32[]{:S(2)}, u32[]{:S(2)}) collective-permute-start(bf16[336,384]{1,0:T(8,128)(2,1)S(1)} %terms_1.1.refs_3_.refs_1_), channel_id=1, source_target_pairs={{0,1},{1,0},{2,3},{3,2},{4,5},{5,4},{6,7},{7,6},{8,9},{9,8},{10,11... | collective-permute-start | bytes 774152 | tf_op jit(solution)/shard_map/ppermute | solution.py:106
  21.9 0.0 collective-permute-done.5.refs_2_.refs_6_
  21.9 1.3 %terms_2.1.refs_2_.refs_0_ = bf16[336,384]{1,0:T(8,128)(2,1)S(1)} custom-call(bf16[432,2048]{1,0:T(8,128)(2,1)S(1)} %get-tuple-element.23.refs_2_.refs_0_, bf16[96,1024]{1,0:T(8,128)(2,1)S(1)} %hand_on.3.refs_4_.refs_1_.refs_5_, bf16[96,1024]{1,0:T(8,128)(2,1)S(1)} %collective-permute-done.5.refs_2_.refs_6_, bf16[336,384]{1,0:T(8,128)(2,1)S(1)} %terms_1.1.refs_3_.refs_1_), custom_call_target="tpu_custom_call" | custom-call | flops 1 | bytes 1 | tf_op jit(solution)/shard_map/terms_2/pallas_call | solution.py:145
  23.2 0.3 collective-permute-start.12
  23.6 3.8 %collective-permute-done.7.refs_1_.refs_2_ = bf16[2,96,1024]{2,1,0:T(8,128)(2,1)S(1)} collective-permute-done((bf16[2,96,1024]{2,1,0:T(8,128)(2,1)S(1)}, bf16[2,96,1024]{2,1,0:T(8,128)(2,1)S(1)}, u32[]{:S(2)}, u32[]{:S(2)}) %collective-permute-start.7) | collective-permute-done | bytes 393248 | tf_op jit(solution)/shard_map/ppermute | solution.py:432
  27.5 0.4 collective-permute-start.13
  27.9 4.0 %collective-permute-done.6.refs_0_ = bf16[96,1024]{1,0:T(8,128)(2,1)S(1)} collective-permute-done((bf16[96,1024]{1,0:T(8,128)(2,1)S(1)}, bf16[96,1024]{1,0:T(8,128)(2,1)S(1)}, u32[]{:S(2)}, u32[]{:S(2)}) %collective-permute-start.6) | collective-permute-done | bytes 196640 | tf_op jit(solution)/shard_map/ppermute | solution.py:432
  31.9 0.1 collective-permute-start.9
  32.0 0.5 %collective-permute-start.10 = (bf16[96,512]{1,0:T(8,128)(2,1)S(1)}, bf16[96,512]{1,0:T(8,128)(2,1)S(1)}, u32[]{:S(2)}, u32[]{:S(2)}) collective-permute-start(bf16[96,512]{1,0:T(8,128)(2,1)S(1)} %get-tuple-element.30), channel_id=1, source_target_pairs={{0,2},{2,0},{1,3},{3,1},{4,6},{6,4},{5,7},{7,5},{8,10},{10,8},{9,1... | collective-permute-start | bytes 294920 | tf_op jit(solution)/shard_map/ppermute | solution.py:106
  32.5 0.8 %collective-permute-done.9.refs_0_ = bf16[96,512]{1,0:T(8,128)(2,1)S(1)} collective-permute-done((bf16[96,512]{1,0:T(8,128)(2,1)S(1)}, bf16[96,512]{1,0:T(8,128)(2,1)S(1)}, u32[]{:S(2)}, u32[]{:S(2)}) %collective-permute-start.9) | collective-permute-done | bytes 98336 | tf_op jit(solution)/shard_map/ppermute | solution.py:106
  33.3 0.2 collective-permute-done.10.refs_1_
  33.5 0.0 collective-permute-done.11.refs_3_
  33.5 1.5 %terms_3.1.refs_9_.refs_4_.refs_1_ = bf16[336,384]{1,0:T(8,128)(2,1)S(1)} custom-call(bf16[432,2048]{1,0:T(8,128)(2,1)S(1)} %get-tuple-element.23.refs_2_.refs_0_, bf16[96,1024]{1,0:T(8,128)(2,1)S(1)} %get-tuple-element.28.refs_1_.refs_7_, bf16[96,1024]{1,0:T(8,128)(2,1)S(1)} %join.1.refs_2_.refs_8_, bf16[336,384]{1,0:T(8,128)(2,1)S(1)} %collective-permute-done.11.refs_3_), custom_call_target="tpu_custom_call" | custom-call | flops 1 | bytes 1 | tf_op jit(solution)/shard_map/terms_3/pallas_call | solution.py:145
  35.0 0.6 %collective-permute-start.15 = (bf16[336,384]{1,0:T(8,128)(2,1)S(1)}, bf16[336,384]{1,0:T(8,128)(2,1)S(1)}, u32[]{:S(2)}, u32[]{:S(2)}) collective-permute-start(bf16[336,384]{1,0:T(8,128)(2,1)S(1)} %terms_3.1.refs_9_.refs_4_.refs_1_), channel_id=1, source_target_pairs={{0,1},{1,0},{2,3},{3,2},{4,5},{5,4},{6,7},{7,6},{8,9},{9,8},{10,11... | collective-permute-start | bytes 774152 | tf_op jit(solution)/shard_map/ppermute | solution.py:106
  35.7 0.1 sums_0.1.refs_5_.refs_0_
  35.8 0.0 copy-start
  35.8 0.1 collective-permute-start.14
  35.9 0.0 collective-permute-done.12.refs_10_.refs_2_
  35.9 4.1 %conv.1 = (bf16[96,1,4,256]{3,2,1,0:T(4,128)(2,1)}, f32[8,128]{1,0:T(8,128)S(1)}) custom-call(bf16[2592,384]{1,0:T(8,128)(2,1)S(1)} %get-tuple-element.21.refs_0_, bf16[96,1024]{1,0:T(8,128)(2,1)S(1)} %get-tuple-element.19.refs_0_.refs_1_, bf16[96,1024]{1,0:T(8,128)(2,1)S(1)} %collective-permute-done.refs_1_.refs_2_, ...), custom_call_target="tpu_custom_call" | custom-call | flops 1 | bytes 1 | tf_op jit(solution)/shard_map/conv/pallas_call | solution.py:145
  40.0 0.0 collective-permute-done.13.refs_3_
  40.0 0.0 copy-done
  40.0 1.4 %feature_grad.1 = (bf16[96,1,4,256]{3,2,1,0:T(4,128)(2,1)}, f32[8,128]{1,0:T(8,128)S(1)}) custom-call(bf16[96,1,4,256]{3,2,1,0:T(4,128)(2,1)S(1)} %copy-done, f32[96,1024]{1,0:T(8,128)S(1)} %get-tuple-element.25.refs_1_.refs_3_, bf16[2,96,1024]{2,1,0:T(8,128)(2,1)S(1)} %collective-permute-done.7.refs_1_.refs_2_, ...), custom_call_target="tpu_custom_call" | custom-call | flops 3000000000 | bytes 1 | tf_op jit(solution)/shard_map/feature_grad/pallas_call | solution.py:145
  41.5 2.1 %collective-permute-done.15.refs_3_ = bf16[336,384]{1,0:T(8,128)(2,1)S(1)} collective-permute-done((bf16[336,384]{1,0:T(8,128)(2,1)S(1)}, bf16[336,384]{1,0:T(8,128)(2,1)S(1)}, u32[]{:S(2)}, u32[]{:S(2)}) %collective-permute-start.15) | collective-permute-done | bytes 258080 | tf_op jit(solution)/shard_map/ppermute | solution.py:106
  43.6 0.1 sums_2.1.refs_1_
  43.7 0.1 collective-permute-start.16
  43.8 1.6 %kernel_grad_0.1.refs_2_ = f32[3,864,384]{2,1,0:T(8,128)} custom-call(bf16[672,384]{1,0:T(8,128)(2,1)S(1)} %sums_0.1.refs_5_.refs_0_, bf16[672,384]{1,0:T(8,128)(2,1)S(1)} %sums_2.1.refs_1_), custom_call_target="tpu_custom_call" | custom-call | flops 1 | bytes 1 | tf_op jit(solution)/shard_map/kernel_grad_0/pallas_call | solution.py:145
  45.4 0.0 collective-permute-done.14.refs_0_
  45.4 0.2 collective-permute-done.16.refs_1_
  45.7 1.6 %kernel_grad_1.1 = f32[3,864,384]{2,1,0:T(8,128)} custom-call(bf16[672,384]{1,0:T(8,128)(2,1)S(1)} %collective-permute-done.14.refs_0_, bf16[672,384]{1,0:T(8,128)(2,1)S(1)} %collective-permute-done.16.refs_1_, f32[3,864,384]{2,1,0:T(8,128)} %kernel_grad_0.1.refs_2_), custom_call_target="tpu_custom_call", output_to_operand_aliasing={{}: (2, {})} | custom-call | flops 1 | bytes 1 | tf_op jit(solution)/shard_map/kernel_grad_1/pallas_call | solution.py:145
  (5 shorter events, 0.1 us)
Async XLA Ops:
  0.6 7.9 %collective-permute-start.1 = (bf16[96,1,4,256]{3,2,1,0:T(4,128)(2,1)}, bf16[96,1,4,256]{3,2,1,0:T(4,128)(2,1)S(1)}, u32[]{:S(2)}, u32[]{:S(2)}) collective-permute-start(bf16[96,1,4,256]{3,2,1,0:T(4,128)(2,1)} %refs_1_.1), channel_id=1, source_target_pairs={{0,2},{2,0},{1,3},{3,1},{4,6},{6,4},{5,7},{7,5},{8,10},{10,8},{9,1... | collective-permute-start | bytes 589832 | tf_op jit(solution)/shard_map/ppermute | solution.py:106
  2.8 5.7 %collective-permute-start = (bf16[96,1024]{1,0:T(8,128)(2,1)S(1)}, bf16[96,1024]{1,0:T(8,128)(2,1)S(1)}, u32[]{:S(2)}, u32[]{:S(2)}) collective-permute-start(bf16[96,1024]{1,0:T(8,128)(2,1)S(1)} %get-tuple-element.19.refs_0_.refs_1_), channel_id=1, source_target_pairs={{0,2},{2,0},{1,3},{3,1},{4,6},{6,4},{5,7},{7,5},{8,10},{10,8},{9,1... | collective-permute-start | bytes 589832 | tf_op jit(solution)/shard_map/ppermute | solution.py:106
  2.9 12.9 %collective-permute-start.2 = (bf16[96,1024]{1,0:T(8,128)(2,1)S(1)}, bf16[96,1024]{1,0:T(8,128)(2,1)S(1)}, u32[]{:S(2)}, u32[]{:S(2)}) collective-permute-start(bf16[96,1024]{1,0:T(8,128)(2,1)S(1)} %get-tuple-element.19.refs_0_.refs_1_), channel_id=1, source_target_pairs={{0,4},{4,0},{8,12},{12,8},{1,5},{5,1},{9,13},{13,9},{2,6},{6,2},{1... | collective-permute-start | bytes 589832 | tf_op jit(solution)/shard_map/ppermute | solution.py:432
  5.9 11.3 %collective-permute-start.4 = (bf16[96,1024]{1,0:T(8,128)(2,1)S(1)}, bf16[96,1024]{1,0:T(8,128)(2,1)S(1)}, u32[]{:S(2)}, u32[]{:S(2)}) collective-permute-start(bf16[96,1024]{1,0:T(8,128)(2,1)S(1)} %get-tuple-element.19.refs_0_.refs_1_), channel_id=1, source_target_pairs={{0,8},{4,12},{8,0},{12,4},{1,9},{5,13},{9,1},{13,5},{2,10},{6,14},... | collective-permute-start | bytes 589832 | tf_op jit(solution)/shard_map/ppermute | solution.py:432
  10.5 8.2 %collective-permute-start.8 = (bf16[336,384]{1,0:T(8,128)(2,1)S(1)}, bf16[336,384]{1,0:T(8,128)(2,1)S(1)}, u32[]{:S(2)}, u32[]{:S(2)}) collective-permute-start(bf16[336,384]{1,0:T(8,128)(2,1)S(1)} %get-tuple-element.24.refs_3_.refs_0_), channel_id=1, source_target_pairs={{0,1},{1,0},{2,3},{3,2},{4,5},{5,4},{6,7},{7,6},{8,9},{9,8},{10,11... | collective-permute-start | bytes 774152 | tf_op jit(solution)/shard_map/ppermute | solution.py:106
  15.3 12.1 %collective-permute-start.7 = (bf16[2,96,1024]{2,1,0:T(8,128)(2,1)S(1)}, bf16[2,96,1024]{2,1,0:T(8,128)(2,1)S(1)}, u32[]{:S(2)}, u32[]{:S(2)}) collective-permute-start(bf16[2,96,1024]{2,1,0:T(8,128)(2,1)S(1)} %get-tuple-element.27), channel_id=1, source_target_pairs={{0,4},{4,0},{8,12},{12,8},{1,5},{5,1},{9,13},{13,9},{2,6},{6,2},{1... | collective-permute-start | bytes 1179656 | tf_op jit(solution)/shard_map/ppermute | solution.py:432
  15.8 2.9 %collective-permute-start.3 = (bf16[96,1024]{1,0:T(8,128)(2,1)S(1)}, bf16[96,1024]{1,0:T(8,128)(2,1)S(1)}, u32[]{:S(2)}, u32[]{:S(2)}) collective-permute-start(bf16[96,1024]{1,0:T(8,128)(2,1)S(1)} %hand_on.2.refs_1_.refs_3_), channel_id=1, source_target_pairs={{0,2},{2,0},{1,3},{3,1},{4,6},{6,4},{5,7},{7,5},{8,10},{10,8},{9,1... | collective-permute-start | bytes 589832 | tf_op jit(solution)/shard_map/ppermute | solution.py:106
  17.2 4.6 %collective-permute-start.5 = (bf16[96,1024]{1,0:T(8,128)(2,1)S(1)}, bf16[96,1024]{1,0:T(8,128)(2,1)S(1)}, u32[]{:S(2)}, u32[]{:S(2)}) collective-permute-start(bf16[96,1024]{1,0:T(8,128)(2,1)S(1)} %hand_on.3.refs_4_.refs_1_.refs_5_), channel_id=1, source_target_pairs={{0,2},{2,0},{1,3},{3,1},{4,6},{6,4},{5,7},{7,5},{8,10},{10,8},{9,1... | collective-permute-start | bytes 589832 | tf_op jit(solution)/shard_map/ppermute | solution.py:106
  17.2 14.7 %collective-permute-start.6 = (bf16[96,1024]{1,0:T(8,128)(2,1)S(1)}, bf16[96,1024]{1,0:T(8,128)(2,1)S(1)}, u32[]{:S(2)}, u32[]{:S(2)}) collective-permute-start(bf16[96,1024]{1,0:T(8,128)(2,1)S(1)} %hand_on.3.refs_4_.refs_1_.refs_5_), channel_id=1, source_target_pairs={{0,4},{4,0},{8,12},{12,8},{1,5},{5,1},{9,13},{13,9},{2,6},{6,2},{1... | collective-permute-start | bytes 589832 | tf_op jit(solution)/shard_map/ppermute | solution.py:432
  20.1 13.4 %collective-permute-start.11 = (bf16[336,384]{1,0:T(8,128)(2,1)S(1)}, bf16[336,384]{1,0:T(8,128)(2,1)S(1)}, u32[]{:S(2)}, u32[]{:S(2)}) collective-permute-start(bf16[336,384]{1,0:T(8,128)(2,1)S(1)} %terms_1.1.refs_3_.refs_1_), channel_id=1, source_target_pairs={{0,1},{1,0},{2,3},{3,2},{4,5},{5,4},{6,7},{7,6},{8,9},{9,8},{10,11... | collective-permute-start | bytes 774152 | tf_op jit(solution)/shard_map/ppermute | solution.py:106
  23.2 12.7 %collective-permute-start.12 = (bf16[336,384]{1,0:T(8,128)(2,1)S(1)}, bf16[336,384]{1,0:T(8,128)(2,1)S(1)}, u32[]{:S(2)}, u32[]{:S(2)}) collective-permute-start(bf16[336,384]{1,0:T(8,128)(2,1)S(1)} %terms_2.1.refs_2_.refs_0_), channel_id=1, source_target_pairs={{0,1},{1,0},{2,3},{3,2},{4,5},{5,4},{6,7},{7,6},{8,9},{9,8},{10,11... | collective-permute-start | bytes 774152 | tf_op jit(solution)/shard_map/ppermute | solution.py:106
  27.5 12.6 %collective-permute-start.13 = (bf16[96,1024]{1,0:T(8,128)(2,1)S(1)}, bf16[96,1024]{1,0:T(8,128)(2,1)S(1)}, u32[]{:S(2)}, u32[]{:S(2)}) collective-permute-start(bf16[96,1024]{1,0:T(8,128)(2,1)S(1)} %carry_share.1.refs_1_), channel_id=1, source_target_pairs={{0,8},{4,12},{8,0},{12,4},{1,9},{5,13},{9,1},{13,5},{2,10},{6,14},... | collective-permute-start | bytes 589832 | tf_op jit(solution)/shard_map/ppermute | solution.py:432
  31.9 1.4 %collective-permute-start.9 = (bf16[96,512]{1,0:T(8,128)(2,1)S(1)}, bf16[96,512]{1,0:T(8,128)(2,1)S(1)}, u32[]{:S(2)}, u32[]{:S(2)}) collective-permute-start(bf16[96,512]{1,0:T(8,128)(2,1)S(1)} %get-tuple-element.29), channel_id=1, source_target_pairs={{0,2},{2,0},{1,3},{3,1},{4,6},{6,4},{5,7},{7,5},{8,10},{10,8},{9,1... | collective-permute-start | bytes 294920 | tf_op jit(solution)/shard_map/ppermute | solution.py:106
  32.0 1.4 %collective-permute-start.10 = (bf16[96,512]{1,0:T(8,128)(2,1)S(1)}, bf16[96,512]{1,0:T(8,128)(2,1)S(1)}, u32[]{:S(2)}, u32[]{:S(2)}) collective-permute-start(bf16[96,512]{1,0:T(8,128)(2,1)S(1)} %get-tuple-element.30), channel_id=1, source_target_pairs={{0,2},{2,0},{1,3},{3,1},{4,6},{6,4},{5,7},{7,5},{8,10},{10,8},{9,1... | collective-permute-start | bytes 294920 | tf_op jit(solution)/shard_map/ppermute | solution.py:106
  35.0 8.5 %collective-permute-start.15 = (bf16[336,384]{1,0:T(8,128)(2,1)S(1)}, bf16[336,384]{1,0:T(8,128)(2,1)S(1)}, u32[]{:S(2)}, u32[]{:S(2)}) collective-permute-start(bf16[336,384]{1,0:T(8,128)(2,1)S(1)} %terms_3.1.refs_9_.refs_4_.refs_1_), channel_id=1, source_target_pairs={{0,1},{1,0},{2,3},{3,2},{4,5},{5,4},{6,7},{7,6},{8,9},{9,8},{10,11... | collective-permute-start | bytes 774152 | tf_op jit(solution)/shard_map/ppermute | solution.py:106
  35.8 4.2 %copy-start = (bf16[96,1,4,256]{3,2,1,0:T(4,128)(2,1)S(1)}, bf16[96,1,4,256]{3,2,1,0:T(4,128)(2,1)}, u32[]{:S(2)}) copy-start(bf16[96,1,4,256]{3,2,1,0:T(4,128)(2,1)} %refs_0_.3) | copy-start | bytes 589828
  35.8 9.6 %collective-permute-start.14 = (bf16[672,384]{1,0:T(8,128)(2,1)S(1)}, bf16[672,384]{1,0:T(8,128)(2,1)S(1)}, u32[]{:S(2)}, u32[]{:S(2)}) collective-permute-start(bf16[672,384]{1,0:T(8,128)(2,1)S(1)} %sums_0.1.refs_5_.refs_0_), channel_id=1, source_target_pairs={{0,2},{2,0},{1,3},{3,1},{4,6},{6,4},{5,7},{7,5},{8,10},{10,8},{9,1... | collective-permute-start | bytes 1548296 | tf_op jit(solution)/shard_map/ppermute | solution.py:106
  43.7 2.0 %collective-permute-start.16 = (bf16[672,384]{1,0:T(8,128)(2,1)S(1)}, bf16[672,384]{1,0:T(8,128)(2,1)S(1)}, u32[]{:S(2)}, u32[]{:S(2)}) collective-permute-start(bf16[672,384]{1,0:T(8,128)(2,1)S(1)} %sums_2.1.refs_1_), channel_id=1, source_target_pairs={{0,2},{2,0},{1,3},{3,1},{4,6},{6,4},{5,7},{7,5},{8,10},{10,8},{9,1... | collective-permute-start | bytes 1548296 | tf_op jit(solution)/shard_map/ppermute | solution.py:106

commit v8 on v7

--- a/solution.py
+++ b/solution.py
@@ -15,7 +15,7 @@
 VMEM_LIMIT = 24 * 1024 * 1024
 TOKEN = (8, 128)
 FEATURE_COST = 3 * 10**9
-FAR_COST = 6 * 10**8
+FAR_COST = 10**9
 NEAR_COST = 3 * 10**9
 
 
@@ -267,7 +267,7 @@
     block_terms(pixels, k, stack, here, there, out, rhs)
 
 
-def share_kernel(pixels, weights, flat, mine, own, kept, sent, window, other, total):
+def share_kernel(pixels, weights, flat, mine, own, kept, near, passed, window, other, total):
     rows, length = own.shape
     frames, half = length // pixels, mine.shape[0]
     count = weights.shape[1] // rows
@@ -304,25 +304,23 @@
 
     own[...] = part(0)
     kept[...] = part(2)
-    sent[0] = part(1).astype(BF16)
-    sent[1] = part(3).astype(BF16)
-
-
-def split_kernel(block, out, first, second):
+    near[...] = part(1).astype(BF16)
+    passed[...] = part(3).astype(BF16)
+
+
+def pack_kernel(block, share, out, message):
     out[...] = block[...]
-    middle = block.shape[1] // 2
-    first[...] = block[:, :middle]
-    second[...] = block[:, middle:]
-
-
-def join_kernel(first, second, out):
-    middle = out.shape[1] // 2
-    out[:, :middle] = first[...]
-    out[:, middle:] = second[...]
+    message[0] = block[...]
+    message[1] = share[...]
+
+
+def unpack_kernel(message, block, share):
+    block[...] = message[0]
+    share[...] = message[1]
 
 
 def add_kernel(kept, came, out):
-    out[...] = (kept[...] + came[1].astype(F32)).astype(out.dtype)
+    out[...] = (kept[...] + came[...].astype(F32)).astype(out.dtype)
 
 
 def conv_kernel(pixels, weights, *refs):
@@ -361,7 +359,7 @@
 def feature_kernel(pixels, features, own, first, second, out, token):
     token[...] = jnp.zeros(TOKEN, F32)
     frames = features.shape[2]
-    total = own[...] + first[0].astype(F32) + second[...].astype(F32)
+    total = own[...] + first[...].astype(F32) + second[...].astype(F32)
     v = features[:, 0].astype(F32)
     s = 1.0 / (1.0 + jnp.exp(-v))
     slope = s * (1.0 + v * (1.0 - s))
@@ -481,16 +479,17 @@
         got.append(rotate(term, "dp", 1))
         return term
 
-    own_share, kept, sent = run(
+    own_share, kept, near_share, passed_share = run(
         functools.partial(share_kernel, pixels),
         (weights, flat, stack),
         waits=(own_term,),
         out_shape=(
             sds((rows, length), F32),
             sds((rows, length), F32),
-            sds((2, rows, length), BF16),
+            block_shape,
+            block_shape,
         ),
-        out_specs=(whole(),) * 3,
+        out_specs=(whole(),) * 4,
         scratch_shapes=[
             pltpu.VMEM((half, (frames + 2) * pixels), BF16),
             pltpu.VMEM((half, (frames + 2) * pixels), BF16),
@@ -498,37 +497,36 @@
         ],
         name="shares",
     )
-    first_share = swap(sent, 1)
+    first_share = swap(near_share, 1)
     near = after(near, own_share, flops=NEAR_COST)
-    far = after(far, own_share, flops=FAR_COST)
-    last = swap(far, 1)
+    far, message = run(
+        pack_kernel,
+        (far, passed_share),
+        out_shape=(block_shape, sds((2, rows, length), BF16)),
+        out_specs=(whole(),) * 2,
+        cost_estimate=cost(FAR_COST),
+        name="pack",
+    )
+    message = swap(message, 1)
     term = terms_of(1, near, rotate(near, "tm", 1), (own_share, far, got[0]))
     term = terms_of(2, far, rotate(far, "tm", 1), (term,))
+    last, passed_share = run(
+        unpack_kernel,
+        (message,),
+        waits=(term, got[1]),
+        out_shape=(block_shape, block_shape),
+        out_specs=(whole(),) * 2,
+        name="unpack",
+    )
     carry = run(
         add_kernel,
-        (kept, first_share),
-        waits=(term,),
+        (kept, passed_share),
         out_shape=block_shape,
         out_specs=whole(),
         name="carry_share",
     )
     second_share = swap(carry, 2)
-    last, *parts = run(
-        split_kernel,
-        (last,),
-        waits=(carry,),
-        out_shape=(block_shape,) + (sds((rows, length // 2), BF16),) * 2,
-        out_specs=(whole(),) * 3,
-        name="split",
-    )
-    last_other = run(
-        join_kernel,
-        [rotate(part, "tm", 1) for part in parts],
-        out_shape=block_shape,
-        out_specs=whole(),
-        name="join",
-    )
-    term = terms_of(3, last, last_other, (got[1],))
+    term = terms_of(3, last, rotate(last, "tm", 1), (carry,))
 
     def sums(first, stop, waits=()):
         return run(

time: 47.6 us -> 46.3 us (0.973)
  waiting for transfers between devices: 12.6 us -> 8.83 us
  starting transfers between devices: 13.8 us -> 16.3 us
    ppermute x5, waiting for transfers between devices: 9.31 us -> 7.13 us  [swap(): return lax.ppermute(x, 'chan', [(z, z ^ far) for z in range(count)])]
    ppermute x5, starting transfers between devices: 8 us -> 10.1 us  [swap(): return lax.ppermute(x, 'chan', [(z, z ^ far) for z in range(count)])]
    ppermute x12 -> x11, waiting for transfers between devices: 3.32 us -> 1.7 us  [rotate(): return lax.ppermute(x, axis, [(i, (i + by) % size) for i in range(size)])]
    ppermute x12 -> x11, starting transfers between devices: 5.77 us -> 6.2 us  [rotate(): return lax.ppermute(x, axis, [(i, (i + by) % size) for i in range(size)])]
  transfers between devices with their start and end apart: 17 -> 16, of which waited for: 7 -> 5; matrix products, arithmetic and copies ran while one was open for 0% -> 0% of each run, Pallas kernels for 39% -> 40%
where the time goes in v8:
time: 46.3 us; the launch traced here: 46.2 us
  Pallas kernels  20.1 us (43%)
  starting transfers between devices  16.3 us (35%)
  waiting for transfers between devices  8.83 us (19%)
  between operations  0.95 us (2%)
    pallas_call x15, Pallas kernels, run(): pl.pallas_call(body, compiler_params=pltpu.CompilerParams(vmem_limit_byte...  20.1 us
    ppermute x5, starting transfers between devices, swap(): return lax.ppermute(x, 'chan', [(z, z ^ far) for z in range(count)])  10.1 us
    ppermute x5, waiting for transfers between devices, swap(): return lax.ppermute(x, 'chan', [(z, z ^ far) for z in range(count)])  7.13 us
    ppermute x11, starting transfers between devices, rotate(): return lax.ppermute(x, axis, [(i, (i + by) % size) for i in range(size)])  6.2 us
    ppermute x11, waiting for transfers between devices, rotate(): return lax.ppermute(x, axis, [(i, (i + by) % size) for i in range(size)])  1.7 us
  transfers between devices with their start and end apart: 16, of which 5 were waited for; matrix products, arithmetic and copies ran while one was open for 0% of the time, Pallas kernels for 40%

profile of v8, /device:TPU:0, one launch (start us, length us, event | category | flops | bytes accessed | tf_op | source)
XLA Modules:
  0.0 46.2 jit_solution(11391737789334726392)
XLA Ops:
  0.6 0.5 %collective-permute-start.1 = (bf16[96,1,4,256]{3,2,1,0:T(4,128)(2,1)}, bf16[96,1,4,256]{3,2,1,0:T(4,128)(2,1)S(1)}, u32[]{:S(2)}, u32[]{:S(2)}) collective-permute-start(bf16[96,1,4,256]{3,2,1,0:T(4,128)(2,1)} %refs_1_.1), channel_id=1, source_target_pairs={{0,2},{2,0},{1,3},{3,1},{4,6},{6,4},{5,7},{7,5},{8,10},{10,8},{9,1... | collective-permute-start | bytes 589832 | tf_op jit(solution)/shard_map/ppermute | solution.py:106
  1.1 1.6 %activate.1 = (bf16[96,1024]{1,0:T(8,128)(2,1)S(1)}, f32[96,1024]{1,0:T(8,128)S(1)}) custom-call(bf16[96,1,4,256]{3,2,1,0:T(4,128)(2,1)} %refs_0_.3, bf16[96,1,4,256]{3,2,1,0:T(4,128)(2,1)} %refs_1_.1), custom_call_target="tpu_custom_call" | custom-call | flops 1 | bytes 1 | tf_op jit(solution)/shard_map/activate/pallas_call | solution.py:145
  2.8 0.1 collective-permute-start
  2.9 3.0 %collective-permute-start.2 = (bf16[96,1024]{1,0:T(8,128)(2,1)S(1)}, bf16[96,1024]{1,0:T(8,128)(2,1)S(1)}, u32[]{:S(2)}, u32[]{:S(2)}) collective-permute-start(bf16[96,1024]{1,0:T(8,128)(2,1)S(1)} %get-tuple-element.21.refs_0_.refs_1_), channel_id=1, source_target_pairs={{0,4},{4,0},{8,12},{12,8},{1,5},{5,1},{9,13},{13,9},{2,6},{6,2},{1... | collective-permute-start | bytes 589832 | tf_op jit(solution)/shard_map/ppermute | solution.py:430
  5.9 2.6 %collective-permute-start.4 = (bf16[96,1024]{1,0:T(8,128)(2,1)S(1)}, bf16[96,1024]{1,0:T(8,128)(2,1)S(1)}, u32[]{:S(2)}, u32[]{:S(2)}) collective-permute-start(bf16[96,1024]{1,0:T(8,128)(2,1)S(1)} %get-tuple-element.21.refs_0_.refs_1_), channel_id=1, source_target_pairs={{0,8},{4,12},{8,0},{12,4},{1,9},{5,13},{9,1},{13,5},{2,10},{6,14},... | collective-permute-start | bytes 589832 | tf_op jit(solution)/shard_map/ppermute | solution.py:430
  8.5 0.0 collective-permute-done.1.refs_3_
  8.5 0.0 collective-permute-done.refs_1_.refs_2_
  8.5 2.0 %own_terms.1 = (bf16[336,384]{1,0:T(8,128)(2,1)S(1)}, bf16[432,2048]{1,0:T(8,128)(2,1)S(1)}, f32[96,2048]{1,0:T(8,128)S(1)}, bf16[2592,384]{1,0:T(8,128)(2,1)S(1)}) custom-call(bf16[96,1024]{1,0:T(8,128)(2,1)S(1)} %get-tuple-element.21.refs_0_.refs_1_, bf16[96,1024]{1,0:T(8,128)(2,1)S(1)} %collective-permute-done.refs_1_.refs_2_, ...), custom_call_target="tpu_custom_call" | custom-call | flops 1 | bytes 1 | tf_op jit(solution)/shard_map/own_terms/pallas_call | solution.py:145
  10.5 1.6 %collective-permute-start.7 = (bf16[336,384]{1,0:T(8,128)(2,1)S(1)}, bf16[336,384]{1,0:T(8,128)(2,1)S(1)}, u32[]{:S(2)}, u32[]{:S(2)}) collective-permute-start(bf16[336,384]{1,0:T(8,128)(2,1)S(1)} %get-tuple-element.26.refs_3_.refs_0_), channel_id=1, source_target_pairs={{0,1},{1,0},{2,3},{3,2},{4,5},{5,4},{6,7},{7,6},{8,9},{9,8},{10,11... | collective-permute-start | bytes 774152 | tf_op jit(solution)/shard_map/ppermute | solution.py:106
  12.1 3.2 %shares.1 = (f32[96,1024]{1,0:T(8,128)S(1)}, f32[96,1024]{1,0:T(8,128)S(1)}, bf16[96,1024]{1,0:T(8,128)(2,1)S(1)}, bf16[96,1024]{1,0:T(8,128)(2,1)S(1)}) custom-call(bf16[2592,384]{1,0:T(8,128)(2,1)S(1)} %get-tuple-element.23.refs_0_, f32[96,2048]{1,0:T(8,128)S(1)} %get-tuple-element.24.refs_1_, bf16[432,2048]{1,0:T(8,128)(2,1)S(1)} %get-tuple-element.25.refs_2_.refs_0_, ...), custom_call_target="tpu_custom_call" | custom-call | flops 1 | bytes 1 | tf_op jit(solution)/shard_map/shares/pallas_call | solution.py:145
  15.3 0.0 collective-permute-done.2.refs_0_
  15.3 0.1 collective-permute-start.3
  15.4 2.3 %collective-permute-done.4.refs_0_ = bf16[96,1024]{1,0:T(8,128)(2,1)S(1)} collective-permute-done((bf16[96,1024]{1,0:T(8,128)(2,1)S(1)}, bf16[96,1024]{1,0:T(8,128)(2,1)S(1)}, u32[]{:S(2)}, u32[]{:S(2)}) %collective-permute-start.4) | collective-permute-done | bytes 196640 | tf_op jit(solution)/shard_map/ppermute | solution.py:430
  17.7 0.5 %collective-permute-start.6 = (bf16[2,96,1024]{2,1,0:T(8,128)(2,1)S(1)}, bf16[2,96,1024]{2,1,0:T(8,128)(2,1)S(1)}, u32[]{:S(2)}, u32[]{:S(2)}) collective-permute-start(bf16[2,96,1024]{2,1,0:T(8,128)(2,1)S(1)} %get-tuple-element.30), channel_id=1, source_target_pairs={{0,4},{4,0},{8,12},{12,8},{1,5},{5,1},{9,13},{13,9},{2,6},{6,2},{1... | collective-permute-start | bytes 1179656 | tf_op jit(solution)/shard_map/ppermute | solution.py:430
  18.3 0.0 collective-permute-done.3.refs_2_.refs_4_
  18.3 0.0 collective-permute-done.7.refs_5_.refs_2_
  18.3 1.3 %terms_1.1.refs_3_.refs_1_ = bf16[336,384]{1,0:T(8,128)(2,1)S(1)} custom-call(bf16[432,2048]{1,0:T(8,128)(2,1)S(1)} %get-tuple-element.25.refs_2_.refs_0_, bf16[96,1024]{1,0:T(8,128)(2,1)S(1)} %hand_on.1.refs_1_.refs_3_, bf16[96,1024]{1,0:T(8,128)(2,1)S(1)} %collective-permute-done.3.refs_2_.refs_4_, f32[96,1024]{1,0:T(8,128)S(1)} %get-tuple-element.27.refs_1_.refs_3_, ...), custom_call_target="tpu_custom_call" | custom-call | flops 1 | bytes 1 | tf_op jit(solution)/shard_map/terms_1/pallas_call | solution.py:145
  19.6 1.6 %collective-permute-start.8 = (bf16[336,384]{1,0:T(8,128)(2,1)S(1)}, bf16[336,384]{1,0:T(8,128)(2,1)S(1)}, u32[]{:S(2)}, u32[]{:S(2)}) collective-permute-start(bf16[336,384]{1,0:T(8,128)(2,1)S(1)} %terms_1.1.refs_3_.refs_1_), channel_id=1, source_target_pairs={{0,1},{1,0},{2,3},{3,2},{4,5},{5,4},{6,7},{7,6},{8,9},{9,8},{10,11... | collective-permute-start | bytes 774152 | tf_op jit(solution)/shard_map/ppermute | solution.py:106
  21.2 0.0 collective-permute-start.5
  21.2 1.4 %collective-permute-done.5.refs_2_.refs_6_ = bf16[96,1024]{1,0:T(8,128)(2,1)S(1)} collective-permute-done((bf16[96,1024]{1,0:T(8,128)(2,1)S(1)}, bf16[96,1024]{1,0:T(8,128)(2,1)S(1)}, u32[]{:S(2)}, u32[]{:S(2)}) %collective-permute-start.5) | collective-permute-done | bytes 196640 | tf_op jit(solution)/shard_map/ppermute | solution.py:106
  22.6 1.3 %terms_2.1.refs_1_.refs_0_ = bf16[336,384]{1,0:T(8,128)(2,1)S(1)} custom-call(bf16[432,2048]{1,0:T(8,128)(2,1)S(1)} %get-tuple-element.25.refs_2_.refs_0_, bf16[96,1024]{1,0:T(8,128)(2,1)S(1)} %get-tuple-element.29.refs_4_.refs_1_.refs_5_, bf16[96,1024]{1,0:T(8,128)(2,1)S(1)} %collective-permute-done.5.refs_2_.refs_6_, ...), custom_call_target="tpu_custom_call" | custom-call | flops 1 | bytes 1 | tf_op jit(solution)/shard_map/terms_2/pallas_call | solution.py:145
  23.9 0.6 %collective-permute-start.10 = (bf16[336,384]{1,0:T(8,128)(2,1)S(1)}, bf16[336,384]{1,0:T(8,128)(2,1)S(1)}, u32[]{:S(2)}, u32[]{:S(2)}) collective-permute-start(bf16[336,384]{1,0:T(8,128)(2,1)S(1)} %terms_2.1.refs_1_.refs_0_), channel_id=1, source_target_pairs={{0,1},{1,0},{2,3},{3,2},{4,5},{5,4},{6,7},{7,6},{8,9},{9,8},{10,11... | collective-permute-start | bytes 774152 | tf_op jit(solution)/shard_map/ppermute | solution.py:106
  24.5 2.5 %collective-permute-done.6.refs_0_ = bf16[2,96,1024]{2,1,0:T(8,128)(2,1)S(1)} collective-permute-done((bf16[2,96,1024]{2,1,0:T(8,128)(2,1)S(1)}, bf16[2,96,1024]{2,1,0:T(8,128)(2,1)S(1)}, u32[]{:S(2)}, u32[]{:S(2)}) %collective-permute-start.6) | collective-permute-done | bytes 393248 | tf_op jit(solution)/shard_map/ppermute | solution.py:430
  27.0 0.0 collective-permute-done.8.refs_2_.refs_3_
  27.1 0.1 collective-permute-start.9
  27.1 1.5 %collective-permute-start.11 = (bf16[96,1024]{1,0:T(8,128)(2,1)S(1)}, bf16[96,1024]{1,0:T(8,128)(2,1)S(1)}, u32[]{:S(2)}, u32[]{:S(2)}) collective-permute-start(bf16[96,1024]{1,0:T(8,128)(2,1)S(1)} %get-tuple-element.35), channel_id=1, source_target_pairs={{0,4},{4,0},{8,12},{12,8},{1,5},{5,1},{9,13},{13,9},{2,6},{6,2},{1... | collective-permute-start | bytes 589832 | tf_op jit(solution)/shard_map/ppermute | solution.py:430
  28.7 2.4 %collective-permute-start.12 = (bf16[96,1024]{1,0:T(8,128)(2,1)S(1)}, bf16[96,1024]{1,0:T(8,128)(2,1)S(1)}, u32[]{:S(2)}, u32[]{:S(2)}) collective-permute-start(bf16[96,1024]{1,0:T(8,128)(2,1)S(1)} %carry_share.1.refs_3_), channel_id=1, source_target_pairs={{0,8},{4,12},{8,0},{12,4},{1,9},{5,13},{9,1},{13,5},{2,10},{6,14},... | collective-permute-start | bytes 589832 | tf_op jit(solution)/shard_map/ppermute | solution.py:430
  31.1 0.0 collective-permute-done.9.refs_2_.refs_8_
  31.1 1.5 %terms_3.1.refs_9_.refs_4_.refs_1_ = bf16[336,384]{1,0:T(8,128)(2,1)S(1)} custom-call(bf16[432,2048]{1,0:T(8,128)(2,1)S(1)} %get-tuple-element.25.refs_2_.refs_0_, bf16[96,1024]{1,0:T(8,128)(2,1)S(1)} %get-tuple-element.31.refs_1_.refs_7_, bf16[96,1024]{1,0:T(8,128)(2,1)S(1)} %collective-permute-done.9.refs_2_.refs_8_, bf16[96,1024]{1,0:T(8,128)(2,1)S(1)} %carry_share.1.refs_3_), custom_call_target="tpu_custom_call" | custom-call | flops 1 | bytes 1 | tf_op jit(solution)/shard_map/terms_3/pallas_call | solution.py:145
  32.6 1.6 %collective-permute-start.14 = (bf16[336,384]{1,0:T(8,128)(2,1)S(1)}, bf16[336,384]{1,0:T(8,128)(2,1)S(1)}, u32[]{:S(2)}, u32[]{:S(2)}) collective-permute-start(bf16[336,384]{1,0:T(8,128)(2,1)S(1)} %terms_3.1.refs_9_.refs_4_.refs_1_), channel_id=1, source_target_pairs={{0,1},{1,0},{2,3},{3,2},{4,5},{5,4},{6,7},{7,6},{8,9},{9,8},{10,11... | collective-permute-start | bytes 774152 | tf_op jit(solution)/shard_map/ppermute | solution.py:106
  34.2 0.1 sums_0.1.refs_5_.refs_0_
  34.3 0.0 copy-start
  34.3 0.1 collective-permute-start.13
  34.4 0.0 collective-permute-done.10.refs_10_.refs_2_
  34.4 4.1 %conv.1 = (bf16[96,1,4,256]{3,2,1,0:T(4,128)(2,1)}, f32[8,128]{1,0:T(8,128)S(1)}) custom-call(bf16[2592,384]{1,0:T(8,128)(2,1)S(1)} %get-tuple-element.23.refs_0_, bf16[96,1024]{1,0:T(8,128)(2,1)S(1)} %get-tuple-element.21.refs_0_.refs_1_, bf16[96,1024]{1,0:T(8,128)(2,1)S(1)} %collective-permute-done.refs_1_.refs_2_, ...), custom_call_target="tpu_custom_call" | custom-call | flops 1 | bytes 1 | tf_op jit(solution)/shard_map/conv/pallas_call | solution.py:145
  38.5 0.0 collective-permute-done.11.refs_2_
  38.5 2.3 %collective-permute-done.12.refs_3_ = bf16[96,1024]{1,0:T(8,128)(2,1)S(1)} collective-permute-done((bf16[96,1024]{1,0:T(8,128)(2,1)S(1)}, bf16[96,1024]{1,0:T(8,128)(2,1)S(1)}, u32[]{:S(2)}, u32[]{:S(2)}) %collective-permute-start.12) | collective-permute-done | bytes 196640 | tf_op jit(solution)/shard_map/ppermute | solution.py:430
  40.9 0.0 copy-done
  40.9 1.4 %feature_grad.1 = (bf16[96,1,4,256]{3,2,1,0:T(4,128)(2,1)}, f32[8,128]{1,0:T(8,128)S(1)}) custom-call(bf16[96,1,4,256]{3,2,1,0:T(4,128)(2,1)S(1)} %copy-done, f32[96,1024]{1,0:T(8,128)S(1)} %get-tuple-element.27.refs_1_.refs_3_, bf16[96,1024]{1,0:T(8,128)(2,1)S(1)} %collective-permute-done.11.refs_2_, bf16[96,1024]{1,0:T(8,128)(2,1)S(1)} %collective-permute-done.12.refs_3_, ...), custom_call_target="tpu_custom_call" | custom-call | flops 3000000000 | bytes 1 | tf_op jit(solution)/shard_map/feature_grad/pallas_call | solution.py:145
  42.3 0.0 collective-permute-done.14.refs_3_
  42.3 0.1 sums_2.1.refs_1_
  42.4 0.1 collective-permute-start.15
  42.5 1.6 %kernel_grad_0.1.refs_2_ = f32[3,864,384]{2,1,0:T(8,128)} custom-call(bf16[672,384]{1,0:T(8,128)(2,1)S(1)} %sums_0.1.refs_5_.refs_0_, bf16[672,384]{1,0:T(8,128)(2,1)S(1)} %sums_2.1.refs_1_), custom_call_target="tpu_custom_call" | custom-call | flops 1 | bytes 1 | tf_op jit(solution)/shard_map/kernel_grad_0/pallas_call | solution.py:145
  44.1 0.0 collective-permute-done.13.refs_0_
  44.2 0.2 collective-permute-done.15.refs_1_
  44.4 1.6 %kernel_grad_1.1 = f32[3,864,384]{2,1,0:T(8,128)} custom-call(bf16[672,384]{1,0:T(8,128)(2,1)S(1)} %collective-permute-done.13.refs_0_, bf16[672,384]{1,0:T(8,128)(2,1)S(1)} %collective-permute-done.15.refs_1_, f32[3,864,384]{2,1,0:T(8,128)} %kernel_grad_0.1.refs_2_), custom_call_target="tpu_custom_call", output_to_operand_aliasing={{}: (2, {})} | custom-call | flops 1 | bytes 1 | tf_op jit(solution)/shard_map/kernel_grad_1/pallas_call | solution.py:145
  (4 shorter events, 0.1 us)
Async XLA Ops:
  0.6 7.9 %collective-permute-start.1 = (bf16[96,1,4,256]{3,2,1,0:T(4,128)(2,1)}, bf16[96,1,4,256]{3,2,1,0:T(4,128)(2,1)S(1)}, u32[]{:S(2)}, u32[]{:S(2)}) collective-permute-start(bf16[96,1,4,256]{3,2,1,0:T(4,128)(2,1)} %refs_1_.1), channel_id=1, source_target_pairs={{0,2},{2,0},{1,3},{3,1},{4,6},{6,4},{5,7},{7,5},{8,10},{10,8},{9,1... | collective-permute-start | bytes 589832 | tf_op jit(solution)/shard_map/ppermute | solution.py:106
  2.8 5.7 %collective-permute-start = (bf16[96,1024]{1,0:T(8,128)(2,1)S(1)}, bf16[96,1024]{1,0:T(8,128)(2,1)S(1)}, u32[]{:S(2)}, u32[]{:S(2)}) collective-permute-start(bf16[96,1024]{1,0:T(8,128)(2,1)S(1)} %get-tuple-element.21.refs_0_.refs_1_), channel_id=1, source_target_pairs={{0,2},{2,0},{1,3},{3,1},{4,6},{6,4},{5,7},{7,5},{8,10},{10,8},{9,1... | collective-permute-start | bytes 589832 | tf_op jit(solution)/shard_map/ppermute | solution.py:106
  2.9 12.4 %collective-permute-start.2 = (bf16[96,1024]{1,0:T(8,128)(2,1)S(1)}, bf16[96,1024]{1,0:T(8,128)(2,1)S(1)}, u32[]{:S(2)}, u32[]{:S(2)}) collective-permute-start(bf16[96,1024]{1,0:T(8,128)(2,1)S(1)} %get-tuple-element.21.refs_0_.refs_1_), channel_id=1, source_target_pairs={{0,4},{4,0},{8,12},{12,8},{1,5},{5,1},{9,13},{13,9},{2,6},{6,2},{1... | collective-permute-start | bytes 589832 | tf_op jit(solution)/shard_map/ppermute | solution.py:430
  5.9 11.8 %collective-permute-start.4 = (bf16[96,1024]{1,0:T(8,128)(2,1)S(1)}, bf16[96,1024]{1,0:T(8,128)(2,1)S(1)}, u32[]{:S(2)}, u32[]{:S(2)}) collective-permute-start(bf16[96,1024]{1,0:T(8,128)(2,1)S(1)} %get-tuple-element.21.refs_0_.refs_1_), channel_id=1, source_target_pairs={{0,8},{4,12},{8,0},{12,4},{1,9},{5,13},{9,1},{13,5},{2,10},{6,14},... | collective-permute-start | bytes 589832 | tf_op jit(solution)/shard_map/ppermute | solution.py:430
  10.5 7.7 %collective-permute-start.7 = (bf16[336,384]{1,0:T(8,128)(2,1)S(1)}, bf16[336,384]{1,0:T(8,128)(2,1)S(1)}, u32[]{:S(2)}, u32[]{:S(2)}) collective-permute-start(bf16[336,384]{1,0:T(8,128)(2,1)S(1)} %get-tuple-element.26.refs_3_.refs_0_), channel_id=1, source_target_pairs={{0,1},{1,0},{2,3},{3,2},{4,5},{5,4},{6,7},{7,6},{8,9},{9,8},{10,11... | collective-permute-start | bytes 774152 | tf_op jit(solution)/shard_map/ppermute | solution.py:106
  15.3 2.9 %collective-permute-start.3 = (bf16[96,1024]{1,0:T(8,128)(2,1)S(1)}, bf16[96,1024]{1,0:T(8,128)(2,1)S(1)}, u32[]{:S(2)}, u32[]{:S(2)}) collective-permute-start(bf16[96,1024]{1,0:T(8,128)(2,1)S(1)} %hand_on.1.refs_1_.refs_3_), channel_id=1, source_target_pairs={{0,2},{2,0},{1,3},{3,1},{4,6},{6,4},{5,7},{7,5},{8,10},{10,8},{9,1... | collective-permute-start | bytes 589832 | tf_op jit(solution)/shard_map/ppermute | solution.py:106
  17.7 9.3 %collective-permute-start.6 = (bf16[2,96,1024]{2,1,0:T(8,128)(2,1)S(1)}, bf16[2,96,1024]{2,1,0:T(8,128)(2,1)S(1)}, u32[]{:S(2)}, u32[]{:S(2)}) collective-permute-start(bf16[2,96,1024]{2,1,0:T(8,128)(2,1)S(1)} %get-tuple-element.30), channel_id=1, source_target_pairs={{0,4},{4,0},{8,12},{12,8},{1,5},{5,1},{9,13},{13,9},{2,6},{6,2},{1... | collective-permute-start | bytes 1179656 | tf_op jit(solution)/shard_map/ppermute | solution.py:430
  19.6 7.4 %collective-permute-start.8 = (bf16[336,384]{1,0:T(8,128)(2,1)S(1)}, bf16[336,384]{1,0:T(8,128)(2,1)S(1)}, u32[]{:S(2)}, u32[]{:S(2)}) collective-permute-start(bf16[336,384]{1,0:T(8,128)(2,1)S(1)} %terms_1.1.refs_3_.refs_1_), channel_id=1, source_target_pairs={{0,1},{1,0},{2,3},{3,2},{4,5},{5,4},{6,7},{7,6},{8,9},{9,8},{10,11... | collective-permute-start | bytes 774152 | tf_op jit(solution)/shard_map/ppermute | solution.py:106
  21.2 1.4 %collective-permute-start.5 = (bf16[96,1024]{1,0:T(8,128)(2,1)S(1)}, bf16[96,1024]{1,0:T(8,128)(2,1)S(1)}, u32[]{:S(2)}, u32[]{:S(2)}) collective-permute-start(bf16[96,1024]{1,0:T(8,128)(2,1)S(1)} %get-tuple-element.29.refs_4_.refs_1_.refs_5_), channel_id=1, source_target_pairs={{0,2},{2,0},{1,3},{3,1},{4,6},{6,4},{5,7},{7,5},{8,10},{10,8},{9,1... | collective-permute-start | bytes 589832 | tf_op jit(solution)/shard_map/ppermute | solution.py:106
  23.9 10.5 %collective-permute-start.10 = (bf16[336,384]{1,0:T(8,128)(2,1)S(1)}, bf16[336,384]{1,0:T(8,128)(2,1)S(1)}, u32[]{:S(2)}, u32[]{:S(2)}) collective-permute-start(bf16[336,384]{1,0:T(8,128)(2,1)S(1)} %terms_2.1.refs_1_.refs_0_), channel_id=1, source_target_pairs={{0,1},{1,0},{2,3},{3,2},{4,5},{5,4},{6,7},{7,6},{8,9},{9,8},{10,11... | collective-permute-start | bytes 774152 | tf_op jit(solution)/shard_map/ppermute | solution.py:106
  27.1 4.1 %collective-permute-start.9 = (bf16[96,1024]{1,0:T(8,128)(2,1)S(1)}, bf16[96,1024]{1,0:T(8,128)(2,1)S(1)}, u32[]{:S(2)}, u32[]{:S(2)}) collective-permute-start(bf16[96,1024]{1,0:T(8,128)(2,1)S(1)} %get-tuple-element.31.refs_1_.refs_7_), channel_id=1, source_target_pairs={{0,2},{2,0},{1,3},{3,1},{4,6},{6,4},{5,7},{7,5},{8,10},{10,8},{9,1... | collective-permute-start | bytes 589832 | tf_op jit(solution)/shard_map/ppermute | solution.py:106
  27.1 11.4 %collective-permute-start.11 = (bf16[96,1024]{1,0:T(8,128)(2,1)S(1)}, bf16[96,1024]{1,0:T(8,128)(2,1)S(1)}, u32[]{:S(2)}, u32[]{:S(2)}) collective-permute-start(bf16[96,1024]{1,0:T(8,128)(2,1)S(1)} %get-tuple-element.35), channel_id=1, source_target_pairs={{0,4},{4,0},{8,12},{12,8},{1,5},{5,1},{9,13},{13,9},{2,6},{6,2},{1... | collective-permute-start | bytes 589832 | tf_op jit(solution)/shard_map/ppermute | solution.py:430
  28.7 12.2 %collective-permute-start.12 = (bf16[96,1024]{1,0:T(8,128)(2,1)S(1)}, bf16[96,1024]{1,0:T(8,128)(2,1)S(1)}, u32[]{:S(2)}, u32[]{:S(2)}) collective-permute-start(bf16[96,1024]{1,0:T(8,128)(2,1)S(1)} %carry_share.1.refs_3_), channel_id=1, source_target_pairs={{0,8},{4,12},{8,0},{12,4},{1,9},{5,13},{9,1},{13,5},{2,10},{6,14},... | collective-permute-start | bytes 589832 | tf_op jit(solution)/shard_map/ppermute | solution.py:430
  32.6 9.7 %collective-permute-start.14 = (bf16[336,384]{1,0:T(8,128)(2,1)S(1)}, bf16[336,384]{1,0:T(8,128)(2,1)S(1)}, u32[]{:S(2)}, u32[]{:S(2)}) collective-permute-start(bf16[336,384]{1,0:T(8,128)(2,1)S(1)} %terms_3.1.refs_9_.refs_4_.refs_1_), channel_id=1, source_target_pairs={{0,1},{1,0},{2,3},{3,2},{4,5},{5,4},{6,7},{7,6},{8,9},{9,8},{10,11... | collective-permute-start | bytes 774152 | tf_op jit(solution)/shard_map/ppermute | solution.py:106
  34.3 6.5 %copy-start = (bf16[96,1,4,256]{3,2,1,0:T(4,128)(2,1)S(1)}, bf16[96,1,4,256]{3,2,1,0:T(4,128)(2,1)}, u32[]{:S(2)}) copy-start(bf16[96,1,4,256]{3,2,1,0:T(4,128)(2,1)} %refs_0_.3) | copy-start | bytes 589828
  34.3 9.8 %collective-permute-start.13 = (bf16[672,384]{1,0:T(8,128)(2,1)S(1)}, bf16[672,384]{1,0:T(8,128)(2,1)S(1)}, u32[]{:S(2)}, u32[]{:S(2)}) collective-permute-start(bf16[672,384]{1,0:T(8,128)(2,1)S(1)} %sums_0.1.refs_5_.refs_0_), channel_id=1, source_target_pairs={{0,2},{2,0},{1,3},{3,1},{4,6},{6,4},{5,7},{7,5},{8,10},{10,8},{9,1... | collective-permute-start | bytes 1548296 | tf_op jit(solution)/shard_map/ppermute | solution.py:106
  42.4 2.0 %collective-permute-start.15 = (bf16[672,384]{1,0:T(8,128)(2,1)S(1)}, bf16[672,384]{1,0:T(8,128)(2,1)S(1)}, u32[]{:S(2)}, u32[]{:S(2)}) collective-permute-start(bf16[672,384]{1,0:T(8,128)(2,1)S(1)} %sums_2.1.refs_1_), channel_id=1, source_target_pairs={{0,2},{2,0},{1,3},{3,1},{4,6},{6,4},{5,7},{7,5},{8,10},{10,8},{9,1... | collective-permute-start | bytes 1548296 | tf_op jit(solution)/shard_map/ppermute | solution.py:106

commit v9 on v8

--- a/solution.py
+++ b/solution.py
@@ -356,16 +356,19 @@
         out[:, 0, t, :] = acc.astype(BF16)
 
 
-def feature_kernel(pixels, features, own, first, second, out, token):
-    token[...] = jnp.zeros(TOKEN, F32)
-    frames = features.shape[2]
-    total = own[...] + first[...].astype(F32) + second[...].astype(F32)
+def slope_kernel(pixels, features, slope):
     v = features[:, 0].astype(F32)
     s = 1.0 / (1.0 + jnp.exp(-v))
-    slope = s * (1.0 + v * (1.0 - s))
-    for t in range(frames):
-        piece = total[:, t * pixels : (t + 1) * pixels] * slope[:, t, :]
-        out[:, 0, t, :] = piece.astype(BF16)
+    factor = s * (1.0 + v * (1.0 - s))
+    for t in range(factor.shape[1]):
+        slope[:, t * pixels : (t + 1) * pixels] = factor[:, t, :]
+
+
+def feature_kernel(pixels, slope, own, first, second, out, token):
+    token[...] = jnp.zeros(TOKEN, F32)
+    total = (own[...] + first[...].astype(F32) + second[...].astype(F32)) * slope[...]
+    for t in range(out.shape[2]):
+        out[:, 0, t, :] = total[:, t * pixels : (t + 1) * pixels].astype(BF16)
 
 
 def sum_kernel(main, *refs):
@@ -394,10 +397,10 @@
             total = None
             for k, shard in enumerate(shards):
                 source, place = (early, k) if k < first else (late, k - first)
-                piece = source[place * main + base : place * main + base + unit, :].astype(F32)
+                piece = source[place * main + base : place * main + base + unit, :]
                 mask = in_slot(channels, rows, lax.rem(shard + step, count))
                 total = piece if total is None else jnp.where(mask, piece, total)
-            total = total * scale
+            total = total.astype(F32) * scale
             if step:
                 total = pltpu.roll(total, channels - step * rows, 1)
             laid[a, q * unit : (q + 1) * unit, :] = total
@@ -510,10 +513,18 @@
     message = swap(message, 1)
     term = terms_of(1, near, rotate(near, "tm", 1), (own_share, far, got[0]))
     term = terms_of(2, far, rotate(far, "tm", 1), (term,))
+    slope = run(
+        functools.partial(slope_kernel, pixels),
+        (features,),
+        waits=(term,),
+        out_shape=sds((rows, length), F32),
+        out_specs=whole(),
+        name="slope",
+    )
     last, passed_share = run(
         unpack_kernel,
         (message,),
-        waits=(term, got[1]),
+        waits=(slope, got[1]),
         out_shape=(block_shape, block_shape),
         out_specs=(whole(),) * 2,
         name="unpack",
@@ -550,7 +561,7 @@
     early = sums(0, 2, (term,))
     feature_grad, token = run(
         functools.partial(feature_kernel, pixels),
-        (features, own_share, first_share, second_share),
+        (slope, own_share, first_share, second_share),
         waits=(token, early),
         out_shape=(sds(features.shape, BF16), sds(TOKEN, F32)),
         out_specs=(whole(),) * 2,

time: 46.3 us -> 45.9 us (level)
    pallas_call x15 -> x16, Pallas kernels: 20.1 us -> 19.9 us  [run(): pl.pallas_call(body, compiler_params=pltpu.CompilerParams(vmem_limit_byte...]
where the time goes in v9:
time: 45.9 us; the launch traced here: 45.8 us
  Pallas kernels  19.9 us (43%)
  starting transfers between devices  16.3 us (36%)
  waiting for transfers between devices  8.68 us (19%)
  between operations  0.95 us (2%)
    pallas_call x16, Pallas kernels, run(): pl.pallas_call(body, compiler_params=pltpu.CompilerParams(vmem_limit_byte...  19.9 us
    ppermute x5, starting transfers between devices, swap(): return lax.ppermute(x, 'chan', [(z, z ^ far) for z in range(count)])  10.1 us
    ppermute x5, waiting for transfers between devices, swap(): return lax.ppermute(x, 'chan', [(z, z ^ far) for z in range(count)])  6.86 us
    ppermute x11, starting transfers between devices, rotate(): return lax.ppermute(x, axis, [(i, (i + by) % size) for i in range(size)])  6.19 us
    ppermute x11, waiting for transfers between devices, rotate(): return lax.ppermute(x, axis, [(i, (i + by) % size) for i in range(size)])  1.82 us
  transfers between devices with their start and end apart: 16, of which 5 were waited for; matrix products, arithmetic and copies ran while one was open for 0% of the time, Pallas kernels for 40%

profile of v9, /device:TPU:0, one launch (start us, length us, event | category | flops | bytes accessed | tf_op | source)
XLA Modules:
  0.0 45.8 jit_solution(14008469216290008076)
XLA Ops:
  0.6 0.5 %collective-permute-start.1 = (bf16[96,1,4,256]{3,2,1,0:T(4,128)(2,1)}, bf16[96,1,4,256]{3,2,1,0:T(4,128)(2,1)S(1)}, u32[]{:S(2)}, u32[]{:S(2)}) collective-permute-start(bf16[96,1,4,256]{3,2,1,0:T(4,128)(2,1)} %refs_1_.1), channel_id=1, source_target_pairs={{0,2},{2,0},{1,3},{3,1},{4,6},{6,4},{5,7},{7,5},{8,10},{10,8},{9,1... | collective-permute-start | bytes 589832 | tf_op jit(solution)/shard_map/ppermute | solution.py:106
  1.1 1.6 %activate.1 = (bf16[96,1024]{1,0:T(8,128)(2,1)S(1)}, f32[96,1024]{1,0:T(8,128)S(1)}) custom-call(bf16[96,1,4,256]{3,2,1,0:T(4,128)(2,1)} %refs_0_.3, bf16[96,1,4,256]{3,2,1,0:T(4,128)(2,1)} %refs_1_.1), custom_call_target="tpu_custom_call" | custom-call | flops 1 | bytes 1 | tf_op jit(solution)/shard_map/activate/pallas_call | solution.py:145
  2.8 0.1 collective-permute-start
  2.9 3.0 %collective-permute-start.2 = (bf16[96,1024]{1,0:T(8,128)(2,1)S(1)}, bf16[96,1024]{1,0:T(8,128)(2,1)S(1)}, u32[]{:S(2)}, u32[]{:S(2)}) collective-permute-start(bf16[96,1024]{1,0:T(8,128)(2,1)S(1)} %get-tuple-element.21.refs_0_.refs_1_), channel_id=1, source_target_pairs={{0,4},{4,0},{8,12},{12,8},{1,5},{5,1},{9,13},{13,9},{2,6},{6,2},{1... | collective-permute-start | bytes 589832 | tf_op jit(solution)/shard_map/ppermute | solution.py:433
  5.9 2.6 %collective-permute-start.4 = (bf16[96,1024]{1,0:T(8,128)(2,1)S(1)}, bf16[96,1024]{1,0:T(8,128)(2,1)S(1)}, u32[]{:S(2)}, u32[]{:S(2)}) collective-permute-start(bf16[96,1024]{1,0:T(8,128)(2,1)S(1)} %get-tuple-element.21.refs_0_.refs_1_), channel_id=1, source_target_pairs={{0,8},{4,12},{8,0},{12,4},{1,9},{5,13},{9,1},{13,5},{2,10},{6,14},... | collective-permute-start | bytes 589832 | tf_op jit(solution)/shard_map/ppermute | solution.py:433
  8.5 0.0 collective-permute-done.1.refs_3_
  8.5 0.0 collective-permute-done.refs_1_.refs_2_
  8.5 2.0 %own_terms.1 = (bf16[336,384]{1,0:T(8,128)(2,1)S(1)}, bf16[432,2048]{1,0:T(8,128)(2,1)S(1)}, f32[96,2048]{1,0:T(8,128)S(1)}, bf16[2592,384]{1,0:T(8,128)(2,1)S(1)}) custom-call(bf16[96,1024]{1,0:T(8,128)(2,1)S(1)} %get-tuple-element.21.refs_0_.refs_1_, bf16[96,1024]{1,0:T(8,128)(2,1)S(1)} %collective-permute-done.refs_1_.refs_2_, ...), custom_call_target="tpu_custom_call" | custom-call | flops 1 | bytes 1 | tf_op jit(solution)/shard_map/own_terms/pallas_call | solution.py:145
  10.5 1.6 %collective-permute-start.7 = (bf16[336,384]{1,0:T(8,128)(2,1)S(1)}, bf16[336,384]{1,0:T(8,128)(2,1)S(1)}, u32[]{:S(2)}, u32[]{:S(2)}) collective-permute-start(bf16[336,384]{1,0:T(8,128)(2,1)S(1)} %get-tuple-element.26.refs_3_.refs_0_), channel_id=1, source_target_pairs={{0,1},{1,0},{2,3},{3,2},{4,5},{5,4},{6,7},{7,6},{8,9},{9,8},{10,11... | collective-permute-start | bytes 774152 | tf_op jit(solution)/shard_map/ppermute | solution.py:106
  12.1 3.2 %shares.1 = (f32[96,1024]{1,0:T(8,128)S(1)}, f32[96,1024]{1,0:T(8,128)S(1)}, bf16[96,1024]{1,0:T(8,128)(2,1)S(1)}, bf16[96,1024]{1,0:T(8,128)(2,1)S(1)}) custom-call(bf16[2592,384]{1,0:T(8,128)(2,1)S(1)} %get-tuple-element.23.refs_0_, f32[96,2048]{1,0:T(8,128)S(1)} %get-tuple-element.24.refs_1_, bf16[432,2048]{1,0:T(8,128)(2,1)S(1)} %get-tuple-element.25.refs_2_.refs_0_, ...), custom_call_target="tpu_custom_call" | custom-call | flops 1 | bytes 1 | tf_op jit(solution)/shard_map/shares/pallas_call | solution.py:145
  15.3 0.0 collective-permute-done.2.refs_0_
  15.3 0.1 collective-permute-start.3
  15.4 2.3 %collective-permute-done.4.refs_0_ = bf16[96,1024]{1,0:T(8,128)(2,1)S(1)} collective-permute-done((bf16[96,1024]{1,0:T(8,128)(2,1)S(1)}, bf16[96,1024]{1,0:T(8,128)(2,1)S(1)}, u32[]{:S(2)}, u32[]{:S(2)}) %collective-permute-start.4) | collective-permute-done | bytes 196640 | tf_op jit(solution)/shard_map/ppermute | solution.py:433
  17.7 0.5 %collective-permute-start.6 = (bf16[2,96,1024]{2,1,0:T(8,128)(2,1)S(1)}, bf16[2,96,1024]{2,1,0:T(8,128)(2,1)S(1)}, u32[]{:S(2)}, u32[]{:S(2)}) collective-permute-start(bf16[2,96,1024]{2,1,0:T(8,128)(2,1)S(1)} %get-tuple-element.30), channel_id=1, source_target_pairs={{0,4},{4,0},{8,12},{12,8},{1,5},{5,1},{9,13},{13,9},{2,6},{6,2},{1... | collective-permute-start | bytes 1179656 | tf_op jit(solution)/shard_map/ppermute | solution.py:433
  18.3 0.0 collective-permute-done.3.refs_2_.refs_4_
  18.3 0.0 collective-permute-done.7.refs_5_.refs_2_
  18.3 1.3 %terms_1.1.refs_3_.refs_1_ = bf16[336,384]{1,0:T(8,128)(2,1)S(1)} custom-call(bf16[432,2048]{1,0:T(8,128)(2,1)S(1)} %get-tuple-element.25.refs_2_.refs_0_, bf16[96,1024]{1,0:T(8,128)(2,1)S(1)} %hand_on.1.refs_1_.refs_3_, bf16[96,1024]{1,0:T(8,128)(2,1)S(1)} %collective-permute-done.3.refs_2_.refs_4_, f32[96,1024]{1,0:T(8,128)S(1)} %get-tuple-element.27.refs_1_.refs_3_, ...), custom_call_target="tpu_custom_call" | custom-call | flops 1 | bytes 1 | tf_op jit(solution)/shard_map/terms_1/pallas_call | solution.py:145
  19.6 0.0 copy-start
  19.6 1.6 %collective-permute-start.8 = (bf16[336,384]{1,0:T(8,128)(2,1)S(1)}, bf16[336,384]{1,0:T(8,128)(2,1)S(1)}, u32[]{:S(2)}, u32[]{:S(2)}) collective-permute-start(bf16[336,384]{1,0:T(8,128)(2,1)S(1)} %terms_1.1.refs_3_.refs_1_), channel_id=1, source_target_pairs={{0,1},{1,0},{2,3},{3,2},{4,5},{5,4},{6,7},{7,6},{8,9},{9,8},{10,11... | collective-permute-start | bytes 774152 | tf_op jit(solution)/shard_map/ppermute | solution.py:106
  21.2 0.0 collective-permute-start.5
  21.2 1.4 %collective-permute-done.5.refs_2_.refs_6_ = bf16[96,1024]{1,0:T(8,128)(2,1)S(1)} collective-permute-done((bf16[96,1024]{1,0:T(8,128)(2,1)S(1)}, bf16[96,1024]{1,0:T(8,128)(2,1)S(1)}, u32[]{:S(2)}, u32[]{:S(2)}) %collective-permute-start.5) | collective-permute-done | bytes 196640 | tf_op jit(solution)/shard_map/ppermute | solution.py:106
  22.6 1.3 %terms_2.1.refs_1_.refs_0_ = bf16[336,384]{1,0:T(8,128)(2,1)S(1)} custom-call(bf16[432,2048]{1,0:T(8,128)(2,1)S(1)} %get-tuple-element.25.refs_2_.refs_0_, bf16[96,1024]{1,0:T(8,128)(2,1)S(1)} %get-tuple-element.29.refs_4_.refs_1_.refs_5_, bf16[96,1024]{1,0:T(8,128)(2,1)S(1)} %collective-permute-done.5.refs_2_.refs_6_, ...), custom_call_target="tpu_custom_call" | custom-call | flops 1 | bytes 1 | tf_op jit(solution)/shard_map/terms_2/pallas_call | solution.py:145
  24.0 0.6 %collective-permute-start.10 = (bf16[336,384]{1,0:T(8,128)(2,1)S(1)}, bf16[336,384]{1,0:T(8,128)(2,1)S(1)}, u32[]{:S(2)}, u32[]{:S(2)}) collective-permute-start(bf16[336,384]{1,0:T(8,128)(2,1)S(1)} %terms_2.1.refs_1_.refs_0_), channel_id=1, source_target_pairs={{0,1},{1,0},{2,3},{3,2},{4,5},{5,4},{6,7},{7,6},{8,9},{9,8},{10,11... | collective-permute-start | bytes 774152 | tf_op jit(solution)/shard_map/ppermute | solution.py:106
  24.6 0.0 copy-done
  24.6 0.3 slope.1.refs_1_.refs_0_
  24.8 2.2 %collective-permute-done.6.refs_0_ = bf16[2,96,1024]{2,1,0:T(8,128)(2,1)S(1)} collective-permute-done((bf16[2,96,1024]{2,1,0:T(8,128)(2,1)S(1)}, bf16[2,96,1024]{2,1,0:T(8,128)(2,1)S(1)}, u32[]{:S(2)}, u32[]{:S(2)}) %collective-permute-start.6) | collective-permute-done | bytes 393248 | tf_op jit(solution)/shard_map/ppermute | solution.py:433
  27.0 0.0 collective-permute-done.8.refs_2_.refs_3_
  27.1 0.1 collective-permute-start.9
  27.1 1.5 %collective-permute-start.11 = (bf16[96,1024]{1,0:T(8,128)(2,1)S(1)}, bf16[96,1024]{1,0:T(8,128)(2,1)S(1)}, u32[]{:S(2)}, u32[]{:S(2)}) collective-permute-start(bf16[96,1024]{1,0:T(8,128)(2,1)S(1)} %get-tuple-element.35), channel_id=1, source_target_pairs={{0,4},{4,0},{8,12},{12,8},{1,5},{5,1},{9,13},{13,9},{2,6},{6,2},{1... | collective-permute-start | bytes 589832 | tf_op jit(solution)/shard_map/ppermute | solution.py:433
  28.7 2.4 %collective-permute-start.12 = (bf16[96,1024]{1,0:T(8,128)(2,1)S(1)}, bf16[96,1024]{1,0:T(8,128)(2,1)S(1)}, u32[]{:S(2)}, u32[]{:S(2)}) collective-permute-start(bf16[96,1024]{1,0:T(8,128)(2,1)S(1)} %carry_share.1.refs_3_), channel_id=1, source_target_pairs={{0,8},{4,12},{8,0},{12,4},{1,9},{5,13},{9,1},{13,5},{2,10},{6,14},... | collective-permute-start | bytes 589832 | tf_op jit(solution)/shard_map/ppermute | solution.py:433
  31.1 0.0 collective-permute-done.9.refs_2_.refs_8_
  31.1 1.5 %terms_3.1.refs_9_.refs_4_.refs_1_ = bf16[336,384]{1,0:T(8,128)(2,1)S(1)} custom-call(bf16[432,2048]{1,0:T(8,128)(2,1)S(1)} %get-tuple-element.25.refs_2_.refs_0_, bf16[96,1024]{1,0:T(8,128)(2,1)S(1)} %get-tuple-element.31.refs_1_.refs_7_, bf16[96,1024]{1,0:T(8,128)(2,1)S(1)} %collective-permute-done.9.refs_2_.refs_8_, bf16[96,1024]{1,0:T(8,128)(2,1)S(1)} %carry_share.1.refs_3_), custom_call_target="tpu_custom_call" | custom-call | flops 1 | bytes 1 | tf_op jit(solution)/shard_map/terms_3/pallas_call | solution.py:145
  32.6 1.6 %collective-permute-start.14 = (bf16[336,384]{1,0:T(8,128)(2,1)S(1)}, bf16[336,384]{1,0:T(8,128)(2,1)S(1)}, u32[]{:S(2)}, u32[]{:S(2)}) collective-permute-start(bf16[336,384]{1,0:T(8,128)(2,1)S(1)} %terms_3.1.refs_9_.refs_4_.refs_1_), channel_id=1, source_target_pairs={{0,1},{1,0},{2,3},{3,2},{4,5},{5,4},{6,7},{7,6},{8,9},{9,8},{10,11... | collective-permute-start | bytes 774152 | tf_op jit(solution)/shard_map/ppermute | solution.py:106
  34.2 0.1 sums_0.1.refs_5_.refs_0_
  34.3 0.1 collective-permute-start.13
  34.4 0.0 collective-permute-done.10.refs_10_.refs_2_
  34.4 4.1 %conv.1 = (bf16[96,1,4,256]{3,2,1,0:T(4,128)(2,1)}, f32[8,128]{1,0:T(8,128)S(1)}) custom-call(bf16[2592,384]{1,0:T(8,128)(2,1)S(1)} %get-tuple-element.23.refs_0_, bf16[96,1024]{1,0:T(8,128)(2,1)S(1)} %get-tuple-element.21.refs_0_.refs_1_, bf16[96,1024]{1,0:T(8,128)(2,1)S(1)} %collective-permute-done.refs_1_.refs_2_, ...), custom_call_target="tpu_custom_call" | custom-call | flops 1 | bytes 1 | tf_op jit(solution)/shard_map/conv/pallas_call | solution.py:145
  38.5 0.0 collective-permute-done.11.refs_2_
  38.5 2.4 %collective-permute-done.12.refs_3_ = bf16[96,1024]{1,0:T(8,128)(2,1)S(1)} collective-permute-done((bf16[96,1024]{1,0:T(8,128)(2,1)S(1)}, bf16[96,1024]{1,0:T(8,128)(2,1)S(1)}, u32[]{:S(2)}, u32[]{:S(2)}) %collective-permute-start.12) | collective-permute-done | bytes 196640 | tf_op jit(solution)/shard_map/ppermute | solution.py:433
  40.9 1.1 %feature_grad.1 = (bf16[96,1,4,256]{3,2,1,0:T(4,128)(2,1)}, f32[8,128]{1,0:T(8,128)S(1)}) custom-call(f32[96,1024]{1,0:T(8,128)S(1)} %slope.1.refs_1_.refs_0_, f32[96,1024]{1,0:T(8,128)S(1)} %get-tuple-element.27.refs_1_.refs_3_, bf16[96,1024]{1,0:T(8,128)(2,1)S(1)} %collective-permute-done.11.refs_2_, bf16[96,1024]{1,0:T(8,128)(2,1)S(1)} %collective-permute-done.12.refs_3_, ...), custom_call_target="tpu_custom_call" | custom-call | flops 3000000000 | bytes 1 | tf_op jit(solution)/shard_map/feature_grad/pallas_call | solution.py:145
  42.0 0.0 collective-permute-done.14.refs_3_
  42.0 0.1 sums_2.1.refs_1_
  42.2 0.1 collective-permute-start.15
  42.2 1.5 %kernel_grad_0.1.refs_2_ = f32[3,864,384]{2,1,0:T(8,128)} custom-call(bf16[672,384]{1,0:T(8,128)(2,1)S(1)} %sums_0.1.refs_5_.refs_0_, bf16[672,384]{1,0:T(8,128)(2,1)S(1)} %sums_2.1.refs_1_), custom_call_target="tpu_custom_call" | custom-call | flops 1 | bytes 1 | tf_op jit(solution)/shard_map/kernel_grad_0/pallas_call | solution.py:145
  43.7 0.0 collective-permute-done.13.refs_0_
  43.8 0.4 collective-permute-done.15.refs_1_
  44.1 1.5 %kernel_grad_1.1 = f32[3,864,384]{2,1,0:T(8,128)} custom-call(bf16[672,384]{1,0:T(8,128)(2,1)S(1)} %collective-permute-done.13.refs_0_, bf16[672,384]{1,0:T(8,128)(2,1)S(1)} %collective-permute-done.15.refs_1_, f32[3,864,384]{2,1,0:T(8,128)} %kernel_grad_0.1.refs_2_), custom_call_target="tpu_custom_call", output_to_operand_aliasing={{}: (2, {})} | custom-call | flops 1 | bytes 1 | tf_op jit(solution)/shard_map/kernel_grad_1/pallas_call | solution.py:145
  (4 shorter events, 0.1 us)
Async XLA Ops:
  0.6 7.9 %collective-permute-start.1 = (bf16[96,1,4,256]{3,2,1,0:T(4,128)(2,1)}, bf16[96,1,4,256]{3,2,1,0:T(4,128)(2,1)S(1)}, u32[]{:S(2)}, u32[]{:S(2)}) collective-permute-start(bf16[96,1,4,256]{3,2,1,0:T(4,128)(2,1)} %refs_1_.1), channel_id=1, source_target_pairs={{0,2},{2,0},{1,3},{3,1},{4,6},{6,4},{5,7},{7,5},{8,10},{10,8},{9,1... | collective-permute-start | bytes 589832 | tf_op jit(solution)/shard_map/ppermute | solution.py:106
  2.8 5.7 %collective-permute-start = (bf16[96,1024]{1,0:T(8,128)(2,1)S(1)}, bf16[96,1024]{1,0:T(8,128)(2,1)S(1)}, u32[]{:S(2)}, u32[]{:S(2)}) collective-permute-start(bf16[96,1024]{1,0:T(8,128)(2,1)S(1)} %get-tuple-element.21.refs_0_.refs_1_), channel_id=1, source_target_pairs={{0,2},{2,0},{1,3},{3,1},{4,6},{6,4},{5,7},{7,5},{8,10},{10,8},{9,1... | collective-permute-start | bytes 589832 | tf_op jit(solution)/shard_map/ppermute | solution.py:106
  2.9 12.4 %collective-permute-start.2 = (bf16[96,1024]{1,0:T(8,128)(2,1)S(1)}, bf16[96,1024]{1,0:T(8,128)(2,1)S(1)}, u32[]{:S(2)}, u32[]{:S(2)}) collective-permute-start(bf16[96,1024]{1,0:T(8,128)(2,1)S(1)} %get-tuple-element.21.refs_0_.refs_1_), channel_id=1, source_target_pairs={{0,4},{4,0},{8,12},{12,8},{1,5},{5,1},{9,13},{13,9},{2,6},{6,2},{1... | collective-permute-start | bytes 589832 | tf_op jit(solution)/shard_map/ppermute | solution.py:433
  5.9 11.8 %collective-permute-start.4 = (bf16[96,1024]{1,0:T(8,128)(2,1)S(1)}, bf16[96,1024]{1,0:T(8,128)(2,1)S(1)}, u32[]{:S(2)}, u32[]{:S(2)}) collective-permute-start(bf16[96,1024]{1,0:T(8,128)(2,1)S(1)} %get-tuple-element.21.refs_0_.refs_1_), channel_id=1, source_target_pairs={{0,8},{4,12},{8,0},{12,4},{1,9},{5,13},{9,1},{13,5},{2,10},{6,14},... | collective-permute-start | bytes 589832 | tf_op jit(solution)/shard_map/ppermute | solution.py:433
  10.5 7.7 %collective-permute-start.7 = (bf16[336,384]{1,0:T(8,128)(2,1)S(1)}, bf16[336,384]{1,0:T(8,128)(2,1)S(1)}, u32[]{:S(2)}, u32[]{:S(2)}) collective-permute-start(bf16[336,384]{1,0:T(8,128)(2,1)S(1)} %get-tuple-element.26.refs_3_.refs_0_), channel_id=1, source_target_pairs={{0,1},{1,0},{2,3},{3,2},{4,5},{5,4},{6,7},{7,6},{8,9},{9,8},{10,11... | collective-permute-start | bytes 774152 | tf_op jit(solution)/shard_map/ppermute | solution.py:106
  15.3 2.9 %collective-permute-start.3 = (bf16[96,1024]{1,0:T(8,128)(2,1)S(1)}, bf16[96,1024]{1,0:T(8,128)(2,1)S(1)}, u32[]{:S(2)}, u32[]{:S(2)}) collective-permute-start(bf16[96,1024]{1,0:T(8,128)(2,1)S(1)} %hand_on.1.refs_1_.refs_3_), channel_id=1, source_target_pairs={{0,2},{2,0},{1,3},{3,1},{4,6},{6,4},{5,7},{7,5},{8,10},{10,8},{9,1... | collective-permute-start | bytes 589832 | tf_op jit(solution)/shard_map/ppermute | solution.py:106
  17.7 9.3 %collective-permute-start.6 = (bf16[2,96,1024]{2,1,0:T(8,128)(2,1)S(1)}, bf16[2,96,1024]{2,1,0:T(8,128)(2,1)S(1)}, u32[]{:S(2)}, u32[]{:S(2)}) collective-permute-start(bf16[2,96,1024]{2,1,0:T(8,128)(2,1)S(1)} %get-tuple-element.30), channel_id=1, source_target_pairs={{0,4},{4,0},{8,12},{12,8},{1,5},{5,1},{9,13},{13,9},{2,6},{6,2},{1... | collective-permute-start | bytes 1179656 | tf_op jit(solution)/shard_map/ppermute | solution.py:433
  19.6 5.0 %copy-start = (bf16[96,1,4,256]{3,2,1,0:T(4,128)(2,1)S(1)}, bf16[96,1,4,256]{3,2,1,0:T(4,128)(2,1)}, u32[]{:S(2)}) copy-start(bf16[96,1,4,256]{3,2,1,0:T(4,128)(2,1)} %refs_0_.3) | copy-start | bytes 589828
  19.6 7.4 %collective-permute-start.8 = (bf16[336,384]{1,0:T(8,128)(2,1)S(1)}, bf16[336,384]{1,0:T(8,128)(2,1)S(1)}, u32[]{:S(2)}, u32[]{:S(2)}) collective-permute-start(bf16[336,384]{1,0:T(8,128)(2,1)S(1)} %terms_1.1.refs_3_.refs_1_), channel_id=1, source_target_pairs={{0,1},{1,0},{2,3},{3,2},{4,5},{5,4},{6,7},{7,6},{8,9},{9,8},{10,11... | collective-permute-start | bytes 774152 | tf_op jit(solution)/shard_map/ppermute | solution.py:106
  21.2 1.4 %collective-permute-start.5 = (bf16[96,1024]{1,0:T(8,128)(2,1)S(1)}, bf16[96,1024]{1,0:T(8,128)(2,1)S(1)}, u32[]{:S(2)}, u32[]{:S(2)}) collective-permute-start(bf16[96,1024]{1,0:T(8,128)(2,1)S(1)} %get-tuple-element.29.refs_4_.refs_1_.refs_5_), channel_id=1, source_target_pairs={{0,2},{2,0},{1,3},{3,1},{4,6},{6,4},{5,7},{7,5},{8,10},{10,8},{9,1... | collective-permute-start | bytes 589832 | tf_op jit(solution)/shard_map/ppermute | solution.py:106
  24.0 10.4 %collective-permute-start.10 = (bf16[336,384]{1,0:T(8,128)(2,1)S(1)}, bf16[336,384]{1,0:T(8,128)(2,1)S(1)}, u32[]{:S(2)}, u32[]{:S(2)}) collective-permute-start(bf16[336,384]{1,0:T(8,128)(2,1)S(1)} %terms_2.1.refs_1_.refs_0_), channel_id=1, source_target_pairs={{0,1},{1,0},{2,3},{3,2},{4,5},{5,4},{6,7},{7,6},{8,9},{9,8},{10,11... | collective-permute-start | bytes 774152 | tf_op jit(solution)/shard_map/ppermute | solution.py:106
  27.1 4.1 %collective-permute-start.9 = (bf16[96,1024]{1,0:T(8,128)(2,1)S(1)}, bf16[96,1024]{1,0:T(8,128)(2,1)S(1)}, u32[]{:S(2)}, u32[]{:S(2)}) collective-permute-start(bf16[96,1024]{1,0:T(8,128)(2,1)S(1)} %get-tuple-element.31.refs_1_.refs_7_), channel_id=1, source_target_pairs={{0,2},{2,0},{1,3},{3,1},{4,6},{6,4},{5,7},{7,5},{8,10},{10,8},{9,1... | collective-permute-start | bytes 589832 | tf_op jit(solution)/shard_map/ppermute | solution.py:106
  27.1 11.4 %collective-permute-start.11 = (bf16[96,1024]{1,0:T(8,128)(2,1)S(1)}, bf16[96,1024]{1,0:T(8,128)(2,1)S(1)}, u32[]{:S(2)}, u32[]{:S(2)}) collective-permute-start(bf16[96,1024]{1,0:T(8,128)(2,1)S(1)} %get-tuple-element.35), channel_id=1, source_target_pairs={{0,4},{4,0},{8,12},{12,8},{1,5},{5,1},{9,13},{13,9},{2,6},{6,2},{1... | collective-permute-start | bytes 589832 | tf_op jit(solution)/shard_map/ppermute | solution.py:433
  28.7 12.2 %collective-permute-start.12 = (bf16[96,1024]{1,0:T(8,128)(2,1)S(1)}, bf16[96,1024]{1,0:T(8,128)(2,1)S(1)}, u32[]{:S(2)}, u32[]{:S(2)}) collective-permute-start(bf16[96,1024]{1,0:T(8,128)(2,1)S(1)} %carry_share.1.refs_3_), channel_id=1, source_target_pairs={{0,8},{4,12},{8,0},{12,4},{1,9},{5,13},{9,1},{13,5},{2,10},{6,14},... | collective-permute-start | bytes 589832 | tf_op jit(solution)/shard_map/ppermute | solution.py:433
  32.6 9.4 %collective-permute-start.14 = (bf16[336,384]{1,0:T(8,128)(2,1)S(1)}, bf16[336,384]{1,0:T(8,128)(2,1)S(1)}, u32[]{:S(2)}, u32[]{:S(2)}) collective-permute-start(bf16[336,384]{1,0:T(8,128)(2,1)S(1)} %terms_3.1.refs_9_.refs_4_.refs_1_), channel_id=1, source_target_pairs={{0,1},{1,0},{2,3},{3,2},{4,5},{5,4},{6,7},{7,6},{8,9},{9,8},{10,11... | collective-permute-start | bytes 774152 | tf_op jit(solution)/shard_map/ppermute | solution.py:106
  34.3 9.4 %collective-permute-start.13 = (bf16[672,384]{1,0:T(8,128)(2,1)S(1)}, bf16[672,384]{1,0:T(8,128)(2,1)S(1)}, u32[]{:S(2)}, u32[]{:S(2)}) collective-permute-start(bf16[672,384]{1,0:T(8,128)(2,1)S(1)} %sums_0.1.refs_5_.refs_0_), channel_id=1, source_target_pairs={{0,2},{2,0},{1,3},{3,1},{4,6},{6,4},{5,7},{7,5},{8,10},{10,8},{9,1... | collective-permute-start | bytes 1548296 | tf_op jit(solution)/shard_map/ppermute | solution.py:106
  42.2 2.0 %collective-permute-start.15 = (bf16[672,384]{1,0:T(8,128)(2,1)S(1)}, bf16[672,384]{1,0:T(8,128)(2,1)S(1)}, u32[]{:S(2)}, u32[]{:S(2)}) collective-permute-start(bf16[672,384]{1,0:T(8,128)(2,1)S(1)} %sums_2.1.refs_1_), channel_id=1, source_target_pairs={{0,2},{2,0},{1,3},{3,1},{4,6},{6,4},{5,7},{7,5},{8,10},{10,8},{9,1... | collective-permute-start | bytes 1548296 | tf_op jit(solution)/shard_map/ppermute | solution.py:106

commit v10 on v9

--- a/solution.py
+++ b/solution.py
@@ -15,6 +15,7 @@
 VMEM_LIMIT = 24 * 1024 * 1024
 TOKEN = (8, 128)
 FEATURE_COST = 3 * 10**9
+GATHER_COST = 10**8
 FAR_COST = 10**9
 NEAR_COST = 3 * 10**9
 
@@ -364,11 +365,15 @@
         slope[:, t * pixels : (t + 1) * pixels] = factor[:, t, :]
 
 
-def feature_kernel(pixels, slope, own, first, second, out, token):
+def gather_share_kernel(own, second, out):
+    out[...] = own[...] + second[...].astype(F32)
+
+
+def feature_kernel(pixels, slope, gathered, first, out, token):
     token[...] = jnp.zeros(TOKEN, F32)
-    total = (own[...] + first[...].astype(F32) + second[...].astype(F32)) * slope[...]
-    for t in range(out.shape[2]):
-        out[:, 0, t, :] = total[:, t * pixels : (t + 1) * pixels].astype(BF16)
+    total = (gathered[...] + first[...].astype(F32)) * slope[...]
+    frames = [total[:, t * pixels : (t + 1) * pixels] for t in range(out.shape[2])]
+    out[:, 0] = jnp.stack(frames, axis=1).astype(BF16)
 
 
 def sum_kernel(main, *refs):
@@ -559,10 +564,18 @@
         name="conv",
     )
     early = sums(0, 2, (term,))
+    gathered = run(
+        gather_share_kernel,
+        (own_share, second_share),
+        waits=(token, early),
+        out_shape=sds((rows, length), F32),
+        out_specs=whole(),
+        cost_estimate=cost(GATHER_COST),
+        name="gather_share",
+    )
     feature_grad, token = run(
         functools.partial(feature_kernel, pixels),
-        (slope, own_share, first_share, second_share),
-        waits=(token, early),
+        (slope, gathered, first_share),
         out_shape=(sds(features.shape, BF16), sds(TOKEN, F32)),
         out_specs=(whole(),) * 2,
         cost_estimate=cost(FEATURE_COST),

time: 45.9 us -> 44.7 us (0.974)
  waiting for transfers between devices: 8.68 us -> 7.52 us
    ppermute x5, waiting for transfers between devices: 6.86 us -> 5.71 us  [swap(): return lax.ppermute(x, 'chan', [(z, z ^ far) for z in range(count)])]
    pallas_call x16 -> x17, Pallas kernels: 19.9 us -> 19.8 us  [run(): pl.pallas_call(body, compiler_params=pltpu.CompilerParams(vmem_limit_byte...]
  transfers between devices with their start and end apart: 16 -> 16, of which waited for: 5 -> 5; matrix products, arithmetic and copies ran while one was open for 0% -> 0% of each run, Pallas kernels for 40% -> 41%
where the time goes in v10:
time: 44.7 us; the launch traced here: 44.5 us
  Pallas kernels  19.8 us (44%)
  starting transfers between devices  16.2 us (36%)
  waiting for transfers between devices  7.52 us (17%)
  between operations  0.97 us (2%)
    pallas_call x17, Pallas kernels, run(): pl.pallas_call(body, compiler_params=pltpu.CompilerParams(vmem_limit_byte...  19.8 us
    ppermute x5, starting transfers between devices, swap(): return lax.ppermute(x, 'chan', [(z, z ^ far) for z in range(count)])  10 us
    ppermute x11, starting transfers between devices, rotate(): return lax.ppermute(x, axis, [(i, (i + by) % size) for i in range(size)])  6.19 us
    ppermute x5, waiting for transfers between devices, swap(): return lax.ppermute(x, 'chan', [(z, z ^ far) for z in range(count)])  5.71 us
    ppermute x11, waiting for transfers between devices, rotate(): return lax.ppermute(x, axis, [(i, (i + by) % size) for i in range(size)])  1.81 us
  transfers between devices with their start and end apart: 16, of which 5 were waited for; matrix products, arithmetic and copies ran while one was open for 0% of the time, Pallas kernels for 41%

profile of v10, /device:TPU:0, one launch (start us, length us, event | category | flops | bytes accessed | tf_op | source)
XLA Modules:
  0.0 44.5 jit_solution(16225633625810939041)
XLA Ops:
  0.6 0.5 %collective-permute-start.1 = (bf16[96,1,4,256]{3,2,1,0:T(4,128)(2,1)}, bf16[96,1,4,256]{3,2,1,0:T(4,128)(2,1)S(1)}, u32[]{:S(2)}, u32[]{:S(2)}) collective-permute-start(bf16[96,1,4,256]{3,2,1,0:T(4,128)(2,1)} %refs_1_.1), channel_id=1, source_target_pairs={{0,2},{2,0},{1,3},{3,1},{4,6},{6,4},{5,7},{7,5},{8,10},{10,8},{9,1... | collective-permute-start | bytes 589832 | tf_op jit(solution)/shard_map/ppermute | solution.py:107
  1.1 1.6 %activate.1 = (bf16[96,1024]{1,0:T(8,128)(2,1)S(1)}, f32[96,1024]{1,0:T(8,128)S(1)}) custom-call(bf16[96,1,4,256]{3,2,1,0:T(4,128)(2,1)} %refs_0_.3, bf16[96,1,4,256]{3,2,1,0:T(4,128)(2,1)} %refs_1_.1), custom_call_target="tpu_custom_call" | custom-call | flops 1 | bytes 1 | tf_op jit(solution)/shard_map/activate/pallas_call | solution.py:146
  2.8 0.1 collective-permute-start
  2.9 3.0 %collective-permute-start.2 = (bf16[96,1024]{1,0:T(8,128)(2,1)S(1)}, bf16[96,1024]{1,0:T(8,128)(2,1)S(1)}, u32[]{:S(2)}, u32[]{:S(2)}) collective-permute-start(bf16[96,1024]{1,0:T(8,128)(2,1)S(1)} %get-tuple-element.21.refs_0_.refs_1_), channel_id=1, source_target_pairs={{0,4},{4,0},{8,12},{12,8},{1,5},{5,1},{9,13},{13,9},{2,6},{6,2},{1... | collective-permute-start | bytes 589832 | tf_op jit(solution)/shard_map/ppermute | solution.py:438
  5.9 2.6 %collective-permute-start.4 = (bf16[96,1024]{1,0:T(8,128)(2,1)S(1)}, bf16[96,1024]{1,0:T(8,128)(2,1)S(1)}, u32[]{:S(2)}, u32[]{:S(2)}) collective-permute-start(bf16[96,1024]{1,0:T(8,128)(2,1)S(1)} %get-tuple-element.21.refs_0_.refs_1_), channel_id=1, source_target_pairs={{0,8},{4,12},{8,0},{12,4},{1,9},{5,13},{9,1},{13,5},{2,10},{6,14},... | collective-permute-start | bytes 589832 | tf_op jit(solution)/shard_map/ppermute | solution.py:438
  8.5 0.0 collective-permute-done.1.refs_3_
  8.5 0.0 collective-permute-done.refs_1_.refs_2_
  8.5 2.0 %own_terms.1 = (bf16[336,384]{1,0:T(8,128)(2,1)S(1)}, bf16[432,2048]{1,0:T(8,128)(2,1)S(1)}, f32[96,2048]{1,0:T(8,128)S(1)}, bf16[2592,384]{1,0:T(8,128)(2,1)S(1)}) custom-call(bf16[96,1024]{1,0:T(8,128)(2,1)S(1)} %get-tuple-element.21.refs_0_.refs_1_, bf16[96,1024]{1,0:T(8,128)(2,1)S(1)} %collective-permute-done.refs_1_.refs_2_, ...), custom_call_target="tpu_custom_call" | custom-call | flops 1 | bytes 1 | tf_op jit(solution)/shard_map/own_terms/pallas_call | solution.py:146
  10.5 1.6 %collective-permute-start.7 = (bf16[336,384]{1,0:T(8,128)(2,1)S(1)}, bf16[336,384]{1,0:T(8,128)(2,1)S(1)}, u32[]{:S(2)}, u32[]{:S(2)}) collective-permute-start(bf16[336,384]{1,0:T(8,128)(2,1)S(1)} %get-tuple-element.26.refs_3_.refs_0_), channel_id=1, source_target_pairs={{0,1},{1,0},{2,3},{3,2},{4,5},{5,4},{6,7},{7,6},{8,9},{9,8},{10,11... | collective-permute-start | bytes 774152 | tf_op jit(solution)/shard_map/ppermute | solution.py:107
  12.1 3.2 %shares.1 = (f32[96,1024]{1,0:T(8,128)S(1)}, f32[96,1024]{1,0:T(8,128)S(1)}, bf16[96,1024]{1,0:T(8,128)(2,1)S(1)}, bf16[96,1024]{1,0:T(8,128)(2,1)S(1)}) custom-call(bf16[2592,384]{1,0:T(8,128)(2,1)S(1)} %get-tuple-element.23.refs_0_, f32[96,2048]{1,0:T(8,128)S(1)} %get-tuple-element.24.refs_1_, bf16[432,2048]{1,0:T(8,128)(2,1)S(1)} %get-tuple-element.25.refs_2_.refs_0_, ...), custom_call_target="tpu_custom_call" | custom-call | flops 1 | bytes 1 | tf_op jit(solution)/shard_map/shares/pallas_call | solution.py:146
  15.3 0.0 collective-permute-done.2.refs_0_
  15.3 0.1 collective-permute-start.3
  15.4 2.3 %collective-permute-done.4.refs_0_ = bf16[96,1024]{1,0:T(8,128)(2,1)S(1)} collective-permute-done((bf16[96,1024]{1,0:T(8,128)(2,1)S(1)}, bf16[96,1024]{1,0:T(8,128)(2,1)S(1)}, u32[]{:S(2)}, u32[]{:S(2)}) %collective-permute-start.4) | collective-permute-done | bytes 196640 | tf_op jit(solution)/shard_map/ppermute | solution.py:438
  17.7 0.5 %collective-permute-start.6 = (bf16[2,96,1024]{2,1,0:T(8,128)(2,1)S(1)}, bf16[2,96,1024]{2,1,0:T(8,128)(2,1)S(1)}, u32[]{:S(2)}, u32[]{:S(2)}) collective-permute-start(bf16[2,96,1024]{2,1,0:T(8,128)(2,1)S(1)} %get-tuple-element.30), channel_id=1, source_target_pairs={{0,4},{4,0},{8,12},{12,8},{1,5},{5,1},{9,13},{13,9},{2,6},{6,2},{1... | collective-permute-start | bytes 1179656 | tf_op jit(solution)/shard_map/ppermute | solution.py:438
  18.3 0.0 collective-permute-done.3.refs_2_.refs_4_
  18.3 0.0 collective-permute-done.7.refs_5_.refs_2_
  18.3 1.3 %terms_1.1.refs_3_.refs_1_ = bf16[336,384]{1,0:T(8,128)(2,1)S(1)} custom-call(bf16[432,2048]{1,0:T(8,128)(2,1)S(1)} %get-tuple-element.25.refs_2_.refs_0_, bf16[96,1024]{1,0:T(8,128)(2,1)S(1)} %hand_on.1.refs_1_.refs_3_, bf16[96,1024]{1,0:T(8,128)(2,1)S(1)} %collective-permute-done.3.refs_2_.refs_4_, ...), custom_call_target="tpu_custom_call" | custom-call | flops 1 | bytes 1 | tf_op jit(solution)/shard_map/terms_1/pallas_call | solution.py:146
  19.6 0.0 copy-start
  19.6 1.6 %collective-permute-start.8 = (bf16[336,384]{1,0:T(8,128)(2,1)S(1)}, bf16[336,384]{1,0:T(8,128)(2,1)S(1)}, u32[]{:S(2)}, u32[]{:S(2)}) collective-permute-start(bf16[336,384]{1,0:T(8,128)(2,1)S(1)} %terms_1.1.refs_3_.refs_1_), channel_id=1, source_target_pairs={{0,1},{1,0},{2,3},{3,2},{4,5},{5,4},{6,7},{7,6},{8,9},{9,8},{10,11... | collective-permute-start | bytes 774152 | tf_op jit(solution)/shard_map/ppermute | solution.py:107
  21.2 0.0 collective-permute-start.5
  21.2 1.4 %collective-permute-done.5.refs_2_.refs_6_ = bf16[96,1024]{1,0:T(8,128)(2,1)S(1)} collective-permute-done((bf16[96,1024]{1,0:T(8,128)(2,1)S(1)}, bf16[96,1024]{1,0:T(8,128)(2,1)S(1)}, u32[]{:S(2)}, u32[]{:S(2)}) %collective-permute-start.5) | collective-permute-done | bytes 196640 | tf_op jit(solution)/shard_map/ppermute | solution.py:107
  22.6 1.3 %terms_2.1.refs_1_.refs_0_ = bf16[336,384]{1,0:T(8,128)(2,1)S(1)} custom-call(bf16[432,2048]{1,0:T(8,128)(2,1)S(1)} %get-tuple-element.25.refs_2_.refs_0_, bf16[96,1024]{1,0:T(8,128)(2,1)S(1)} %get-tuple-element.29.refs_4_.refs_1_.refs_5_, bf16[96,1024]{1,0:T(8,128)(2,1)S(1)} %collective-permute-done.5.refs_2_.refs_6_, ...), custom_call_target="tpu_custom_call" | custom-call | flops 1 | bytes 1 | tf_op jit(solution)/shard_map/terms_2/pallas_call | solution.py:146
  24.0 0.6 %collective-permute-start.10 = (bf16[336,384]{1,0:T(8,128)(2,1)S(1)}, bf16[336,384]{1,0:T(8,128)(2,1)S(1)}, u32[]{:S(2)}, u32[]{:S(2)}) collective-permute-start(bf16[336,384]{1,0:T(8,128)(2,1)S(1)} %terms_2.1.refs_1_.refs_0_), channel_id=1, source_target_pairs={{0,1},{1,0},{2,3},{3,2},{4,5},{5,4},{6,7},{7,6},{8,9},{9,8},{10,11... | collective-permute-start | bytes 774152 | tf_op jit(solution)/shard_map/ppermute | solution.py:107
  24.6 0.0 copy-done
  24.6 0.3 slope.1.refs_1_.refs_0_
  24.8 2.2 %collective-permute-done.6.refs_0_ = bf16[2,96,1024]{2,1,0:T(8,128)(2,1)S(1)} collective-permute-done((bf16[2,96,1024]{2,1,0:T(8,128)(2,1)S(1)}, bf16[2,96,1024]{2,1,0:T(8,128)(2,1)S(1)}, u32[]{:S(2)}, u32[]{:S(2)}) %collective-permute-start.6) | collective-permute-done | bytes 393248 | tf_op jit(solution)/shard_map/ppermute | solution.py:438
  27.0 0.0 collective-permute-done.8.refs_2_.refs_3_
  27.1 0.1 collective-permute-start.9
  27.2 2.1 %collective-permute-start.11 = (bf16[96,1024]{1,0:T(8,128)(2,1)S(1)}, bf16[96,1024]{1,0:T(8,128)(2,1)S(1)}, u32[]{:S(2)}, u32[]{:S(2)}) collective-permute-start(bf16[96,1024]{1,0:T(8,128)(2,1)S(1)} %carry_share.1.refs_3_), channel_id=1, source_target_pairs={{0,8},{4,12},{8,0},{12,4},{1,9},{5,13},{9,1},{13,5},{2,10},{6,14},... | collective-permute-start | bytes 589832 | tf_op jit(solution)/shard_map/ppermute | solution.py:438
  29.3 1.7 %collective-permute-start.12 = (bf16[96,1024]{1,0:T(8,128)(2,1)S(1)}, bf16[96,1024]{1,0:T(8,128)(2,1)S(1)}, u32[]{:S(2)}, u32[]{:S(2)}) collective-permute-start(bf16[96,1024]{1,0:T(8,128)(2,1)S(1)} %get-tuple-element.36), channel_id=1, source_target_pairs={{0,4},{4,0},{8,12},{12,8},{1,5},{5,1},{9,13},{13,9},{2,6},{6,2},{1... | collective-permute-start | bytes 589832 | tf_op jit(solution)/shard_map/ppermute | solution.py:438
  31.1 0.0 collective-permute-done.9.refs_2_.refs_8_
  31.1 1.5 %terms_3.1.refs_9_.refs_4_.refs_1_ = bf16[336,384]{1,0:T(8,128)(2,1)S(1)} custom-call(bf16[432,2048]{1,0:T(8,128)(2,1)S(1)} %get-tuple-element.25.refs_2_.refs_0_, bf16[96,1024]{1,0:T(8,128)(2,1)S(1)} %get-tuple-element.31.refs_1_.refs_7_, bf16[96,1024]{1,0:T(8,128)(2,1)S(1)} %collective-permute-done.9.refs_2_.refs_8_, bf16[96,1024]{1,0:T(8,128)(2,1)S(1)} %carry_share.1.refs_3_), custom_call_target="tpu_custom_call" | custom-call | flops 1 | bytes 1 | tf_op jit(solution)/shard_map/terms_3/pallas_call | solution.py:146
  32.6 1.6 %collective-permute-start.14 = (bf16[336,384]{1,0:T(8,128)(2,1)S(1)}, bf16[336,384]{1,0:T(8,128)(2,1)S(1)}, u32[]{:S(2)}, u32[]{:S(2)}) collective-permute-start(bf16[336,384]{1,0:T(8,128)(2,1)S(1)} %terms_3.1.refs_9_.refs_4_.refs_1_), channel_id=1, source_target_pairs={{0,1},{1,0},{2,3},{3,2},{4,5},{5,4},{6,7},{7,6},{8,9},{9,8},{10,11... | collective-permute-start | bytes 774152 | tf_op jit(solution)/shard_map/ppermute | solution.py:107
  34.1 0.1 sums_0.1.refs_3_.refs_0_
  34.3 0.1 collective-permute-start.13
  34.3 0.0 collective-permute-done.10.refs_10_.refs_2_
  34.4 4.1 %conv.1 = (bf16[96,1,4,256]{3,2,1,0:T(4,128)(2,1)}, f32[8,128]{1,0:T(8,128)S(1)}) custom-call(bf16[2592,384]{1,0:T(8,128)(2,1)S(1)} %get-tuple-element.23.refs_0_, bf16[96,1024]{1,0:T(8,128)(2,1)S(1)} %get-tuple-element.21.refs_0_.refs_1_, bf16[96,1024]{1,0:T(8,128)(2,1)S(1)} %collective-permute-done.refs_1_.refs_2_, ...), custom_call_target="tpu_custom_call" | custom-call | flops 1 | bytes 1 | tf_op jit(solution)/shard_map/conv/pallas_call | solution.py:146
  38.5 1.2 %collective-permute-done.11.refs_1_ = bf16[96,1024]{1,0:T(8,128)(2,1)S(1)} collective-permute-done((bf16[96,1024]{1,0:T(8,128)(2,1)S(1)}, bf16[96,1024]{1,0:T(8,128)(2,1)S(1)}, u32[]{:S(2)}, u32[]{:S(2)}) %collective-permute-start.11) | collective-permute-done | bytes 196640 | tf_op jit(solution)/shard_map/ppermute | solution.py:438
  39.7 0.0 collective-permute-done.12.refs_2_
  39.7 1.0 %feature_grad.1 = (bf16[96,1,4,256]{3,2,1,0:T(4,128)(2,1)}, f32[8,128]{1,0:T(8,128)S(1)}) custom-call(f32[96,1024]{1,0:T(8,128)S(1)} %slope.1.refs_1_.refs_0_, f32[96,1024]{1,0:T(8,128)S(1)} %gather_share.1.refs_1_, bf16[96,1024]{1,0:T(8,128)(2,1)S(1)} %collective-permute-done.12.refs_2_), custom_call_target="tpu_custom_call" | custom-call | flops 3000000000 | bytes 1 | tf_op jit(solution)/shard_map/feature_grad/pallas_call | solution.py:146
  40.7 0.0 collective-permute-done.14.refs_3_
  40.7 0.1 sums_2.1.refs_1_
  40.9 0.1 collective-permute-start.15
  40.9 1.5 %kernel_grad_0.1.refs_2_ = f32[3,864,384]{2,1,0:T(8,128)} custom-call(bf16[672,384]{1,0:T(8,128)(2,1)S(1)} %sums_0.1.refs_3_.refs_0_, bf16[672,384]{1,0:T(8,128)(2,1)S(1)} %sums_2.1.refs_1_), custom_call_target="tpu_custom_call" | custom-call | flops 1 | bytes 1 | tf_op jit(solution)/shard_map/kernel_grad_0/pallas_call | solution.py:146
  42.5 0.0 collective-permute-done.13.refs_0_
  42.5 0.3 collective-permute-done.15.refs_1_
  42.8 1.5 %kernel_grad_1.1 = f32[3,864,384]{2,1,0:T(8,128)} custom-call(bf16[672,384]{1,0:T(8,128)(2,1)S(1)} %collective-permute-done.13.refs_0_, bf16[672,384]{1,0:T(8,128)(2,1)S(1)} %collective-permute-done.15.refs_1_, f32[3,864,384]{2,1,0:T(8,128)} %kernel_grad_0.1.refs_2_), custom_call_target="tpu_custom_call", output_to_operand_aliasing={{}: (2, {})} | custom-call | flops 1 | bytes 1 | tf_op jit(solution)/shard_map/kernel_grad_1/pallas_call | solution.py:146
  (5 shorter events, 0.2 us)
Async XLA Ops:
  0.6 7.9 %collective-permute-start.1 = (bf16[96,1,4,256]{3,2,1,0:T(4,128)(2,1)}, bf16[96,1,4,256]{3,2,1,0:T(4,128)(2,1)S(1)}, u32[]{:S(2)}, u32[]{:S(2)}) collective-permute-start(bf16[96,1,4,256]{3,2,1,0:T(4,128)(2,1)} %refs_1_.1), channel_id=1, source_target_pairs={{0,2},{2,0},{1,3},{3,1},{4,6},{6,4},{5,7},{7,5},{8,10},{10,8},{9,1... | collective-permute-start | bytes 589832 | tf_op jit(solution)/shard_map/ppermute | solution.py:107
  2.8 5.7 %collective-permute-start = (bf16[96,1024]{1,0:T(8,128)(2,1)S(1)}, bf16[96,1024]{1,0:T(8,128)(2,1)S(1)}, u32[]{:S(2)}, u32[]{:S(2)}) collective-permute-start(bf16[96,1024]{1,0:T(8,128)(2,1)S(1)} %get-tuple-element.21.refs_0_.refs_1_), channel_id=1, source_target_pairs={{0,2},{2,0},{1,3},{3,1},{4,6},{6,4},{5,7},{7,5},{8,10},{10,8},{9,1... | collective-permute-start | bytes 589832 | tf_op jit(solution)/shard_map/ppermute | solution.py:107
  2.9 12.4 %collective-permute-start.2 = (bf16[96,1024]{1,0:T(8,128)(2,1)S(1)}, bf16[96,1024]{1,0:T(8,128)(2,1)S(1)}, u32[]{:S(2)}, u32[]{:S(2)}) collective-permute-start(bf16[96,1024]{1,0:T(8,128)(2,1)S(1)} %get-tuple-element.21.refs_0_.refs_1_), channel_id=1, source_target_pairs={{0,4},{4,0},{8,12},{12,8},{1,5},{5,1},{9,13},{13,9},{2,6},{6,2},{1... | collective-permute-start | bytes 589832 | tf_op jit(solution)/shard_map/ppermute | solution.py:438
  5.9 11.8 %collective-permute-start.4 = (bf16[96,1024]{1,0:T(8,128)(2,1)S(1)}, bf16[96,1024]{1,0:T(8,128)(2,1)S(1)}, u32[]{:S(2)}, u32[]{:S(2)}) collective-permute-start(bf16[96,1024]{1,0:T(8,128)(2,1)S(1)} %get-tuple-element.21.refs_0_.refs_1_), channel_id=1, source_target_pairs={{0,8},{4,12},{8,0},{12,4},{1,9},{5,13},{9,1},{13,5},{2,10},{6,14},... | collective-permute-start | bytes 589832 | tf_op jit(solution)/shard_map/ppermute | solution.py:438
  10.5 7.7 %collective-permute-start.7 = (bf16[336,384]{1,0:T(8,128)(2,1)S(1)}, bf16[336,384]{1,0:T(8,128)(2,1)S(1)}, u32[]{:S(2)}, u32[]{:S(2)}) collective-permute-start(bf16[336,384]{1,0:T(8,128)(2,1)S(1)} %get-tuple-element.26.refs_3_.refs_0_), channel_id=1, source_target_pairs={{0,1},{1,0},{2,3},{3,2},{4,5},{5,4},{6,7},{7,6},{8,9},{9,8},{10,11... | collective-permute-start | bytes 774152 | tf_op jit(solution)/shard_map/ppermute | solution.py:107
  15.3 2.9 %collective-permute-start.3 = (bf16[96,1024]{1,0:T(8,128)(2,1)S(1)}, bf16[96,1024]{1,0:T(8,128)(2,1)S(1)}, u32[]{:S(2)}, u32[]{:S(2)}) collective-permute-start(bf16[96,1024]{1,0:T(8,128)(2,1)S(1)} %hand_on.1.refs_1_.refs_3_), channel_id=1, source_target_pairs={{0,2},{2,0},{1,3},{3,1},{4,6},{6,4},{5,7},{7,5},{8,10},{10,8},{9,1... | collective-permute-start | bytes 589832 | tf_op jit(solution)/shard_map/ppermute | solution.py:107
  17.7 9.3 %collective-permute-start.6 = (bf16[2,96,1024]{2,1,0:T(8,128)(2,1)S(1)}, bf16[2,96,1024]{2,1,0:T(8,128)(2,1)S(1)}, u32[]{:S(2)}, u32[]{:S(2)}) collective-permute-start(bf16[2,96,1024]{2,1,0:T(8,128)(2,1)S(1)} %get-tuple-element.30), channel_id=1, source_target_pairs={{0,4},{4,0},{8,12},{12,8},{1,5},{5,1},{9,13},{13,9},{2,6},{6,2},{1... | collective-permute-start | bytes 1179656 | tf_op jit(solution)/shard_map/ppermute | solution.py:438
  19.6 5.0 %copy-start = (bf16[96,1,4,256]{3,2,1,0:T(4,128)(2,1)S(1)}, bf16[96,1,4,256]{3,2,1,0:T(4,128)(2,1)}, u32[]{:S(2)}) copy-start(bf16[96,1,4,256]{3,2,1,0:T(4,128)(2,1)} %refs_0_.3) | copy-start | bytes 589828
  19.6 7.4 %collective-permute-start.8 = (bf16[336,384]{1,0:T(8,128)(2,1)S(1)}, bf16[336,384]{1,0:T(8,128)(2,1)S(1)}, u32[]{:S(2)}, u32[]{:S(2)}) collective-permute-start(bf16[336,384]{1,0:T(8,128)(2,1)S(1)} %terms_1.1.refs_3_.refs_1_), channel_id=1, source_target_pairs={{0,1},{1,0},{2,3},{3,2},{4,5},{5,4},{6,7},{7,6},{8,9},{9,8},{10,11... | collective-permute-start | bytes 774152 | tf_op jit(solution)/shard_map/ppermute | solution.py:107
  21.2 1.4 %collective-permute-start.5 = (bf16[96,1024]{1,0:T(8,128)(2,1)S(1)}, bf16[96,1024]{1,0:T(8,128)(2,1)S(1)}, u32[]{:S(2)}, u32[]{:S(2)}) collective-permute-start(bf16[96,1024]{1,0:T(8,128)(2,1)S(1)} %get-tuple-element.29.refs_4_.refs_1_.refs_5_), channel_id=1, source_target_pairs={{0,2},{2,0},{1,3},{3,1},{4,6},{6,4},{5,7},{7,5},{8,10},{10,8},{9,1... | collective-permute-start | bytes 589832 | tf_op jit(solution)/shard_map/ppermute | solution.py:107
  24.0 10.4 %collective-permute-start.10 = (bf16[336,384]{1,0:T(8,128)(2,1)S(1)}, bf16[336,384]{1,0:T(8,128)(2,1)S(1)}, u32[]{:S(2)}, u32[]{:S(2)}) collective-permute-start(bf16[336,384]{1,0:T(8,128)(2,1)S(1)} %terms_2.1.refs_1_.refs_0_), channel_id=1, source_target_pairs={{0,1},{1,0},{2,3},{3,2},{4,5},{5,4},{6,7},{7,6},{8,9},{9,8},{10,11... | collective-permute-start | bytes 774152 | tf_op jit(solution)/shard_map/ppermute | solution.py:107
  27.1 4.0 %collective-permute-start.9 = (bf16[96,1024]{1,0:T(8,128)(2,1)S(1)}, bf16[96,1024]{1,0:T(8,128)(2,1)S(1)}, u32[]{:S(2)}, u32[]{:S(2)}) collective-permute-start(bf16[96,1024]{1,0:T(8,128)(2,1)S(1)} %get-tuple-element.31.refs_1_.refs_7_), channel_id=1, source_target_pairs={{0,2},{2,0},{1,3},{3,1},{4,6},{6,4},{5,7},{7,5},{8,10},{10,8},{9,1... | collective-permute-start | bytes 589832 | tf_op jit(solution)/shard_map/ppermute | solution.py:107
  27.2 12.5 %collective-permute-start.11 = (bf16[96,1024]{1,0:T(8,128)(2,1)S(1)}, bf16[96,1024]{1,0:T(8,128)(2,1)S(1)}, u32[]{:S(2)}, u32[]{:S(2)}) collective-permute-start(bf16[96,1024]{1,0:T(8,128)(2,1)S(1)} %carry_share.1.refs_3_), channel_id=1, source_target_pairs={{0,8},{4,12},{8,0},{12,4},{1,9},{5,13},{9,1},{13,5},{2,10},{6,14},... | collective-permute-start | bytes 589832 | tf_op jit(solution)/shard_map/ppermute | solution.py:438
  29.3 10.4 %collective-permute-start.12 = (bf16[96,1024]{1,0:T(8,128)(2,1)S(1)}, bf16[96,1024]{1,0:T(8,128)(2,1)S(1)}, u32[]{:S(2)}, u32[]{:S(2)}) collective-permute-start(bf16[96,1024]{1,0:T(8,128)(2,1)S(1)} %get-tuple-element.36), channel_id=1, source_target_pairs={{0,4},{4,0},{8,12},{12,8},{1,5},{5,1},{9,13},{13,9},{2,6},{6,2},{1... | collective-permute-start | bytes 589832 | tf_op jit(solution)/shard_map/ppermute | solution.py:438
  32.6 8.1 %collective-permute-start.14 = (bf16[336,384]{1,0:T(8,128)(2,1)S(1)}, bf16[336,384]{1,0:T(8,128)(2,1)S(1)}, u32[]{:S(2)}, u32[]{:S(2)}) collective-permute-start(bf16[336,384]{1,0:T(8,128)(2,1)S(1)} %terms_3.1.refs_9_.refs_4_.refs_1_), channel_id=1, source_target_pairs={{0,1},{1,0},{2,3},{3,2},{4,5},{5,4},{6,7},{7,6},{8,9},{9,8},{10,11... | collective-permute-start | bytes 774152 | tf_op jit(solution)/shard_map/ppermute | solution.py:107
  34.3 8.2 %collective-permute-start.13 = (bf16[672,384]{1,0:T(8,128)(2,1)S(1)}, bf16[672,384]{1,0:T(8,128)(2,1)S(1)}, u32[]{:S(2)}, u32[]{:S(2)}) collective-permute-start(bf16[672,384]{1,0:T(8,128)(2,1)S(1)} %sums_0.1.refs_3_.refs_0_), channel_id=1, source_target_pairs={{0,2},{2,0},{1,3},{3,1},{4,6},{6,4},{5,7},{7,5},{8,10},{10,8},{9,1... | collective-permute-start | bytes 1548296 | tf_op jit(solution)/shard_map/ppermute | solution.py:107
  40.9 2.0 %collective-permute-start.15 = (bf16[672,384]{1,0:T(8,128)(2,1)S(1)}, bf16[672,384]{1,0:T(8,128)(2,1)S(1)}, u32[]{:S(2)}, u32[]{:S(2)}) collective-permute-start(bf16[672,384]{1,0:T(8,128)(2,1)S(1)} %sums_2.1.refs_1_), channel_id=1, source_target_pairs={{0,2},{2,0},{1,3},{3,1},{4,6},{6,4},{5,7},{7,5},{8,10},{10,8},{9,1... | collective-permute-start | bytes 1548296 | tf_op jit(solution)/shard_map/ppermute | solution.py:107

commit v11 on v10

--- a/solution.py
+++ b/solution.py
@@ -392,7 +392,6 @@
     rows, half = channels // count, out.shape[1] // 2
     unit = rows // 2
     which = lax.rem(lax.axis_index("tm") + whose, 2)
-    at = pl.ds(pl.multiple_of(which * half, 8), half)
     shards = [shard_at(count, k) for k in range(count)]
     copies = []
     for a in range(3):
@@ -405,13 +404,18 @@
                 piece = source[place * main + base : place * main + base + unit, :]
                 mask = in_slot(channels, rows, lax.rem(shard + step, count))
                 total = piece if total is None else jnp.where(mask, piece, total)
-            total = total.astype(F32) * scale
             if step:
                 total = pltpu.roll(total, channels - step * rows, 1)
+            total = total.astype(F32) * scale
             laid[a, q * unit : (q + 1) * unit, :] = total
-        copy = pltpu.make_async_copy(laid.at[a], out.at[a, at], sems.at[a])
-        copy.start()
-        copies.append(copy)
+            if q % 3 == 2:
+                part = pl.ds((q - 2) * unit, 3 * unit)
+                there = pl.ds(pl.multiple_of(which * half + (q - 2) * unit, 8), 3 * unit)
+                copy = pltpu.make_async_copy(
+                    laid.at[a, part], out.at[a, there], sems.at[len(copies)]
+                )
+                copy.start()
+                copies.append(copy)
     for copy in copies:
         copy.wait()
 
@@ -593,7 +597,7 @@
             out_shape=sds((3, 9 * rows, channels), F32),
             out_specs=anywhere,
             input_output_aliases={2: 0} if base else {},
-            scratch_shapes=[pltpu.VMEM((3, half, channels), F32), pltpu.SemaphoreType.DMA((3,))],
+            scratch_shapes=[pltpu.VMEM((3, half, channels), F32), pltpu.SemaphoreType.DMA((9,))],
             name=f"kernel_grad_{whose}",
         )
 

time: 44.7 us -> 44.7 us (level)
  no operation moved by 1% of the time
where the time goes in v11:
time: 44.7 us; the launch traced here: 44.5 us
  Pallas kernels  19.8 us (44%)
  starting transfers between devices  16.2 us (36%)
  waiting for transfers between devices  7.53 us (17%)
  between operations  0.97 us (2%)
    pallas_call x17, Pallas kernels, run(): pl.pallas_call(body, compiler_params=pltpu.CompilerParams(vmem_limit_byte...  19.8 us
    ppermute x5, starting transfers between devices, swap(): return lax.ppermute(x, 'chan', [(z, z ^ far) for z in range(count)])  10 us
    ppermute x11, starting transfers between devices, rotate(): return lax.ppermute(x, axis, [(i, (i + by) % size) for i in range(size)])  6.19 us
    ppermute x5, waiting for transfers between devices, swap(): return lax.ppermute(x, 'chan', [(z, z ^ far) for z in range(count)])  5.71 us
    ppermute x11, waiting for transfers between devices, rotate(): return lax.ppermute(x, axis, [(i, (i + by) % size) for i in range(size)])  1.82 us
  transfers between devices with their start and end apart: 16, of which 5 were waited for; matrix products, arithmetic and copies ran while one was open for 0% of the time, Pallas kernels for 41%

profile of v11, /device:TPU:0, one launch (start us, length us, event | category | flops | bytes accessed | tf_op | source)
XLA Modules:
  0.0 44.5 jit_solution(5292968566345002632)
XLA Ops:
  0.6 0.5 %collective-permute-start.1 = (bf16[96,1,4,256]{3,2,1,0:T(4,128)(2,1)}, bf16[96,1,4,256]{3,2,1,0:T(4,128)(2,1)S(1)}, u32[]{:S(2)}, u32[]{:S(2)}) collective-permute-start(bf16[96,1,4,256]{3,2,1,0:T(4,128)(2,1)} %refs_1_.1), channel_id=1, source_target_pairs={{0,2},{2,0},{1,3},{3,1},{4,6},{6,4},{5,7},{7,5},{8,10},{10,8},{9,1... | collective-permute-start | bytes 589832 | tf_op jit(solution)/shard_map/ppermute | solution.py:107
  1.1 1.6 %activate.1 = (bf16[96,1024]{1,0:T(8,128)(2,1)S(1)}, f32[96,1024]{1,0:T(8,128)S(1)}) custom-call(bf16[96,1,4,256]{3,2,1,0:T(4,128)(2,1)} %refs_0_.3, bf16[96,1,4,256]{3,2,1,0:T(4,128)(2,1)} %refs_1_.1), custom_call_target="tpu_custom_call" | custom-call | flops 1 | bytes 1 | tf_op jit(solution)/shard_map/activate/pallas_call | solution.py:146
  2.8 0.1 collective-permute-start
  2.9 3.0 %collective-permute-start.2 = (bf16[96,1024]{1,0:T(8,128)(2,1)S(1)}, bf16[96,1024]{1,0:T(8,128)(2,1)S(1)}, u32[]{:S(2)}, u32[]{:S(2)}) collective-permute-start(bf16[96,1024]{1,0:T(8,128)(2,1)S(1)} %get-tuple-element.21.refs_0_.refs_1_), channel_id=1, source_target_pairs={{0,4},{4,0},{8,12},{12,8},{1,5},{5,1},{9,13},{13,9},{2,6},{6,2},{1... | collective-permute-start | bytes 589832 | tf_op jit(solution)/shard_map/ppermute | solution.py:442
  5.9 2.6 %collective-permute-start.4 = (bf16[96,1024]{1,0:T(8,128)(2,1)S(1)}, bf16[96,1024]{1,0:T(8,128)(2,1)S(1)}, u32[]{:S(2)}, u32[]{:S(2)}) collective-permute-start(bf16[96,1024]{1,0:T(8,128)(2,1)S(1)} %get-tuple-element.21.refs_0_.refs_1_), channel_id=1, source_target_pairs={{0,8},{4,12},{8,0},{12,4},{1,9},{5,13},{9,1},{13,5},{2,10},{6,14},... | collective-permute-start | bytes 589832 | tf_op jit(solution)/shard_map/ppermute | solution.py:442
  8.5 0.0 collective-permute-done.1.refs_3_
  8.5 0.0 collective-permute-done.refs_1_.refs_2_
  8.5 2.0 %own_terms.1 = (bf16[336,384]{1,0:T(8,128)(2,1)S(1)}, bf16[432,2048]{1,0:T(8,128)(2,1)S(1)}, f32[96,2048]{1,0:T(8,128)S(1)}, bf16[2592,384]{1,0:T(8,128)(2,1)S(1)}) custom-call(bf16[96,1024]{1,0:T(8,128)(2,1)S(1)} %get-tuple-element.21.refs_0_.refs_1_, bf16[96,1024]{1,0:T(8,128)(2,1)S(1)} %collective-permute-done.refs_1_.refs_2_, ...), custom_call_target="tpu_custom_call" | custom-call | flops 1 | bytes 1 | tf_op jit(solution)/shard_map/own_terms/pallas_call | solution.py:146
  10.5 1.6 %collective-permute-start.7 = (bf16[336,384]{1,0:T(8,128)(2,1)S(1)}, bf16[336,384]{1,0:T(8,128)(2,1)S(1)}, u32[]{:S(2)}, u32[]{:S(2)}) collective-permute-start(bf16[336,384]{1,0:T(8,128)(2,1)S(1)} %get-tuple-element.26.refs_3_.refs_0_), channel_id=1, source_target_pairs={{0,1},{1,0},{2,3},{3,2},{4,5},{5,4},{6,7},{7,6},{8,9},{9,8},{10,11... | collective-permute-start | bytes 774152 | tf_op jit(solution)/shard_map/ppermute | solution.py:107
  12.1 3.2 %shares.1 = (f32[96,1024]{1,0:T(8,128)S(1)}, f32[96,1024]{1,0:T(8,128)S(1)}, bf16[96,1024]{1,0:T(8,128)(2,1)S(1)}, bf16[96,1024]{1,0:T(8,128)(2,1)S(1)}) custom-call(bf16[2592,384]{1,0:T(8,128)(2,1)S(1)} %get-tuple-element.23.refs_0_, f32[96,2048]{1,0:T(8,128)S(1)} %get-tuple-element.24.refs_1_, bf16[432,2048]{1,0:T(8,128)(2,1)S(1)} %get-tuple-element.25.refs_2_.refs_0_, ...), custom_call_target="tpu_custom_call" | custom-call | flops 1 | bytes 1 | tf_op jit(solution)/shard_map/shares/pallas_call | solution.py:146
  15.3 0.0 collective-permute-done.2.refs_0_
  15.3 0.1 collective-permute-start.3
  15.4 2.3 %collective-permute-done.4.refs_0_ = bf16[96,1024]{1,0:T(8,128)(2,1)S(1)} collective-permute-done((bf16[96,1024]{1,0:T(8,128)(2,1)S(1)}, bf16[96,1024]{1,0:T(8,128)(2,1)S(1)}, u32[]{:S(2)}, u32[]{:S(2)}) %collective-permute-start.4) | collective-permute-done | bytes 196640 | tf_op jit(solution)/shard_map/ppermute | solution.py:442
  17.7 0.5 %collective-permute-start.6 = (bf16[2,96,1024]{2,1,0:T(8,128)(2,1)S(1)}, bf16[2,96,1024]{2,1,0:T(8,128)(2,1)S(1)}, u32[]{:S(2)}, u32[]{:S(2)}) collective-permute-start(bf16[2,96,1024]{2,1,0:T(8,128)(2,1)S(1)} %get-tuple-element.30), channel_id=1, source_target_pairs={{0,4},{4,0},{8,12},{12,8},{1,5},{5,1},{9,13},{13,9},{2,6},{6,2},{1... | collective-permute-start | bytes 1179656 | tf_op jit(solution)/shard_map/ppermute | solution.py:442
  18.3 0.0 collective-permute-done.3.refs_2_.refs_4_
  18.3 0.0 collective-permute-done.7.refs_5_.refs_2_
  18.3 1.3 %terms_1.1.refs_3_.refs_1_ = bf16[336,384]{1,0:T(8,128)(2,1)S(1)} custom-call(bf16[432,2048]{1,0:T(8,128)(2,1)S(1)} %get-tuple-element.25.refs_2_.refs_0_, bf16[96,1024]{1,0:T(8,128)(2,1)S(1)} %hand_on.1.refs_1_.refs_3_, bf16[96,1024]{1,0:T(8,128)(2,1)S(1)} %collective-permute-done.3.refs_2_.refs_4_, ...), custom_call_target="tpu_custom_call" | custom-call | flops 1 | bytes 1 | tf_op jit(solution)/shard_map/terms_1/pallas_call | solution.py:146
  19.6 0.0 copy-start
  19.6 1.6 %collective-permute-start.8 = (bf16[336,384]{1,0:T(8,128)(2,1)S(1)}, bf16[336,384]{1,0:T(8,128)(2,1)S(1)}, u32[]{:S(2)}, u32[]{:S(2)}) collective-permute-start(bf16[336,384]{1,0:T(8,128)(2,1)S(1)} %terms_1.1.refs_3_.refs_1_), channel_id=1, source_target_pairs={{0,1},{1,0},{2,3},{3,2},{4,5},{5,4},{6,7},{7,6},{8,9},{9,8},{10,11... | collective-permute-start | bytes 774152 | tf_op jit(solution)/shard_map/ppermute | solution.py:107
  21.2 0.0 collective-permute-start.5
  21.2 1.4 %collective-permute-done.5.refs_2_.refs_6_ = bf16[96,1024]{1,0:T(8,128)(2,1)S(1)} collective-permute-done((bf16[96,1024]{1,0:T(8,128)(2,1)S(1)}, bf16[96,1024]{1,0:T(8,128)(2,1)S(1)}, u32[]{:S(2)}, u32[]{:S(2)}) %collective-permute-start.5) | collective-permute-done | bytes 196640 | tf_op jit(solution)/shard_map/ppermute | solution.py:107
  22.6 1.3 %terms_2.1.refs_1_.refs_0_ = bf16[336,384]{1,0:T(8,128)(2,1)S(1)} custom-call(bf16[432,2048]{1,0:T(8,128)(2,1)S(1)} %get-tuple-element.25.refs_2_.refs_0_, bf16[96,1024]{1,0:T(8,128)(2,1)S(1)} %get-tuple-element.29.refs_4_.refs_1_.refs_5_, bf16[96,1024]{1,0:T(8,128)(2,1)S(1)} %collective-permute-done.5.refs_2_.refs_6_, ...), custom_call_target="tpu_custom_call" | custom-call | flops 1 | bytes 1 | tf_op jit(solution)/shard_map/terms_2/pallas_call | solution.py:146
  24.0 0.6 %collective-permute-start.10 = (bf16[336,384]{1,0:T(8,128)(2,1)S(1)}, bf16[336,384]{1,0:T(8,128)(2,1)S(1)}, u32[]{:S(2)}, u32[]{:S(2)}) collective-permute-start(bf16[336,384]{1,0:T(8,128)(2,1)S(1)} %terms_2.1.refs_1_.refs_0_), channel_id=1, source_target_pairs={{0,1},{1,0},{2,3},{3,2},{4,5},{5,4},{6,7},{7,6},{8,9},{9,8},{10,11... | collective-permute-start | bytes 774152 | tf_op jit(solution)/shard_map/ppermute | solution.py:107
  24.6 0.0 copy-done
  24.6 0.3 slope.1.refs_1_.refs_0_
  24.8 2.2 %collective-permute-done.6.refs_0_ = bf16[2,96,1024]{2,1,0:T(8,128)(2,1)S(1)} collective-permute-done((bf16[2,96,1024]{2,1,0:T(8,128)(2,1)S(1)}, bf16[2,96,1024]{2,1,0:T(8,128)(2,1)S(1)}, u32[]{:S(2)}, u32[]{:S(2)}) %collective-permute-start.6) | collective-permute-done | bytes 393248 | tf_op jit(solution)/shard_map/ppermute | solution.py:442
  27.0 0.0 collective-permute-done.8.refs_2_.refs_3_
  27.1 0.1 collective-permute-start.9
  27.2 2.1 %collective-permute-start.11 = (bf16[96,1024]{1,0:T(8,128)(2,1)S(1)}, bf16[96,1024]{1,0:T(8,128)(2,1)S(1)}, u32[]{:S(2)}, u32[]{:S(2)}) collective-permute-start(bf16[96,1024]{1,0:T(8,128)(2,1)S(1)} %carry_share.1.refs_3_), channel_id=1, source_target_pairs={{0,8},{4,12},{8,0},{12,4},{1,9},{5,13},{9,1},{13,5},{2,10},{6,14},... | collective-permute-start | bytes 589832 | tf_op jit(solution)/shard_map/ppermute | solution.py:442
  29.3 1.7 %collective-permute-start.12 = (bf16[96,1024]{1,0:T(8,128)(2,1)S(1)}, bf16[96,1024]{1,0:T(8,128)(2,1)S(1)}, u32[]{:S(2)}, u32[]{:S(2)}) collective-permute-start(bf16[96,1024]{1,0:T(8,128)(2,1)S(1)} %get-tuple-element.36), channel_id=1, source_target_pairs={{0,4},{4,0},{8,12},{12,8},{1,5},{5,1},{9,13},{13,9},{2,6},{6,2},{1... | collective-permute-start | bytes 589832 | tf_op jit(solution)/shard_map/ppermute | solution.py:442
  31.1 0.0 collective-permute-done.9.refs_2_.refs_8_
  31.1 1.5 %terms_3.1.refs_9_.refs_4_.refs_1_ = bf16[336,384]{1,0:T(8,128)(2,1)S(1)} custom-call(bf16[432,2048]{1,0:T(8,128)(2,1)S(1)} %get-tuple-element.25.refs_2_.refs_0_, bf16[96,1024]{1,0:T(8,128)(2,1)S(1)} %get-tuple-element.31.refs_1_.refs_7_, bf16[96,1024]{1,0:T(8,128)(2,1)S(1)} %collective-permute-done.9.refs_2_.refs_8_, bf16[96,1024]{1,0:T(8,128)(2,1)S(1)} %carry_share.1.refs_3_), custom_call_target="tpu_custom_call" | custom-call | flops 1 | bytes 1 | tf_op jit(solution)/shard_map/terms_3/pallas_call | solution.py:146
  32.6 1.6 %collective-permute-start.14 = (bf16[336,384]{1,0:T(8,128)(2,1)S(1)}, bf16[336,384]{1,0:T(8,128)(2,1)S(1)}, u32[]{:S(2)}, u32[]{:S(2)}) collective-permute-start(bf16[336,384]{1,0:T(8,128)(2,1)S(1)} %terms_3.1.refs_9_.refs_4_.refs_1_), channel_id=1, source_target_pairs={{0,1},{1,0},{2,3},{3,2},{4,5},{5,4},{6,7},{7,6},{8,9},{9,8},{10,11... | collective-permute-start | bytes 774152 | tf_op jit(solution)/shard_map/ppermute | solution.py:107
  34.1 0.1 sums_0.1.refs_3_.refs_0_
  34.3 0.1 collective-permute-start.13
  34.3 0.0 collective-permute-done.10.refs_10_.refs_2_
  34.4 4.1 %conv.1 = (bf16[96,1,4,256]{3,2,1,0:T(4,128)(2,1)}, f32[8,128]{1,0:T(8,128)S(1)}) custom-call(bf16[2592,384]{1,0:T(8,128)(2,1)S(1)} %get-tuple-element.23.refs_0_, bf16[96,1024]{1,0:T(8,128)(2,1)S(1)} %get-tuple-element.21.refs_0_.refs_1_, bf16[96,1024]{1,0:T(8,128)(2,1)S(1)} %collective-permute-done.refs_1_.refs_2_, ...), custom_call_target="tpu_custom_call" | custom-call | flops 1 | bytes 1 | tf_op jit(solution)/shard_map/conv/pallas_call | solution.py:146
  38.5 1.2 %collective-permute-done.11.refs_1_ = bf16[96,1024]{1,0:T(8,128)(2,1)S(1)} collective-permute-done((bf16[96,1024]{1,0:T(8,128)(2,1)S(1)}, bf16[96,1024]{1,0:T(8,128)(2,1)S(1)}, u32[]{:S(2)}, u32[]{:S(2)}) %collective-permute-start.11) | collective-permute-done | bytes 196640 | tf_op jit(solution)/shard_map/ppermute | solution.py:442
  39.7 0.0 collective-permute-done.12.refs_2_
  39.7 1.0 %feature_grad.1 = (bf16[96,1,4,256]{3,2,1,0:T(4,128)(2,1)}, f32[8,128]{1,0:T(8,128)S(1)}) custom-call(f32[96,1024]{1,0:T(8,128)S(1)} %slope.1.refs_1_.refs_0_, f32[96,1024]{1,0:T(8,128)S(1)} %gather_share.1.refs_1_, bf16[96,1024]{1,0:T(8,128)(2,1)S(1)} %collective-permute-done.12.refs_2_), custom_call_target="tpu_custom_call" | custom-call | flops 3000000000 | bytes 1 | tf_op jit(solution)/shard_map/feature_grad/pallas_call | solution.py:146
  40.7 0.0 collective-permute-done.14.refs_3_
  40.7 0.1 sums_2.1.refs_1_
  40.9 0.1 collective-permute-start.15
  40.9 1.5 %kernel_grad_0.1.refs_2_ = f32[3,864,384]{2,1,0:T(8,128)} custom-call(bf16[672,384]{1,0:T(8,128)(2,1)S(1)} %sums_0.1.refs_3_.refs_0_, bf16[672,384]{1,0:T(8,128)(2,1)S(1)} %sums_2.1.refs_1_), custom_call_target="tpu_custom_call" | custom-call | flops 1 | bytes 1 | tf_op jit(solution)/shard_map/kernel_grad_0/pallas_call | solution.py:146
  42.5 0.0 collective-permute-done.13.refs_0_
  42.5 0.4 collective-permute-done.15.refs_1_
  42.8 1.5 %kernel_grad_1.1 = f32[3,864,384]{2,1,0:T(8,128)} custom-call(bf16[672,384]{1,0:T(8,128)(2,1)S(1)} %collective-permute-done.13.refs_0_, bf16[672,384]{1,0:T(8,128)(2,1)S(1)} %collective-permute-done.15.refs_1_, f32[3,864,384]{2,1,0:T(8,128)} %kernel_grad_0.1.refs_2_), custom_call_target="tpu_custom_call", output_to_operand_aliasing={{}: (2, {})} | custom-call | flops 1 | bytes 1 | tf_op jit(solution)/shard_map/kernel_grad_1/pallas_call | solution.py:146
  (5 shorter events, 0.2 us)
Async XLA Ops:
  0.6 7.9 %collective-permute-start.1 = (bf16[96,1,4,256]{3,2,1,0:T(4,128)(2,1)}, bf16[96,1,4,256]{3,2,1,0:T(4,128)(2,1)S(1)}, u32[]{:S(2)}, u32[]{:S(2)}) collective-permute-start(bf16[96,1,4,256]{3,2,1,0:T(4,128)(2,1)} %refs_1_.1), channel_id=1, source_target_pairs={{0,2},{2,0},{1,3},{3,1},{4,6},{6,4},{5,7},{7,5},{8,10},{10,8},{9,1... | collective-permute-start | bytes 589832 | tf_op jit(solution)/shard_map/ppermute | solution.py:107
  2.8 5.7 %collective-permute-start = (bf16[96,1024]{1,0:T(8,128)(2,1)S(1)}, bf16[96,1024]{1,0:T(8,128)(2,1)S(1)}, u32[]{:S(2)}, u32[]{:S(2)}) collective-permute-start(bf16[96,1024]{1,0:T(8,128)(2,1)S(1)} %get-tuple-element.21.refs_0_.refs_1_), channel_id=1, source_target_pairs={{0,2},{2,0},{1,3},{3,1},{4,6},{6,4},{5,7},{7,5},{8,10},{10,8},{9,1... | collective-permute-start | bytes 589832 | tf_op jit(solution)/shard_map/ppermute | solution.py:107
  2.9 12.4 %collective-permute-start.2 = (bf16[96,1024]{1,0:T(8,128)(2,1)S(1)}, bf16[96,1024]{1,0:T(8,128)(2,1)S(1)}, u32[]{:S(2)}, u32[]{:S(2)}) collective-permute-start(bf16[96,1024]{1,0:T(8,128)(2,1)S(1)} %get-tuple-element.21.refs_0_.refs_1_), channel_id=1, source_target_pairs={{0,4},{4,0},{8,12},{12,8},{1,5},{5,1},{9,13},{13,9},{2,6},{6,2},{1... | collective-permute-start | bytes 589832 | tf_op jit(solution)/shard_map/ppermute | solution.py:442
  5.9 11.8 %collective-permute-start.4 = (bf16[96,1024]{1,0:T(8,128)(2,1)S(1)}, bf16[96,1024]{1,0:T(8,128)(2,1)S(1)}, u32[]{:S(2)}, u32[]{:S(2)}) collective-permute-start(bf16[96,1024]{1,0:T(8,128)(2,1)S(1)} %get-tuple-element.21.refs_0_.refs_1_), channel_id=1, source_target_pairs={{0,8},{4,12},{8,0},{12,4},{1,9},{5,13},{9,1},{13,5},{2,10},{6,14},... | collective-permute-start | bytes 589832 | tf_op jit(solution)/shard_map/ppermute | solution.py:442
  10.5 7.7 %collective-permute-start.7 = (bf16[336,384]{1,0:T(8,128)(2,1)S(1)}, bf16[336,384]{1,0:T(8,128)(2,1)S(1)}, u32[]{:S(2)}, u32[]{:S(2)}) collective-permute-start(bf16[336,384]{1,0:T(8,128)(2,1)S(1)} %get-tuple-element.26.refs_3_.refs_0_), channel_id=1, source_target_pairs={{0,1},{1,0},{2,3},{3,2},{4,5},{5,4},{6,7},{7,6},{8,9},{9,8},{10,11... | collective-permute-start | bytes 774152 | tf_op jit(solution)/shard_map/ppermute | solution.py:107
  15.3 2.9 %collective-permute-start.3 = (bf16[96,1024]{1,0:T(8,128)(2,1)S(1)}, bf16[96,1024]{1,0:T(8,128)(2,1)S(1)}, u32[]{:S(2)}, u32[]{:S(2)}) collective-permute-start(bf16[96,1024]{1,0:T(8,128)(2,1)S(1)} %hand_on.1.refs_1_.refs_3_), channel_id=1, source_target_pairs={{0,2},{2,0},{1,3},{3,1},{4,6},{6,4},{5,7},{7,5},{8,10},{10,8},{9,1... | collective-permute-start | bytes 589832 | tf_op jit(solution)/shard_map/ppermute | solution.py:107
  17.7 9.3 %collective-permute-start.6 = (bf16[2,96,1024]{2,1,0:T(8,128)(2,1)S(1)}, bf16[2,96,1024]{2,1,0:T(8,128)(2,1)S(1)}, u32[]{:S(2)}, u32[]{:S(2)}) collective-permute-start(bf16[2,96,1024]{2,1,0:T(8,128)(2,1)S(1)} %get-tuple-element.30), channel_id=1, source_target_pairs={{0,4},{4,0},{8,12},{12,8},{1,5},{5,1},{9,13},{13,9},{2,6},{6,2},{1... | collective-permute-start | bytes 1179656 | tf_op jit(solution)/shard_map/ppermute | solution.py:442
  19.6 5.0 %copy-start = (bf16[96,1,4,256]{3,2,1,0:T(4,128)(2,1)S(1)}, bf16[96,1,4,256]{3,2,1,0:T(4,128)(2,1)}, u32[]{:S(2)}) copy-start(bf16[96,1,4,256]{3,2,1,0:T(4,128)(2,1)} %refs_0_.3) | copy-start | bytes 589828
  19.6 7.4 %collective-permute-start.8 = (bf16[336,384]{1,0:T(8,128)(2,1)S(1)}, bf16[336,384]{1,0:T(8,128)(2,1)S(1)}, u32[]{:S(2)}, u32[]{:S(2)}) collective-permute-start(bf16[336,384]{1,0:T(8,128)(2,1)S(1)} %terms_1.1.refs_3_.refs_1_), channel_id=1, source_target_pairs={{0,1},{1,0},{2,3},{3,2},{4,5},{5,4},{6,7},{7,6},{8,9},{9,8},{10,11... | collective-permute-start | bytes 774152 | tf_op jit(solution)/shard_map/ppermute | solution.py:107
  21.2 1.4 %collective-permute-start.5 = (bf16[96,1024]{1,0:T(8,128)(2,1)S(1)}, bf16[96,1024]{1,0:T(8,128)(2,1)S(1)}, u32[]{:S(2)}, u32[]{:S(2)}) collective-permute-start(bf16[96,1024]{1,0:T(8,128)(2,1)S(1)} %get-tuple-element.29.refs_4_.refs_1_.refs_5_), channel_id=1, source_target_pairs={{0,2},{2,0},{1,3},{3,1},{4,6},{6,4},{5,7},{7,5},{8,10},{10,8},{9,1... | collective-permute-start | bytes 589832 | tf_op jit(solution)/shard_map/ppermute | solution.py:107
  24.0 10.4 %collective-permute-start.10 = (bf16[336,384]{1,0:T(8,128)(2,1)S(1)}, bf16[336,384]{1,0:T(8,128)(2,1)S(1)}, u32[]{:S(2)}, u32[]{:S(2)}) collective-permute-start(bf16[336,384]{1,0:T(8,128)(2,1)S(1)} %terms_2.1.refs_1_.refs_0_), channel_id=1, source_target_pairs={{0,1},{1,0},{2,3},{3,2},{4,5},{5,4},{6,7},{7,6},{8,9},{9,8},{10,11... | collective-permute-start | bytes 774152 | tf_op jit(solution)/shard_map/ppermute | solution.py:107
  27.1 4.0 %collective-permute-start.9 = (bf16[96,1024]{1,0:T(8,128)(2,1)S(1)}, bf16[96,1024]{1,0:T(8,128)(2,1)S(1)}, u32[]{:S(2)}, u32[]{:S(2)}) collective-permute-start(bf16[96,1024]{1,0:T(8,128)(2,1)S(1)} %get-tuple-element.31.refs_1_.refs_7_), channel_id=1, source_target_pairs={{0,2},{2,0},{1,3},{3,1},{4,6},{6,4},{5,7},{7,5},{8,10},{10,8},{9,1... | collective-permute-start | bytes 589832 | tf_op jit(solution)/shard_map/ppermute | solution.py:107
  27.2 12.5 %collective-permute-start.11 = (bf16[96,1024]{1,0:T(8,128)(2,1)S(1)}, bf16[96,1024]{1,0:T(8,128)(2,1)S(1)}, u32[]{:S(2)}, u32[]{:S(2)}) collective-permute-start(bf16[96,1024]{1,0:T(8,128)(2,1)S(1)} %carry_share.1.refs_3_), channel_id=1, source_target_pairs={{0,8},{4,12},{8,0},{12,4},{1,9},{5,13},{9,1},{13,5},{2,10},{6,14},... | collective-permute-start | bytes 589832 | tf_op jit(solution)/shard_map/ppermute | solution.py:442
  29.3 10.4 %collective-permute-start.12 = (bf16[96,1024]{1,0:T(8,128)(2,1)S(1)}, bf16[96,1024]{1,0:T(8,128)(2,1)S(1)}, u32[]{:S(2)}, u32[]{:S(2)}) collective-permute-start(bf16[96,1024]{1,0:T(8,128)(2,1)S(1)} %get-tuple-element.36), channel_id=1, source_target_pairs={{0,4},{4,0},{8,12},{12,8},{1,5},{5,1},{9,13},{13,9},{2,6},{6,2},{1... | collective-permute-start | bytes 589832 | tf_op jit(solution)/shard_map/ppermute | solution.py:442
  32.6 8.1 %collective-permute-start.14 = (bf16[336,384]{1,0:T(8,128)(2,1)S(1)}, bf16[336,384]{1,0:T(8,128)(2,1)S(1)}, u32[]{:S(2)}, u32[]{:S(2)}) collective-permute-start(bf16[336,384]{1,0:T(8,128)(2,1)S(1)} %terms_3.1.refs_9_.refs_4_.refs_1_), channel_id=1, source_target_pairs={{0,1},{1,0},{2,3},{3,2},{4,5},{5,4},{6,7},{7,6},{8,9},{9,8},{10,11... | collective-permute-start | bytes 774152 | tf_op jit(solution)/shard_map/ppermute | solution.py:107
  34.3 8.2 %collective-permute-start.13 = (bf16[672,384]{1,0:T(8,128)(2,1)S(1)}, bf16[672,384]{1,0:T(8,128)(2,1)S(1)}, u32[]{:S(2)}, u32[]{:S(2)}) collective-permute-start(bf16[672,384]{1,0:T(8,128)(2,1)S(1)} %sums_0.1.refs_3_.refs_0_), channel_id=1, source_target_pairs={{0,2},{2,0},{1,3},{3,1},{4,6},{6,4},{5,7},{7,5},{8,10},{10,8},{9,1... | collective-permute-start | bytes 1548296 | tf_op jit(solution)/shard_map/ppermute | solution.py:107
  40.9 2.0 %collective-permute-start.15 = (bf16[672,384]{1,0:T(8,128)(2,1)S(1)}, bf16[672,384]{1,0:T(8,128)(2,1)S(1)}, u32[]{:S(2)}, u32[]{:S(2)}) collective-permute-start(bf16[672,384]{1,0:T(8,128)(2,1)S(1)} %sums_2.1.refs_1_), channel_id=1, source_target_pairs={{0,2},{2,0},{1,3},{3,1},{4,6},{6,4},{5,7},{7,5},{8,10},{10,8},{9,1... | collective-permute-start | bytes 1548296 | tf_op jit(solution)/shard_map/ppermute | solution.py:107

commit v12 on v11

--- a/solution.py
+++ b/solution.py
@@ -14,8 +14,8 @@
 BF16 = jnp.bfloat16
 VMEM_LIMIT = 24 * 1024 * 1024
 TOKEN = (8, 128)
-FEATURE_COST = 3 * 10**9
-GATHER_COST = 10**8
+FEATURE_COST = 2 * 10**10
+GATHER_COST = 3 * 10**9
 FAR_COST = 10**9
 NEAR_COST = 3 * 10**9
 
@@ -577,6 +577,23 @@
         cost_estimate=cost(GATHER_COST),
         name="gather_share",
     )
+    late = sums(2, count, (gathered,))
+    scale = 1.0 / math.sqrt(lax.axis_size("dp") * lax.axis_size("tm") * length)
+
+    def finish(whose, sums, base=(), waits=()):
+        anywhere = pl.BlockSpec(memory_space=pl.ANY)
+        return run(
+            functools.partial(finish_kernel, scale, main, whose),
+            (*sums, *base),
+            waits=waits,
+            in_specs=[whole()] * 2 + [anywhere] * len(base),
+            out_shape=sds((3, 9 * rows, channels), F32),
+            out_specs=anywhere,
+            input_output_aliases={2: 0} if base else {},
+            scratch_shapes=[pltpu.VMEM((3, half, channels), F32), pltpu.SemaphoreType.DMA((9,))],
+            name=f"kernel_grad_{whose}",
+        )
+
     feature_grad, token = run(
         functools.partial(feature_kernel, pixels),
         (slope, gathered, first_share),
@@ -585,23 +602,7 @@
         cost_estimate=cost(FEATURE_COST),
         name="feature_grad",
     )
-    late = sums(2, count, (token,))
-    scale = 1.0 / math.sqrt(lax.axis_size("dp") * lax.axis_size("tm") * length)
-
-    def finish(whose, sums, base=()):
-        anywhere = pl.BlockSpec(memory_space=pl.ANY)
-        return run(
-            functools.partial(finish_kernel, scale, main, whose),
-            (*sums, *base),
-            in_specs=[whole()] * 2 + [anywhere] * len(base),
-            out_shape=sds((3, 9 * rows, channels), F32),
-            out_specs=anywhere,
-            input_output_aliases={2: 0} if base else {},
-            scratch_shapes=[pltpu.VMEM((3, half, channels), F32), pltpu.SemaphoreType.DMA((9,))],
-            name=f"kernel_grad_{whose}",
-        )
-
-    kernel_grad = finish(0, (early, late))
+    kernel_grad = finish(0, (early, late), (), (token,))
     kernel_grad = finish(1, (rotate(early, "tm", 1), rotate(late, "tm", 1)), (kernel_grad,))
     kernel_grad = jnp.transpose(kernel_grad.reshape(taps, rows, channels), (1, 0, 2))
     return (conv_out, feature_grad, kernel_grad)

time: 44.7 us -> 45.3 us (1.013)
  waiting for transfers between devices: 7.53 us -> 8.15 us
    ppermute x11, waiting for transfers between devices: 1.82 us -> 2.44 us  [rotate(): return lax.ppermute(x, axis, [(i, (i + by) % size) for i in range(size)])]
where the time goes in v12:
time: 45.3 us; the launch traced here: 45.1 us
  Pallas kernels  19.8 us (44%)
  starting transfers between devices  16.2 us (36%)
  waiting for transfers between devices  8.15 us (18%)
  between operations  0.97 us (2%)
    pallas_call x17, Pallas kernels, run(): pl.pallas_call(body, compiler_params=pltpu.CompilerParams(vmem_limit_byte...  19.8 us
    ppermute x5, starting transfers between devices, swap(): return lax.ppermute(x, 'chan', [(z, z ^ far) for z in range(count)])  10 us
    ppermute x11, starting transfers between devices, rotate(): return lax.ppermute(x, axis, [(i, (i + by) % size) for i in range(size)])  6.19 us
    ppermute x5, waiting for transfers between devices, swap(): return lax.ppermute(x, 'chan', [(z, z ^ far) for z in range(count)])  5.71 us
    ppermute x11, waiting for transfers between devices, rotate(): return lax.ppermute(x, axis, [(i, (i + by) % size) for i in range(size)])  2.44 us
  transfers between devices with their start and end apart: 16, of which 5 were waited for; matrix products, arithmetic and copies ran while one was open for 0% of the time, Pallas kernels for 41%

profile of v12, /device:TPU:0, one launch (start us, length us, event | category | flops | bytes accessed | tf_op | source)
XLA Modules:
  0.0 45.1 jit_solution(12350005014899273705)
XLA Ops:
  0.6 0.5 %collective-permute-start.1 = (bf16[96,1,4,256]{3,2,1,0:T(4,128)(2,1)}, bf16[96,1,4,256]{3,2,1,0:T(4,128)(2,1)S(1)}, u32[]{:S(2)}, u32[]{:S(2)}) collective-permute-start(bf16[96,1,4,256]{3,2,1,0:T(4,128)(2,1)} %refs_1_.1), channel_id=1, source_target_pairs={{0,2},{2,0},{1,3},{3,1},{4,6},{6,4},{5,7},{7,5},{8,10},{10,8},{9,1... | collective-permute-start | bytes 589832 | tf_op jit(solution)/shard_map/ppermute | solution.py:107
  1.1 1.6 %activate.1 = (bf16[96,1024]{1,0:T(8,128)(2,1)S(1)}, f32[96,1024]{1,0:T(8,128)S(1)}) custom-call(bf16[96,1,4,256]{3,2,1,0:T(4,128)(2,1)} %refs_0_.3, bf16[96,1,4,256]{3,2,1,0:T(4,128)(2,1)} %refs_1_.1), custom_call_target="tpu_custom_call" | custom-call | flops 1 | bytes 1 | tf_op jit(solution)/shard_map/activate/pallas_call | solution.py:146
  2.8 0.1 collective-permute-start
  2.9 3.0 %collective-permute-start.2 = (bf16[96,1024]{1,0:T(8,128)(2,1)S(1)}, bf16[96,1024]{1,0:T(8,128)(2,1)S(1)}, u32[]{:S(2)}, u32[]{:S(2)}) collective-permute-start(bf16[96,1024]{1,0:T(8,128)(2,1)S(1)} %get-tuple-element.21.refs_0_.refs_1_), channel_id=1, source_target_pairs={{0,4},{4,0},{8,12},{12,8},{1,5},{5,1},{9,13},{13,9},{2,6},{6,2},{1... | collective-permute-start | bytes 589832 | tf_op jit(solution)/shard_map/ppermute | solution.py:442
  5.9 2.6 %collective-permute-start.4 = (bf16[96,1024]{1,0:T(8,128)(2,1)S(1)}, bf16[96,1024]{1,0:T(8,128)(2,1)S(1)}, u32[]{:S(2)}, u32[]{:S(2)}) collective-permute-start(bf16[96,1024]{1,0:T(8,128)(2,1)S(1)} %get-tuple-element.21.refs_0_.refs_1_), channel_id=1, source_target_pairs={{0,8},{4,12},{8,0},{12,4},{1,9},{5,13},{9,1},{13,5},{2,10},{6,14},... | collective-permute-start | bytes 589832 | tf_op jit(solution)/shard_map/ppermute | solution.py:442
  8.5 0.0 collective-permute-done.1.refs_3_
  8.5 0.0 collective-permute-done.refs_1_.refs_2_
  8.5 2.0 %own_terms.1 = (bf16[336,384]{1,0:T(8,128)(2,1)S(1)}, bf16[432,2048]{1,0:T(8,128)(2,1)S(1)}, f32[96,2048]{1,0:T(8,128)S(1)}, bf16[2592,384]{1,0:T(8,128)(2,1)S(1)}) custom-call(bf16[96,1024]{1,0:T(8,128)(2,1)S(1)} %get-tuple-element.21.refs_0_.refs_1_, bf16[96,1024]{1,0:T(8,128)(2,1)S(1)} %collective-permute-done.refs_1_.refs_2_, ...), custom_call_target="tpu_custom_call" | custom-call | flops 1 | bytes 1 | tf_op jit(solution)/shard_map/own_terms/pallas_call | solution.py:146
  10.5 1.6 %collective-permute-start.7 = (bf16[336,384]{1,0:T(8,128)(2,1)S(1)}, bf16[336,384]{1,0:T(8,128)(2,1)S(1)}, u32[]{:S(2)}, u32[]{:S(2)}) collective-permute-start(bf16[336,384]{1,0:T(8,128)(2,1)S(1)} %get-tuple-element.26.refs_3_.refs_0_), channel_id=1, source_target_pairs={{0,1},{1,0},{2,3},{3,2},{4,5},{5,4},{6,7},{7,6},{8,9},{9,8},{10,11... | collective-permute-start | bytes 774152 | tf_op jit(solution)/shard_map/ppermute | solution.py:107
  12.1 3.2 %shares.1 = (f32[96,1024]{1,0:T(8,128)S(1)}, f32[96,1024]{1,0:T(8,128)S(1)}, bf16[96,1024]{1,0:T(8,128)(2,1)S(1)}, bf16[96,1024]{1,0:T(8,128)(2,1)S(1)}) custom-call(bf16[2592,384]{1,0:T(8,128)(2,1)S(1)} %get-tuple-element.23.refs_0_, f32[96,2048]{1,0:T(8,128)S(1)} %get-tuple-element.24.refs_1_, bf16[432,2048]{1,0:T(8,128)(2,1)S(1)} %get-tuple-element.25.refs_2_.refs_0_, ...), custom_call_target="tpu_custom_call" | custom-call | flops 1 | bytes 1 | tf_op jit(solution)/shard_map/shares/pallas_call | solution.py:146
  15.3 0.0 collective-permute-done.2.refs_0_
  15.3 0.1 collective-permute-start.3
  15.4 2.3 %collective-permute-done.4.refs_0_ = bf16[96,1024]{1,0:T(8,128)(2,1)S(1)} collective-permute-done((bf16[96,1024]{1,0:T(8,128)(2,1)S(1)}, bf16[96,1024]{1,0:T(8,128)(2,1)S(1)}, u32[]{:S(2)}, u32[]{:S(2)}) %collective-permute-start.4) | collective-permute-done | bytes 196640 | tf_op jit(solution)/shard_map/ppermute | solution.py:442
  17.7 0.5 %collective-permute-start.6 = (bf16[2,96,1024]{2,1,0:T(8,128)(2,1)S(1)}, bf16[2,96,1024]{2,1,0:T(8,128)(2,1)S(1)}, u32[]{:S(2)}, u32[]{:S(2)}) collective-permute-start(bf16[2,96,1024]{2,1,0:T(8,128)(2,1)S(1)} %get-tuple-element.30), channel_id=1, source_target_pairs={{0,4},{4,0},{8,12},{12,8},{1,5},{5,1},{9,13},{13,9},{2,6},{6,2},{1... | collective-permute-start | bytes 1179656 | tf_op jit(solution)/shard_map/ppermute | solution.py:442
  18.3 0.0 collective-permute-done.3.refs_2_.refs_4_
  18.3 0.0 collective-permute-done.7.refs_5_.refs_2_
  18.3 1.3 %terms_1.1.refs_3_.refs_1_ = bf16[336,384]{1,0:T(8,128)(2,1)S(1)} custom-call(bf16[432,2048]{1,0:T(8,128)(2,1)S(1)} %get-tuple-element.25.refs_2_.refs_0_, bf16[96,1024]{1,0:T(8,128)(2,1)S(1)} %hand_on.1.refs_1_.refs_3_, bf16[96,1024]{1,0:T(8,128)(2,1)S(1)} %collective-permute-done.3.refs_2_.refs_4_, ...), custom_call_target="tpu_custom_call" | custom-call | flops 1 | bytes 1 | tf_op jit(solution)/shard_map/terms_1/pallas_call | solution.py:146
  19.6 0.0 copy-start
  19.6 1.6 %collective-permute-start.8 = (bf16[336,384]{1,0:T(8,128)(2,1)S(1)}, bf16[336,384]{1,0:T(8,128)(2,1)S(1)}, u32[]{:S(2)}, u32[]{:S(2)}) collective-permute-start(bf16[336,384]{1,0:T(8,128)(2,1)S(1)} %terms_1.1.refs_3_.refs_1_), channel_id=1, source_target_pairs={{0,1},{1,0},{2,3},{3,2},{4,5},{5,4},{6,7},{7,6},{8,9},{9,8},{10,11... | collective-permute-start | bytes 774152 | tf_op jit(solution)/shard_map/ppermute | solution.py:107
  21.2 0.0 collective-permute-start.5
  21.2 1.4 %collective-permute-done.5.refs_2_.refs_6_ = bf16[96,1024]{1,0:T(8,128)(2,1)S(1)} collective-permute-done((bf16[96,1024]{1,0:T(8,128)(2,1)S(1)}, bf16[96,1024]{1,0:T(8,128)(2,1)S(1)}, u32[]{:S(2)}, u32[]{:S(2)}) %collective-permute-start.5) | collective-permute-done | bytes 196640 | tf_op jit(solution)/shard_map/ppermute | solution.py:107
  22.6 1.3 %terms_2.1.refs_1_.refs_0_ = bf16[336,384]{1,0:T(8,128)(2,1)S(1)} custom-call(bf16[432,2048]{1,0:T(8,128)(2,1)S(1)} %get-tuple-element.25.refs_2_.refs_0_, bf16[96,1024]{1,0:T(8,128)(2,1)S(1)} %get-tuple-element.29.refs_4_.refs_1_.refs_5_, bf16[96,1024]{1,0:T(8,128)(2,1)S(1)} %collective-permute-done.5.refs_2_.refs_6_, ...), custom_call_target="tpu_custom_call" | custom-call | flops 1 | bytes 1 | tf_op jit(solution)/shard_map/terms_2/pallas_call | solution.py:146
  24.0 0.6 %collective-permute-start.10 = (bf16[336,384]{1,0:T(8,128)(2,1)S(1)}, bf16[336,384]{1,0:T(8,128)(2,1)S(1)}, u32[]{:S(2)}, u32[]{:S(2)}) collective-permute-start(bf16[336,384]{1,0:T(8,128)(2,1)S(1)} %terms_2.1.refs_1_.refs_0_), channel_id=1, source_target_pairs={{0,1},{1,0},{2,3},{3,2},{4,5},{5,4},{6,7},{7,6},{8,9},{9,8},{10,11... | collective-permute-start | bytes 774152 | tf_op jit(solution)/shard_map/ppermute | solution.py:107
  24.6 0.0 copy-done
  24.6 0.3 slope.1.refs_1_.refs_0_
  24.8 2.2 %collective-permute-done.6.refs_0_ = bf16[2,96,1024]{2,1,0:T(8,128)(2,1)S(1)} collective-permute-done((bf16[2,96,1024]{2,1,0:T(8,128)(2,1)S(1)}, bf16[2,96,1024]{2,1,0:T(8,128)(2,1)S(1)}, u32[]{:S(2)}, u32[]{:S(2)}) %collective-permute-start.6) | collective-permute-done | bytes 393248 | tf_op jit(solution)/shard_map/ppermute | solution.py:442
  27.0 0.0 collective-permute-done.8.refs_2_.refs_3_
  27.1 0.1 collective-permute-start.9
  27.2 2.1 %collective-permute-start.11 = (bf16[96,1024]{1,0:T(8,128)(2,1)S(1)}, bf16[96,1024]{1,0:T(8,128)(2,1)S(1)}, u32[]{:S(2)}, u32[]{:S(2)}) collective-permute-start(bf16[96,1024]{1,0:T(8,128)(2,1)S(1)} %carry_share.1.refs_3_), channel_id=1, source_target_pairs={{0,8},{4,12},{8,0},{12,4},{1,9},{5,13},{9,1},{13,5},{2,10},{6,14},... | collective-permute-start | bytes 589832 | tf_op jit(solution)/shard_map/ppermute | solution.py:442
  29.3 1.7 %collective-permute-start.12 = (bf16[96,1024]{1,0:T(8,128)(2,1)S(1)}, bf16[96,1024]{1,0:T(8,128)(2,1)S(1)}, u32[]{:S(2)}, u32[]{:S(2)}) collective-permute-start(bf16[96,1024]{1,0:T(8,128)(2,1)S(1)} %get-tuple-element.36), channel_id=1, source_target_pairs={{0,4},{4,0},{8,12},{12,8},{1,5},{5,1},{9,13},{13,9},{2,6},{6,2},{1... | collective-permute-start | bytes 589832 | tf_op jit(solution)/shard_map/ppermute | solution.py:442
  31.1 0.0 collective-permute-done.9.refs_2_.refs_8_
  31.1 1.5 %terms_3.1.refs_9_.refs_4_.refs_1_ = bf16[336,384]{1,0:T(8,128)(2,1)S(1)} custom-call(bf16[432,2048]{1,0:T(8,128)(2,1)S(1)} %get-tuple-element.25.refs_2_.refs_0_, bf16[96,1024]{1,0:T(8,128)(2,1)S(1)} %get-tuple-element.31.refs_1_.refs_7_, bf16[96,1024]{1,0:T(8,128)(2,1)S(1)} %collective-permute-done.9.refs_2_.refs_8_, bf16[96,1024]{1,0:T(8,128)(2,1)S(1)} %carry_share.1.refs_3_), custom_call_target="tpu_custom_call" | custom-call | flops 1 | bytes 1 | tf_op jit(solution)/shard_map/terms_3/pallas_call | solution.py:146
  32.6 1.6 %collective-permute-start.14 = (bf16[336,384]{1,0:T(8,128)(2,1)S(1)}, bf16[336,384]{1,0:T(8,128)(2,1)S(1)}, u32[]{:S(2)}, u32[]{:S(2)}) collective-permute-start(bf16[336,384]{1,0:T(8,128)(2,1)S(1)} %terms_3.1.refs_9_.refs_4_.refs_1_), channel_id=1, source_target_pairs={{0,1},{1,0},{2,3},{3,2},{4,5},{5,4},{6,7},{7,6},{8,9},{9,8},{10,11... | collective-permute-start | bytes 774152 | tf_op jit(solution)/shard_map/ppermute | solution.py:107
  34.1 0.1 sums_0.1.refs_3_.refs_0_
  34.3 0.1 collective-permute-start.13
  34.3 0.0 collective-permute-done.10.refs_10_.refs_2_
  34.4 4.1 %conv.1 = (bf16[96,1,4,256]{3,2,1,0:T(4,128)(2,1)}, f32[8,128]{1,0:T(8,128)S(1)}) custom-call(bf16[2592,384]{1,0:T(8,128)(2,1)S(1)} %get-tuple-element.23.refs_0_, bf16[96,1024]{1,0:T(8,128)(2,1)S(1)} %get-tuple-element.21.refs_0_.refs_1_, bf16[96,1024]{1,0:T(8,128)(2,1)S(1)} %collective-permute-done.refs_1_.refs_2_, ...), custom_call_target="tpu_custom_call" | custom-call | flops 1 | bytes 1 | tf_op jit(solution)/shard_map/conv/pallas_call | solution.py:146
  38.5 1.2 %collective-permute-done.11.refs_1_ = bf16[96,1024]{1,0:T(8,128)(2,1)S(1)} collective-permute-done((bf16[96,1024]{1,0:T(8,128)(2,1)S(1)}, bf16[96,1024]{1,0:T(8,128)(2,1)S(1)}, u32[]{:S(2)}, u32[]{:S(2)}) %collective-permute-start.11) | collective-permute-done | bytes 196640 | tf_op jit(solution)/shard_map/ppermute | solution.py:442
  39.7 0.1 gather_share.1.refs_1_.refs_4_
  39.7 1.0 %collective-permute-done.14.refs_3_ = bf16[336,384]{1,0:T(8,128)(2,1)S(1)} collective-permute-done((bf16[336,384]{1,0:T(8,128)(2,1)S(1)}, bf16[336,384]{1,0:T(8,128)(2,1)S(1)}, u32[]{:S(2)}, u32[]{:S(2)}) %collective-permute-start.14) | collective-permute-done | bytes 258080 | tf_op jit(solution)/shard_map/ppermute | solution.py:107
  40.7 0.1 sums_2.1.refs_1_
  40.8 0.1 collective-permute-start.15
  40.9 0.0 collective-permute-done.12.refs_2_
  40.9 1.0 %feature_grad.1 = (bf16[96,1,4,256]{3,2,1,0:T(4,128)(2,1)}, f32[8,128]{1,0:T(8,128)S(1)}) custom-call(f32[96,1024]{1,0:T(8,128)S(1)} %slope.1.refs_1_.refs_0_, f32[96,1024]{1,0:T(8,128)S(1)} %gather_share.1.refs_1_.refs_4_, bf16[96,1024]{1,0:T(8,128)(2,1)S(1)} %collective-permute-done.12.refs_2_), custom_call_target="tpu_custom_call" | custom-call | flops 20000000000 | bytes 1 | tf_op jit(solution)/shard_map/feature_grad/pallas_call | solution.py:146
  41.9 1.5 %kernel_grad_0.1.refs_2_ = f32[3,864,384]{2,1,0:T(8,128)} custom-call(bf16[672,384]{1,0:T(8,128)(2,1)S(1)} %sums_0.1.refs_3_.refs_0_, bf16[672,384]{1,0:T(8,128)(2,1)S(1)} %sums_2.1.refs_1_, f32[8,128]{1,0:T(8,128)S(1)} %get-tuple-element.38.refs_2_), custom_call_target="tpu_custom_call" | custom-call | flops 1 | bytes 1 | tf_op jit(solution)/shard_map/kernel_grad_0/pallas_call | solution.py:146
  43.4 0.0 collective-permute-done.13.refs_0_
  43.4 0.0 collective-permute-done.15.refs_1_
  43.4 1.5 %kernel_grad_1.1 = f32[3,864,384]{2,1,0:T(8,128)} custom-call(bf16[672,384]{1,0:T(8,128)(2,1)S(1)} %collective-permute-done.13.refs_0_, bf16[672,384]{1,0:T(8,128)(2,1)S(1)} %collective-permute-done.15.refs_1_, f32[3,864,384]{2,1,0:T(8,128)} %kernel_grad_0.1.refs_2_), custom_call_target="tpu_custom_call", output_to_operand_aliasing={{}: (2, {})} | custom-call | flops 1 | bytes 1 | tf_op jit(solution)/shard_map/kernel_grad_1/pallas_call | solution.py:146
  (4 shorter events, 0.1 us)
Async XLA Ops:
  0.6 7.9 %collective-permute-start.1 = (bf16[96,1,4,256]{3,2,1,0:T(4,128)(2,1)}, bf16[96,1,4,256]{3,2,1,0:T(4,128)(2,1)S(1)}, u32[]{:S(2)}, u32[]{:S(2)}) collective-permute-start(bf16[96,1,4,256]{3,2,1,0:T(4,128)(2,1)} %refs_1_.1), channel_id=1, source_target_pairs={{0,2},{2,0},{1,3},{3,1},{4,6},{6,4},{5,7},{7,5},{8,10},{10,8},{9,1... | collective-permute-start | bytes 589832 | tf_op jit(solution)/shard_map/ppermute | solution.py:107
  2.8 5.7 %collective-permute-start = (bf16[96,1024]{1,0:T(8,128)(2,1)S(1)}, bf16[96,1024]{1,0:T(8,128)(2,1)S(1)}, u32[]{:S(2)}, u32[]{:S(2)}) collective-permute-start(bf16[96,1024]{1,0:T(8,128)(2,1)S(1)} %get-tuple-element.21.refs_0_.refs_1_), channel_id=1, source_target_pairs={{0,2},{2,0},{1,3},{3,1},{4,6},{6,4},{5,7},{7,5},{8,10},{10,8},{9,1... | collective-permute-start | bytes 589832 | tf_op jit(solution)/shard_map/ppermute | solution.py:107
  2.9 12.4 %collective-permute-start.2 = (bf16[96,1024]{1,0:T(8,128)(2,1)S(1)}, bf16[96,1024]{1,0:T(8,128)(2,1)S(1)}, u32[]{:S(2)}, u32[]{:S(2)}) collective-permute-start(bf16[96,1024]{1,0:T(8,128)(2,1)S(1)} %get-tuple-element.21.refs_0_.refs_1_), channel_id=1, source_target_pairs={{0,4},{4,0},{8,12},{12,8},{1,5},{5,1},{9,13},{13,9},{2,6},{6,2},{1... | collective-permute-start | bytes 589832 | tf_op jit(solution)/shard_map/ppermute | solution.py:442
  5.9 11.8 %collective-permute-start.4 = (bf16[96,1024]{1,0:T(8,128)(2,1)S(1)}, bf16[96,1024]{1,0:T(8,128)(2,1)S(1)}, u32[]{:S(2)}, u32[]{:S(2)}) collective-permute-start(bf16[96,1024]{1,0:T(8,128)(2,1)S(1)} %get-tuple-element.21.refs_0_.refs_1_), channel_id=1, source_target_pairs={{0,8},{4,12},{8,0},{12,4},{1,9},{5,13},{9,1},{13,5},{2,10},{6,14},... | collective-permute-start | bytes 589832 | tf_op jit(solution)/shard_map/ppermute | solution.py:442
  10.5 7.7 %collective-permute-start.7 = (bf16[336,384]{1,0:T(8,128)(2,1)S(1)}, bf16[336,384]{1,0:T(8,128)(2,1)S(1)}, u32[]{:S(2)}, u32[]{:S(2)}) collective-permute-start(bf16[336,384]{1,0:T(8,128)(2,1)S(1)} %get-tuple-element.26.refs_3_.refs_0_), channel_id=1, source_target_pairs={{0,1},{1,0},{2,3},{3,2},{4,5},{5,4},{6,7},{7,6},{8,9},{9,8},{10,11... | collective-permute-start | bytes 774152 | tf_op jit(solution)/shard_map/ppermute | solution.py:107
  15.3 2.9 %collective-permute-start.3 = (bf16[96,1024]{1,0:T(8,128)(2,1)S(1)}, bf16[96,1024]{1,0:T(8,128)(2,1)S(1)}, u32[]{:S(2)}, u32[]{:S(2)}) collective-permute-start(bf16[96,1024]{1,0:T(8,128)(2,1)S(1)} %hand_on.1.refs_1_.refs_3_), channel_id=1, source_target_pairs={{0,2},{2,0},{1,3},{3,1},{4,6},{6,4},{5,7},{7,5},{8,10},{10,8},{9,1... | collective-permute-start | bytes 589832 | tf_op jit(solution)/shard_map/ppermute | solution.py:107
  17.7 9.3 %collective-permute-start.6 = (bf16[2,96,1024]{2,1,0:T(8,128)(2,1)S(1)}, bf16[2,96,1024]{2,1,0:T(8,128)(2,1)S(1)}, u32[]{:S(2)}, u32[]{:S(2)}) collective-permute-start(bf16[2,96,1024]{2,1,0:T(8,128)(2,1)S(1)} %get-tuple-element.30), channel_id=1, source_target_pairs={{0,4},{4,0},{8,12},{12,8},{1,5},{5,1},{9,13},{13,9},{2,6},{6,2},{1... | collective-permute-start | bytes 1179656 | tf_op jit(solution)/shard_map/ppermute | solution.py:442
  19.6 5.0 %copy-start = (bf16[96,1,4,256]{3,2,1,0:T(4,128)(2,1)S(1)}, bf16[96,1,4,256]{3,2,1,0:T(4,128)(2,1)}, u32[]{:S(2)}) copy-start(bf16[96,1,4,256]{3,2,1,0:T(4,128)(2,1)} %refs_0_.3) | copy-start | bytes 589828
  19.6 7.4 %collective-permute-start.8 = (bf16[336,384]{1,0:T(8,128)(2,1)S(1)}, bf16[336,384]{1,0:T(8,128)(2,1)S(1)}, u32[]{:S(2)}, u32[]{:S(2)}) collective-permute-start(bf16[336,384]{1,0:T(8,128)(2,1)S(1)} %terms_1.1.refs_3_.refs_1_), channel_id=1, source_target_pairs={{0,1},{1,0},{2,3},{3,2},{4,5},{5,4},{6,7},{7,6},{8,9},{9,8},{10,11... | collective-permute-start | bytes 774152 | tf_op jit(solution)/shard_map/ppermute | solution.py:107
  21.2 1.4 %collective-permute-start.5 = (bf16[96,1024]{1,0:T(8,128)(2,1)S(1)}, bf16[96,1024]{1,0:T(8,128)(2,1)S(1)}, u32[]{:S(2)}, u32[]{:S(2)}) collective-permute-start(bf16[96,1024]{1,0:T(8,128)(2,1)S(1)} %get-tuple-element.29.refs_4_.refs_1_.refs_5_), channel_id=1, source_target_pairs={{0,2},{2,0},{1,3},{3,1},{4,6},{6,4},{5,7},{7,5},{8,10},{10,8},{9,1... | collective-permute-start | bytes 589832 | tf_op jit(solution)/shard_map/ppermute | solution.py:107
  24.0 10.4 %collective-permute-start.10 = (bf16[336,384]{1,0:T(8,128)(2,1)S(1)}, bf16[336,384]{1,0:T(8,128)(2,1)S(1)}, u32[]{:S(2)}, u32[]{:S(2)}) collective-permute-start(bf16[336,384]{1,0:T(8,128)(2,1)S(1)} %terms_2.1.refs_1_.refs_0_), channel_id=1, source_target_pairs={{0,1},{1,0},{2,3},{3,2},{4,5},{5,4},{6,7},{7,6},{8,9},{9,8},{10,11... | collective-permute-start | bytes 774152 | tf_op jit(solution)/shard_map/ppermute | solution.py:107
  27.1 4.0 %collective-permute-start.9 = (bf16[96,1024]{1,0:T(8,128)(2,1)S(1)}, bf16[96,1024]{1,0:T(8,128)(2,1)S(1)}, u32[]{:S(2)}, u32[]{:S(2)}) collective-permute-start(bf16[96,1024]{1,0:T(8,128)(2,1)S(1)} %get-tuple-element.31.refs_1_.refs_7_), channel_id=1, source_target_pairs={{0,2},{2,0},{1,3},{3,1},{4,6},{6,4},{5,7},{7,5},{8,10},{10,8},{9,1... | collective-permute-start | bytes 589832 | tf_op jit(solution)/shard_map/ppermute | solution.py:107
  27.2 12.5 %collective-permute-start.11 = (bf16[96,1024]{1,0:T(8,128)(2,1)S(1)}, bf16[96,1024]{1,0:T(8,128)(2,1)S(1)}, u32[]{:S(2)}, u32[]{:S(2)}) collective-permute-start(bf16[96,1024]{1,0:T(8,128)(2,1)S(1)} %carry_share.1.refs_3_), channel_id=1, source_target_pairs={{0,8},{4,12},{8,0},{12,4},{1,9},{5,13},{9,1},{13,5},{2,10},{6,14},... | collective-permute-start | bytes 589832 | tf_op jit(solution)/shard_map/ppermute | solution.py:442
  29.3 11.6 %collective-permute-start.12 = (bf16[96,1024]{1,0:T(8,128)(2,1)S(1)}, bf16[96,1024]{1,0:T(8,128)(2,1)S(1)}, u32[]{:S(2)}, u32[]{:S(2)}) collective-permute-start(bf16[96,1024]{1,0:T(8,128)(2,1)S(1)} %get-tuple-element.36), channel_id=1, source_target_pairs={{0,4},{4,0},{8,12},{12,8},{1,5},{5,1},{9,13},{13,9},{2,6},{6,2},{1... | collective-permute-start | bytes 589832 | tf_op jit(solution)/shard_map/ppermute | solution.py:442
  32.6 8.1 %collective-permute-start.14 = (bf16[336,384]{1,0:T(8,128)(2,1)S(1)}, bf16[336,384]{1,0:T(8,128)(2,1)S(1)}, u32[]{:S(2)}, u32[]{:S(2)}) collective-permute-start(bf16[336,384]{1,0:T(8,128)(2,1)S(1)} %terms_3.1.refs_9_.refs_4_.refs_1_), channel_id=1, source_target_pairs={{0,1},{1,0},{2,3},{3,2},{4,5},{5,4},{6,7},{7,6},{8,9},{9,8},{10,11... | collective-permute-start | bytes 774152 | tf_op jit(solution)/shard_map/ppermute | solution.py:107
  34.3 9.1 %collective-permute-start.13 = (bf16[672,384]{1,0:T(8,128)(2,1)S(1)}, bf16[672,384]{1,0:T(8,128)(2,1)S(1)}, u32[]{:S(2)}, u32[]{:S(2)}) collective-permute-start(bf16[672,384]{1,0:T(8,128)(2,1)S(1)} %sums_0.1.refs_3_.refs_0_), channel_id=1, source_target_pairs={{0,2},{2,0},{1,3},{3,1},{4,6},{6,4},{5,7},{7,5},{8,10},{10,8},{9,1... | collective-permute-start | bytes 1548296 | tf_op jit(solution)/shard_map/ppermute | solution.py:107
  40.8 2.6 %collective-permute-start.15 = (bf16[672,384]{1,0:T(8,128)(2,1)S(1)}, bf16[672,384]{1,0:T(8,128)(2,1)S(1)}, u32[]{:S(2)}, u32[]{:S(2)}) collective-permute-start(bf16[672,384]{1,0:T(8,128)(2,1)S(1)} %sums_2.1.refs_1_), channel_id=1, source_target_pairs={{0,2},{2,0},{1,3},{3,1},{4,6},{6,4},{5,7},{7,5},{8,10},{10,8},{9,1... | collective-permute-start | bytes 1548296 | tf_op jit(solution)/shard_map/ppermute | solution.py:107

commit v13 on v11

--- a/solution.py
+++ b/solution.py
@@ -15,7 +15,7 @@
 VMEM_LIMIT = 24 * 1024 * 1024
 TOKEN = (8, 128)
 FEATURE_COST = 3 * 10**9
-GATHER_COST = 10**8
+GATHER_COST = 3 * 10**9
 FAR_COST = 10**9
 NEAR_COST = 3 * 10**9
 
@@ -509,7 +509,6 @@
         ],
         name="shares",
     )
-    first_share = swap(near_share, 1)
     near = after(near, own_share, flops=NEAR_COST)
     far, message = run(
         pack_kernel,
@@ -547,6 +546,7 @@
     )
     second_share = swap(carry, 2)
     term = terms_of(3, last, rotate(last, "tm", 1), (carry,))
+    first_share = swap(after(near_share, term), 1)
 
     def sums(first, stop, waits=()):
         return run(

time: 44.7 us -> 47.9 us (1.072)
  waiting for transfers between devices: 7.53 us -> 10.8 us
    ppermute x5, waiting for transfers between devices: 5.71 us -> 8.98 us  [swap(): return lax.ppermute(x, 'chan', [(z, z ^ far) for z in range(count)])]
    ppermute x5, starting transfers between devices: 10 us -> 9.38 us  [swap(): return lax.ppermute(x, 'chan', [(z, z ^ far) for z in range(count)])]
    ppermute x11, starting transfers between devices: 6.19 us -> 6.8 us  [rotate(): return lax.ppermute(x, axis, [(i, (i + by) % size) for i in range(size)])]
  transfers between devices with their start and end apart: 16 -> 16, of which waited for: 5 -> 6; matrix products, arithmetic and copies ran while one was open for 0% -> 0% of each run, Pallas kernels for 41% -> 38%
where the time goes in v13:
time: 47.9 us; the launch traced here: 47.7 us
  Pallas kernels  19.8 us (41%)
  starting transfers between devices  16.2 us (34%)
  waiting for transfers between devices  10.8 us (23%)
  between operations  0.96 us (2%)
    pallas_call x17, Pallas kernels, run(): pl.pallas_call(body, compiler_params=pltpu.CompilerParams(vmem_limit_byte...  19.8 us
    ppermute x5, starting transfers between devices, swap(): return lax.ppermute(x, 'chan', [(z, z ^ far) for z in range(count)])  9.38 us
    ppermute x5, waiting for transfers between devices, swap(): return lax.ppermute(x, 'chan', [(z, z ^ far) for z in range(count)])  8.98 us
    ppermute x11, starting transfers between devices, rotate(): return lax.ppermute(x, axis, [(i, (i + by) % size) for i in range(size)])  6.8 us
    ppermute x11, waiting for transfers between devices, rotate(): return lax.ppermute(x, axis, [(i, (i + by) % size) for i in range(size)])  1.82 us
  transfers between devices with their start and end apart: 16, of which 6 were waited for; matrix products, arithmetic and copies ran while one was open for 0% of the time, Pallas kernels for 38%

profile of v13, /device:TPU:0, one launch (start us, length us, event | category | flops | bytes accessed | tf_op | source)
XLA Modules:
  0.0 47.7 jit_solution(1114175523600910017)
XLA Ops:
  0.6 0.5 %collective-permute-start.1 = (bf16[96,1,4,256]{3,2,1,0:T(4,128)(2,1)}, bf16[96,1,4,256]{3,2,1,0:T(4,128)(2,1)S(1)}, u32[]{:S(2)}, u32[]{:S(2)}) collective-permute-start(bf16[96,1,4,256]{3,2,1,0:T(4,128)(2,1)} %refs_1_.1), channel_id=1, source_target_pairs={{0,2},{2,0},{1,3},{3,1},{4,6},{6,4},{5,7},{7,5},{8,10},{10,8},{9,1... | collective-permute-start | bytes 589832 | tf_op jit(solution)/shard_map/ppermute | solution.py:107
  1.1 1.6 %activate.1 = (bf16[96,1024]{1,0:T(8,128)(2,1)S(1)}, f32[96,1024]{1,0:T(8,128)S(1)}) custom-call(bf16[96,1,4,256]{3,2,1,0:T(4,128)(2,1)} %refs_0_.3, bf16[96,1,4,256]{3,2,1,0:T(4,128)(2,1)} %refs_1_.1), custom_call_target="tpu_custom_call" | custom-call | flops 1 | bytes 1 | tf_op jit(solution)/shard_map/activate/pallas_call | solution.py:146
  2.8 0.1 collective-permute-start
  2.9 3.0 %collective-permute-start.2 = (bf16[96,1024]{1,0:T(8,128)(2,1)S(1)}, bf16[96,1024]{1,0:T(8,128)(2,1)S(1)}, u32[]{:S(2)}, u32[]{:S(2)}) collective-permute-start(bf16[96,1024]{1,0:T(8,128)(2,1)S(1)} %get-tuple-element.21.refs_0_.refs_1_), channel_id=1, source_target_pairs={{0,4},{4,0},{8,12},{12,8},{1,5},{5,1},{9,13},{13,9},{2,6},{6,2},{1... | collective-permute-start | bytes 589832 | tf_op jit(solution)/shard_map/ppermute | solution.py:442
  5.9 2.6 %collective-permute-start.4 = (bf16[96,1024]{1,0:T(8,128)(2,1)S(1)}, bf16[96,1024]{1,0:T(8,128)(2,1)S(1)}, u32[]{:S(2)}, u32[]{:S(2)}) collective-permute-start(bf16[96,1024]{1,0:T(8,128)(2,1)S(1)} %get-tuple-element.21.refs_0_.refs_1_), channel_id=1, source_target_pairs={{0,8},{4,12},{8,0},{12,4},{1,9},{5,13},{9,1},{13,5},{2,10},{6,14},... | collective-permute-start | bytes 589832 | tf_op jit(solution)/shard_map/ppermute | solution.py:442
  8.5 0.0 collective-permute-done.1.refs_3_
  8.5 0.0 collective-permute-done.refs_1_.refs_2_
  8.5 2.0 %own_terms.1 = (bf16[336,384]{1,0:T(8,128)(2,1)S(1)}, bf16[432,2048]{1,0:T(8,128)(2,1)S(1)}, f32[96,2048]{1,0:T(8,128)S(1)}, bf16[2592,384]{1,0:T(8,128)(2,1)S(1)}) custom-call(bf16[96,1024]{1,0:T(8,128)(2,1)S(1)} %get-tuple-element.21.refs_0_.refs_1_, bf16[96,1024]{1,0:T(8,128)(2,1)S(1)} %collective-permute-done.refs_1_.refs_2_, ...), custom_call_target="tpu_custom_call" | custom-call | flops 1 | bytes 1 | tf_op jit(solution)/shard_map/own_terms/pallas_call | solution.py:146
  10.5 1.6 %collective-permute-start.7 = (bf16[336,384]{1,0:T(8,128)(2,1)S(1)}, bf16[336,384]{1,0:T(8,128)(2,1)S(1)}, u32[]{:S(2)}, u32[]{:S(2)}) collective-permute-start(bf16[336,384]{1,0:T(8,128)(2,1)S(1)} %get-tuple-element.26.refs_3_.refs_0_), channel_id=1, source_target_pairs={{0,1},{1,0},{2,3},{3,2},{4,5},{5,4},{6,7},{7,6},{8,9},{9,8},{10,11... | collective-permute-start | bytes 774152 | tf_op jit(solution)/shard_map/ppermute | solution.py:107
  12.1 3.2 %shares.1 = (f32[96,1024]{1,0:T(8,128)S(1)}, f32[96,1024]{1,0:T(8,128)S(1)}, bf16[96,1024]{1,0:T(8,128)(2,1)S(1)}, bf16[96,1024]{1,0:T(8,128)(2,1)S(1)}) custom-call(bf16[2592,384]{1,0:T(8,128)(2,1)S(1)} %get-tuple-element.23.refs_0_, f32[96,2048]{1,0:T(8,128)S(1)} %get-tuple-element.24.refs_1_, bf16[432,2048]{1,0:T(8,128)(2,1)S(1)} %get-tuple-element.25.refs_2_.refs_0_, ...), custom_call_target="tpu_custom_call" | custom-call | flops 1 | bytes 1 | tf_op jit(solution)/shard_map/shares/pallas_call | solution.py:146
  15.3 0.0 collective-permute-done.2.refs_0_
  15.3 0.1 collective-permute-start.3
  15.4 2.3 %collective-permute-done.4.refs_0_ = bf16[96,1024]{1,0:T(8,128)(2,1)S(1)} collective-permute-done((bf16[96,1024]{1,0:T(8,128)(2,1)S(1)}, bf16[96,1024]{1,0:T(8,128)(2,1)S(1)}, u32[]{:S(2)}, u32[]{:S(2)}) %collective-permute-start.4) | collective-permute-done | bytes 196640 | tf_op jit(solution)/shard_map/ppermute | solution.py:442
  17.7 0.5 %collective-permute-start.6 = (bf16[2,96,1024]{2,1,0:T(8,128)(2,1)S(1)}, bf16[2,96,1024]{2,1,0:T(8,128)(2,1)S(1)}, u32[]{:S(2)}, u32[]{:S(2)}) collective-permute-start(bf16[2,96,1024]{2,1,0:T(8,128)(2,1)S(1)} %get-tuple-element.30), channel_id=1, source_target_pairs={{0,4},{4,0},{8,12},{12,8},{1,5},{5,1},{9,13},{13,9},{2,6},{6,2},{1... | collective-permute-start | bytes 1179656 | tf_op jit(solution)/shard_map/ppermute | solution.py:442
  18.3 0.0 collective-permute-done.3.refs_2_.refs_4_
  18.3 0.0 collective-permute-done.7.refs_5_.refs_2_
  18.3 1.3 %terms_1.1.refs_3_.refs_1_ = bf16[336,384]{1,0:T(8,128)(2,1)S(1)} custom-call(bf16[432,2048]{1,0:T(8,128)(2,1)S(1)} %get-tuple-element.25.refs_2_.refs_0_, bf16[96,1024]{1,0:T(8,128)(2,1)S(1)} %hand_on.2.refs_1_.refs_3_, bf16[96,1024]{1,0:T(8,128)(2,1)S(1)} %collective-permute-done.3.refs_2_.refs_4_, ...), custom_call_target="tpu_custom_call" | custom-call | flops 1 | bytes 1 | tf_op jit(solution)/shard_map/terms_1/pallas_call | solution.py:146
  19.6 0.0 copy-start
  19.6 1.6 %collective-permute-start.8 = (bf16[336,384]{1,0:T(8,128)(2,1)S(1)}, bf16[336,384]{1,0:T(8,128)(2,1)S(1)}, u32[]{:S(2)}, u32[]{:S(2)}) collective-permute-start(bf16[336,384]{1,0:T(8,128)(2,1)S(1)} %terms_1.1.refs_3_.refs_1_), channel_id=1, source_target_pairs={{0,1},{1,0},{2,3},{3,2},{4,5},{5,4},{6,7},{7,6},{8,9},{9,8},{10,11... | collective-permute-start | bytes 774152 | tf_op jit(solution)/shard_map/ppermute | solution.py:107
  21.2 0.0 collective-permute-start.5
  21.2 1.4 %collective-permute-done.5.refs_2_.refs_6_ = bf16[96,1024]{1,0:T(8,128)(2,1)S(1)} collective-permute-done((bf16[96,1024]{1,0:T(8,128)(2,1)S(1)}, bf16[96,1024]{1,0:T(8,128)(2,1)S(1)}, u32[]{:S(2)}, u32[]{:S(2)}) %collective-permute-start.5) | collective-permute-done | bytes 196640 | tf_op jit(solution)/shard_map/ppermute | solution.py:107
  22.6 1.3 %terms_2.1.refs_1_.refs_0_ = bf16[336,384]{1,0:T(8,128)(2,1)S(1)} custom-call(bf16[432,2048]{1,0:T(8,128)(2,1)S(1)} %get-tuple-element.25.refs_2_.refs_0_, bf16[96,1024]{1,0:T(8,128)(2,1)S(1)} %get-tuple-element.29.refs_4_.refs_1_.refs_5_, bf16[96,1024]{1,0:T(8,128)(2,1)S(1)} %collective-permute-done.5.refs_2_.refs_6_, ...), custom_call_target="tpu_custom_call" | custom-call | flops 1 | bytes 1 | tf_op jit(solution)/shard_map/terms_2/pallas_call | solution.py:146
  24.0 0.6 %collective-permute-start.10 = (bf16[336,384]{1,0:T(8,128)(2,1)S(1)}, bf16[336,384]{1,0:T(8,128)(2,1)S(1)}, u32[]{:S(2)}, u32[]{:S(2)}) collective-permute-start(bf16[336,384]{1,0:T(8,128)(2,1)S(1)} %terms_2.1.refs_1_.refs_0_), channel_id=1, source_target_pairs={{0,1},{1,0},{2,3},{3,2},{4,5},{5,4},{6,7},{7,6},{8,9},{9,8},{10,11... | collective-permute-start | bytes 774152 | tf_op jit(solution)/shard_map/ppermute | solution.py:107
  24.6 0.0 copy-done
  24.6 0.3 slope.1.refs_1_.refs_0_
  24.8 2.2 %collective-permute-done.6.refs_0_ = bf16[2,96,1024]{2,1,0:T(8,128)(2,1)S(1)} collective-permute-done((bf16[2,96,1024]{2,1,0:T(8,128)(2,1)S(1)}, bf16[2,96,1024]{2,1,0:T(8,128)(2,1)S(1)}, u32[]{:S(2)}, u32[]{:S(2)}) %collective-permute-start.6) | collective-permute-done | bytes 393248 | tf_op jit(solution)/shard_map/ppermute | solution.py:442
  27.0 0.0 collective-permute-done.8.refs_2_.refs_3_
  27.1 0.1 collective-permute-start.9
  27.2 2.1 %collective-permute-start.11 = (bf16[96,1024]{1,0:T(8,128)(2,1)S(1)}, bf16[96,1024]{1,0:T(8,128)(2,1)S(1)}, u32[]{:S(2)}, u32[]{:S(2)}) collective-permute-start(bf16[96,1024]{1,0:T(8,128)(2,1)S(1)} %carry_share.1.refs_3_), channel_id=1, source_target_pairs={{0,8},{4,12},{8,0},{12,4},{1,9},{5,13},{9,1},{13,5},{2,10},{6,14},... | collective-permute-start | bytes 589832 | tf_op jit(solution)/shard_map/ppermute | solution.py:442
  29.3 0.0 collective-permute-done.9.refs_2_.refs_8_
  29.3 1.5 %terms_3.1.refs_9_.refs_4_.refs_1_ = bf16[336,384]{1,0:T(8,128)(2,1)S(1)} custom-call(bf16[432,2048]{1,0:T(8,128)(2,1)S(1)} %get-tuple-element.25.refs_2_.refs_0_, bf16[96,1024]{1,0:T(8,128)(2,1)S(1)} %get-tuple-element.31.refs_1_.refs_7_, bf16[96,1024]{1,0:T(8,128)(2,1)S(1)} %collective-permute-done.9.refs_2_.refs_8_, bf16[96,1024]{1,0:T(8,128)(2,1)S(1)} %carry_share.1.refs_3_), custom_call_target="tpu_custom_call" | custom-call | flops 1 | bytes 1 | tf_op jit(solution)/shard_map/terms_3/pallas_call | solution.py:146
  30.8 2.2 %collective-permute-start.14 = (bf16[336,384]{1,0:T(8,128)(2,1)S(1)}, bf16[336,384]{1,0:T(8,128)(2,1)S(1)}, u32[]{:S(2)}, u32[]{:S(2)}) collective-permute-start(bf16[336,384]{1,0:T(8,128)(2,1)S(1)} %terms_3.1.refs_9_.refs_4_.refs_1_), channel_id=1, source_target_pairs={{0,1},{1,0},{2,3},{3,2},{4,5},{5,4},{6,7},{7,6},{8,9},{9,8},{10,11... | collective-permute-start | bytes 774152 | tf_op jit(solution)/shard_map/ppermute | solution.py:107
  33.0 1.1 %collective-permute-start.12 = (bf16[96,1024]{1,0:T(8,128)(2,1)S(1)}, bf16[96,1024]{1,0:T(8,128)(2,1)S(1)}, u32[]{:S(2)}, u32[]{:S(2)}) collective-permute-start(bf16[96,1024]{1,0:T(8,128)(2,1)S(1)} %hand_on.3), channel_id=1, source_target_pairs={{0,4},{4,0},{8,12},{12,8},{1,5},{5,1},{9,13},{13,9},{2,6},{6,2},{1... | collective-permute-start | bytes 589832 | tf_op jit(solution)/shard_map/ppermute | solution.py:442
  34.1 0.1 sums_0.1.refs_3_.refs_0_
  34.3 0.1 collective-permute-start.13
  34.3 0.0 collective-permute-done.10.refs_10_.refs_2_
  34.4 4.1 %conv.1 = (bf16[96,1,4,256]{3,2,1,0:T(4,128)(2,1)}, f32[8,128]{1,0:T(8,128)S(1)}) custom-call(bf16[2592,384]{1,0:T(8,128)(2,1)S(1)} %get-tuple-element.23.refs_0_, bf16[96,1024]{1,0:T(8,128)(2,1)S(1)} %get-tuple-element.21.refs_0_.refs_1_, bf16[96,1024]{1,0:T(8,128)(2,1)S(1)} %collective-permute-done.refs_1_.refs_2_, ...), custom_call_target="tpu_custom_call" | custom-call | flops 1 | bytes 1 | tf_op jit(solution)/shard_map/conv/pallas_call | solution.py:146
  38.5 1.3 %collective-permute-done.11.refs_1_ = bf16[96,1024]{1,0:T(8,128)(2,1)S(1)} collective-permute-done((bf16[96,1024]{1,0:T(8,128)(2,1)S(1)}, bf16[96,1024]{1,0:T(8,128)(2,1)S(1)}, u32[]{:S(2)}, u32[]{:S(2)}) %collective-permute-start.11) | collective-permute-done | bytes 196640 | tf_op jit(solution)/shard_map/ppermute | solution.py:442
  39.8 3.2 %collective-permute-done.12.refs_2_ = bf16[96,1024]{1,0:T(8,128)(2,1)S(1)} collective-permute-done((bf16[96,1024]{1,0:T(8,128)(2,1)S(1)}, bf16[96,1024]{1,0:T(8,128)(2,1)S(1)}, u32[]{:S(2)}, u32[]{:S(2)}) %collective-permute-start.12) | collective-permute-done | bytes 196640 | tf_op jit(solution)/shard_map/ppermute | solution.py:442
  43.0 1.0 %feature_grad.1 = (bf16[96,1,4,256]{3,2,1,0:T(4,128)(2,1)}, f32[8,128]{1,0:T(8,128)S(1)}) custom-call(f32[96,1024]{1,0:T(8,128)S(1)} %slope.1.refs_1_.refs_0_, f32[96,1024]{1,0:T(8,128)S(1)} %gather_share.1.refs_1_, bf16[96,1024]{1,0:T(8,128)(2,1)S(1)} %collective-permute-done.12.refs_2_), custom_call_target="tpu_custom_call" | custom-call | flops 3000000000 | bytes 1 | tf_op jit(solution)/shard_map/feature_grad/pallas_call | solution.py:146
  44.0 0.0 collective-permute-done.14.refs_3_
  44.0 0.1 sums_2.1.refs_1_
  44.1 0.1 collective-permute-start.15
  44.2 1.5 %kernel_grad_0.1.refs_2_ = f32[3,864,384]{2,1,0:T(8,128)} custom-call(bf16[672,384]{1,0:T(8,128)(2,1)S(1)} %sums_0.1.refs_3_.refs_0_, bf16[672,384]{1,0:T(8,128)(2,1)S(1)} %sums_2.1.refs_1_), custom_call_target="tpu_custom_call" | custom-call | flops 1 | bytes 1 | tf_op jit(solution)/shard_map/kernel_grad_0/pallas_call | solution.py:146
  45.7 0.0 collective-permute-done.13.refs_0_
  45.7 0.4 collective-permute-done.15.refs_1_
  46.1 1.5 %kernel_grad_1.1 = f32[3,864,384]{2,1,0:T(8,128)} custom-call(bf16[672,384]{1,0:T(8,128)(2,1)S(1)} %collective-permute-done.13.refs_0_, bf16[672,384]{1,0:T(8,128)(2,1)S(1)} %collective-permute-done.15.refs_1_, f32[3,864,384]{2,1,0:T(8,128)} %kernel_grad_0.1.refs_2_), custom_call_target="tpu_custom_call", output_to_operand_aliasing={{}: (2, {})} | custom-call | flops 1 | bytes 1 | tf_op jit(solution)/shard_map/kernel_grad_1/pallas_call | solution.py:146
  (6 shorter events, 0.1 us)
Async XLA Ops:
  0.6 7.9 %collective-permute-start.1 = (bf16[96,1,4,256]{3,2,1,0:T(4,128)(2,1)}, bf16[96,1,4,256]{3,2,1,0:T(4,128)(2,1)S(1)}, u32[]{:S(2)}, u32[]{:S(2)}) collective-permute-start(bf16[96,1,4,256]{3,2,1,0:T(4,128)(2,1)} %refs_1_.1), channel_id=1, source_target_pairs={{0,2},{2,0},{1,3},{3,1},{4,6},{6,4},{5,7},{7,5},{8,10},{10,8},{9,1... | collective-permute-start | bytes 589832 | tf_op jit(solution)/shard_map/ppermute | solution.py:107
  2.8 5.7 %collective-permute-start = (bf16[96,1024]{1,0:T(8,128)(2,1)S(1)}, bf16[96,1024]{1,0:T(8,128)(2,1)S(1)}, u32[]{:S(2)}, u32[]{:S(2)}) collective-permute-start(bf16[96,1024]{1,0:T(8,128)(2,1)S(1)} %get-tuple-element.21.refs_0_.refs_1_), channel_id=1, source_target_pairs={{0,2},{2,0},{1,3},{3,1},{4,6},{6,4},{5,7},{7,5},{8,10},{10,8},{9,1... | collective-permute-start | bytes 589832 | tf_op jit(solution)/shard_map/ppermute | solution.py:107
  2.9 12.4 %collective-permute-start.2 = (bf16[96,1024]{1,0:T(8,128)(2,1)S(1)}, bf16[96,1024]{1,0:T(8,128)(2,1)S(1)}, u32[]{:S(2)}, u32[]{:S(2)}) collective-permute-start(bf16[96,1024]{1,0:T(8,128)(2,1)S(1)} %get-tuple-element.21.refs_0_.refs_1_), channel_id=1, source_target_pairs={{0,4},{4,0},{8,12},{12,8},{1,5},{5,1},{9,13},{13,9},{2,6},{6,2},{1... | collective-permute-start | bytes 589832 | tf_op jit(solution)/shard_map/ppermute | solution.py:442
  5.9 11.8 %collective-permute-start.4 = (bf16[96,1024]{1,0:T(8,128)(2,1)S(1)}, bf16[96,1024]{1,0:T(8,128)(2,1)S(1)}, u32[]{:S(2)}, u32[]{:S(2)}) collective-permute-start(bf16[96,1024]{1,0:T(8,128)(2,1)S(1)} %get-tuple-element.21.refs_0_.refs_1_), channel_id=1, source_target_pairs={{0,8},{4,12},{8,0},{12,4},{1,9},{5,13},{9,1},{13,5},{2,10},{6,14},... | collective-permute-start | bytes 589832 | tf_op jit(solution)/shard_map/ppermute | solution.py:442
  10.5 7.7 %collective-permute-start.7 = (bf16[336,384]{1,0:T(8,128)(2,1)S(1)}, bf16[336,384]{1,0:T(8,128)(2,1)S(1)}, u32[]{:S(2)}, u32[]{:S(2)}) collective-permute-start(bf16[336,384]{1,0:T(8,128)(2,1)S(1)} %get-tuple-element.26.refs_3_.refs_0_), channel_id=1, source_target_pairs={{0,1},{1,0},{2,3},{3,2},{4,5},{5,4},{6,7},{7,6},{8,9},{9,8},{10,11... | collective-permute-start | bytes 774152 | tf_op jit(solution)/shard_map/ppermute | solution.py:107
  15.3 2.9 %collective-permute-start.3 = (bf16[96,1024]{1,0:T(8,128)(2,1)S(1)}, bf16[96,1024]{1,0:T(8,128)(2,1)S(1)}, u32[]{:S(2)}, u32[]{:S(2)}) collective-permute-start(bf16[96,1024]{1,0:T(8,128)(2,1)S(1)} %hand_on.2.refs_1_.refs_3_), channel_id=1, source_target_pairs={{0,2},{2,0},{1,3},{3,1},{4,6},{6,4},{5,7},{7,5},{8,10},{10,8},{9,1... | collective-permute-start | bytes 589832 | tf_op jit(solution)/shard_map/ppermute | solution.py:107
  17.7 9.3 %collective-permute-start.6 = (bf16[2,96,1024]{2,1,0:T(8,128)(2,1)S(1)}, bf16[2,96,1024]{2,1,0:T(8,128)(2,1)S(1)}, u32[]{:S(2)}, u32[]{:S(2)}) collective-permute-start(bf16[2,96,1024]{2,1,0:T(8,128)(2,1)S(1)} %get-tuple-element.30), channel_id=1, source_target_pairs={{0,4},{4,0},{8,12},{12,8},{1,5},{5,1},{9,13},{13,9},{2,6},{6,2},{1... | collective-permute-start | bytes 1179656 | tf_op jit(solution)/shard_map/ppermute | solution.py:442
  19.6 5.0 %copy-start = (bf16[96,1,4,256]{3,2,1,0:T(4,128)(2,1)S(1)}, bf16[96,1,4,256]{3,2,1,0:T(4,128)(2,1)}, u32[]{:S(2)}) copy-start(bf16[96,1,4,256]{3,2,1,0:T(4,128)(2,1)} %refs_0_.3) | copy-start | bytes 589828
  19.6 7.4 %collective-permute-start.8 = (bf16[336,384]{1,0:T(8,128)(2,1)S(1)}, bf16[336,384]{1,0:T(8,128)(2,1)S(1)}, u32[]{:S(2)}, u32[]{:S(2)}) collective-permute-start(bf16[336,384]{1,0:T(8,128)(2,1)S(1)} %terms_1.1.refs_3_.refs_1_), channel_id=1, source_target_pairs={{0,1},{1,0},{2,3},{3,2},{4,5},{5,4},{6,7},{7,6},{8,9},{9,8},{10,11... | collective-permute-start | bytes 774152 | tf_op jit(solution)/shard_map/ppermute | solution.py:107
  21.2 1.4 %collective-permute-start.5 = (bf16[96,1024]{1,0:T(8,128)(2,1)S(1)}, bf16[96,1024]{1,0:T(8,128)(2,1)S(1)}, u32[]{:S(2)}, u32[]{:S(2)}) collective-permute-start(bf16[96,1024]{1,0:T(8,128)(2,1)S(1)} %get-tuple-element.29.refs_4_.refs_1_.refs_5_), channel_id=1, source_target_pairs={{0,2},{2,0},{1,3},{3,1},{4,6},{6,4},{5,7},{7,5},{8,10},{10,8},{9,1... | collective-permute-start | bytes 589832 | tf_op jit(solution)/shard_map/ppermute | solution.py:107
  24.0 10.4 %collective-permute-start.10 = (bf16[336,384]{1,0:T(8,128)(2,1)S(1)}, bf16[336,384]{1,0:T(8,128)(2,1)S(1)}, u32[]{:S(2)}, u32[]{:S(2)}) collective-permute-start(bf16[336,384]{1,0:T(8,128)(2,1)S(1)} %terms_2.1.refs_1_.refs_0_), channel_id=1, source_target_pairs={{0,1},{1,0},{2,3},{3,2},{4,5},{5,4},{6,7},{7,6},{8,9},{9,8},{10,11... | collective-permute-start | bytes 774152 | tf_op jit(solution)/shard_map/ppermute | solution.py:107
  27.1 2.3 %collective-permute-start.9 = (bf16[96,1024]{1,0:T(8,128)(2,1)S(1)}, bf16[96,1024]{1,0:T(8,128)(2,1)S(1)}, u32[]{:S(2)}, u32[]{:S(2)}) collective-permute-start(bf16[96,1024]{1,0:T(8,128)(2,1)S(1)} %get-tuple-element.31.refs_1_.refs_7_), channel_id=1, source_target_pairs={{0,2},{2,0},{1,3},{3,1},{4,6},{6,4},{5,7},{7,5},{8,10},{10,8},{9,1... | collective-permute-start | bytes 589832 | tf_op jit(solution)/shard_map/ppermute | solution.py:107
  27.2 12.6 %collective-permute-start.11 = (bf16[96,1024]{1,0:T(8,128)(2,1)S(1)}, bf16[96,1024]{1,0:T(8,128)(2,1)S(1)}, u32[]{:S(2)}, u32[]{:S(2)}) collective-permute-start(bf16[96,1024]{1,0:T(8,128)(2,1)S(1)} %carry_share.1.refs_3_), channel_id=1, source_target_pairs={{0,8},{4,12},{8,0},{12,4},{1,9},{5,13},{9,1},{13,5},{2,10},{6,14},... | collective-permute-start | bytes 589832 | tf_op jit(solution)/shard_map/ppermute | solution.py:442
  30.8 13.1 %collective-permute-start.14 = (bf16[336,384]{1,0:T(8,128)(2,1)S(1)}, bf16[336,384]{1,0:T(8,128)(2,1)S(1)}, u32[]{:S(2)}, u32[]{:S(2)}) collective-permute-start(bf16[336,384]{1,0:T(8,128)(2,1)S(1)} %terms_3.1.refs_9_.refs_4_.refs_1_), channel_id=1, source_target_pairs={{0,1},{1,0},{2,3},{3,2},{4,5},{5,4},{6,7},{7,6},{8,9},{9,8},{10,11... | collective-permute-start | bytes 774152 | tf_op jit(solution)/shard_map/ppermute | solution.py:107
  33.0 10.0 %collective-permute-start.12 = (bf16[96,1024]{1,0:T(8,128)(2,1)S(1)}, bf16[96,1024]{1,0:T(8,128)(2,1)S(1)}, u32[]{:S(2)}, u32[]{:S(2)}) collective-permute-start(bf16[96,1024]{1,0:T(8,128)(2,1)S(1)} %hand_on.3), channel_id=1, source_target_pairs={{0,4},{4,0},{8,12},{12,8},{1,5},{5,1},{9,13},{13,9},{2,6},{6,2},{1... | collective-permute-start | bytes 589832 | tf_op jit(solution)/shard_map/ppermute | solution.py:442
  34.3 11.4 %collective-permute-start.13 = (bf16[672,384]{1,0:T(8,128)(2,1)S(1)}, bf16[672,384]{1,0:T(8,128)(2,1)S(1)}, u32[]{:S(2)}, u32[]{:S(2)}) collective-permute-start(bf16[672,384]{1,0:T(8,128)(2,1)S(1)} %sums_0.1.refs_3_.refs_0_), channel_id=1, source_target_pairs={{0,2},{2,0},{1,3},{3,1},{4,6},{6,4},{5,7},{7,5},{8,10},{10,8},{9,1... | collective-permute-start | bytes 1548296 | tf_op jit(solution)/shard_map/ppermute | solution.py:107
  44.1 2.0 %collective-permute-start.15 = (bf16[672,384]{1,0:T(8,128)(2,1)S(1)}, bf16[672,384]{1,0:T(8,128)(2,1)S(1)}, u32[]{:S(2)}, u32[]{:S(2)}) collective-permute-start(bf16[672,384]{1,0:T(8,128)(2,1)S(1)} %sums_2.1.refs_1_), channel_id=1, source_target_pairs={{0,2},{2,0},{1,3},{3,1},{4,6},{6,4},{5,7},{7,5},{8,10},{10,8},{9,1... | collective-permute-start | bytes 1548296 | tf_op jit(solution)/shard_map/ppermute | solution.py:107
